TPU v7x, 128 devices: a whole 4x4x4 slice. The times are simulated.
128 devices in a mesh: dp: 16 (over x, y), tp: 8 (over z, core).
Axes of the slice: x: 4, y: 4, z: 4, core: 2. Of those that a mesh axis runs over, the one named last changes fastest.
Arguments:
- hidden: bfloat16 [32768, 8192], P('dp', 'tp'), may hold values from -6 to 6
- value_weight: bfloat16 [8192, 1024], P('tp'), may hold values from -0.0625 to 0.0625
- down_weights: bfloat16 [2048, 64, 8192], P('dp', None, 'tp'), may hold values from -0.0625 to 0.0625
- up_weights: bfloat16 [2048, 64, 1024], P('dp', None, 'tp'), may hold values from -0.75 to 0.75
- group_adapter_id: int32 [512], replicated, may hold values from 0 to 2047, as said below
- adapter_storage_row: int32 [2048], replicated, may hold values from 0 to 2047, as said below
- group_live_count: int32 [512], replicated, may hold values from 1 to 64, as said below
Outputs:
- projected: bfloat16 [32768, 1024], P('dp', 'tp')
Inputs may be any that keep to these rules, and one draw needn't show every extreme that they name: Adapter a is stored at row adapter_storage_row[a] of down_weights and up_weights, that is on index adapter_storage_row[a] // 128 of dp; a permutation. `group_adapter_id`: the 32 groups of one index of dp name different adapters; at most 6 of them are stored on one index of dp, and some index of dp stores exactly 6 of every index's groups. `group_live_count`: slots of a group at and beyond its count are padding; every index of dp has a group of 64 live slots.
All inputs are finite; a program needn't handle non-finite values.
Results may differ from a plain program's by a relative error of at most 0.0029.
Values may be sent and summed in bfloat16 or wider, within the bound.
No kernel may reach another device: no remote copies, remote signals or barrier semaphores. Data moves between devices by JAX's collectives and lax.ppermute only.
A program may use at most 192 MiB of HBM per device.

v0:
```python
import jax
import jax.numpy as jnp
from jax import lax
from jax.sharding import PartitionSpec as P

ADAPTER_SCALE = 0.5


def on_device(
    hidden,
    value_weight,
    down_weights,
    up_weights,
    group_adapter_id,
    adapter_storage_row,
    group_live_count,
):
    dp_count = lax.axis_size("dp")
    my_index = lax.axis_index("dp")
    owned_count = down_weights.shape[0]
    request_groups = group_adapter_id.shape[0] // dp_count
    batch_rows, width = hidden.shape
    capacity_rows = batch_rows // request_groups
    per_peer = 3 * request_groups // dp_count
    stored = adapter_storage_row[group_adapter_id]
    owners = (stored // owned_count).reshape(dp_count, request_groups)
    slot_pos = (stored % owned_count).reshape(dp_count, request_groups)
    positions = jnp.arange(request_groups)
    same_owner = owners[:, :, None] == owners[:, None, :]
    earlier = positions[None, None, :] < positions[None, :, None]
    ranking = jnp.sum(same_owner & earlier, axis=2)
    peer_slots = jnp.arange(per_peer)
    matches = (owners == my_index)[:, :, None] & (ranking[:, :, None] == peer_slots[None, None, :])
    served_rows = jnp.sum(jnp.where(matches, slot_pos[:, :, None], 0), axis=1)
    my_owners = lax.dynamic_index_in_dim(owners, my_index, 0, keepdims=False)
    my_ranking = lax.dynamic_index_in_dim(ranking, my_index, 0, keepdims=False)
    picked = my_owners * per_peer + my_ranking
    grouped = hidden.reshape(request_groups, capacity_rows, width)
    counts = lax.dynamic_slice_in_dim(group_live_count, my_index * request_groups, request_groups)
    active_rows = jnp.arange(capacity_rows)[None, :, None] < counts[:, None, None]
    base_terms = jnp.dot(hidden, value_weight, preferred_element_type=jnp.float32)
    base_output = lax.psum_scatter(base_terms, "tp", scatter_dimension=1, tiled=True)
    down_sent = down_weights[served_rows]
    up_sent = up_weights[served_rows]
    a_arrived, b_arrived = (
        lax.all_to_all(down_sent, "dp", split_axis=0, concat_axis=0, tiled=True),
        lax.all_to_all(up_sent, "dp", split_axis=0, concat_axis=0, tiled=True),
    )
    a_mine = a_arrived.reshape(dp_count * per_peer, a_arrived.shape[2], width)[picked]
    b_mine = b_arrived.reshape(dp_count * per_peer, b_arrived.shape[2], b_arrived.shape[3])[picked]
    partial_value = jnp.einsum("gcd,grd->gcr", grouped, a_mine, preferred_element_type=jnp.float32)
    summed = lax.psum(partial_value, "tp").astype(jnp.bfloat16)
    adapter_delta_rows = jnp.einsum(
        "gcr,grv->gcv", summed, b_mine, preferred_element_type=jnp.float32
    )
    merged_output = (
        base_output.reshape(request_groups, capacity_rows, -1) + ADAPTER_SCALE * adapter_delta_rows
    )
    finished = jnp.where(active_rows, merged_output, jnp.float32(0.0)).astype(jnp.bfloat16)
    return finished.reshape(batch_rows, -1)


def solution(mesh):
    return jax.shard_map(
        on_device,
        mesh=mesh,
        in_specs=(
            P("dp", "tp"),
            P("tp", None),
            P("dp", None, "tp"),
            P("dp", None, "tp"),
            P(),
            P(),
            P(),
        ),
        out_specs=P("dp", "tp"),
        check_vma=False,
    )
```

profile of v0, /device:TPU:1, one launch (start us, length us, event | category | flops | bytes accessed | tf_op | source)
XLA Modules:
  0.0 333.8 jit_solution(11740314920742992087)
XLA Ops:
  6.5 0.0 copy-start
  6.5 0.0 reduce-scatter.2.cloned.1.call-start
  6.5 1.6 copy-done
  8.1 8.9 %fusion.8 = f32[2048,1024]{1,0:T(8,128)} fusion(bf16[2048,1024]{1,0:T(8,128)(2,1)} %param.7, bf16[1024,1024]{1,0:T(8,128)(2,1)S(1)} %copy-done), kind=kOutput, calls=%fused_computation.33 | convolution fusion | flops 4294967296 | bytes 14680064 | tf_op jit(solution)/shard_map/dot_general | solution.py:41
  17.1 0.0 copy-start.3
  17.1 0.0 copy-start.2
  17.1 0.0 reduce-scatter.2.cloned.1.call-update
  17.1 0.6 copy-done.3
  17.8 0.0 copy-done.2
  17.8 3.1 gather_fusion
  20.9 0.1 gather.18
  21.0 0.5 convert_reduce_fusion
  21.5 0.2 select_reduce_fusion
  21.7 0.1 copy.10
  21.8 0.1 reshape.205
  21.9 3.5 %gather_fusion.3 = bf16[96,64,128]{2,1,0:T(8,128)(2,1)} fusion(bf16[128,64,128]{2,1,0:T(8,128)(2,1)} %param.10, s32[1024]{0:T(1024)S(1)} %pad_clamp_fusion.1), kind=kCustom, calls=%fused_computation.3 | custom fusion | bytes 3146112 | tf_op jit(solution)/shard_map/gather | solution.py:44
  25.4 7.6 %all-to-all-start.1 = ((bf16[16,6,64,128]{3,2,1,0:T(8,128)(2,1)}), bf16[16,6,64,128]{3,2,1,0:T(8,128)(2,1)S(1)}, u32[]{:S(2)}, u32[]{:S(2)}) async-start(bf16[16,6,64,128]{3,2,1,0:T(8,128)(2,1)} %bitcast.8), calls=%async_computation.2 | async-start | bytes 3145728 | tf_op jit(solution)/shard_map/all_to_all | solution.py:47
  33.0 12.8 %gather_fusion.1 = bf16[96,64,1024]{2,1,0:T(8,128)(2,1)} fusion(bf16[128,64,1024]{2,1,0:T(8,128)(2,1)} %param.9, s32[1024]{0:T(1024)S(1)} %pad_clamp_fusion.1), kind=kCustom, calls=%fused_computation.1 | custom fusion | bytes 25166208 | tf_op jit(solution)/shard_map/gather | solution.py:43
  45.8 7.8 %all-to-all-done.1 = bf16[16,6,64,128]{3,2,1,0:T(8,128)(2,1)S(1)} async-done(((bf16[16,6,64,128]{3,2,1,0:T(8,128)(2,1)}), bf16[16,6,64,128]{3,2,1,0:T(8,128)(2,1)S(1)}, u32[]{:S(2)}, u32[]{:S(2)}) %all-to-all-start.1) | async-done | bytes 1572896 | tf_op jit(solution)/shard_map/all_to_all | solution.py:47
  53.6 5.4 %all-to-all-start = ((bf16[16,6,64,1024]{3,2,1,0:T(8,128)(2,1)}), bf16[16,6,64,1024]{3,2,1,0:T(8,128)(2,1)}, u32[]{:S(2)}, u32[]{:S(2)}) async-start(bf16[16,6,64,1024]{3,2,1,0:T(8,128)(2,1)} %bitcast.23), calls=%async_computation.1 | async-start | bytes 25165824 | tf_op jit(solution)/shard_map/all_to_all | solution.py:46
  59.0 0.8 dynamic_slice.10
  59.8 0.1 iota_compare_fusion.2
  59.9 1.4 gather_fusion.4
  61.3 192.1 %all-to-all-done = bf16[16,6,64,1024]{3,2,1,0:T(8,128)(2,1)} async-done(((bf16[16,6,64,1024]{3,2,1,0:T(8,128)(2,1)}), bf16[16,6,64,1024]{3,2,1,0:T(8,128)(2,1)}, u32[]{:S(2)}, u32[]{:S(2)}) %all-to-all-start) | async-done | bytes 12582944 | tf_op jit(solution)/shard_map/all_to_all | solution.py:46
  253.4 7.3 %gather_fusion.2 = bf16[32,64,1024]{2,1,0:T(8,128)(2,1)} fusion(bf16[96,64,1024]{2,1,0:T(8,128)(2,1)} %bitcast.3, s32[1024]{0:T(1024)S(1)} %pad_clamp_fusion), kind=kCustom, calls=%fused_computation.2 | custom fusion | bytes 8388736 | tf_op jit(solution)/shard_map/gather | solution.py:49
  260.7 0.0 copy-start.1
  260.7 4.8 %convolution_bitcast_fusion = f32[32,64,64]{1,2,0:T(8,128)S(1)} fusion(bf16[32,64,1024]{2,1,0:T(8,128)(2,1)} %gather_fusion.2, bf16[32,64,1024]{2,1,0:T(8,128)(2,1)} %bitcast.24), kind=kOutput, calls=%fused_computation.8 | convolution fusion | flops 268435456 | bytes 8912896 | tf_op jit(solution)/shard_map/gcd,grd->gcr/dot_general | solution.py:51
  265.6 58.5 %all-reduce.1 = bf16[32,64,64]{1,2,0:T(8,128)(2,1)} all-reduce(f32[32,64,64]{1,2,0:T(8,128)S(1)} %convolution_bitcast_fusion), channel_id=1, replica_groups=mesh['dp'=16,'tp'=8] {'tp'}, use_global_device_ids=true, to_apply=%region_3.4 | all-reduce | flops 131072 | bytes 786432 | tf_op jit(solution)/shard_map/psum | solution.py:52
  324.0 0.0 reduce-scatter.2.cloned.1.call-done
  324.0 2.9 fusion.2
  326.9 0.0 copy-done.1
  (9 shorter events, 0.1 us)
Async XLA Ops:
  6.5 1.6 copy-start
  6.5 317.5 %reduce-scatter.2.cloned.1.call-start = ((), (), s32[]{:S(2)}) async-start(), calls=%async_computation.3 | async-start | bytes 9437184 | tf_op jit(solution)/shard_map/reduce_scatter | solution.py:42
  17.1 0.7 copy-start.3
  17.1 0.7 copy-start.2
  25.4 28.2 %all-to-all-start.1 = ((bf16[16,6,64,128]{3,2,1,0:T(8,128)(2,1)}), bf16[16,6,64,128]{3,2,1,0:T(8,128)(2,1)S(1)}, u32[]{:S(2)}, u32[]{:S(2)}) async-start(bf16[16,6,64,128]{3,2,1,0:T(8,128)(2,1)} %bitcast.8), calls=%async_computation.2 | async-start | bytes 3145728 | tf_op jit(solution)/shard_map/all_to_all | solution.py:47
  53.6 199.7 %all-to-all-start = ((bf16[16,6,64,1024]{3,2,1,0:T(8,128)(2,1)}), bf16[16,6,64,1024]{3,2,1,0:T(8,128)(2,1)}, u32[]{:S(2)}, u32[]{:S(2)}) async-start(bf16[16,6,64,1024]{3,2,1,0:T(8,128)(2,1)} %bitcast.23), calls=%async_computation.1 | async-start | bytes 25165824 | tf_op jit(solution)/shard_map/all_to_all | solution.py:46
  260.7 66.2 %copy-start.1 = (bf16[1024,1024]{1,0:T(8,128)(2,1)S(1)}, bf16[1024,1024]{1,0:T(8,128)(2,1)}, u32[]{:S(2)}) copy-start(bf16[1024,1024]{1,0:T(8,128)(2,1)} %param.8) | copy-start | bytes 6291460
Sparse Core Ops, SparseCore 0:
  17.2 55.1 reduce-scatter.1
where the time goes:
time: 338 us; the launch traced here: 334 us
  waiting for transfers between devices  200 us (59%)
  blocking collectives  58.5 us (17%)
  local copies, waits for them, and re-layouts  31.5 us (9%)
  matrix products  16.6 us (5%)
  between operations  13.5 us (4%)
  starting transfers between devices  13 us (4%)
    all_to_all x1, waiting for transfers between devices, on_device(): lax.all_to_all(down_sent, 'dp', split_axis=0, concat_axis=0, tiled=True)  192 us
    psum x1, blocking collectives, on_device(): summed = lax.psum(partial_value, 'tp').astype(jnp.bfloat16)  58.5 us
    gather x1, local copies, waits for them, and re-layouts, on_device(): down_sent = down_weights[served_rows]  12.8 us
    dot_general x1, matrix products, on_device(): jnp.dot(hidden, value_weight, preferred_element_type=jnp.float32)  8.93 us
    all_to_all x1, waiting for transfers between devices, on_device(): lax.all_to_all(up_sent, 'dp', split_axis=0, concat_axis=0, tiled=True)  7.8 us
    all_to_all x1, starting transfers between devices, on_device(): lax.all_to_all(up_sent, 'dp', split_axis=0, concat_axis=0, tiled=True)  7.58 us
    gather x1, local copies, waits for them, and re-layouts, on_device(): a_arrived.reshape(dp_count * per_peer, a_arrived.shape[2], width)[picked]  7.34 us
  transfers between devices with their start and end apart: 3, of which 2 were waited for; matrix products, arithmetic and copies ran while one was open for 10% of the time, Pallas kernels for 0%

commit v1 on v0

v1 whole, which is shorter than its diff:
```python
import jax
import jax.numpy as jnp
from jax import lax
from jax.sharding import PartitionSpec as P

ADAPTER_SCALE = 0.5
MAIN = 2
MOST = 6
EXTRA = MOST - MAIN


def low_rank_sum(partial):
    rows, rank = partial.shape
    tp_count = lax.axis_size("tp")
    pieces = lax.all_to_all(partial, "tp", split_axis=0, concat_axis=0, tiled=True)
    mine = jnp.sum(pieces.reshape(tp_count, rows // tp_count, rank), axis=0).astype(jnp.bfloat16)
    return lax.all_gather(mine, "tp", axis=0, tiled=True)


def finish(base, low, ups, counts):
    groups = counts.shape[0]
    cap = base.shape[0] // groups
    delta = jnp.einsum(
        "gcr,grv->gcv", low.reshape(groups, cap, -1), ups, preferred_element_type=jnp.float32
    )
    merged = base.reshape(groups, cap, -1) + ADAPTER_SCALE * delta
    active = jnp.arange(cap)[None, :, None] < counts[:, None, None]
    out = jnp.where(active, merged, jnp.float32(0.0)).astype(jnp.bfloat16)
    return out.reshape(base.shape)


def packed(down, up):
    count = down.shape[0]
    up_rows = up.reshape(count, 8, 8, up.shape[2]).transpose(0, 2, 1, 3)
    return jnp.concatenate([down, up_rows.reshape(count, 8, -1)], axis=1)


def unpacked(rows, rank):
    count = rows.shape[0]
    up = rows[:, rank:].reshape(count, 8, 8, -1).transpose(0, 2, 1, 3)
    return rows[:, :rank], up.reshape(count, rank, -1)


def on_device(
    hidden,
    value_weight,
    down_weights,
    up_weights,
    group_adapter_id,
    adapter_storage_row,
    group_live_count,
):
    dp_count = lax.axis_size("dp")
    me = lax.axis_index("dp")
    owned, rank, width = down_weights.shape
    groups = group_adapter_id.shape[0] // dp_count
    cap = hidden.shape[0] // groups
    stored = adapter_storage_row[group_adapter_id]
    owners = (stored // owned).reshape(dp_count, groups)
    slots = (stored % owned).reshape(dp_count, groups)
    same = owners[:, :, None] == owners[:, None, :]
    earlier = jnp.arange(groups)[None, None, :] < jnp.arange(groups)[None, :, None]
    ranking = jnp.sum(same & earlier, axis=2)
    loads = jnp.sum(owners[:, :, None] == jnp.arange(dp_count)[None, None, :], axis=1)
    hot = jnp.argmax(jnp.sum(loads, axis=0)).astype(jnp.int32)
    fits = jnp.all((loads <= MAIN) | (jnp.arange(dp_count) == hot)[None, :])
    counts = lax.dynamic_slice_in_dim(group_live_count, me * groups, groups)
    my_owners = lax.dynamic_index_in_dim(owners, me, 0, keepdims=False)
    my_ranking = lax.dynamic_index_in_dim(ranking, me, 0, keepdims=False)

    def rows_for(owner, ranks):
        hits = (owners == owner)[:, :, None] & (ranking[:, :, None] == ranks[None, None, :])
        return jnp.sum(jnp.where(hits, slots[:, :, None], 0), axis=1)

    def wide(hidden, value_weight, down_weights, up_weights):
        base_terms = jnp.dot(hidden, value_weight, preferred_element_type=jnp.float32)
        base = lax.psum_scatter(base_terms, "tp", scatter_dimension=1, tiled=True)
        rows = rows_for(me, jnp.arange(MOST)).reshape(-1)
        downs = lax.all_to_all(down_weights[rows], "dp", 0, 0, tiled=True)
        ups = lax.all_to_all(up_weights[rows], "dp", 0, 0, tiled=True)
        picked = my_owners * MOST + my_ranking
        partial = jnp.einsum(
            "gcd,grd->gcr",
            hidden.reshape(groups, cap, width),
            downs[picked],
            preferred_element_type=jnp.float32,
        )
        low = low_rank_sum(partial.reshape(groups * cap, rank))
        return finish(base, low, ups[picked], counts)

    def narrow(hidden, value_weight, down_weights, up_weights):
        main_rows = rows_for(me, jnp.arange(MAIN)).reshape(-1)
        main_sent = packed(down_weights[main_rows], up_weights[main_rows])
        extra_rows = rows_for(hot, MAIN + jnp.arange(EXTRA)).reshape(-1)
        extra_sent = jnp.where(
            me == hot, packed(down_weights[extra_rows], up_weights[extra_rows]), jnp.bfloat16(0)
        )
        extra = lax.psum_scatter(extra_sent, "dp", scatter_dimension=0, tiled=True)
        main = lax.all_to_all(main_sent, "dp", 0, 0, tiled=True)
        base_terms = jnp.dot(hidden, value_weight, preferred_element_type=jnp.float32)
        base = lax.psum_scatter(base_terms, "tp", scatter_dimension=1, tiled=True)
        picked = jnp.where(
            my_ranking < MAIN,
            my_owners * MAIN + my_ranking,
            dp_count * MAIN + my_ranking - MAIN,
        )
        arrived = jnp.concatenate([main, extra], axis=0)[picked]
        downs, ups = unpacked(arrived, rank)
        partial = jnp.einsum(
            "gcd,grd->gcr",
            hidden.reshape(groups, cap, width),
            downs,
            preferred_element_type=jnp.float32,
        )
        low = low_rank_sum(partial.reshape(groups * cap, rank))
        return finish(base, low, ups, counts)

    return lax.cond(fits, narrow, wide, hidden, value_weight, down_weights, up_weights)


def solution(mesh):
    return jax.shard_map(
        on_device,
        mesh=mesh,
        in_specs=(
            P("dp", "tp"),
            P("tp", None),
            P("dp", None, "tp"),
            P("dp", None, "tp"),
            P(),
            P(),
            P(),
        ),
        out_specs=P("dp", "tp"),
        check_vma=False,
    )
```

time: 338 us -> 268 us (0.79); the launches traced: 334 us -> 268 us
  waiting for transfers between devices: 200 us -> 145 us
  blocking collectives: 58.5 us -> 14 us
  other arithmetic: 0.77 us -> 25.7 us
  local copies, waits for them, and re-layouts: 31.5 us -> 35.5 us
    all_to_all x2, waiting for transfers between devices: 200 us -> 102 us  [the longest x1 89.8 us: narrow(): main = lax.all_to_all(main_sent, 'dp', 0, 0, tiled=True)]
    psum x1 -> x0, blocking collectives: 58.5 us -> none  [on_device(): summed = lax.psum(partial_value, 'tp').astype(jnp.bfloat16)]
    reduce_scatter x1 -> x2, waiting for transfers between devices: 0.01 us -> 42.9 us  [the longest x1 32.4 us: narrow(): extra = lax.psum_scatter(extra_sent, 'dp', scatter_dimension=0, tiled=True)]
    all_gather x0 -> x1, blocking collectives: none -> 14 us  [low_rank_sum(): return lax.all_gather(mine, 'tp', axis=0, tiled=True)]
    concatenate x0 -> x2, other arithmetic: none -> 10.5 us  [the longest x1 5.3 us: narrow(): arrived = jnp.concatenate([main, extra], axis=0)[picked]]
    select_n x3 -> x6, other arithmetic: 0.02 us -> 10.4 us  [the longest x1 10.4 us: narrow(): jnp.where(me == hot, packed(down_weights[extra_rows], up_weights[extra_ro...]
    gather x4 -> x5, local copies, waits for them, and re-layouts: 25.1 us -> 27.5 us  [the longest x1 11.5 us: narrow(): down_weights[extra_rows]]
  transfers between devices with their start and end apart: 3 -> 4, of which waited for: 2 -> 4; matrix products, arithmetic and copies ran while one was open for 10% -> 16% of each run, Pallas kernels for 0% -> 0%
where the time goes in v1:
time: 268 us
  waiting for transfers between devices  145 us (54%)
  local copies, waits for them, and re-layouts  35.5 us (13%)
  other arithmetic  25.7 us (10%)
  matrix products  17.9 us (7%)
  between operations  14.1 us (5%)
  starting transfers between devices  14 us (5%)
  blocking collectives  14 us (5%)
    all_to_all x1, waiting for transfers between devices, narrow(): main = lax.all_to_all(main_sent, 'dp', 0, 0, tiled=True)  89.8 us
    reduce_scatter x1, waiting for transfers between devices, narrow(): extra = lax.psum_scatter(extra_sent, 'dp', scatter_dimension=0, tiled=True)  32.4 us
    all_gather x1, blocking collectives, low_rank_sum(): return lax.all_gather(mine, 'tp', axis=0, tiled=True)  14 us
    all_to_all x1, waiting for transfers between devices, low_rank_sum(): lax.all_to_all(partial, 'tp', split_axis=0, concat_axis=0, tiled=True)  12.5 us
    gather x1, local copies, waits for them, and re-layouts, narrow(): down_weights[extra_rows]  11.5 us
    dot_general x1, matrix products, narrow(): jnp.dot(hidden, value_weight, preferred_element_type=jnp.float32)  10.7 us
    reduce_scatter x1, waiting for transfers between devices, narrow(): base = lax.psum_scatter(base_terms, 'tp', scatter_dimension=1, tiled=True)  10.5 us
    select_n x1, other arithmetic, narrow(): jnp.where(me == hot, packed(down_weights[extra_rows], up_weights[extra_ro...  10.4 us
  transfers between devices with their start and end apart: 4, of which 4 were waited for; matrix products, arithmetic and copies ran while one was open for 16% of the time, Pallas kernels for 0%

profile of v1, /device:TPU:1, one launch (start us, length us, event | category | flops | bytes accessed | tf_op | source)
XLA Modules:
  0.0 267.7 jit_solution(17026264124905371015)
XLA Ops:
  6.5 0.7 compare_select_fusion.6
  7.2 3.1 %gather_fusion.9 = s32[512]{0:T(512)S(1)} fusion(s32[2048]{0:T(1024)S(1)} %copy-done, s32[1024]{0:T(1024)S(1)} %pad_clamp_fusion.5), kind=kCustom, calls=%fused_computation.9 | custom fusion | bytes 6144 | tf_op jit(solution)/shard_map/gather | solution.py:58
  10.5 0.5 convert_reduce_fusion
  11.0 0.8 dynamic_slice.10
  11.7 0.4 convert_reduce_fusion.1
  12.1 0.7 iota_reduce_fusion
  12.9 0.7 iota_compare_fusion.6
  13.6 0.6 or_reduce_fusion
  14.9 244.5 %conditional.1 = (bf16[2048,128]{1,0:T(8,128)(2,1)S(1)}) conditional(s32[]{:T(128)} %convert_element_type.22, (s32[32]{0:T(128)S(1)}, bf16[2048,1024]{1,0:T(8,128)(2,1)}, bf16[1024,1024]{1,0:T(8,128)(2,1)}, s32[]{:T(128)}, s32[16,32]{1,0:T(8,128)S(1)}, /*index=5*/s32[16,32]{1,0:T(8,128)S(1)}, s32[512]{0:T(512)S(1)}, ...), branch_computations={%region_5.9_spmd, %region_9.15_spmd} | conditional | flops 4633823232 | bytes 189698784 | solution.py:118
  15.8 0.7 broadcast_compare_fusion.2
  17.0 11.5 %gather_fusion.6 = bf16[64,64,1024]{2,1,0:T(8,128)(2,1)} fusion(bf16[128,64,1024]{2,1,0:T(8,128)(2,1)} %get-tuple-element.68, s32[1024]{0:T(1024)S(1)} %pad_clamp_fusion.3), kind=kCustom, calls=%fused_computation.6 | custom fusion | bytes 16777472 | tf_op jit(solution)/shard_map/cond/branch_1_fun/gather | solution.py:96
  28.6 0.7 gather_fusion.7
  29.3 10.4 %maximum_select_fusion = bf16[64,72,1024]{2,1,0:T(8,128)(2,1)} fusion(bf16[64,8,1024]{2,1,0:T(8,128)(2,1)S(1)} %bitcast.55, bf16[64,64,1024]{2,1,0:T(8,128)(2,1)} %gather_fusion.6, pred[]{:T(512)S(6)} %eq.51), kind=kLoop, calls=%fused_computation.25 | loop fusion | flops 23592960 | bytes 18874368 | tf_op jit(solution)/shard_map/cond/branch_1_fun/jit(_where)/select_n | solution.py:95
  39.8 10.7 %fusion.20 = f32[2048,1024]{1,0:T(8,128)} fusion(bf16[2048,1024]{1,0:T(8,128)(2,1)} %get-tuple-element.66, bf16[1024,1024]{1,0:T(8,128)(2,1)} %get-tuple-element.67), kind=kOutput, calls=%fused_computation.77 | convolution fusion | flops 4294967296 | bytes 14680064 | tf_op jit(solution)/shard_map/cond/branch_1_fun/dot_general | solution.py:100
  50.8 9.0 %gather_fusion.4 = bf16[32,64,1024]{2,1,0:T(8,128)(2,1)} fusion(bf16[128,64,1024]{2,1,0:T(8,128)(2,1)} %get-tuple-element.68, s32[1024]{0:T(1024)S(1)} %pad_clamp_fusion.4), kind=kCustom, calls=%fused_computation.4 | custom fusion | bytes 8388736 | tf_op jit(solution)/shard_map/cond/branch_1_fun/gather | solution.py:93
  59.9 0.6 gather_fusion.5
  60.5 5.3 %pad_maximum_fusion.1 = bf16[32,72,1024]{2,1,0:T(8,128)(2,1)} fusion(bf16[32,8,1024]{2,1,0:T(8,128)(2,1)S(1)} %bitcast.58, bf16[32,64,1024]{2,1,0:T(8,128)(2,1)} %gather_fusion.4), kind=kLoop, calls=%fused_computation.27 | loop fusion | flops 9437184 | bytes 9437184 | tf_op jit(solution)/shard_map/cond/branch_1_fun/concatenate | solution.py:35
  65.8 8.0 %all-to-all-start.3 = ((bf16[32,72,1024]{2,1,0:T(8,128)(2,1)}), bf16[32,72,1024]{2,1,0:T(8,128)(2,1)}, u32[]{:S(2)}, u32[]{:S(2)}) async-start(bf16[32,72,1024]{2,1,0:T(8,128)(2,1)} %pad_maximum_fusion.1), calls=%async_computation.5 | async-start | bytes 9437184 | tf_op jit(solution)/shard_map/cond/branch_1_fun/all_to_all | solution.py:99
  73.8 89.8 %all-to-all-done.3 = bf16[32,72,1024]{2,1,0:T(8,128)(2,1)} async-done(((bf16[32,72,1024]{2,1,0:T(8,128)(2,1)}), bf16[32,72,1024]{2,1,0:T(8,128)(2,1)}, u32[]{:S(2)}, u32[]{:S(2)}) %all-to-all-start.3) | async-done | bytes 4718624 | tf_op jit(solution)/shard_map/cond/branch_1_fun/all_to_all | solution.py:99
  163.6 32.4 %reduce-scatter.8.cloned.1.call-done = bf16[4,72,1024]{2,1,0:T(8,128)(2,1)} async-done(((bf16[64,72,1024]{2,1,0:T(8,128)(2,1)}), bf16[4,72,1024]{2,1,0:T(8,128)(2,1)}) %reduce-scatter.8.cloned.1.call-update) | async-done | bytes 589840 | tf_op jit(solution)/shard_map/cond/branch_1_fun/reduce_scatter | solution.py:98
  195.9 5.3 %pad_maximum_fusion = bf16[36,72,1024]{2,1,0:T(8,128)(2,1)} fusion(bf16[4,72,1024]{2,1,0:T(8,128)(2,1)} %reduce-scatter.8.cloned.1.call-done, bf16[32,72,1024]{2,1,0:T(8,128)(2,1)} %all-to-all-done.3), kind=kLoop, calls=%fused_computation.26 | loop fusion | flops 2654208 | bytes 10616832 | tf_op jit(solution)/shard_map/cond/branch_1_fun/concatenate | solution.py:107
  201.2 5.5 %gather_fusion.8 = bf16[32,72,1024]{2,1,0:T(8,128)(2,1)} fusion(bf16[36,72,1024]{2,1,0:T(8,128)(2,1)} %pad_maximum_fusion, s32[1024]{0:T(1024)S(1)} %pad_clamp_fusion.2), kind=kCustom, calls=%fused_computation.8 | custom fusion | bytes 9437312 | tf_op jit(solution)/shard_map/cond/branch_1_fun/gather | solution.py:107
  206.8 5.4 %fusion.7 = f32[32,64,64]{1,2,0:T(8,128)S(1)} fusion(bf16[32,64,1024]{2,1,0:T(8,128)(2,1)} %bitcast.54, bf16[32,72,1024]{2,1,0:T(8,128)(2,1)} %gather_fusion.8), kind=kOutput, calls=%fused_computation.30 | convolution fusion | flops 268435456 | bytes 8912896 | tf_op jit(solution)/shard_map/cond/branch_1_fun/gcd,grd->gcr/dot_general | solution.py:109
  212.2 0.6 copy.27
  213.1 1.0 copy.28
  214.0 5.7 %all-to-all-start.4 = ((f32[8,256,64]{1,2,0:T(8,128)}), f32[8,256,64]{1,2,0:T(8,128)S(1)}, u32[]{:S(2)}, u32[]{:S(2)}) async-start(f32[8,256,64]{1,2,0:T(8,128)} %copy.28), calls=%async_computation.7 | async-start | bytes 1048576 | tf_op jit(solution)/shard_map/cond/branch_1_fun/all_to_all | solution.py:15
  219.8 12.5 %all-to-all-done.4 = f32[8,256,64]{1,2,0:T(8,128)S(1)} async-done(((f32[8,256,64]{1,2,0:T(8,128)}), f32[8,256,64]{1,2,0:T(8,128)S(1)}, u32[]{:S(2)}, u32[]{:S(2)}) %all-to-all-start.4) | async-done | bytes 524320 | tf_op jit(solution)/shard_map/cond/branch_1_fun/all_to_all | solution.py:15
  232.4 14.0 %all_gather.5 = bf16[2048,64]{0,1:T(8,128)(2,1)S(1)} all-gather(bf16[256,64]{0,1:T(8,128)(2,1)S(1)} %reduce_sum.68), channel_id=1, replica_groups=mesh['dp'=16,'tp'=8] {'tp'}, dimensions={0}, use_global_device_ids=true | all-gather | bytes 294912 | tf_op jit(solution)/shard_map/cond/branch_1_fun/all_gather | solution.py:17
  246.8 10.5 %reduce-scatter.6.cloned.1.call-done = f32[2048,128]{1,0:T(8,128)} async-done(((f32[2048,1024]{1,0:T(8,128)}), f32[2048,128]{1,0:T(8,128)}) %reduce-scatter.6.cloned.1.call-update) | async-done | bytes 1048592 | tf_op jit(solution)/shard_map/cond/branch_1_fun/reduce_scatter | solution.py:101
  257.3 1.8 fusion.12
  259.3 0.8 copy-done.4
  260.1 0.7 copy-done.1
  (34 shorter events, 1.9 us)
Async XLA Ops:
  6.5 0.7 copy-start
  14.9 181.1 %reduce-scatter.8.cloned.1.call-start = ((), (), s32[]{:S(2)}) async-start(), calls=%async_computation.10 | async-start | bytes 10027008 | tf_op jit(solution)/shard_map/cond/branch_1_fun/reduce_scatter | solution.py:98
  17.0 11.6 %copy-start.3 = (bf16[128,64,128]{2,1,0:T(8,128)(2,1)S(1)}, bf16[128,64,128]{2,1,0:T(8,128)(2,1)}, u32[]{:S(2)}) copy-start(bf16[128,64,128]{2,1,0:T(8,128)(2,1)} %get-tuple-element.73) | copy-start | bytes 6291460 | tf_op jit(solution)/shard_map/cond
  39.7 217.6 %reduce-scatter.6.cloned.1.call-start = ((), (), s32[]{:S(2)}) async-start(), calls=%async_computation.9 | async-start | bytes 9437184 | tf_op jit(solution)/shard_map/cond/branch_1_fun/reduce_scatter | solution.py:101
  65.8 97.8 %all-to-all-start.3 = ((bf16[32,72,1024]{2,1,0:T(8,128)(2,1)}), bf16[32,72,1024]{2,1,0:T(8,128)(2,1)}, u32[]{:S(2)}, u32[]{:S(2)}) async-start(bf16[32,72,1024]{2,1,0:T(8,128)(2,1)} %pad_maximum_fusion.1), calls=%async_computation.5 | async-start | bytes 9437184 | tf_op jit(solution)/shard_map/cond/branch_1_fun/all_to_all | solution.py:99
  214.0 18.4 %all-to-all-start.4 = ((f32[8,256,64]{1,2,0:T(8,128)}), f32[8,256,64]{1,2,0:T(8,128)S(1)}, u32[]{:S(2)}, u32[]{:S(2)}) async-start(f32[8,256,64]{1,2,0:T(8,128)} %copy.28), calls=%async_computation.7 | async-start | bytes 1048576 | tf_op jit(solution)/shard_map/cond/branch_1_fun/all_to_all | solution.py:15
  259.3 0.8 copy-start.4
  260.1 0.7 copy-start.1
Sparse Core Ops, SparseCore 0:
  39.8 156.0 reduce-scatter.7
  198.3 58.8 reduce-scatter.5

commit v2 on v1

--- a/solution.py
+++ b/solution.py
@@ -1,6 +1,10 @@
+import math
+
 import jax
 import jax.numpy as jnp
 from jax import lax
+from jax.experimental import pallas as pl
+from jax.experimental.pallas import tpu as pltpu
 from jax.sharding import PartitionSpec as P
 
 ADAPTER_SCALE = 0.5
@@ -29,16 +33,178 @@
     return out.reshape(base.shape)
 
 
-def packed(down, up):
-    count = down.shape[0]
-    up_rows = up.reshape(count, 8, 8, up.shape[2]).transpose(0, 2, 1, 3)
-    return jnp.concatenate([down, up_rows.reshape(count, 8, -1)], axis=1)
-
-
-def unpacked(rows, rank):
+def shift(value, dx, dy):
+    side = math.isqrt(lax.axis_size("dp"))
+    pairs = [
+        (x * side + y, (x + dx) % side * side + (y + dy) % side)
+        for x in range(side)
+        for y in range(side)
+    ]
+    return lax.ppermute(value, "dp", pairs)
+
+
+def copy_units(rows, down, up, out, up_in, up_out, down_sem, up_sem, out_sem):
+    units = out.shape[0]
+    rank = down.shape[1]
+    lanes = up.shape[2]
+    down_copies, up_copies = [], []
+    for i in range(units * 2):
+        row = rows[i]
+        unit, half = i // 2, i % 2
+        up_copies.append(pltpu.make_async_copy(up.at[row], up_in.at[i], up_sem.at[i]))
+        down_copies.append(
+            pltpu.make_async_copy(
+                down.at[row], out.at[unit, pl.ds(half * rank, rank)], down_sem.at[i]
+            )
+        )
+        up_copies[-1].start()
+        down_copies[-1].start()
+    for i in range(units * 2):
+        unit, half = i // 2, i % 2
+        up_copies[i].wait()
+        for part in range(rank // 16):
+            at = (half * (rank // 16) + part) * lanes
+            up_out[unit, :, at : at + lanes] = up_in[i, part * 16 : part * 16 + 16, :]
+    last = pltpu.make_async_copy(up_out, out.at[:, pl.ds(2 * rank, 16)], out_sem)
+    last.start()
+    for copy in down_copies:
+        copy.wait()
+    last.wait()
+
+
+def gather_kernel(active, rows, down, up, out, *scratch):
+    @pl.when(active[0] == 1)
+    def _():
+        copy_units(rows, down, up, out, *scratch)
+
+
+def gather_units(active, rows, down, up):
     count = rows.shape[0]
-    up = rows[:, rank:].reshape(count, 8, 8, -1).transpose(0, 2, 1, 3)
-    return rows[:, :rank], up.reshape(count, rank, -1)
+    _, rank, width = down.shape
+    lanes = up.shape[2]
+    smem = pl.BlockSpec(memory_space=pltpu.SMEM)
+    hbm = pl.BlockSpec(memory_space=pl.ANY)
+    return pl.pallas_call(
+        gather_kernel,
+        out_shape=jax.ShapeDtypeStruct((count // 2, 2 * rank + 16, width), down.dtype),
+        in_specs=[smem, smem, hbm, hbm],
+        out_specs=hbm,
+        scratch_shapes=[
+            pltpu.VMEM((count, rank, lanes), up.dtype),
+            pltpu.VMEM((count // 2, 16, width), up.dtype),
+            pltpu.SemaphoreType.DMA((count,)),
+            pltpu.SemaphoreType.DMA((count,)),
+            pltpu.SemaphoreType.DMA,
+        ],
+        compiler_params=pltpu.CompilerParams(vmem_limit_bytes=12 << 20),
+        cost_estimate=pl.CostEstimate(
+            flops=0, bytes_accessed=count * rank * (width + lanes) * 4, transcendentals=0
+        ),
+    )(active, rows, down, up)
+
+
+def low_kernel(order, sources, hidden, units, out):
+    groups = order.shape[0]
+    pairs = groups // 2
+    rank = out.shape[1] // 2
+    cap = out.shape[0] // pairs
+
+    def one(j):
+        g = pl.multiple_of(order[j] * cap, cap)
+        at = pl.multiple_of(sources[j], 16)
+        return lax.dot_general(
+            hidden[pl.ds(g, cap), :],
+            units[pl.ds(at, rank), :],
+            (((1,), (1,)), ((), ())),
+            preferred_element_type=jnp.float32,
+        )
+
+    def body(i, carry):
+        both = jnp.concatenate([one(i), one(i + pairs)], axis=1)
+        out[pl.ds(pl.multiple_of(i * cap, cap), cap), :] = both
+        return carry
+
+    lax.fori_loop(0, pairs, body, 0, unroll=2)
+
+
+def low_partial(order, sources, hidden, units, cap, rank):
+    groups = order.shape[0]
+    smem = pl.BlockSpec(memory_space=pltpu.SMEM)
+    vmem = pl.BlockSpec(memory_space=pltpu.VMEM)
+    return pl.pallas_call(
+        low_kernel,
+        out_shape=jax.ShapeDtypeStruct((groups // 2 * cap, 2 * rank), jnp.float32),
+        in_specs=[smem, smem, vmem, vmem],
+        out_specs=vmem,
+        compiler_params=pltpu.CompilerParams(vmem_limit_bytes=24 << 20),
+        cost_estimate=pl.CostEstimate(
+            flops=groups * cap * rank * 2 * hidden.shape[1],
+            bytes_accessed=(hidden.size + units.size) * 2,
+            transcendentals=0,
+        ),
+    )(order, sources, hidden, units)
+
+
+def out_kernel(order, places, counts, base, low, packs, out):
+    groups = order.shape[0]
+    pairs = groups // 2
+    rank = low.shape[1] // 2
+    cap = base.shape[0] // groups
+    lanes = base.shape[1]
+    rows = lax.broadcasted_iota(jnp.int32, (cap, lanes), 0)
+
+    def one(j, factor):
+        g = order[j]
+        place = places[j]
+        unit = place // 2
+        at = (place % 2) * (rank // 16) * lanes
+        up = jnp.concatenate(
+            [
+                packs[unit, :, pl.ds(pl.multiple_of(at + part * lanes, lanes), lanes)]
+                for part in range(rank // 16)
+            ],
+            axis=0,
+        )
+        delta = jnp.dot(factor, up, preferred_element_type=jnp.float32)
+        here = pl.ds(pl.multiple_of(g * cap, cap), cap)
+        merged = base[here, :] + ADAPTER_SCALE * delta
+        out[here, :] = jnp.where(rows < counts[g], merged, 0.0).astype(out.dtype)
+
+    def body(i, carry):
+        both = low[pl.ds(pl.multiple_of(i * cap, cap), cap), :]
+        one(i, both[:, :rank])
+        one(i + pairs, both[:, rank:])
+        return carry
+
+    lax.fori_loop(0, pairs, body, 0, unroll=2)
+
+
+def combine(order, places, counts, base, low, packs):
+    smem = pl.BlockSpec(memory_space=pltpu.SMEM)
+    vmem = pl.BlockSpec(memory_space=pltpu.VMEM)
+    return pl.pallas_call(
+        out_kernel,
+        out_shape=jax.ShapeDtypeStruct(base.shape, jnp.bfloat16),
+        in_specs=[smem, smem, smem, vmem, vmem, vmem],
+        out_specs=vmem,
+        compiler_params=pltpu.CompilerParams(vmem_limit_bytes=12 << 20),
+        cost_estimate=pl.CostEstimate(
+            flops=base.size * low.shape[1], bytes_accessed=base.size * 8, transcendentals=0
+        ),
+    )(order, places, counts, base, low, packs)
+
+
+def spread(units, along, across, a, b):
+    plus = along(units[2, :2], 1)
+    minus = along(units[2, 2:], -1)
+    plus = along(jnp.where(a == 0, units[1], jnp.concatenate([plus, plus])), 1)
+    minus = along(jnp.where(a == 0, units[3], jnp.concatenate([minus, minus])), -1)
+    far = jnp.concatenate([plus[:2], minus[2:]])
+    line = jnp.where(a == 0, units[0], jnp.where(a == 1, plus, jnp.where(a == 3, minus, far)))
+    back = across(line[3], -1)
+    ahead = across(line[2], 1)
+    ahead = across(jnp.where(b == 0, line[1], ahead), 1)
+    return jnp.where(b == 0, line[0], jnp.where(b == 3, back, ahead))
 
 
 def on_device(
@@ -89,31 +255,43 @@
         return finish(base, low, ups[picked], counts)
 
     def narrow(hidden, value_weight, down_weights, up_weights):
+        side = math.isqrt(dp_count)
+        always = jnp.ones((1,), jnp.int32)
         main_rows = rows_for(me, jnp.arange(MAIN)).reshape(-1)
-        main_sent = packed(down_weights[main_rows], up_weights[main_rows])
-        extra_rows = rows_for(hot, MAIN + jnp.arange(EXTRA)).reshape(-1)
-        extra_sent = jnp.where(
-            me == hot, packed(down_weights[extra_rows], up_weights[extra_rows]), jnp.bfloat16(0)
-        )
-        extra = lax.psum_scatter(extra_sent, "dp", scatter_dimension=0, tiled=True)
+        main_sent = gather_units(always, main_rows, down_weights, up_weights)
         main = lax.all_to_all(main_sent, "dp", 0, 0, tiled=True)
+        extra_rows = rows_for(hot, MAIN + jnp.arange(EXTRA))
+        steps = jnp.arange(side)
+        xs = (hot // side + steps) % side
+        ys = (hot % side + steps) % side
+        by_x = (xs[:, None] * side + ys[None, :]).reshape(-1)
+        by_y = (xs[None, :] * side + ys[:, None]).reshape(-1)
+        is_hot = (me == hot).astype(jnp.int32).reshape(1)
+        asked = jnp.concatenate([extra_rows[by_x, :2].reshape(-1), extra_rows[by_y, 2:].reshape(-1)])
+        sent = gather_units(is_hot, asked, down_weights, up_weights)
+        sent = sent.reshape(2, side, side, *sent.shape[1:])
+        a = (me // side - hot // side) % side
+        b = (me % side - hot % side) % side
+        along_x = lambda value, step: shift(value, step, 0)
+        along_y = lambda value, step: shift(value, 0, step)
+        extra_x = spread(sent[0], along_x, along_y, a, b)
+        extra_y = spread(sent[1], along_y, along_x, b, a)
         base_terms = jnp.dot(hidden, value_weight, preferred_element_type=jnp.float32)
         base = lax.psum_scatter(base_terms, "tp", scatter_dimension=1, tiled=True)
-        picked = jnp.where(
-            my_ranking < MAIN,
-            my_owners * MAIN + my_ranking,
-            dp_count * MAIN + my_ranking - MAIN,
-        )
-        arrived = jnp.concatenate([main, extra], axis=0)[picked]
-        downs, ups = unpacked(arrived, rank)
-        partial = jnp.einsum(
-            "gcd,grd->gcr",
-            hidden.reshape(groups, cap, width),
-            downs,
-            preferred_element_type=jnp.float32,
-        )
-        low = low_rank_sum(partial.reshape(groups * cap, rank))
-        return finish(base, low, ups, counts)
+        unit_rows = main.shape[1]
+        late = (my_owners == hot) & (my_ranking >= MAIN)
+        place = jnp.where(
+            late, dp_count * MAIN + my_ranking - MAIN, my_owners * MAIN + my_ranking
+        )
+        turn = jnp.where(late, groups - EXTRA + my_ranking - MAIN, jnp.cumsum(~late) - 1)
+        here = turn[None, :] == jnp.arange(groups)[:, None]
+        order = jnp.sum(jnp.where(here, jnp.arange(groups)[None, :], 0), axis=1)
+        places = jnp.sum(jnp.where(here, place[None, :], 0), axis=1)
+        units = jnp.concatenate([main, extra_x[None], extra_y[None]], axis=0)
+        sources = places // 2 * unit_rows + places % 2 * rank
+        partial = low_partial(order, sources, hidden, units.reshape(-1, width), cap, rank)
+        low = low_rank_sum(partial)
+        return combine(order, places, counts, base, low, units[:, 2 * rank :])
 
     return lax.cond(fits, narrow, wide, hidden, value_weight, down_weights, up_weights)
 

time: 268 us -> 251 us (0.937)
  waiting for transfers between devices: 145 us -> 114 us
  starting transfers between devices: 14 us -> 34.5 us
  Pallas kernels: 0 us -> 11.6 us
  matrix products: 17.9 us -> 8.98 us
  local copies, waits for them, and re-layouts: 35.5 us -> 27.1 us
  other arithmetic: 25.7 us -> 21.7 us
  loops' own time: 1.14 us -> 4.04 us
    ppermute x0 -> x14, waiting for transfers between devices: none -> 105 us  [shift(): return lax.ppermute(value, 'dp', pairs)]
    all_to_all x1, waiting for transfers between devices: 89.8 us -> 0.01 us  [narrow(): main = lax.all_to_all(main_sent, 'dp', 0, 0, tiled=True)]
    reduce_scatter x1 -> x0, waiting for transfers between devices: 32.4 us -> none  [narrow(): extra = lax.psum_scatter(extra_sent, 'dp', scatter_dimension=0, tiled=True)]
    gather x5 -> x6, local copies, waits for them, and re-layouts: 27.5 us -> 2.91 us  [the longest x3 1.45 us: narrow(): extra_rows[by_y, 2:].reshape(-1)]
    ppermute x0 -> x14, starting transfers between devices: none -> 18.1 us  [shift(): return lax.ppermute(value, 'dp', pairs)]
    pallas_call x0 -> x4, Pallas kernels: none -> 11.6 us  [the longest x2 5.32 us: gather_units(): pl.pallas_call(gather_kernel, out_shape=jax.ShapeDtypeStruct((count // 2,...]
    reduce_scatter x1, waiting for transfers between devices: 10.5 us -> 0.01 us  [narrow(): base = lax.psum_scatter(base_terms, 'tp', scatter_dimension=1, tiled=True)]
    slice x0 -> x6, local copies, waits for them, and re-layouts: none -> 8.7 us  [the longest x1 5.32 us: narrow(): extra_x = spread(sent[0], along_x, along_y, a, b)]
  transfers between devices with their start and end apart: 4 -> 17, of which waited for: 4 -> 10; matrix products, arithmetic and copies ran while one was open for 16% -> 14% of each run, Pallas kernels for 0% -> 4%
where the time goes in v2:
time: 251 us; the launch traced here: 249 us
  waiting for transfers between devices  114 us (45%)
  starting transfers between devices  34.5 us (14%)
  local copies, waits for them, and re-layouts  27.1 us (11%)
  other arithmetic  21.7 us (9%)
  between operations  14.1 us (6%)
  blocking collectives  13.5 us (5%)
  Pallas kernels  11.6 us (5%)
  matrix products  8.98 us (4%)
  loops' own time  4.04 us (2%)
    ppermute x14, waiting for transfers between devices, shift(): return lax.ppermute(value, 'dp', pairs)  105 us
    ppermute x14, starting transfers between devices, shift(): return lax.ppermute(value, 'dp', pairs)  18.1 us
    all_gather x1, blocking collectives, low_rank_sum(): return lax.all_gather(mine, 'tp', axis=0, tiled=True)  13.5 us
    dot_general x1, matrix products, narrow(): jnp.dot(hidden, value_weight, preferred_element_type=jnp.float32)  8.98 us
    all_to_all x1, waiting for transfers between devices, low_rank_sum(): lax.all_to_all(partial, 'tp', split_axis=0, concat_axis=0, tiled=True)  8.37 us
    all_to_all x1, starting transfers between devices, narrow(): main = lax.all_to_all(main_sent, 'dp', 0, 0, tiled=True)  8.14 us
    all_to_all x1, starting transfers between devices, low_rank_sum(): lax.all_to_all(partial, 'tp', split_axis=0, concat_axis=0, tiled=True)  8.07 us
    pallas_call x2, Pallas kernels, gather_units(): pl.pallas_call(gather_kernel, out_shape=jax.ShapeDtypeStruct((count // 2,...  5.32 us
  transfers between devices with their start and end apart: 17, of which 10 were waited for; matrix products, arithmetic and copies ran while one was open for 14% of the time, Pallas kernels for 4%

profile of v2, /device:TPU:1, one launch (start us, length us, event | category | flops | bytes accessed | tf_op | source)
XLA Modules:
  0.0 249.2 jit_solution(4990398279890422582)
XLA Ops:
  7.4 3.1 %gather_fusion.8 = s32[512]{0:T(512)S(1)} fusion(s32[2048]{0:T(1024)S(1)} %copy-done, s32[1024]{0:T(1024)S(1)} %pad_clamp_fusion.2), kind=kCustom, calls=%fused_computation.8 | custom fusion | bytes 6144 | tf_op jit(solution)/shard_map/gather | solution.py:224
  15.0 225.9 %conditional.1 = (bf16[2048,128]{1,0:T(8,128)(2,1)S(1)}) conditional(s32[]{:T(128)} %convert_element_type.22, (s32[32]{0:T(128)S(1)}, bf16[2048,1024]{1,0:T(8,128)(2,1)}, bf16[1024,1024]{1,0:T(8,128)(2,1)S(1)}, s32[]{:T(128)}, s32[16,32]{1,0:T(8,128)S(1)}, /*index=5*/s32[16,32]{1,0:T(8,128)S(1)}, s32[512]{0:T(512)S(1)}, ...), branch_computations={%region_5.9_spmd, %region_9.17_spmd} | conditional | flops 4612722688 | bytes 312327520 | solution.py:296
  15.3 9.0 %fusion.25 = f32[2048,1024]{1,0:T(8,128)} fusion(bf16[2048,1024]{1,0:T(8,128)(2,1)} %get-tuple-element.69.hidden, bf16[1024,1024]{1,0:T(8,128)(2,1)S(1)} %get-tuple-element.70), kind=kOutput, calls=%fused_computation.125 | convolution fusion | flops 4294967296 | bytes 14680064 | tf_op jit(solution)/shard_map/cond/branch_1_fun/dot_general | solution.py:279
  32.9 1.7 branch_1_fun.5
  34.6 5.3 %fusion.23 = (bf16[16,144,1024]{2,1,0:T(8,128)(2,1)}, bf16[16,144,1024]{2,1,0:T(8,128)(2,1)}) fusion(bf16[32,144,1024]{2,1,0:T(8,128)(2,1)S(1)} %branch_1_fun.5), kind=kLoop, calls=%fused_computation.123 | loop fusion | bytes 18874368 | tf_op jit(solution)/shard_map/cond/branch_1_fun/slice | solution.py:277
  39.9 1.5 copy-done.2
  41.4 2.4 slice_bitcast_fusion.2
  43.8 2.1 collective-permute-start
  47.2 13.0 %collective-permute-done = bf16[2,144,1024]{2,1,0:T(8,128)(2,1)S(1)} collective-permute-done((bf16[2,144,1024]{2,1,0:T(8,128)(2,1)}, bf16[2,144,1024]{2,1,0:T(8,128)(2,1)S(1)}, u32[]{:S(2)}, u32[]{:S(2)}) %collective-permute-start) | collective-permute-done | bytes 589856 | tf_op jit(solution)/shard_map/cond/branch_1_fun/ppermute | solution.py:43
  60.1 3.5 %slice_select_fusion.3 = (bf16[4,144,1024]{2,1,0:T(8,128)(2,1)}, bf16[4,144,1024]{2,1,0:T(8,128)(2,1)}) fusion(bf16[32,144,1024]{2,1,0:T(8,128)(2,1)} %copy-done.2, bf16[2,144,1024]{2,1,0:T(8,128)(2,1)S(1)} %collective-permute-done.2, pred[]{:T(512)S(6)} %eq.78, bf16[2,144,1024]{2,1,0:T(8,128)(2,1)S(1)} %collective-permute-done), kind=kLoop, calls=%fused_computation.28 | loop fusion | flops 2359296 | bytes 5898241 | tf_op jit(solution)/shard_map/cond/branch_1_fun/jit(_where)/select_n | solution.py:201
  64.9 1.4 collective-permute-start.3
  66.7 3.6 %branch_1_fun.4 = bf16[16,144,1024]{2,1,0:T(8,128)(2,1)S(1)} custom-call(s32[1]{0:T(128)} %constant.173.clone.active, s32[32]{0:T(128)S(1)} %reshape.347.rows, bf16[128,64,1024]{2,1,0:T(8,128)(2,1)} %get-tuple-element.75.down, bf16[128,64,128]{2,1,0:T(8,128)(2,1)S(1)} %copy-done.7), custom_call_target="tpu_custom_call" | custom-call | bytes 9437184 | tf_op jit(solution)/shard_map/cond/branch_1_fun/pallas_call | solution.py:87
  70.3 2.2 copy-done.4
  72.5 8.1 %all-to-all-start.3 = ((bf16[16,144,1024]{2,1,0:T(8,128)(2,1)}), bf16[16,144,1024]{2,1,0:T(8,128)(2,1)}, u32[]{:S(2)}, u32[]{:S(2)}) async-start(bf16[16,144,1024]{2,1,0:T(8,128)(2,1)} %copy-done.4), calls=%async_computation.5 | async-start | bytes 9437184 | tf_op jit(solution)/shard_map/cond/branch_1_fun/all_to_all | solution.py:262
  81.9 2.3 collective-permute-start.7
  84.7 6.2 %collective-permute-done.1 = bf16[4,144,1024]{2,1,0:T(8,128)(2,1)} collective-permute-done((bf16[4,144,1024]{2,1,0:T(8,128)(2,1)}, bf16[4,144,1024]{2,1,0:T(8,128)(2,1)}, u32[]{:S(2)}, u32[]{:S(2)}) %collective-permute-start.1) | collective-permute-done | bytes 1179680 | tf_op jit(solution)/shard_map/cond/branch_1_fun/ppermute | solution.py:43
  93.2 52.1 %collective-permute-done.7 = bf16[2,144,1024]{2,1,0:T(8,128)(2,1)S(1)} collective-permute-done((bf16[2,144,1024]{2,1,0:T(8,128)(2,1)S(1)}, bf16[2,144,1024]{2,1,0:T(8,128)(2,1)S(1)}, u32[]{:S(2)}, u32[]{:S(2)}) %collective-permute-start.7) | collective-permute-done | bytes 589856 | tf_op jit(solution)/shard_map/cond/branch_1_fun/ppermute | solution.py:43
  145.2 3.4 %slice_select_fusion.5 = (bf16[4,144,1024]{2,1,0:T(8,128)(2,1)S(1)}, bf16[4,144,1024]{2,1,0:T(8,128)(2,1)}, bf16[4,144,1024]{2,1,0:T(8,128)(2,1)}) fusion(bf16[32,144,1024]{2,1,0:T(8,128)(2,1)} %copy-done.2, bf16[4,144,1024]{2,1,0:T(8,128)(2,1)} %collective-permute-done.1, bf16[4,144,1024]{2,1,0:T(8,128)(2,1)} %collective-permute-done.3, ...), kind=kLoop, calls=%fused_computation.30 | loop fusion | flops 4718592 | bytes 11796484 | tf_op jit(solution)/shard_map/cond/branch_1_fun/jit(_where)/select_n | solution.py:203
  148.6 2.7 %collective-permute-start.10 = (bf16[4,144,1024]{2,1,0:T(8,128)(2,1)}, bf16[4,144,1024]{2,1,0:T(8,128)(2,1)S(1)}, u32[]{:S(2)}, u32[]{:S(2)}) collective-permute-start(bf16[4,144,1024]{2,1,0:T(8,128)(2,1)} %get-tuple-element.89), channel_id=1, source_target_pairs={{0,24},{8,0},{16,8},{24,16},{32,56},{40,32},{48,40},{56,48},{64,88... | collective-permute-start | bytes 3538952 | tf_op jit(solution)/shard_map/cond/branch_1_fun/ppermute | solution.py:43
  155.7 20.6 %collective-permute-done.8 = bf16[4,144,1024]{2,1,0:T(8,128)(2,1)S(1)} collective-permute-done((bf16[4,144,1024]{2,1,0:T(8,128)(2,1)}, bf16[4,144,1024]{2,1,0:T(8,128)(2,1)S(1)}, u32[]{:S(2)}, u32[]{:S(2)}) %collective-permute-start.8) | collective-permute-done | bytes 1179680 | tf_op jit(solution)/shard_map/cond/branch_1_fun/ppermute | solution.py:43
  176.4 1.4 collective-permute-done.10
  177.8 1.6 slice_select_fusion.2
  180.7 1.9 collective-permute-done.5
  183.9 2.8 %collective-permute-done.12 = bf16[144,1024]{1,0:T(8,128)(2,1)S(1)} collective-permute-done((bf16[144,1024]{1,0:T(8,128)(2,1)S(1)}, bf16[144,1024]{1,0:T(8,128)(2,1)S(1)}, u32[]{:S(2)}, u32[]{:S(2)}) %collective-permute-start.12) | collective-permute-done | bytes 294944 | tf_op jit(solution)/shard_map/cond/branch_1_fun/ppermute | solution.py:43
  186.8 4.1 %collective-permute-start.13 = (bf16[144,1024]{1,0:T(8,128)(2,1)S(1)}, bf16[144,1024]{1,0:T(8,128)(2,1)S(1)}, u32[]{:S(2)}, u32[]{:S(2)}) collective-permute-start(bf16[144,1024]{1,0:T(8,128)(2,1)S(1)} %fusion.7), channel_id=1, source_target_pairs={{0,32},{8,40},{16,48},{24,56},{32,64},{40,72},{48,80},{56,88},{64,... | collective-permute-start | bytes 884744 | tf_op jit(solution)/shard_map/cond/branch_1_fun/ppermute | solution.py:43
  191.1 7.0 %collective-permute-done.13 = bf16[144,1024]{1,0:T(8,128)(2,1)S(1)} collective-permute-done((bf16[144,1024]{1,0:T(8,128)(2,1)S(1)}, bf16[144,1024]{1,0:T(8,128)(2,1)S(1)}, u32[]{:S(2)}, u32[]{:S(2)}) %collective-permute-start.13) | collective-permute-done | bytes 294944 | tf_op jit(solution)/shard_map/cond/branch_1_fun/ppermute | solution.py:43
  198.2 3.7 %pad_maximum_fusion = bf16[18,144,1024]{2,1,0:T(8,128)(2,1)S(1)} fusion(bf16[1,144,1024]{2,1,0:T(8,128)(2,1)S(1)} %fusion.9, bf16[1,144,1024]{2,1,0:T(8,128)(2,1)S(1)} %fusion.12, bf16[16,144,1024]{2,1,0:T(8,128)(2,1)} %all-to-all-done.3), kind=kLoop, calls=%fused_computation.24 | loop fusion | flops 5308416 | bytes 10616832 | tf_op jit(solution)/shard_map/cond/branch_1_fun/concatenate | solution.py:290
  202.0 4.2 %branch_1_fun.6 = f32[1024,128]{1,0:T(8,128)} custom-call(s32[32]{0:T(128)S(1)} %get-tuple-element.81.order, s32[32]{0:T(128)S(1)} %fusion.16.sources, bf16[2048,1024]{1,0:T(8,128)(2,1)S(1)} %copy-done.6, bf16[2592,1024]{1,0:T(8,128)(2,1)S(1)} %bitcast.81), custom_call_target="tpu_custom_call" | custom-call | flops 268435456 | bytes 9502720 | tf_op jit(solution)/shard_map/cond/branch_1_fun/pallas_call | solution.py:134
  206.1 8.1 %all-to-all-start.4 = ((f32[8,128,128]{2,1,0:T(8,128)}), f32[8,128,128]{2,1,0:T(8,128)S(1)}, u32[]{:S(2)}, u32[]{:S(2)}) async-start(f32[8,128,128]{2,1,0:T(8,128)} %bitcast.33), calls=%async_computation.6 | async-start | bytes 1048576 | tf_op jit(solution)/shard_map/cond/branch_1_fun/all_to_all | solution.py:19
  215.3 8.4 %all-to-all-done.4 = f32[8,128,128]{2,1,0:T(8,128)S(1)} async-done(((f32[8,128,128]{2,1,0:T(8,128)}), f32[8,128,128]{2,1,0:T(8,128)S(1)}, u32[]{:S(2)}, u32[]{:S(2)}) %all-to-all-start.4) | async-done | bytes 524320 | tf_op jit(solution)/shard_map/cond/branch_1_fun/all_to_all | solution.py:19
  223.7 13.5 %all_gather.5.low = bf16[1024,128]{1,0:T(8,128)(2,1)S(1)} all-gather(bf16[128,128]{1,0:T(8,128)(2,1)S(1)} %reduce_sum.86), channel_id=1, replica_groups=mesh['dp'=16,'tp'=8] {'tp'}, dimensions={0}, use_global_device_ids=true | all-gather | bytes 294912 | tf_op jit(solution)/shard_map/cond/branch_1_fun/all_gather | solution.py:21
  238.5 2.2 branch_1_fun.7
  (119 shorter events, 27.9 us)
Async XLA Ops:
  6.5 7.8 %copy-start.19 = (bf16[1024,1024]{1,0:T(8,128)(2,1)S(1)}, bf16[1024,1024]{1,0:T(8,128)(2,1)}, u32[]{:S(2)}) copy-start(bf16[1024,1024]{1,0:T(8,128)(2,1)} %param.10) | copy-start | bytes 6291460
  15.0 9.2 %copy-start.12 = (s32[32]{0:T(128)}, s32[32]{0:T(128)S(1)}, u32[]{:S(2)}) copy-start(s32[32]{0:T(128)S(1)} %get-tuple-element.67) | copy-start | bytes 388 | tf_op jit(solution)/shard_map/cond
  15.0 9.2 %copy-start.14 = (s32[32]{0:T(128)}, s32[32]{0:T(128)S(1)}, u32[]{:S(2)}) copy-start(s32[32]{0:T(128)S(1)} %get-tuple-element.65) | copy-start | bytes 388 | tf_op jit(solution)/shard_map/cond
  15.0 9.2 %copy-start.16 = (s32[32]{0:T(128)}, s32[32]{0:T(128)S(1)}, u32[]{:S(2)}) copy-start(s32[32]{0:T(128)S(1)} %get-tuple-element.68.counts) | copy-start | bytes 388 | tf_op jit(solution)/shard_map/cond
  15.0 222.2 %reduce-scatter.5.cloned.1.call-start = ((), (), s32[]{:S(2)}) async-start(), calls=%async_computation.8 | async-start | bytes 9437184 | tf_op jit(solution)/shard_map/cond/branch_1_fun/reduce_scatter | solution.py:280
  24.2 5.3 %copy-start.18 = (s32[2]{0:T(128)S(1)}, s32[2]{0:T(128)}, u32[]{:S(2)}) copy-start(s32[2]{0:T(128)} %constant.197) | copy-start | bytes 28 | tf_op jit(solution)/shard_map/cond
  27.3 5.6 %copy-start.9 = (s32[16,32]{1,0:T(8,128)}, s32[16,32]{1,0:T(8,128)S(1)}, u32[]{:S(2)}) copy-start(s32[16,32]{1,0:T(8,128)S(1)} %broadcast_in_dim.79) | copy-start | bytes 6148 | tf_op jit(solution)/shard_map/cond
  34.6 6.8 %copy-start.2 = (bf16[32,144,1024]{2,1,0:T(8,128)(2,1)}, bf16[32,144,1024]{2,1,0:T(8,128)(2,1)S(1)}, u32[]{:S(2)}) copy-start(bf16[32,144,1024]{2,1,0:T(8,128)(2,1)S(1)} %branch_1_fun.5) | copy-start | bytes 28311556 | tf_op jit(solution)/shard_map/cond
  43.8 16.3 %collective-permute-start = (bf16[2,144,1024]{2,1,0:T(8,128)(2,1)}, bf16[2,144,1024]{2,1,0:T(8,128)(2,1)S(1)}, u32[]{:S(2)}, u32[]{:S(2)}) collective-permute-start(bf16[2,144,1024]{2,1,0:T(8,128)(2,1)} %get-tuple-element.96), channel_id=1, source_target_pairs={{0,32},{8,40},{16,48},{24,56},{32,64},{40,72},{48,80},{56,88},{64,... | collective-permute-start | bytes 1769480 | tf_op jit(solution)/shard_map/cond/branch_1_fun/ppermute | solution.py:43
  45.9 14.3 %collective-permute-start.2 = (bf16[2,144,1024]{2,1,0:T(8,128)(2,1)}, bf16[2,144,1024]{2,1,0:T(8,128)(2,1)S(1)}, u32[]{:S(2)}, u32[]{:S(2)}) collective-permute-start(bf16[2,144,1024]{2,1,0:T(8,128)(2,1)} %get-tuple-element.95), channel_id=1, source_target_pairs={{0,96},{8,104},{16,112},{24,120},{32,0},{40,8},{48,16},{56,24},{64... | collective-permute-start | bytes 1769480 | tf_op jit(solution)/shard_map/cond/branch_1_fun/ppermute | solution.py:43
  47.2 19.2 %copy-start.10 = (s32[16,32]{1,0:T(8,128)S(1)}, s32[16,32]{1,0:T(8,128)}, u32[]{:S(2)}) copy-start(s32[16,32]{1,0:T(8,128)} %copy-done.9) | copy-start | bytes 6148 | tf_op jit(solution)/shard_map/cond
  47.2 19.2 %copy-start.11 = (pred[16,32]{1,0:T(8,128)(4,1)S(1)}, pred[16,32]{1,0:T(8,128)(4,1)}, u32[]{:S(2)}) copy-start(pred[16,32]{1,0:T(8,128)(4,1)} %get-tuple-element.103) | copy-start | bytes 1540 | tf_op jit(solution)/shard_map/cond
  47.2 19.5 %copy-start.7 = (bf16[128,64,128]{2,1,0:T(8,128)(2,1)S(1)}, bf16[128,64,128]{2,1,0:T(8,128)(2,1)}, u32[]{:S(2)}) copy-start(bf16[128,64,128]{2,1,0:T(8,128)(2,1)} %get-tuple-element.76.up) | copy-start | bytes 6291460 | tf_op jit(solution)/shard_map/cond
  63.7 27.3 %collective-permute-start.1 = (bf16[4,144,1024]{2,1,0:T(8,128)(2,1)}, bf16[4,144,1024]{2,1,0:T(8,128)(2,1)}, u32[]{:S(2)}, u32[]{:S(2)}) collective-permute-start(bf16[4,144,1024]{2,1,0:T(8,128)(2,1)} %get-tuple-element.92), channel_id=1, source_target_pairs={{0,32},{8,40},{16,48},{24,56},{32,64},{40,72},{48,80},{56,88},{64,... | collective-permute-start | bytes 3538952 | tf_op jit(solution)/shard_map/cond/branch_1_fun/ppermute | solution.py:43
  64.9 27.1 %collective-permute-start.3 = (bf16[4,144,1024]{2,1,0:T(8,128)(2,1)}, bf16[4,144,1024]{2,1,0:T(8,128)(2,1)}, u32[]{:S(2)}, u32[]{:S(2)}) collective-permute-start(bf16[4,144,1024]{2,1,0:T(8,128)(2,1)} %get-tuple-element.91), channel_id=1, source_target_pairs={{0,96},{8,104},{16,112},{24,120},{32,0},{40,8},{48,16},{56,24},{64... | collective-permute-start | bytes 3538952 | tf_op jit(solution)/shard_map/cond/branch_1_fun/ppermute | solution.py:43
  72.5 125.7 %all-to-all-start.3 = ((bf16[16,144,1024]{2,1,0:T(8,128)(2,1)}), bf16[16,144,1024]{2,1,0:T(8,128)(2,1)}, u32[]{:S(2)}, u32[]{:S(2)}) async-start(bf16[16,144,1024]{2,1,0:T(8,128)(2,1)} %copy-done.4), calls=%async_computation.5 | async-start | bytes 9437184 | tf_op jit(solution)/shard_map/cond/branch_1_fun/all_to_all | solution.py:262
  81.9 63.3 %collective-permute-start.7 = (bf16[2,144,1024]{2,1,0:T(8,128)(2,1)S(1)}, bf16[2,144,1024]{2,1,0:T(8,128)(2,1)S(1)}, u32[]{:S(2)}, u32[]{:S(2)}) collective-permute-start(bf16[2,144,1024]{2,1,0:T(8,128)(2,1)S(1)} %get-tuple-element.98), channel_id=1, source_target_pairs={{0,8},{8,16},{16,24},{24,0},{32,40},{40,48},{48,56},{56,32},{64,72... | collective-permute-start | bytes 1769480 | tf_op jit(solution)/shard_map/cond/branch_1_fun/ppermute | solution.py:43
  84.2 61.1 %collective-permute-start.9 = (bf16[2,144,1024]{2,1,0:T(8,128)(2,1)S(1)}, bf16[2,144,1024]{2,1,0:T(8,128)(2,1)S(1)}, u32[]{:S(2)}, u32[]{:S(2)}) collective-permute-start(bf16[2,144,1024]{2,1,0:T(8,128)(2,1)S(1)} %get-tuple-element.97), channel_id=1, source_target_pairs={{0,24},{8,0},{16,8},{24,16},{32,56},{40,32},{48,40},{56,48},{64,88... | collective-permute-start | bytes 1769480 | tf_op jit(solution)/shard_map/cond/branch_1_fun/ppermute | solution.py:43
  93.1 58.1 %copy-start.13 = (s32[32]{0:T(128)S(1)}, s32[32]{0:T(128)}, u32[]{:S(2)}) copy-start(s32[32]{0:T(128)} %copy-done.12) | copy-start | bytes 388 | tf_op jit(solution)/shard_map/cond
  93.2 58.1 %copy-start.15 = (s32[32]{0:T(128)S(1)}, s32[32]{0:T(128)}, u32[]{:S(2)}) copy-start(s32[32]{0:T(128)} %copy-done.14) | copy-start | bytes 388 | tf_op jit(solution)/shard_map/cond
  148.6 27.7 %collective-permute-start.8 = (bf16[4,144,1024]{2,1,0:T(8,128)(2,1)}, bf16[4,144,1024]{2,1,0:T(8,128)(2,1)S(1)}, u32[]{:S(2)}, u32[]{:S(2)}) collective-permute-start(bf16[4,144,1024]{2,1,0:T(8,128)(2,1)} %get-tuple-element.90), channel_id=1, source_target_pairs={{0,8},{8,16},{16,24},{24,0},{32,40},{40,48},{48,56},{56,32},{64,72... | collective-permute-start | bytes 3538952 | tf_op jit(solution)/shard_map/cond/branch_1_fun/ppermute | solution.py:43
  148.6 29.1 %collective-permute-start.10 = (bf16[4,144,1024]{2,1,0:T(8,128)(2,1)}, bf16[4,144,1024]{2,1,0:T(8,128)(2,1)S(1)}, u32[]{:S(2)}, u32[]{:S(2)}) collective-permute-start(bf16[4,144,1024]{2,1,0:T(8,128)(2,1)} %get-tuple-element.89), channel_id=1, source_target_pairs={{0,24},{8,0},{16,8},{24,16},{32,56},{40,32},{48,40},{56,48},{64,88... | collective-permute-start | bytes 3538952 | tf_op jit(solution)/shard_map/cond/branch_1_fun/ppermute | solution.py:43
  155.6 27.0 %collective-permute-start.5 = (bf16[144,1024]{1,0:T(8,128)(2,1)S(1)}, bf16[144,1024]{1,0:T(8,128)(2,1)S(1)}, u32[]{:S(2)}, u32[]{:S(2)}) collective-permute-start(bf16[144,1024]{1,0:T(8,128)(2,1)S(1)} %get-tuple-element.99), channel_id=1, source_target_pairs={{0,8},{8,16},{16,24},{24,0},{32,40},{40,48},{48,56},{56,32},{64,72... | collective-permute-start | bytes 884744 | tf_op jit(solution)/shard_map/cond/branch_1_fun/ppermute | solution.py:43
  179.4 7.3 %collective-permute-start.12 = (bf16[144,1024]{1,0:T(8,128)(2,1)S(1)}, bf16[144,1024]{1,0:T(8,128)(2,1)S(1)}, u32[]{:S(2)}, u32[]{:S(2)}) collective-permute-start(bf16[144,1024]{1,0:T(8,128)(2,1)S(1)} %get-tuple-element.101), channel_id=1, source_target_pairs={{0,32},{8,40},{16,48},{24,56},{32,64},{40,72},{48,80},{56,88},{64,... | collective-permute-start | bytes 884744 | tf_op jit(solution)/shard_map/cond/branch_1_fun/ppermute | solution.py:43
  179.6 11.3 %collective-permute-start.4 = (bf16[144,1024]{1,0:T(8,128)(2,1)S(1)}, bf16[144,1024]{1,0:T(8,128)(2,1)S(1)}, u32[]{:S(2)}, u32[]{:S(2)}) collective-permute-start(bf16[144,1024]{1,0:T(8,128)(2,1)S(1)} %get-tuple-element.100), channel_id=1, source_target_pairs={{0,24},{8,0},{16,8},{24,16},{32,56},{40,32},{48,40},{56,48},{64,88... | collective-permute-start | bytes 884744 | tf_op jit(solution)/shard_map/cond/branch_1_fun/ppermute | solution.py:43
  182.7 8.3 %collective-permute-start.6 = (bf16[144,1024]{1,0:T(8,128)(2,1)S(1)}, bf16[144,1024]{1,0:T(8,128)(2,1)S(1)}, u32[]{:S(2)}, u32[]{:S(2)}) collective-permute-start(bf16[144,1024]{1,0:T(8,128)(2,1)S(1)} %fusion.10), channel_id=1, source_target_pairs={{0,8},{8,16},{16,24},{24,0},{32,40},{40,48},{48,56},{56,32},{64,72... | collective-permute-start | bytes 884744 | tf_op jit(solution)/shard_map/cond/branch_1_fun/ppermute | solution.py:43
  182.7 8.3 %collective-permute-start.11 = (bf16[144,1024]{1,0:T(8,128)(2,1)S(1)}, bf16[144,1024]{1,0:T(8,128)(2,1)S(1)}, u32[]{:S(2)}, u32[]{:S(2)}) collective-permute-start(bf16[144,1024]{1,0:T(8,128)(2,1)S(1)} %get-tuple-element.102), channel_id=1, source_target_pairs={{0,96},{8,104},{16,112},{24,120},{32,0},{40,8},{48,16},{56,24},{64... | collective-permute-start | bytes 884744 | tf_op jit(solution)/shard_map/cond/branch_1_fun/ppermute | solution.py:43
  186.8 11.4 %collective-permute-start.13 = (bf16[144,1024]{1,0:T(8,128)(2,1)S(1)}, bf16[144,1024]{1,0:T(8,128)(2,1)S(1)}, u32[]{:S(2)}, u32[]{:S(2)}) collective-permute-start(bf16[144,1024]{1,0:T(8,128)(2,1)S(1)} %fusion.7), channel_id=1, source_target_pairs={{0,32},{8,40},{16,48},{24,56},{32,64},{40,72},{48,80},{56,88},{64,... | collective-permute-start | bytes 884744 | tf_op jit(solution)/shard_map/cond/branch_1_fun/ppermute | solution.py:43
  198.2 3.8 %copy-start.6 = (bf16[2048,1024]{1,0:T(8,128)(2,1)S(1)}, bf16[2048,1024]{1,0:T(8,128)(2,1)}, u32[]{:S(2)}) copy-start(bf16[2048,1024]{1,0:T(8,128)(2,1)} %get-tuple-element.69.hidden) | copy-start | bytes 12582916 | tf_op jit(solution)/shard_map/cond
  201.9 4.2 %copy-start.3 = (bf16[18,144,1024]{2,1,0:T(8,128)(2,1)}, bf16[18,144,1024]{2,1,0:T(8,128)(2,1)S(1)}, u32[]{:S(2)}) copy-start(bf16[18,144,1024]{2,1,0:T(8,128)(2,1)S(1)} %pad_maximum_fusion) | copy-start | bytes 15925252 | tf_op jit(solution)/shard_map/cond
  206.1 31.1 %copy-start.17 = (s32[32]{0:T(128)S(1)}, s32[32]{0:T(128)}, u32[]{:S(2)}) copy-start(s32[32]{0:T(128)} %copy-done.16) | copy-start | bytes 388 | tf_op jit(solution)/shard_map/cond
  206.1 17.6 %all-to-all-start.4 = ((f32[8,128,128]{2,1,0:T(8,128)}), f32[8,128,128]{2,1,0:T(8,128)S(1)}, u32[]{:S(2)}, u32[]{:S(2)}) async-start(f32[8,128,128]{2,1,0:T(8,128)} %bitcast.33), calls=%async_computation.6 | async-start | bytes 1048576 | tf_op jit(solution)/shard_map/cond/branch_1_fun/all_to_all | solution.py:19
  (5 other events, 5.8 us)
Sparse Core Ops, SparseCore 0:
  24.4 55.1 reduce-scatter.4

commit v3 on v1

v3 whole, which is shorter than its diff:
```python
import functools
import math

import jax
import jax.numpy as jnp
from jax import lax
from jax.experimental import pallas as pl
from jax.experimental.pallas import tpu as pltpu
from jax.sharding import PartitionSpec as P

ADAPTER_SCALE = 0.5
MAIN = 2
MOST = 6
EXTRA = MOST - MAIN


def low_rank_sum(partial):
    rows, rank = partial.shape
    tp_count = lax.axis_size("tp")
    pieces = lax.all_to_all(partial, "tp", split_axis=0, concat_axis=0, tiled=True)
    mine = jnp.sum(pieces.reshape(tp_count, rows // tp_count, rank), axis=0).astype(jnp.bfloat16)
    return lax.all_gather(mine, "tp", axis=0, tiled=True)


def finish(base, low, ups, counts):
    groups = counts.shape[0]
    cap = base.shape[0] // groups
    delta = jnp.einsum(
        "gcr,grv->gcv", low.reshape(groups, cap, -1), ups, preferred_element_type=jnp.float32
    )
    merged = base.reshape(groups, cap, -1) + ADAPTER_SCALE * delta
    active = jnp.arange(cap)[None, :, None] < counts[:, None, None]
    out = jnp.where(active, merged, jnp.float32(0.0)).astype(jnp.bfloat16)
    return out.reshape(base.shape)


SMEM = pl.BlockSpec(memory_space=pltpu.SMEM)
VMEM = pl.BlockSpec(memory_space=pltpu.VMEM)
HBM = pl.BlockSpec(memory_space=pl.ANY)
LANES = 128
ORDER, PLACE, FLAGS = 0, 1, 2
HOT, FITS = 0, 1


def shift(value, dx, dy):
    side = math.isqrt(lax.axis_size("dp"))
    pairs = [
        (x * side + y, (x + dx) % side * side + (y + dy) % side)
        for x in range(side)
        for y in range(side)
    ]
    return lax.ppermute(value, "dp", pairs)


def index_kernel(me_ref, ids_ref, table_ref, served_ref, mine_ref, owner_ref, rank_ref):
    total = ids_ref.shape[0]
    dp_count = served_ref.shape[0]
    groups = total // dp_count
    chunks = table_ref.shape[0]
    owned = chunks * LANES // dp_count
    me = me_ref[0]
    f32, bf16 = jnp.float32, jnp.bfloat16
    ids = ids_ref[...]
    lane = lax.broadcasted_iota(jnp.int32, (total, LANES), 1)
    found = jnp.zeros((total, LANES), jnp.int32)
    for c in range(chunks):
        found += jnp.where(ids == lane + c * LANES, table_ref[c : c + 1, :], 0)
    stored = jnp.sum(found, axis=1, keepdims=True)
    owner = lax.div(stored, owned)
    slot = stored - owner * owned
    holds = jnp.where(owner == lane, 1.0, 0.0)
    low = lax.broadcasted_iota(jnp.int32, (groups, groups), 0)
    low = jnp.where(low > lax.broadcasted_iota(jnp.int32, (groups, groups), 1), 1.0, 0.0)
    low = low.astype(bf16)
    holds16 = holds.astype(bf16)
    before = jnp.concatenate(
        [
            jnp.dot(low, holds16[r * groups : (r + 1) * groups], preferred_element_type=f32)
            for r in range(dp_count)
        ],
        axis=0,
    )
    ranking = jnp.sum(before * holds, axis=1, keepdims=True).astype(jnp.int32)
    owner_ref[...] = jnp.broadcast_to(owner, (total, LANES))
    rank_ref[...] = jnp.broadcast_to(ranking, (total, LANES))
    block_of = lax.div(lax.broadcasted_iota(jnp.int32, (dp_count, total), 1), groups)
    block = block_of == lax.broadcasted_iota(jnp.int32, (dp_count, total), 0)
    block = jnp.where(block, 1.0, 0.0).astype(bf16)
    loads = jnp.dot(block, holds16, preferred_element_type=f32)
    kept = jnp.where((owner == me) & (ranking == lane), slot, 0).astype(f32).astype(bf16)
    served_ref[...] = jnp.dot(block, kept, preferred_element_type=f32).astype(jnp.int32)
    least = jnp.min(loads, axis=0, keepdims=True)
    row_lane = lax.broadcasted_iota(jnp.int32, (1, LANES), 1)
    hot = jnp.min(jnp.where(least >= MOST, row_lane, LANES), axis=1, keepdims=True)
    spare = jnp.where(row_lane == hot, 0.0, loads)
    most = jnp.max(jnp.max(spare, axis=0, keepdims=True), axis=1, keepdims=True)
    fits = jnp.where(most <= MAIN, 1, 0)
    at = pl.ds(pl.multiple_of(me * groups, groups), groups)
    my_owner = owner_ref[at, :]
    my_rank = rank_ref[at, :]
    late = (my_owner == hot) & (my_rank >= MAIN)
    place = jnp.where(late, dp_count * MAIN + my_rank - MAIN, my_owner * MAIN + my_rank)
    early = jnp.where(late, 0.0, 1.0).astype(bf16)
    ahead = jnp.dot(low, early, preferred_element_type=f32).astype(jnp.int32)
    turn = jnp.where(late, groups - EXTRA + my_rank - MAIN, ahead)
    group_lane = lax.broadcasted_iota(jnp.int32, (groups, LANES), 1)
    group = lax.broadcasted_iota(jnp.int32, (groups, LANES), 0)
    here = turn == group_lane
    mine_ref[...] = jnp.zeros(mine_ref.shape, jnp.int32)
    mine_ref[ORDER : ORDER + 1, :] = jnp.sum(jnp.where(here, group, 0), axis=0, keepdims=True)
    mine_ref[PLACE : PLACE + 1, :] = jnp.sum(jnp.where(here, place, 0), axis=0, keepdims=True)
    mine_ref[FLAGS : FLAGS + 1, :] = jnp.where(
        row_lane == HOT, hot, jnp.where(row_lane == FITS, fits, 0)
    )


def index_tables(me, ids, table, dp_count):
    total = ids.shape[0]
    return pl.pallas_call(
        index_kernel,
        out_shape=(
            jax.ShapeDtypeStruct((dp_count, LANES), jnp.int32),
            jax.ShapeDtypeStruct((8, LANES), jnp.int32),
        ),
        in_specs=[SMEM, VMEM, VMEM],
        out_specs=(VMEM, VMEM),
        scratch_shapes=[pltpu.VMEM((total, LANES), jnp.int32)] * 2,
        compiler_params=pltpu.CompilerParams(vmem_limit_bytes=8 << 20),
    )(me, ids.reshape(total, 1), table.reshape(-1, LANES))


def copy_units(wanted, down, up, up_in, up_out, down_sem, up_sem, out_sem):
    rank = down.shape[1]
    lanes = up.shape[2]
    steps = rank // 16
    waits = []
    ups = []
    for i, (dest, index, rows) in enumerate(wanted):
        for half in range(2):
            n = 2 * i + half
            ups.append(pltpu.make_async_copy(up.at[rows[half]], up_in.at[n], up_sem.at[n]))
            ups[-1].start()
            waits.append(
                pltpu.make_async_copy(
                    down.at[rows[half]], dest.at[index, pl.ds(half * rank, rank)], down_sem.at[n]
                )
            )
            waits[-1].start()
    for i, (dest, index, rows) in enumerate(wanted):
        for half in range(2):
            n = 2 * i + half
            ups[n].wait()
            for part in range(steps):
                at = (half * steps + part) * lanes
                up_out[i, :, at : at + lanes] = up_in[n, part * 16 : part * 16 + 16, :]
        waits.append(
            pltpu.make_async_copy(
                up_out.at[i], dest.at[index, pl.ds(2 * rank, 16)], out_sem.at[i]
            )
        )
        waits[-1].start()
    for copy in waits:
        copy.wait()


def main_kernel(served, down, up, out, *scratch):
    wanted = [(out, p, (served[p, 0], served[p, 1])) for p in range(out.shape[0])]
    copy_units(wanted, down, up, *scratch)


def extra_kernel(lines, me, served, mine, down, up, *refs):
    outs, scratch = refs[: len(lines)], refs[len(lines) :]
    dp_count = served.shape[0]
    side = math.isqrt(dp_count)
    hot = mine[FLAGS, HOT]

    @pl.when(hot == me[0])
    def _():
        hot_x, hot_y = lax.div(hot, side), lax.rem(hot, side)
        wanted = []
        for out, (x_first, a, units) in zip(outs, lines):
            for i, b in enumerate(units):
                dx, dy = (a, b) if x_first else (b, a)
                peer = lax.rem(hot_x + dx, side) * side + lax.rem(hot_y + dy, side)
                first = MAIN if x_first else MAIN + 2
                wanted.append((out, i, (served[peer, first], served[peer, first + 1])))
        copy_units(wanted, down, up, *scratch)


def gather_call(kernel, shapes, count, scalars, down, up):
    _, rank, width = down.shape
    lanes = up.shape[2]
    return pl.pallas_call(
        kernel,
        out_shape=[jax.ShapeDtypeStruct((n, 2 * rank + 16, width), down.dtype) for n in shapes],
        in_specs=[SMEM] * len(scalars) + [HBM, HBM],
        out_specs=[HBM] * len(shapes),
        scratch_shapes=[
            pltpu.VMEM((2 * count, rank, lanes), up.dtype),
            pltpu.VMEM((count, 16, width), up.dtype),
            pltpu.SemaphoreType.DMA((2 * count,)),
            pltpu.SemaphoreType.DMA((2 * count,)),
            pltpu.SemaphoreType.DMA((count,)),
        ],
        compiler_params=pltpu.CompilerParams(vmem_limit_bytes=12 << 20),
        cost_estimate=pl.CostEstimate(
            flops=0, bytes_accessed=count * rank * (width + lanes) * 8, transcendentals=0
        ),
    )(*scalars, down, up)


def local_copies(when, copies, sems):
    @pl.when(when)
    def _():
        started = [
            pltpu.make_async_copy(src, dst, sems.at[i]) for i, (src, dst) in enumerate(copies)
        ]
        for copy in started:
            copy.start()
        for copy in started:
            copy.wait()


def relay_kernel(offsets, *refs):
    sems = refs[-1]
    fresh = refs[:4]
    outs = refs[8:12]
    for i in range(4):
        near = 1 if i % 2 == 0 else 3
        local_copies(offsets[i // 2] == near, [(fresh[i], outs[i].at[pl.ds(0, 2)])], sems)


def relay(offsets, fresh, kept):
    return pl.pallas_call(
        relay_kernel,
        out_shape=[jax.ShapeDtypeStruct(k.shape, k.dtype) for k in kept],
        in_specs=[SMEM] + [HBM] * 8,
        out_specs=[HBM] * 4,
        input_output_aliases={5 + i: i for i in range(4)},
        scratch_shapes=[pltpu.SemaphoreType.DMA((4,))],
        cost_estimate=pl.CostEstimate(flops=0, bytes_accessed=1 << 21, transcendentals=0),
    )(offsets, *fresh, *kept)


def line_kernel(offsets, *refs):
    sems = refs[-1]
    ins, outs = refs[:6], refs[6:14]
    for h in range(2):
        own, plus, minus = ins[3 * h : 3 * h + 3]
        out = outs[4 * h : 4 * h + 4]
        far = [plus.at[0], plus.at[1], minus.at[0], minus.at[1]]
        for a, source in ((0, own), (1, plus), (2, None), (3, minus)):
            copies = [(far[i] if a == 2 else source.at[i], out[i]) for i in range(4)]
            local_copies(offsets[h] == a, copies, sems)


def line(offsets, ins):
    unit = ins[0].shape[1:]
    return pl.pallas_call(
        line_kernel,
        out_shape=[jax.ShapeDtypeStruct(unit, ins[0].dtype)] * 8,
        in_specs=[SMEM] + [HBM] * 6,
        out_specs=[HBM] * 8,
        scratch_shapes=[pltpu.SemaphoreType.DMA((4,))],
        cost_estimate=pl.CostEstimate(flops=0, bytes_accessed=5 << 20, transcendentals=0),
    )(offsets, *ins)


def pass_kernel(offsets, *refs):
    sems = refs[-1]
    for h in range(2):
        local_copies(offsets[1 - h] == 1, [(refs[h], refs[4 + h])], sems)


def pass_on(offsets, fresh, kept):
    return pl.pallas_call(
        pass_kernel,
        out_shape=[jax.ShapeDtypeStruct(k.shape, k.dtype) for k in kept],
        in_specs=[SMEM] + [HBM] * 4,
        out_specs=[HBM] * 2,
        input_output_aliases={3: 0, 4: 1},
        scratch_shapes=[pltpu.SemaphoreType.DMA((2,))],
        cost_estimate=pl.CostEstimate(flops=0, bytes_accessed=1 << 20, transcendentals=0),
    )(offsets, *fresh, *kept)


def low_kernel(mine, hidden, main, *refs):
    extras, out = refs[:-1], refs[-1]
    rank = out.shape[1] // 2
    dp_count = main.shape[0]
    pairs = dp_count
    cap = out.shape[0] // pairs

    def product(j, weights):
        g = pl.multiple_of(mine[ORDER, j] * cap, cap)
        return lax.dot_general(
            hidden[pl.ds(g, cap), :],
            weights,
            (((1,), (1,)), ((), ())),
            preferred_element_type=jnp.float32,
        )

    def one(j):
        place = mine[PLACE, j]
        unit = lax.div(place, 2)
        at = pl.multiple_of((place - 2 * unit) * rank, rank)
        return product(j, main[unit, pl.ds(at, rank), :])

    def store(i, first, second):
        out[pl.ds(pl.multiple_of(i * cap, cap), cap), :] = jnp.concatenate([first, second], axis=1)

    def body(i, carry):
        store(i, one(i), one(i + pairs))
        return carry

    full = pairs - 2 * len(extras)
    lax.fori_loop(0, full, body, 0, unroll=2)
    for e in range(2 * len(extras)):
        weights = extras[e // 2][e % 2 * rank : (e % 2 + 1) * rank, :]
        store(full + e, one(full + e), product(full + e + pairs, weights))


def low_partial(mine, hidden, main, extras, cap, rank):
    pairs = main.shape[0]
    return pl.pallas_call(
        low_kernel,
        out_shape=jax.ShapeDtypeStruct((pairs * cap, 2 * rank), jnp.float32),
        in_specs=[SMEM] + [VMEM] * (2 + len(extras)),
        out_specs=VMEM,
        compiler_params=pltpu.CompilerParams(vmem_limit_bytes=24 << 20),
        cost_estimate=pl.CostEstimate(
            flops=hidden.size * rank * 2,
            bytes_accessed=(hidden.size + main.size) * 2,
            transcendentals=0,
        ),
    )(mine, hidden, main, *extras)


def low_rank_rounds(partial):
    tp_count = lax.axis_size("tp")
    chips = tp_count // 2
    t = lax.axis_index("tp")
    z, core = t // 2, t % 2
    half = partial.shape[0] // 2
    piece = half // chips
    swap = [(i, i ^ 1) for i in range(tp_count)]
    turn = lambda d: [(i, (i + 2 * d) % tp_count) for i in range(tp_count)]
    cut = lambda array, start, size: lax.dynamic_slice_in_dim(array, start, size, 0)
    total = cut(partial, core * half, half) + lax.ppermute(
        cut(partial, (1 - core) * half, half), "tp", swap
    )
    pieces = [
        lax.ppermute(cut(total, (z + d) % chips * piece, piece), "tp", turn(d))
        for d in range(1, chips)
    ]
    summed = (cut(total, z * piece, piece) + sum(pieces)).astype(jnp.bfloat16)
    own = jnp.stack([summed] + [lax.ppermute(summed, "tp", turn(d)) for d in range(1, chips)])
    return own, lax.ppermute(own, "tp", swap)


def out_kernel(where, mine, counts, base, own, other, main, *refs):
    extras, out = refs[:-1], refs[-1]
    groups = counts.shape[0]
    pairs = groups // 2
    cap = base.shape[0] // groups
    chips, piece, rank = own.shape[0], own.shape[1], own.shape[2] // 2
    lanes = base.shape[1]
    z, core = where[0], where[1]
    steps = rank // 16
    rows = lax.broadcasted_iota(jnp.int32, (cap, lanes), 0)
    per_piece = piece // cap

    def factors(i):
        half = lax.div(i, pairs // 2)
        rest = i - half * (pairs // 2)
        quarter = lax.div(rest, per_piece)
        at = pl.multiple_of((rest - quarter * per_piece) * cap, cap)
        slot = lax.rem(z - quarter + chips, chips)
        pick = pl.ds(at, cap)
        return jnp.where(half == core, own[slot, pick, :], other[slot, pick, :])

    def one(j, factor, up):
        g = mine[ORDER, j]
        delta = jnp.dot(factor, up, preferred_element_type=jnp.float32)
        here = pl.ds(pl.multiple_of(g * cap, cap), cap)
        merged = base[here, :] + ADAPTER_SCALE * delta
        out[here, :] = jnp.where(rows < counts[g], merged, 0.0).astype(out.dtype)

    def up_main(j):
        place = mine[PLACE, j]
        unit = lax.div(place, 2)
        at = (place - 2 * unit) * steps * lanes
        parts = [
            main[unit, :, pl.ds(pl.multiple_of(at + part * lanes, lanes), lanes)]
            for part in range(steps)
        ]
        return jnp.concatenate(parts, axis=0)

    def body(i, carry):
        both = factors(i)
        one(i, both[:, :rank], up_main(i))
        one(i + pairs, both[:, rank:], up_main(i + pairs))
        return carry

    full = pairs - 2 * len(extras)
    lax.fori_loop(0, full, body, 0, unroll=2)
    for e in range(2 * len(extras)):
        both = factors(jnp.int32(full + e))
        one(full + e, both[:, :rank], up_main(full + e))
        starts = [(e % 2 * steps + part) * lanes for part in range(steps)]
        up = jnp.concatenate([extras[e // 2][:, s : s + lanes] for s in starts], axis=0)
        one(full + e + pairs, both[:, rank:], up)


def combine(where, mine, counts, base, own, other, main, extras, rank):
    packs = pl.BlockSpec((main.shape[0], 16, main.shape[2]), lambda i: (0, rank // 8, 0))
    pack = pl.BlockSpec((16, main.shape[2]), lambda i: (rank // 8, 0))
    whole = lambda array: pl.BlockSpec(array.shape, lambda i: (0,) * array.ndim)
    return pl.pallas_call(
        out_kernel,
        grid=(1,),
        out_shape=jax.ShapeDtypeStruct(base.shape, jnp.bfloat16),
        in_specs=[SMEM, SMEM, SMEM, whole(base), whole(own), whole(other), packs]
        + [pack] * len(extras),
        out_specs=whole(base),
        compiler_params=pltpu.CompilerParams(vmem_limit_bytes=12 << 20),
        cost_estimate=pl.CostEstimate(
            flops=base.size * rank * 2, bytes_accessed=base.size * 8, transcendentals=0
        ),
    )(where, mine, counts, base, own, other, main, *extras)


def on_device(
    hidden,
    value_weight,
    down_weights,
    up_weights,
    group_adapter_id,
    adapter_storage_row,
    group_live_count,
):
    dp_count = lax.axis_size("dp")
    me = lax.axis_index("dp")
    owned, rank, width = down_weights.shape
    groups = group_adapter_id.shape[0] // dp_count
    cap = hidden.shape[0] // groups
    me_row = me.astype(jnp.int32).reshape(1)
    served, mine = index_tables(me_row, group_adapter_id, adapter_storage_row, dp_count)
    counts = lax.dynamic_slice_in_dim(group_live_count, me * groups, groups)

    def wide(hidden, value_weight, down_weights, up_weights):
        stored = adapter_storage_row[group_adapter_id]
        owners = (stored // owned).reshape(dp_count, groups)
        slots = (stored % owned).reshape(dp_count, groups)
        same = owners[:, :, None] == owners[:, None, :]
        earlier = jnp.arange(groups)[None, None, :] < jnp.arange(groups)[None, :, None]
        ranking = jnp.sum(same & earlier, axis=2)
        hits = (owners == me)[:, :, None] & (ranking[:, :, None] == jnp.arange(MOST))
        rows = jnp.sum(jnp.where(hits, slots[:, :, None], 0), axis=1).reshape(-1)
        my_owners = lax.dynamic_index_in_dim(owners, me, 0, keepdims=False)
        my_ranking = lax.dynamic_index_in_dim(ranking, me, 0, keepdims=False)
        base_terms = jnp.dot(hidden, value_weight, preferred_element_type=jnp.float32)
        base = lax.psum_scatter(base_terms, "tp", scatter_dimension=1, tiled=True)
        downs = lax.all_to_all(down_weights[rows], "dp", 0, 0, tiled=True)
        ups = lax.all_to_all(up_weights[rows], "dp", 0, 0, tiled=True)
        picked = my_owners * MOST + my_ranking
        partial = jnp.einsum(
            "gcd,grd->gcr",
            hidden.reshape(groups, cap, width),
            downs[picked],
            preferred_element_type=jnp.float32,
        )
        low = low_rank_sum(partial.reshape(groups * cap, rank))
        return finish(base, low, ups[picked], counts)

    def narrow(hidden, value_weight, down_weights, up_weights):
        side = math.isqrt(dp_count)
        hot = mine[FLAGS, HOT]
        a = (me // side - hot // side) % side
        b = (me % side - hot % side) % side
        offsets = jnp.stack([a, b]).astype(jnp.int32)
        ends = ((True, 2, (0, 1)), (True, 2, (2, 3)), (False, 2, (0, 1)), (False, 2, (2, 3)))
        rest = tuple((x_first, far, (0, 1, 2, 3)) for x_first in (True, False) for far in (1, 3, 0))
        scalars = (me_row, served, mine)
        first = gather_call(
            functools.partial(extra_kernel, ends), (2,) * 4, 8, scalars, down_weights, up_weights
        )
        moves = ((1, 0), (-1, 0), (0, 1), (0, -1))
        send = lambda values, ways: [shift(v, *way) for v, way in zip(values, ways)]
        fresh = send(first, moves)
        (main_sent,) = gather_call(
            main_kernel, (dp_count,), dp_count, (served,), down_weights, up_weights
        )
        main = lax.all_to_all(main_sent, "dp", 0, 0, tiled=True)
        after, _ = lax.optimization_barrier((served, main_sent))
        later = gather_call(
            functools.partial(extra_kernel, rest),
            (4,) * 6,
            24,
            (me_row, after, mine),
            down_weights,
            up_weights,
        )
        x_plus, x_minus, x_own, y_plus, y_minus, y_own = later
        hidden, _ = lax.optimization_barrier((hidden, after))
        base_terms = jnp.dot(hidden, value_weight, preferred_element_type=jnp.float32)
        base = lax.psum_scatter(base_terms, "tp", scatter_dimension=1, tiled=True)
        fresh = lax.optimization_barrier(fresh)
        got = send(relay(offsets, fresh, (x_plus, x_minus, y_plus, y_minus)), moves)
        got = lax.optimization_barrier(got)
        lines = line(offsets, (x_own, got[0], got[1], y_own, got[2], got[3]))
        x0, x1, x2, x3, y0, y1, y2, y3 = lines
        x_ahead, x_back, y_ahead, y_back = lax.optimization_barrier(
            send((x2, x3, y2, y3), ((0, 1), (0, -1), (1, 0), (-1, 0)))
        )
        x_next, y_next = send(pass_on(offsets, (x_ahead, y_ahead), (x1, y1)), ((0, 1), (1, 0)))
        extra_x = jnp.where(b == 0, x0, jnp.where(b == 3, x_back, x_next))
        extra_y = jnp.where(a == 0, y0, jnp.where(a == 3, y_back, y_next))
        extras = (extra_x, extra_y)
        partial = low_partial(mine, hidden, main, extras, cap, rank)
        own, other = low_rank_rounds(partial)
        t = lax.axis_index("tp")
        where = jnp.stack([t // 2, t % 2]).astype(jnp.int32)
        return combine(where, mine, counts, base, own, other, main, extras, rank)

    return lax.cond(
        mine[FLAGS, FITS] == 1, narrow, wide, hidden, value_weight, down_weights, up_weights
    )


def solution(mesh):
    return jax.shard_map(
        on_device,
        mesh=mesh,
        in_specs=(
            P("dp", "tp"),
            P("tp", None),
            P("dp", None, "tp"),
            P("dp", None, "tp"),
            P(),
            P(),
            P(),
        ),
        out_specs=P("dp", "tp"),
        check_vma=False,
    )
```

time: 268 us -> 340 us (1.27)
  Pallas kernels: 0 us -> 123 us
  starting transfers between devices: 14 us -> 73 us
  waiting for transfers between devices: 145 us -> 106 us
  other arithmetic: 25.7 us -> 1.74 us
  local copies, waits for them, and re-layouts: 35.5 us -> 13.4 us
  blocking collectives: 14 us -> 0 us
  matrix products: 17.9 us -> 6.68 us
    pallas_call x0 -> x9, Pallas kernels: none -> 123 us  [the longest x1 74.4 us: line(): pl.pallas_call(line_kernel, out_shape=[jax.ShapeDtypeStruct(unit, ins[0]....]
    ppermute x0 -> x22, waiting for transfers between devices: none -> 106 us  [the longest x14 98.8 us: shift(): return lax.ppermute(value, 'dp', pairs)]
    all_to_all x1, waiting for transfers between devices: 89.8 us -> 0.01 us  [narrow(): main = lax.all_to_all(main_sent, 'dp', 0, 0, tiled=True)]
    ppermute x0 -> x22, starting transfers between devices: none -> 65.3 us  [the longest x14 47.2 us: shift(): return lax.ppermute(value, 'dp', pairs)]
    reduce_scatter x1 -> x0, waiting for transfers between devices: 32.4 us -> none  [narrow(): extra = lax.psum_scatter(extra_sent, 'dp', scatter_dimension=0, tiled=True)]
    gather x7 -> x0, local copies, waits for them, and re-layouts: 30.7 us -> none  [the longest x1 11.5 us: narrow(): down_weights[extra_rows]]
    all_gather x1 -> x0, blocking collectives: 14 us -> none  [low_rank_sum(): return lax.all_gather(mine, 'tp', axis=0, tiled=True)]
    all_to_all x1 -> x0, waiting for transfers between devices: 12.5 us -> none  [low_rank_sum(): lax.all_to_all(partial, 'tp', split_axis=0, concat_axis=0, tiled=True)]
  transfers between devices with their start and end apart: 4 -> 24, of which waited for: 4 -> 18; matrix products, arithmetic and copies ran while one was open for 16% -> 1% of each run, Pallas kernels for 0% -> 33%
where the time goes in v3:
time: 340 us; the launch traced here: 341 us
  Pallas kernels  123 us (36%)
  waiting for transfers between devices  106 us (31%)
  starting transfers between devices  73 us (21%)
  between operations  14 us (4%)
  local copies, waits for them, and re-layouts  13.4 us (4%)
  matrix products  6.68 us (2%)
    ppermute x14, waiting for transfers between devices, shift(): return lax.ppermute(value, 'dp', pairs)  98.8 us
    pallas_call x1, Pallas kernels, line(): pl.pallas_call(line_kernel, out_shape=[jax.ShapeDtypeStruct(unit, ins[0]....  74.4 us
    ppermute x14, starting transfers between devices, shift(): return lax.ppermute(value, 'dp', pairs)  47.2 us
    pallas_call x1, Pallas kernels, relay(): pl.pallas_call(relay_kernel, out_shape=[jax.ShapeDtypeStruct(k.shape, k.d...  19.7 us
    pallas_call x1, Pallas kernels, pass_on(): pl.pallas_call(pass_kernel, out_shape=[jax.ShapeDtypeStruct(k.shape, k.dt...  10.7 us
    cond x38, local copies, waits for them, and re-layouts  10.6 us
    all_to_all x1, starting transfers between devices, narrow(): main = lax.all_to_all(main_sent, 'dp', 0, 0, tiled=True)  7.66 us
    pallas_call x3, Pallas kernels, gather_call(): pl.pallas_call(kernel, out_shape=[jax.ShapeDtypeStruct((n, 2 * rank + 16,...  7.06 us
  transfers between devices with their start and end apart: 24, of which 18 were waited for; matrix products, arithmetic and copies ran while one was open for 1% of the time, Pallas kernels for 33%

profile of v3, /device:TPU:1, one launch (start us, length us, event | category | flops | bytes accessed | tf_op | source)
XLA Modules:
  0.0 341.0 jit_solution(16118962433564688309)
XLA Ops:
  8.1 1.8 shard_map.75
  11.2 322.9 %conditional.1 = (bf16[2048,128]{1,0:T(8,128)(2,1)}) conditional(s32[]{:T(128)} %bitcast.20, (s32[32]{0:T(128)S(1)}, bf16[2048,1024]{1,0:T(8,128)(2,1)}, bf16[1024,1024]{1,0:T(8,128)(2,1)}, s32[512]{0:T(512)}, s32[2048]{0:T(1024)}, /*index=5*/s32[]{:T(128)}, bf16[128,64,1024]{2,1,0:T(8,128)(2,1)}, bf16[128,64,128]{2,1,0:T(8,128)(2,1)}) %tuple.16, ...), branch_computations={%region_0.5_spmd, %region_5.7_spmd} | conditional | flops 4598219776 | bytes 245403776 | solution.py:526
  11.5 4.1 %branch_1_fun.8 = bf16[16,144,1024]{2,1,0:T(8,128)(2,1)S(1)} custom-call(s32[16,128]{1,0:T(8,128)S(1)} %get-tuple-element.56.served, bf16[128,64,1024]{2,1,0:T(8,128)(2,1)} %get-tuple-element.54.down, bf16[128,64,128]{2,1,0:T(8,128)(2,1)} %get-tuple-element.55.up), custom_call_target="tpu_custom_call" | custom-call | bytes 9437184 | tf_op jit(solution)/shard_map/cond/branch_1_fun/pallas_call | solution.py:193
  15.6 2.1 copy-done
  17.7 6.7 %fusion.8 = f32[2048,1024]{1,0:T(8,128)} fusion(bf16[2048,1024]{1,0:T(8,128)(2,1)S(1)} %copy-done.10, bf16[1024,1024]{1,0:T(8,128)(2,1)S(1)} %copy-done.21), kind=kOutput, calls=%fused_computation.44 | convolution fusion | flops 4294967296 | bytes 14680064 | tf_op jit(solution)/shard_map/cond/branch_1_fun/dot_general | solution.py:506
  24.5 7.7 %all-to-all-start.3 = ((bf16[16,144,1024]{2,1,0:T(8,128)(2,1)}), bf16[16,144,1024]{2,1,0:T(8,128)(2,1)}, u32[]{:S(2)}, u32[]{:S(2)}) async-start(bf16[16,144,1024]{2,1,0:T(8,128)(2,1)} %copy-done), calls=%async_computation.5 | async-start | bytes 9437184 | tf_op jit(solution)/shard_map/cond/branch_1_fun/all_to_all | solution.py:494
  34.6 3.1 collective-permute-start.1
  37.7 2.7 collective-permute-start.3
  43.5 1.8 branch_1_fun.9
  52.2 64.0 %collective-permute-done.refs_0_ = bf16[2,144,1024]{2,1,0:T(8,128)(2,1)S(1)} collective-permute-done((bf16[2,144,1024]{2,1,0:T(8,128)(2,1)S(1)}, bf16[2,144,1024]{2,1,0:T(8,128)(2,1)S(1)}, u32[]{:S(2)}, u32[]{:S(2)}) %collective-permute-start) | collective-permute-done | bytes 589856 | tf_op jit(solution)/shard_map/cond/branch_1_fun/ppermute | solution.py:52
  117.2 19.7 %branch_1_fun.11 = (bf16[4,144,1024]{2,1,0:T(8,128)(2,1)}, bf16[4,144,1024]{2,1,0:T(8,128)(2,1)}, bf16[4,144,1024]{2,1,0:T(8,128)(2,1)}, bf16[4,144,1024]{2,1,0:T(8,128)(2,1)}) custom-call(s32[2]{0:T(128)} %pad_add_fusion.1.offsets, bf16[2,144,1024]{2,1,0:T(8,128)(2,1)} %copy-done.14, ...), custom_call_target="tpu_custom_call", output_to_operand_aliasing={{0}: (5, {}), {1}: (6, {}), {2}: (7, {}), {3}: (8, {})} | custom-call | bytes 2097152 | tf_op jit(solution)/shard_map/cond/branch_1_fun/pallas_call | solution.py:234
  136.9 2.7 collective-permute-start.5
  139.6 16.0 %collective-permute-start.6 = (bf16[4,144,1024]{2,1,0:T(8,128)(2,1)}, bf16[4,144,1024]{2,1,0:T(8,128)(2,1)S(1)}, u32[]{:S(2)}, u32[]{:S(2)}) collective-permute-start(bf16[4,144,1024]{2,1,0:T(8,128)(2,1)} %get-tuple-element.76), channel_id=1, source_target_pairs={{0,8},{8,16},{16,24},{24,0},{32,40},{40,48},{48,56},{56,32},{64,72... | collective-permute-start | bytes 3538952 | tf_op jit(solution)/shard_map/cond/branch_1_fun/ppermute | solution.py:52
  155.6 8.6 %collective-permute-done.4.refs_1_ = bf16[4,144,1024]{2,1,0:T(8,128)(2,1)S(1)} collective-permute-done((bf16[4,144,1024]{2,1,0:T(8,128)(2,1)}, bf16[4,144,1024]{2,1,0:T(8,128)(2,1)S(1)}, u32[]{:S(2)}, u32[]{:S(2)}) %collective-permute-start.4) | collective-permute-done | bytes 1179680 | tf_op jit(solution)/shard_map/cond/branch_1_fun/ppermute | solution.py:52
  164.3 1.8 collective-permute-done.5.refs_2_
  166.0 12.7 %collective-permute-done.6.refs_4_ = bf16[4,144,1024]{2,1,0:T(8,128)(2,1)S(1)} collective-permute-done((bf16[4,144,1024]{2,1,0:T(8,128)(2,1)}, bf16[4,144,1024]{2,1,0:T(8,128)(2,1)S(1)}, u32[]{:S(2)}, u32[]{:S(2)}) %collective-permute-start.6) | collective-permute-done | bytes 1179680 | tf_op jit(solution)/shard_map/cond/branch_1_fun/ppermute | solution.py:52
  178.8 1.9 collective-permute-done.7.refs_5_
  180.7 74.4 %branch_1_fun.12 = (bf16[144,1024]{1,0:T(8,128)(2,1)}, bf16[144,1024]{1,0:T(8,128)(2,1)}, bf16[144,1024]{1,0:T(8,128)(2,1)}, bf16[144,1024]{1,0:T(8,128)(2,1)}, ...) custom-call(s32[2]{0:T(128)} %pad_add_fusion.1.offsets, ...), custom_call_target="tpu_custom_call" | custom-call | bytes 5242880 | tf_op jit(solution)/shard_map/cond/branch_1_fun/pallas_call | solution.py:259
  255.1 7.0 %collective-permute-start.10 = (bf16[144,1024]{1,0:T(8,128)(2,1)}, bf16[144,1024]{1,0:T(8,128)(2,1)S(1)}, u32[]{:S(2)}, u32[]{:S(2)}) collective-permute-start(bf16[144,1024]{1,0:T(8,128)(2,1)} %get-tuple-element.86), channel_id=1, source_target_pairs={{0,32},{8,40},{16,48},{24,56},{32,64},{40,72},{48,80},{56,88},{64,... | collective-permute-start | bytes 884744 | tf_op jit(solution)/shard_map/cond/branch_1_fun/ppermute | solution.py:52
  262.8 2.4 collective-permute-start.8
  268.2 2.0 collective-permute-done.8.refs_0_
  271.3 10.7 %branch_1_fun.13 = (bf16[144,1024]{1,0:T(8,128)(2,1)}, bf16[144,1024]{1,0:T(8,128)(2,1)}) custom-call(s32[2]{0:T(128)} %pad_add_fusion.1.offsets, bf16[144,1024]{1,0:T(8,128)(2,1)} %copy-done.17, bf16[144,1024]{1,0:T(8,128)(2,1)} %copy-done.16, bf16[144,1024]{1,0:T(8,128)(2,1)} %get-tuple-element.91.refs_2_, ...), custom_call_target="tpu_custom_call", output_to_operand_aliasing={{0}: (3, {}), {1}: (4, {})} | custom-call | bytes 1048576 | tf_op jit(solution)/shard_map/cond/branch_1_fun/pallas_call | solution.py:276
  282.1 10.8 %collective-permute-start.12 = (bf16[144,1024]{1,0:T(8,128)(2,1)}, bf16[144,1024]{1,0:T(8,128)(2,1)S(1)}, u32[]{:S(2)}, u32[]{:S(2)}) collective-permute-start(bf16[144,1024]{1,0:T(8,128)(2,1)} %get-tuple-element.93), channel_id=1, source_target_pairs={{0,8},{8,16},{16,24},{24,0},{32,40},{40,48},{48,56},{56,32},{64,72... | collective-permute-start | bytes 884744 | tf_op jit(solution)/shard_map/cond/branch_1_fun/ppermute | solution.py:52
  293.0 3.9 %collective-permute-done.12 = bf16[144,1024]{1,0:T(8,128)(2,1)S(1)} collective-permute-done((bf16[144,1024]{1,0:T(8,128)(2,1)}, bf16[144,1024]{1,0:T(8,128)(2,1)S(1)}, u32[]{:S(2)}, u32[]{:S(2)}) %collective-permute-start.12) | collective-permute-done | bytes 294944 | tf_op jit(solution)/shard_map/cond/branch_1_fun/ppermute | solution.py:52
  297.9 6.2 %branch_1_fun.14 = f32[1024,128]{1,0:T(8,128)S(1)} custom-call(s32[8,128]{1,0:T(8,128)S(1)} %get-tuple-element.50.mine, bf16[2048,1024]{1,0:T(8,128)(2,1)} %get-tuple-element.57.hidden, bf16[16,144,1024]{2,1,0:T(8,128)(2,1)} %all-to-all-done.3.main, bf16[144,1024]{1,0:T(8,128)(2,1)S(1)} %select_select_fusion.1.refs_0_, ...), custom_call_target="tpu_custom_call" | custom-call | flops 268435456 | bytes 8912896 | tf_op jit(solution)/shard_map/cond/branch_1_fun/pallas_call | solution.py:325
  304.2 5.1 %collective-permute-start.14 = (f32[512,128]{1,0:T(8,128)S(1)}, f32[512,128]{1,0:T(8,128)S(1)}, u32[]{:S(2)}, u32[]{:S(2)}) collective-permute-start(f32[512,128]{1,0:T(8,128)S(1)} %constant_dynamic-slice_fusion.3), channel_id=1, source_target_pairs={{0,1},{1,0},{2,3},{3,2},{4,5},{5,4},{6,7},{7,6},{8,9},{9,8},{10,11... | collective-permute-start | bytes 786440 | tf_op jit(solution)/shard_map/cond/branch_1_fun/ppermute | solution.py:349
  310.5 1.8 collective-permute-start.15
  312.2 3.3 collective-permute-start.16
  316.5 2.0 collective-permute-done.16
  319.6 2.3 collective-permute-start.19
  324.7 3.9 %collective-permute-start.21 = (bf16[4,128,128]{2,1,0:T(8,128)(2,1)S(1)}, bf16[4,128,128]{2,1,0:T(8,128)(2,1)S(1)}, u32[]{:S(2)}, u32[]{:S(2)}) collective-permute-start(bf16[4,128,128]{2,1,0:T(8,128)(2,1)S(1)} %pad_maximum_fusion.own), channel_id=1, source_target_pairs={{0,1},{1,0},{2,3},{3,2},{4,5},{5,4},{6,7},{7,6},{8,9},{9,8},{10,11... | collective-permute-start | bytes 393224 | tf_op jit(solution)/shard_map/cond/branch_1_fun/ppermute | solution.py:358
  330.8 3.4 branch_1_fun.15
  (79 shorter events, 27.5 us)
Async XLA Ops:
  11.4 4.2 %copy-start.19 = (s32[32]{0:T(128)}, s32[32]{0:T(128)S(1)}, u32[]{:S(2)}) copy-start(s32[32]{0:T(128)S(1)} %get-tuple-element.51.counts) | copy-start | bytes 388 | tf_op jit(solution)/shard_map/cond
  11.4 318.1 %reduce-scatter.5.cloned.1.call-start = ((), (), s32[]{:S(2)}) async-start(), calls=%async_computation.7 | async-start | bytes 9437184 | tf_op jit(solution)/shard_map/cond/branch_1_fun/reduce_scatter | solution.py:507
  11.4 6.3 %copy-start.10 = (bf16[2048,1024]{1,0:T(8,128)(2,1)S(1)}, bf16[2048,1024]{1,0:T(8,128)(2,1)}, u32[]{:S(2)}) copy-start(bf16[2048,1024]{1,0:T(8,128)(2,1)} %get-tuple-element.57.hidden) | copy-start | bytes 12582916 | tf_op jit(solution)/shard_map/cond
  11.5 6.3 %copy-start.21 = (bf16[1024,1024]{1,0:T(8,128)(2,1)S(1)}, bf16[1024,1024]{1,0:T(8,128)(2,1)}, u32[]{:S(2)}) copy-start(bf16[1024,1024]{1,0:T(8,128)(2,1)} %get-tuple-element.58) | copy-start | bytes 6291460 | tf_op jit(solution)/shard_map/cond
  15.6 2.1 copy-start
  24.5 273.4 %all-to-all-start.3 = ((bf16[16,144,1024]{2,1,0:T(8,128)(2,1)}), bf16[16,144,1024]{2,1,0:T(8,128)(2,1)}, u32[]{:S(2)}, u32[]{:S(2)}) async-start(bf16[16,144,1024]{2,1,0:T(8,128)(2,1)} %copy-done), calls=%async_computation.5 | async-start | bytes 9437184 | tf_op jit(solution)/shard_map/cond/branch_1_fun/all_to_all | solution.py:494
  33.2 82.9 %collective-permute-start = (bf16[2,144,1024]{2,1,0:T(8,128)(2,1)S(1)}, bf16[2,144,1024]{2,1,0:T(8,128)(2,1)S(1)}, u32[]{:S(2)}, u32[]{:S(2)}) collective-permute-start(bf16[2,144,1024]{2,1,0:T(8,128)(2,1)S(1)} %get-tuple-element.62), channel_id=1, source_target_pairs={{0,32},{8,40},{16,48},{24,56},{32,64},{40,72},{48,80},{56,88},{64,... | collective-permute-start | bytes 1769480 | tf_op jit(solution)/shard_map/cond/branch_1_fun/ppermute | solution.py:52
  34.6 81.6 %collective-permute-start.1 = (bf16[2,144,1024]{2,1,0:T(8,128)(2,1)S(1)}, bf16[2,144,1024]{2,1,0:T(8,128)(2,1)S(1)}, u32[]{:S(2)}, u32[]{:S(2)}) collective-permute-start(bf16[2,144,1024]{2,1,0:T(8,128)(2,1)S(1)} %get-tuple-element.63), channel_id=1, source_target_pairs={{0,96},{8,104},{16,112},{24,120},{32,0},{40,8},{48,16},{56,24},{64... | collective-permute-start | bytes 1769480 | tf_op jit(solution)/shard_map/cond/branch_1_fun/ppermute | solution.py:52
  37.7 78.5 %collective-permute-start.2 = (bf16[2,144,1024]{2,1,0:T(8,128)(2,1)S(1)}, bf16[2,144,1024]{2,1,0:T(8,128)(2,1)}, u32[]{:S(2)}, u32[]{:S(2)}) collective-permute-start(bf16[2,144,1024]{2,1,0:T(8,128)(2,1)S(1)} %get-tuple-element.64), channel_id=1, source_target_pairs={{0,8},{8,16},{16,24},{24,0},{32,40},{40,48},{48,56},{56,32},{64,72... | collective-permute-start | bytes 1769480 | tf_op jit(solution)/shard_map/cond/branch_1_fun/ppermute | solution.py:52
  37.7 78.5 %collective-permute-start.3 = (bf16[2,144,1024]{2,1,0:T(8,128)(2,1)S(1)}, bf16[2,144,1024]{2,1,0:T(8,128)(2,1)}, u32[]{:S(2)}, u32[]{:S(2)}) collective-permute-start(bf16[2,144,1024]{2,1,0:T(8,128)(2,1)S(1)} %get-tuple-element.65), channel_id=1, source_target_pairs={{0,24},{8,0},{16,8},{24,16},{32,56},{40,32},{48,40},{56,48},{64,88... | collective-permute-start | bytes 1769480 | tf_op jit(solution)/shard_map/cond/branch_1_fun/ppermute | solution.py:52
  136.9 27.4 %collective-permute-start.4 = (bf16[4,144,1024]{2,1,0:T(8,128)(2,1)}, bf16[4,144,1024]{2,1,0:T(8,128)(2,1)S(1)}, u32[]{:S(2)}, u32[]{:S(2)}) collective-permute-start(bf16[4,144,1024]{2,1,0:T(8,128)(2,1)} %get-tuple-element.74), channel_id=1, source_target_pairs={{0,32},{8,40},{16,48},{24,56},{32,64},{40,72},{48,80},{56,88},{64,... | collective-permute-start | bytes 3538952 | tf_op jit(solution)/shard_map/cond/branch_1_fun/ppermute | solution.py:52
  136.9 29.1 %collective-permute-start.5 = (bf16[4,144,1024]{2,1,0:T(8,128)(2,1)}, bf16[4,144,1024]{2,1,0:T(8,128)(2,1)S(1)}, u32[]{:S(2)}, u32[]{:S(2)}) collective-permute-start(bf16[4,144,1024]{2,1,0:T(8,128)(2,1)} %get-tuple-element.75), channel_id=1, source_target_pairs={{0,96},{8,104},{16,112},{24,120},{32,0},{40,8},{48,16},{56,24},{64... | collective-permute-start | bytes 3538952 | tf_op jit(solution)/shard_map/cond/branch_1_fun/ppermute | solution.py:52
  139.6 39.2 %collective-permute-start.6 = (bf16[4,144,1024]{2,1,0:T(8,128)(2,1)}, bf16[4,144,1024]{2,1,0:T(8,128)(2,1)S(1)}, u32[]{:S(2)}, u32[]{:S(2)}) collective-permute-start(bf16[4,144,1024]{2,1,0:T(8,128)(2,1)} %get-tuple-element.76), channel_id=1, source_target_pairs={{0,8},{8,16},{16,24},{24,0},{32,40},{40,48},{48,56},{56,32},{64,72... | collective-permute-start | bytes 3538952 | tf_op jit(solution)/shard_map/cond/branch_1_fun/ppermute | solution.py:52
  155.6 25.1 %collective-permute-start.7 = (bf16[4,144,1024]{2,1,0:T(8,128)(2,1)}, bf16[4,144,1024]{2,1,0:T(8,128)(2,1)}, u32[]{:S(2)}, u32[]{:S(2)}) collective-permute-start(bf16[4,144,1024]{2,1,0:T(8,128)(2,1)} %get-tuple-element.77), channel_id=1, source_target_pairs={{0,24},{8,0},{16,8},{24,16},{32,56},{40,32},{48,40},{56,48},{64,88... | collective-permute-start | bytes 3538952 | tf_op jit(solution)/shard_map/cond/branch_1_fun/ppermute | solution.py:52
  164.3 16.4 %copy-start.11 = (bf16[4,144,1024]{2,1,0:T(8,128)(2,1)}, bf16[4,144,1024]{2,1,0:T(8,128)(2,1)S(1)}, u32[]{:S(2)}) copy-start(bf16[4,144,1024]{2,1,0:T(8,128)(2,1)S(1)} %collective-permute-done.4.refs_1_) | copy-start | bytes 3538948 | tf_op jit(solution)/shard_map/cond
  166.0 14.7 %copy-start.12 = (bf16[4,144,1024]{2,1,0:T(8,128)(2,1)}, bf16[4,144,1024]{2,1,0:T(8,128)(2,1)S(1)}, u32[]{:S(2)}) copy-start(bf16[4,144,1024]{2,1,0:T(8,128)(2,1)S(1)} %collective-permute-done.5.refs_2_) | copy-start | bytes 3538948 | tf_op jit(solution)/shard_map/cond
  255.1 12.0 %collective-permute-start.10 = (bf16[144,1024]{1,0:T(8,128)(2,1)}, bf16[144,1024]{1,0:T(8,128)(2,1)S(1)}, u32[]{:S(2)}, u32[]{:S(2)}) collective-permute-start(bf16[144,1024]{1,0:T(8,128)(2,1)} %get-tuple-element.86), channel_id=1, source_target_pairs={{0,32},{8,40},{16,48},{24,56},{32,64},{40,72},{48,80},{56,88},{64,... | collective-permute-start | bytes 884744 | tf_op jit(solution)/shard_map/cond/branch_1_fun/ppermute | solution.py:52
  262.1 6.1 %collective-permute-start.11 = (bf16[144,1024]{1,0:T(8,128)(2,1)}, bf16[144,1024]{1,0:T(8,128)(2,1)S(1)}, u32[]{:S(2)}, u32[]{:S(2)}) collective-permute-start(bf16[144,1024]{1,0:T(8,128)(2,1)} %get-tuple-element.87), channel_id=1, source_target_pairs={{0,96},{8,104},{16,112},{24,120},{32,0},{40,8},{48,16},{56,24},{64... | collective-permute-start | bytes 884744 | tf_op jit(solution)/shard_map/cond/branch_1_fun/ppermute | solution.py:52
  262.8 7.3 %collective-permute-start.8 = (bf16[144,1024]{1,0:T(8,128)(2,1)}, bf16[144,1024]{1,0:T(8,128)(2,1)S(1)}, u32[]{:S(2)}, u32[]{:S(2)}) collective-permute-start(bf16[144,1024]{1,0:T(8,128)(2,1)} %get-tuple-element.84), channel_id=1, source_target_pairs={{0,8},{8,16},{16,24},{24,0},{32,40},{40,48},{48,56},{56,32},{64,72... | collective-permute-start | bytes 884744 | tf_op jit(solution)/shard_map/cond/branch_1_fun/ppermute | solution.py:52
  265.2 6.1 %collective-permute-start.9 = (bf16[144,1024]{1,0:T(8,128)(2,1)}, bf16[144,1024]{1,0:T(8,128)(2,1)S(1)}, u32[]{:S(2)}, u32[]{:S(2)}) collective-permute-start(bf16[144,1024]{1,0:T(8,128)(2,1)} %get-tuple-element.85), channel_id=1, source_target_pairs={{0,24},{8,0},{16,8},{24,16},{32,56},{40,32},{48,40},{56,48},{64,88... | collective-permute-start | bytes 884744 | tf_op jit(solution)/shard_map/cond/branch_1_fun/ppermute | solution.py:52
  267.1 4.2 %copy-start.16 = (bf16[144,1024]{1,0:T(8,128)(2,1)}, bf16[144,1024]{1,0:T(8,128)(2,1)S(1)}, u32[]{:S(2)}) copy-start(bf16[144,1024]{1,0:T(8,128)(2,1)S(1)} %collective-permute-done.10.refs_1_) | copy-start | bytes 884740 | tf_op jit(solution)/shard_map/cond
  282.0 10.9 %collective-permute-start.13 = (bf16[144,1024]{1,0:T(8,128)(2,1)}, bf16[144,1024]{1,0:T(8,128)(2,1)S(1)}, u32[]{:S(2)}, u32[]{:S(2)}) collective-permute-start(bf16[144,1024]{1,0:T(8,128)(2,1)} %get-tuple-element.96), channel_id=1, source_target_pairs={{0,32},{8,40},{16,48},{24,56},{32,64},{40,72},{48,80},{56,88},{64,... | collective-permute-start | bytes 884744 | tf_op jit(solution)/shard_map/cond/branch_1_fun/ppermute | solution.py:52
  282.1 14.8 %collective-permute-start.12 = (bf16[144,1024]{1,0:T(8,128)(2,1)}, bf16[144,1024]{1,0:T(8,128)(2,1)S(1)}, u32[]{:S(2)}, u32[]{:S(2)}) collective-permute-start(bf16[144,1024]{1,0:T(8,128)(2,1)} %get-tuple-element.93), channel_id=1, source_target_pairs={{0,8},{8,16},{16,24},{24,0},{32,40},{40,48},{48,56},{56,32},{64,72... | collective-permute-start | bytes 884744 | tf_op jit(solution)/shard_map/cond/branch_1_fun/ppermute | solution.py:52
  297.9 31.6 %copy-start.20 = (s32[32]{0:T(128)S(1)}, s32[32]{0:T(128)}, u32[]{:S(2)}) copy-start(s32[32]{0:T(128)} %copy-done.19) | copy-start | bytes 388 | tf_op jit(solution)/shard_map/cond
  304.2 6.2 %collective-permute-start.14 = (f32[512,128]{1,0:T(8,128)S(1)}, f32[512,128]{1,0:T(8,128)S(1)}, u32[]{:S(2)}, u32[]{:S(2)}) collective-permute-start(f32[512,128]{1,0:T(8,128)S(1)} %constant_dynamic-slice_fusion.3), channel_id=1, source_target_pairs={{0,1},{1,0},{2,3},{3,2},{4,5},{5,4},{6,7},{7,6},{8,9},{9,8},{10,11... | collective-permute-start | bytes 786440 | tf_op jit(solution)/shard_map/cond/branch_1_fun/ppermute | solution.py:349
  310.5 6.1 %collective-permute-start.15 = (f32[128,128]{1,0:T(8,128)S(1)}, f32[128,128]{1,0:T(8,128)S(1)}, u32[]{:S(2)}, u32[]{:S(2)}) collective-permute-start(f32[128,128]{1,0:T(8,128)S(1)} %get-tuple-element.106), channel_id=1, source_target_pairs={{0,2},{1,3},{2,4},{3,5},{4,6},{5,7},{6,0},{7,1},{8,10},{9,11},{10,... | collective-permute-start | bytes 196616 | tf_op jit(solution)/shard_map/cond/branch_1_fun/ppermute | solution.py:353
  312.2 6.3 %collective-permute-start.16 = (f32[128,128]{1,0:T(8,128)S(1)}, f32[128,128]{1,0:T(8,128)S(1)}, u32[]{:S(2)}, u32[]{:S(2)}) collective-permute-start(f32[128,128]{1,0:T(8,128)S(1)} %get-tuple-element.104), channel_id=1, source_target_pairs={{0,4},{1,5},{2,6},{3,7},{4,0},{5,1},{6,2},{7,3},{8,12},{9,13},{10,... | collective-permute-start | bytes 196616 | tf_op jit(solution)/shard_map/cond/branch_1_fun/ppermute | solution.py:353
  315.5 3.4 %collective-permute-start.17 = (f32[128,128]{1,0:T(8,128)S(1)}, f32[128,128]{1,0:T(8,128)S(1)}, u32[]{:S(2)}, u32[]{:S(2)}) collective-permute-start(f32[128,128]{1,0:T(8,128)S(1)} %get-tuple-element.105), channel_id=1, source_target_pairs={{0,6},{1,7},{2,0},{3,1},{4,2},{5,3},{6,4},{7,5},{8,14},{9,15},{10,... | collective-permute-start | bytes 196616 | tf_op jit(solution)/shard_map/cond/branch_1_fun/ppermute | solution.py:353
  319.0 4.0 %collective-permute-start.18 = (bf16[128,128]{1,0:T(8,128)(2,1)S(1)}, bf16[128,128]{1,0:T(8,128)(2,1)S(1)}, u32[]{:S(2)}, u32[]{:S(2)}) collective-permute-start(bf16[128,128]{1,0:T(8,128)(2,1)S(1)} %add_convert_fusion), channel_id=1, source_target_pairs={{0,2},{1,3},{2,4},{3,5},{4,6},{5,7},{6,0},{7,1},{8,10},{9,11},{10,... | collective-permute-start | bytes 98312 | tf_op jit(solution)/shard_map/cond/branch_1_fun/ppermute | solution.py:357
  319.6 4.3 %collective-permute-start.19 = (bf16[128,128]{1,0:T(8,128)(2,1)S(1)}, bf16[128,128]{1,0:T(8,128)(2,1)S(1)}, u32[]{:S(2)}, u32[]{:S(2)}) collective-permute-start(bf16[128,128]{1,0:T(8,128)(2,1)S(1)} %add_convert_fusion), channel_id=1, source_target_pairs={{0,4},{1,5},{2,6},{3,7},{4,0},{5,1},{6,2},{7,3},{8,12},{9,13},{10,... | collective-permute-start | bytes 98312 | tf_op jit(solution)/shard_map/cond/branch_1_fun/ppermute | solution.py:357
  321.9 2.8 collective-permute-start.20
  324.7 4.9 %collective-permute-start.21 = (bf16[4,128,128]{2,1,0:T(8,128)(2,1)S(1)}, bf16[4,128,128]{2,1,0:T(8,128)(2,1)S(1)}, u32[]{:S(2)}, u32[]{:S(2)}) collective-permute-start(bf16[4,128,128]{2,1,0:T(8,128)(2,1)S(1)} %pad_maximum_fusion.own), channel_id=1, source_target_pairs={{0,1},{1,0},{2,3},{3,2},{4,5},{5,4},{6,7},{7,6},{8,9},{9,8},{10,11... | collective-permute-start | bytes 393224 | tf_op jit(solution)/shard_map/cond/branch_1_fun/ppermute | solution.py:358
  (11 other events, 12.4 us)
Sparse Core Ops, SparseCore 0:
  24.6 55.1 reduce-scatter.4

commit v4 on v3

--- a/solution.py
+++ b/solution.py
@@ -209,131 +209,143 @@
     )(*scalars, down, up)
 
 
-def local_copies(when, copies, sems):
-    @pl.when(when)
-    def _():
-        started = [
-            pltpu.make_async_copy(src, dst, sems.at[i]) for i, (src, dst) in enumerate(copies)
-        ]
-        for copy in started:
-            copy.start()
-        for copy in started:
-            copy.wait()
+def vmem_call(kernel, shapes, dtype, scalars, arrays, limit=32):
+    return pl.pallas_call(
+        kernel,
+        out_shape=[jax.ShapeDtypeStruct(shape, dtype) for shape in shapes],
+        in_specs=[SMEM] * len(scalars) + [VMEM] * len(arrays),
+        out_specs=[VMEM] * len(shapes),
+        compiler_params=pltpu.CompilerParams(vmem_limit_bytes=limit << 20),
+        cost_estimate=pl.CostEstimate(
+            flops=0,
+            bytes_accessed=sum(math.prod(shape) for shape in shapes) * 4,
+            transcendentals=0,
+        ),
+    )(*scalars, *arrays)
+
+
+def move(dst, src):
+    rows = src.shape[0]
+
+    def body(i, carry):
+        at = pl.ds(pl.multiple_of(i * 16, 16), 16)
+        dst[at, :] = src[at, :]
+        return carry
+
+    lax.fori_loop(0, rows // 16, body, 0, unroll=3)
 
 
 def relay_kernel(offsets, *refs):
-    sems = refs[-1]
-    fresh = refs[:4]
-    outs = refs[8:12]
+    fresh, near, outs = refs[:4], refs[4:8], refs[8:]
     for i in range(4):
-        near = 1 if i % 2 == 0 else 3
-        local_copies(offsets[i // 2] == near, [(fresh[i], outs[i].at[pl.ds(0, 2)])], sems)
-
-
-def relay(offsets, fresh, kept):
-    return pl.pallas_call(
-        relay_kernel,
-        out_shape=[jax.ShapeDtypeStruct(k.shape, k.dtype) for k in kept],
-        in_specs=[SMEM] + [HBM] * 8,
-        out_specs=[HBM] * 4,
-        input_output_aliases={5 + i: i for i in range(4)},
-        scratch_shapes=[pltpu.SemaphoreType.DMA((4,))],
-        cost_estimate=pl.CostEstimate(flops=0, bytes_accessed=1 << 21, transcendentals=0),
-    )(offsets, *fresh, *kept)
+        at = offsets[i // 2]
+        close = 1 if i % 2 == 0 else 3
+        for source, when in ((near[i], at != close), (fresh[i], at == close)):
+
+            @pl.when(when)
+            def _(source=source, out=outs[i]):
+                for u in range(2):
+                    move(out.at[u], source.at[u])
 
 
 def line_kernel(offsets, *refs):
-    sems = refs[-1]
-    ins, outs = refs[:6], refs[6:14]
+    outs = refs[10:]
     for h in range(2):
-        own, plus, minus = ins[3 * h : 3 * h + 3]
+        own, plus_a, minus_a, plus_b, minus_b = refs[5 * h : 5 * h + 5]
         out = outs[4 * h : 4 * h + 4]
-        far = [plus.at[0], plus.at[1], minus.at[0], minus.at[1]]
-        for a, source in ((0, own), (1, plus), (2, None), (3, minus)):
-            copies = [(far[i] if a == 2 else source.at[i], out[i]) for i in range(4)]
-            local_copies(offsets[h] == a, copies, sems)
-
-
-def line(offsets, ins):
-    unit = ins[0].shape[1:]
-    return pl.pallas_call(
-        line_kernel,
-        out_shape=[jax.ShapeDtypeStruct(unit, ins[0].dtype)] * 8,
-        in_specs=[SMEM] + [HBM] * 6,
-        out_specs=[HBM] * 8,
-        scratch_shapes=[pltpu.SemaphoreType.DMA((4,))],
-        cost_estimate=pl.CostEstimate(flops=0, bytes_accessed=5 << 20, transcendentals=0),
-    )(offsets, *ins)
+        at = offsets[h]
+        low, high = own.at[pl.ds(0, 2)], own.at[pl.ds(2, 2)]
+        picks = ((low, high), (plus_a, plus_b), (plus_a, minus_a), (minus_a, minus_b))
+        for offset, (first, second) in enumerate(picks):
+
+            @pl.when(at == offset)
+            def _(first=first, second=second, out=out):
+                for u in range(2):
+                    move(out[u], first.at[u])
+                    move(out[2 + u], second.at[u])
 
 
 def pass_kernel(offsets, *refs):
-    sems = refs[-1]
     for h in range(2):
-        local_copies(offsets[1 - h] == 1, [(refs[h], refs[4 + h])], sems)
-
-
-def pass_on(offsets, fresh, kept):
-    return pl.pallas_call(
-        pass_kernel,
-        out_shape=[jax.ShapeDtypeStruct(k.shape, k.dtype) for k in kept],
-        in_specs=[SMEM] + [HBM] * 4,
-        out_specs=[HBM] * 2,
-        input_output_aliases={3: 0, 4: 1},
-        scratch_shapes=[pltpu.SemaphoreType.DMA((2,))],
-        cost_estimate=pl.CostEstimate(flops=0, bytes_accessed=1 << 20, transcendentals=0),
-    )(offsets, *fresh, *kept)
-
-
-def low_kernel(mine, hidden, main, *refs):
+        at = offsets[1 - h]
+        for source, when in ((refs[2 + h], at != 1), (refs[h], at == 1)):
+
+            @pl.when(when)
+            def _(source=source, out=refs[4 + h]):
+                move(out, source)
+
+
+def pick_kernel(offsets, *refs):
+    for h in range(2):
+        at = offsets[1 - h]
+        own, back, ahead = refs[3 * h : 3 * h + 3]
+        for source, when in ((own, at == 0), (back, at == 3), (ahead, (at == 1) | (at == 2))):
+
+            @pl.when(when)
+            def _(source=source, out=refs[6 + h]):
+                move(out, source)
+
+
+def paired(hidden, mine, i, pairs, cap, first, second):
+    spots = [pl.multiple_of(mine[ORDER, j] * cap, cap) for j in (i, i + pairs)]
+    rows = jnp.concatenate([hidden[pl.ds(spot, cap), :] for spot in spots], axis=0)
+    product = lax.dot_general(
+        rows,
+        jnp.concatenate([first, second], axis=0),
+        (((1,), (1,)), ((), ())),
+        preferred_element_type=jnp.float32,
+    )
+    lane = lax.broadcasted_iota(jnp.int32, (cap, product.shape[1]), 1)
+    return jnp.where(lane < first.shape[0], product[:cap], product[cap:])
+
+
+def low_main_kernel(cap, mine, hidden, main, out):
+    rank = out.shape[1] // 2
+    pairs = out.shape[0] // cap
+
+    def weights(j):
+        place = mine[PLACE, j]
+        unit = lax.div(place, 2)
+        return main[unit, pl.ds(pl.multiple_of((place - 2 * unit) * rank, rank), rank), :]
+
+    def body(i, carry):
+        at = pl.ds(pl.multiple_of(i * cap, cap), cap)
+        out[at, :] = paired(hidden, mine, i, pairs, cap, weights(i), weights(i + pairs))
+        return carry
+
+    lax.fori_loop(0, pairs, body, 0, unroll=2)
+
+
+def low_extra_kernel(first, cap, mine, hidden, *refs):
     extras, out = refs[:-1], refs[-1]
     rank = out.shape[1] // 2
-    dp_count = main.shape[0]
-    pairs = dp_count
-    cap = out.shape[0] // pairs
-
-    def product(j, weights):
-        g = pl.multiple_of(mine[ORDER, j] * cap, cap)
-        return lax.dot_general(
-            hidden[pl.ds(g, cap), :],
-            weights,
+    for i in range(2):
+        spots = [pl.multiple_of(mine[ORDER, first + 2 * u + i] * cap, cap) for u in range(2)]
+        rows = jnp.concatenate([hidden[pl.ds(spot, cap), :] for spot in spots], axis=0)
+        part = slice(i * rank, (i + 1) * rank)
+        product = lax.dot_general(
+            rows,
+            jnp.concatenate([extras[0][part, :], extras[1][part, :]], axis=0),
             (((1,), (1,)), ((), ())),
             preferred_element_type=jnp.float32,
         )
-
-    def one(j):
-        place = mine[PLACE, j]
-        unit = lax.div(place, 2)
-        at = pl.multiple_of((place - 2 * unit) * rank, rank)
-        return product(j, main[unit, pl.ds(at, rank), :])
-
-    def store(i, first, second):
-        out[pl.ds(pl.multiple_of(i * cap, cap), cap), :] = jnp.concatenate([first, second], axis=1)
-
-    def body(i, carry):
-        store(i, one(i), one(i + pairs))
-        return carry
-
-    full = pairs - 2 * len(extras)
-    lax.fori_loop(0, full, body, 0, unroll=2)
-    for e in range(2 * len(extras)):
-        weights = extras[e // 2][e % 2 * rank : (e % 2 + 1) * rank, :]
-        store(full + e, one(full + e), product(full + e + pairs, weights))
-
-
-def low_partial(mine, hidden, main, extras, cap, rank):
-    pairs = main.shape[0]
+        lane = lax.broadcasted_iota(jnp.int32, (cap, 2 * rank), 1)
+        out[i * cap : (i + 1) * cap, :] = jnp.where(lane < rank, product[:cap], product[cap:])
+
+
+def low_partial(kernel, pairs, cap, rank, mine, hidden, weights):
     return pl.pallas_call(
-        low_kernel,
+        kernel,
         out_shape=jax.ShapeDtypeStruct((pairs * cap, 2 * rank), jnp.float32),
-        in_specs=[SMEM] + [VMEM] * (2 + len(extras)),
+        in_specs=[SMEM] + [VMEM] * (1 + len(weights)),
         out_specs=VMEM,
         compiler_params=pltpu.CompilerParams(vmem_limit_bytes=24 << 20),
         cost_estimate=pl.CostEstimate(
-            flops=hidden.size * rank * 2,
-            bytes_accessed=(hidden.size + main.size) * 2,
+            flops=pairs * cap * rank * 4 * hidden.shape[1],
+            bytes_accessed=sum(w.size for w in weights) * 2,
             transcendentals=0,
         ),
-    )(mine, hidden, main, *extras)
+    )(mine, hidden, *weights)
 
 
 def low_rank_rounds(partial):
@@ -358,76 +370,140 @@
     return own, lax.ppermute(own, "tp", swap)
 
 
-def out_kernel(where, mine, counts, base, own, other, main, *refs):
-    extras, out = refs[:-1], refs[-1]
+def low_rank_doubling(partial):
+    tp_count = lax.axis_size("tp")
+    last = tp_count // 2 - 1
+    z_of = lambda i: i // 2
+    for partner in (
+        lambda i: i ^ 1,
+        lambda i: (z_of(i) ^ 1) * 2 + i % 2,
+        lambda i: (last - z_of(i)) * 2 + i % 2,
+    ):
+        partial += lax.ppermute(partial, "tp", [(i, partner(i)) for i in range(tp_count)])
+    return partial
+
+
+def blend(base, out, counts, mine, j, both, ups, cap):
+    rank = both.shape[1] // 2
+    lane = lax.broadcasted_iota(jnp.int32, both.shape, 1)
+    none = jnp.zeros_like(both)
+    left = jnp.concatenate(
+        [jnp.where(lane < rank, both, none), jnp.where(lane < rank, none, both)], axis=0
+    )
+    delta = jnp.dot(left, jnp.concatenate(ups, axis=0), preferred_element_type=jnp.float32)
+    rows = lax.broadcasted_iota(jnp.int32, (cap, base.shape[1]), 0)
+    for n in range(2):
+        g = mine[ORDER, j[n]]
+        here = pl.ds(pl.multiple_of(g * cap, cap), cap)
+        merged = base[here, :] + ADAPTER_SCALE * delta[n * cap : (n + 1) * cap]
+        out(n, here, jnp.where(rows < counts[g], merged, 0.0).astype(jnp.bfloat16))
+
+
+def out_main_kernel(where, mine, counts, base, own, other, main, out, low):
     groups = counts.shape[0]
-    pairs = groups // 2
     cap = base.shape[0] // groups
     chips, piece, rank = own.shape[0], own.shape[1], own.shape[2] // 2
     lanes = base.shape[1]
     z, core = where[0], where[1]
     steps = rank // 16
-    rows = lax.broadcasted_iota(jnp.int32, (cap, lanes), 0)
-    per_piece = piece // cap
-
-    def factors(i):
-        half = lax.div(i, pairs // 2)
-        rest = i - half * (pairs // 2)
-        quarter = lax.div(rest, per_piece)
-        at = pl.multiple_of((rest - quarter * per_piece) * cap, cap)
-        slot = lax.rem(z - quarter + chips, chips)
-        pick = pl.ds(at, cap)
-        return jnp.where(half == core, own[slot, pick, :], other[slot, pick, :])
-
-    def one(j, factor, up):
-        g = mine[ORDER, j]
-        delta = jnp.dot(factor, up, preferred_element_type=jnp.float32)
-        here = pl.ds(pl.multiple_of(g * cap, cap), cap)
-        merged = base[here, :] + ADAPTER_SCALE * delta
-        out[here, :] = jnp.where(rows < counts[g], merged, 0.0).astype(out.dtype)
-
-    def up_main(j):
+    pairs = low.shape[0] // cap
+    for d in range(chips):
+        quarter = lax.rem(z - d + chips, chips)
+        for ref, half in ((own, core), (other, 1 - core)):
+            at = pl.multiple_of((half * chips + quarter) * piece, 16)
+            low[pl.ds(at, piece), :] = ref[d]
+
+    def up(j):
         place = mine[PLACE, j]
         unit = lax.div(place, 2)
         at = (place - 2 * unit) * steps * lanes
-        parts = [
+        return [
             main[unit, :, pl.ds(pl.multiple_of(at + part * lanes, lanes), lanes)]
             for part in range(steps)
         ]
-        return jnp.concatenate(parts, axis=0)
+
+    def store(n, here, value):
+        out[here, :] = value
 
     def body(i, carry):
-        both = factors(i)
-        one(i, both[:, :rank], up_main(i))
-        one(i + pairs, both[:, rank:], up_main(i + pairs))
+        both = low[pl.ds(pl.multiple_of(i * cap, cap), cap), :]
+        spots = (i, i + pairs)
+        blend(base, store, counts, mine, spots, both, up(i) + up(i + pairs), cap)
         return carry
 
-    full = pairs - 2 * len(extras)
-    lax.fori_loop(0, full, body, 0, unroll=2)
-    for e in range(2 * len(extras)):
-        both = factors(jnp.int32(full + e))
-        one(full + e, both[:, :rank], up_main(full + e))
-        starts = [(e % 2 * steps + part) * lanes for part in range(steps)]
-        up = jnp.concatenate([extras[e // 2][:, s : s + lanes] for s in starts], axis=0)
-        one(full + e + pairs, both[:, rank:], up)
-
-
-def combine(where, mine, counts, base, own, other, main, extras, rank):
+    lax.fori_loop(0, pairs, body, 0, unroll=2)
+
+
+def out_extra_kernel(mine, counts, base, low, first_pack, second_pack, _, out, blocks, sems):
+    groups = counts.shape[0]
+    cap = base.shape[0] // groups
+    rank = low.shape[1] // 2
+    lanes = base.shape[1]
+    steps = rank // 16
+    first = groups - EXTRA
+    copies = []
+    for i in range(2):
+        both = low[i * cap : (i + 1) * cap, :].astype(jnp.bfloat16)
+        ups = [
+            pack[:, (i * steps + part) * lanes : (i * steps + part + 1) * lanes]
+            for pack in (first_pack, second_pack)
+            for part in range(steps)
+        ]
+
+        def store(n, here, value, i=i):
+            blocks[2 * i + n] = value
+            copy = pltpu.make_async_copy(
+                blocks.at[2 * i + n], out.at[here, :], sems.at[2 * i + n]
+            )
+            copy.start()
+            copies.append(copy)
+
+        blend(base, store, counts, mine, (first + i, first + 2 + i), both, ups, cap)
+    for copy in copies:
+        copy.wait()
+
+
+def whole(array):
+    return pl.BlockSpec(array.shape, lambda i: (0,) * array.ndim)
+
+
+def combine_main(where, mine, counts, base, own, other, main, rank):
     packs = pl.BlockSpec((main.shape[0], 16, main.shape[2]), lambda i: (0, rank // 8, 0))
-    pack = pl.BlockSpec((16, main.shape[2]), lambda i: (rank // 8, 0))
-    whole = lambda array: pl.BlockSpec(array.shape, lambda i: (0,) * array.ndim)
     return pl.pallas_call(
-        out_kernel,
+        out_main_kernel,
         grid=(1,),
         out_shape=jax.ShapeDtypeStruct(base.shape, jnp.bfloat16),
-        in_specs=[SMEM, SMEM, SMEM, whole(base), whole(own), whole(other), packs]
-        + [pack] * len(extras),
+        in_specs=[SMEM, SMEM, SMEM, whole(base), whole(own), whole(other), packs],
         out_specs=whole(base),
+        scratch_shapes=[
+            pltpu.VMEM((2 * own.shape[0] * own.shape[1], own.shape[2]), jnp.bfloat16)
+        ],
         compiler_params=pltpu.CompilerParams(vmem_limit_bytes=12 << 20),
         cost_estimate=pl.CostEstimate(
             flops=base.size * rank * 2, bytes_accessed=base.size * 8, transcendentals=0
         ),
-    )(where, mine, counts, base, own, other, main, *extras)
+    )(where, mine, counts, base, own, other, main)
+
+
+def combine_extra(mine, counts, base, low, extras, out, rank):
+    pack = pl.BlockSpec((16, extras[0].shape[1]), lambda i: (rank // 8, 0))
+    cap = base.shape[0] // counts.shape[0]
+    return pl.pallas_call(
+        out_extra_kernel,
+        grid=(1,),
+        out_shape=jax.ShapeDtypeStruct(out.shape, out.dtype),
+        in_specs=[SMEM, SMEM, whole(base), whole(low), pack, pack, HBM],
+        out_specs=HBM,
+        input_output_aliases={6: 0},
+        scratch_shapes=[
+            pltpu.VMEM((EXTRA, cap, base.shape[1]), jnp.bfloat16),
+            pltpu.SemaphoreType.DMA((EXTRA,)),
+        ],
+        compiler_params=pltpu.CompilerParams(vmem_limit_bytes=8 << 20),
+        cost_estimate=pl.CostEstimate(
+            flops=base.size * rank // 4, bytes_accessed=base.size * 4, transcendentals=0
+        ),
+    )(mine, counts, base, low, *extras, out)
 
 
 def on_device(
@@ -479,49 +555,95 @@
         a = (me // side - hot // side) % side
         b = (me % side - hot % side) % side
         offsets = jnp.stack([a, b]).astype(jnp.int32)
-        ends = ((True, 2, (0, 1)), (True, 2, (2, 3)), (False, 2, (0, 1)), (False, 2, (2, 3)))
-        rest = tuple((x_first, far, (0, 1, 2, 3)) for x_first in (True, False) for far in (1, 3, 0))
+        trees = (True, False)
+        soon = [(tree, 2, part) for tree in trees for part in ((0, 1), (2, 3))]
+        soon += [(tree, near, (2, 3)) for tree in trees for near in (1, 3)]
+        late = [(tree, near, (0, 1)) for tree in trees for near in (1, 3)]
+        late += [(tree, 0, (0, 1, 2, 3)) for tree in trees]
+        moves = ((1, 0), (-1, 0), (0, 1), (0, -1))
+        turned = ((0, 1), (0, -1), (1, 0), (-1, 0))
+        send = lambda values, ways: [shift(v, *way) for v, way in zip(values, ways)]
+        barrier = lax.optimization_barrier
         scalars = (me_row, served, mine)
-        first = gather_call(
-            functools.partial(extra_kernel, ends), (2,) * 4, 8, scalars, down_weights, up_weights
-        )
-        moves = ((1, 0), (-1, 0), (0, 1), (0, -1))
-        send = lambda values, ways: [shift(v, *way) for v, way in zip(values, ways)]
-        fresh = send(first, moves)
-        (main_sent,) = gather_call(
-            main_kernel, (dp_count,), dp_count, (served,), down_weights, up_weights
-        )
-        main = lax.all_to_all(main_sent, "dp", 0, 0, tiled=True)
-        after, _ = lax.optimization_barrier((served, main_sent))
+        gathered = gather_call(
+            functools.partial(extra_kernel, soon), (2,) * 8, 16, scalars, down_weights, up_weights
+        )
+        fresh = send(gathered[:4], moves)
+        near_b = send(gathered[4:], moves)
+        later_served, _ = barrier((served, gathered))
         later = gather_call(
-            functools.partial(extra_kernel, rest),
-            (4,) * 6,
-            24,
-            (me_row, after, mine),
+            functools.partial(extra_kernel, late),
+            (2,) * 4 + (4,) * 2,
+            16,
+            (me_row, later_served, mine),
             down_weights,
             up_weights,
         )
-        x_plus, x_minus, x_own, y_plus, y_minus, y_own = later
-        hidden, _ = lax.optimization_barrier((hidden, after))
-        base_terms = jnp.dot(hidden, value_weight, preferred_element_type=jnp.float32)
+        main_served, _ = barrier((served, later))
+        (main_sent,) = gather_call(
+            main_kernel, (dp_count,), dp_count, (main_served,), down_weights, up_weights
+        )
+        fresh, near, main_sent = barrier((fresh, later[:4], main_sent))
+        unit = main_sent.shape[1:]
+        two = (2,) + unit
+        relayed = vmem_call(
+            relay_kernel, (two,) * 4, main_sent.dtype, (offsets,), (*fresh, *near)
+        )
+        main_sent, relayed = barrier((main_sent, relayed))
+        near_a = send(relayed, moves)
+        main = lax.all_to_all(main_sent, "dp", 0, 0, tiled=True)
+        base_hidden, _ = barrier((hidden, relayed))
+        base_terms = jnp.dot(base_hidden, value_weight, preferred_element_type=jnp.float32)
         base = lax.psum_scatter(base_terms, "tp", scatter_dimension=1, tiled=True)
-        fresh = lax.optimization_barrier(fresh)
-        got = send(relay(offsets, fresh, (x_plus, x_minus, y_plus, y_minus)), moves)
-        got = lax.optimization_barrier(got)
-        lines = line(offsets, (x_own, got[0], got[1], y_own, got[2], got[3]))
+        near_a, near_b, base_terms = barrier((near_a, near_b, base_terms))
+        tree_arrays = [
+            (later[4 + h], near_a[2 * h], near_a[2 * h + 1], near_b[2 * h], near_b[2 * h + 1])
+            for h in range(2)
+        ]
+        lines = vmem_call(
+            line_kernel,
+            (unit,) * 8,
+            main_sent.dtype,
+            (offsets,),
+            tree_arrays[0] + tree_arrays[1],
+        )
         x0, x1, x2, x3, y0, y1, y2, y3 = lines
-        x_ahead, x_back, y_ahead, y_back = lax.optimization_barrier(
-            send((x2, x3, y2, y3), ((0, 1), (0, -1), (1, 0), (-1, 0)))
-        )
-        x_next, y_next = send(pass_on(offsets, (x_ahead, y_ahead), (x1, y1)), ((0, 1), (1, 0)))
-        extra_x = jnp.where(b == 0, x0, jnp.where(b == 3, x_back, x_next))
-        extra_y = jnp.where(a == 0, y0, jnp.where(a == 3, y_back, y_next))
-        extras = (extra_x, extra_y)
-        partial = low_partial(mine, hidden, main, extras, cap, rank)
+        x_ahead, x_back, y_ahead, y_back = barrier(send((x2, x3, y2, y3), turned))
+        passed = vmem_call(
+            pass_kernel,
+            (unit,) * 2,
+            main_sent.dtype,
+            (offsets,),
+            (x_ahead, y_ahead, x1, y1),
+        )
+        passed, main = barrier((passed, main))
+        x_next, y_next = send(passed, (turned[0], turned[2]))
+        pairs = (groups - EXTRA) // 2
+        partial = low_partial(
+            functools.partial(low_main_kernel, cap), pairs, cap, rank, mine, hidden, (main,)
+        )
         own, other = low_rank_rounds(partial)
+        extras = vmem_call(
+            pick_kernel,
+            (unit,) * 2,
+            main_sent.dtype,
+            (offsets,),
+            (x0, x_back, x_next, y0, y_back, y_next),
+        )
+        extra_partial = low_partial(
+            functools.partial(low_extra_kernel, groups - EXTRA, cap),
+            EXTRA // 2,
+            cap,
+            rank,
+            mine,
+            hidden,
+            extras,
+        )
+        extra_low = low_rank_doubling(extra_partial)
         t = lax.axis_index("tp")
         where = jnp.stack([t // 2, t % 2]).astype(jnp.int32)
-        return combine(where, mine, counts, base, own, other, main, extras, rank)
+        out = combine_main(where, mine, counts, base, own, other, main, rank)
+        return combine_extra(mine, counts, base, extra_low, extras, out, rank)
 
     return lax.cond(
         mine[FLAGS, FITS] == 1, narrow, wide, hidden, value_weight, down_weights, up_weights

time: 340 us -> 280 us (0.82)
  Pallas kernels: 123 us -> 31.1 us
  waiting for transfers between devices: 106 us -> 142 us
  starting transfers between devices: 73 us -> 57.7 us
  local copies, waits for them, and re-layouts: 13.4 us -> 20.9 us
    pallas_call x5 -> x8, Pallas kernels: 114 us -> 17.6 us  [the longest x2 8.27 us: low_partial(): pl.pallas_call(kernel, out_shape=jax.ShapeDtypeStruct((pairs * cap, 2 * r...]
    ppermute x14 -> x18, waiting for transfers between devices: 98.8 us -> 138 us  [shift(): return lax.ppermute(value, 'dp', pairs)]
    ppermute x14 -> x18, starting transfers between devices: 47.2 us -> 24 us  [shift(): return lax.ppermute(value, 'dp', pairs)]
    cond x38 -> x54, local copies, waits for them, and re-layouts: 10.6 us -> 18.2 us
    all_to_all x1, starting transfers between devices: 7.66 us -> 13.3 us  [narrow(): main = lax.all_to_all(main_sent, 'dp', 0, 0, tiled=True)]
    pallas_call x3, Pallas kernels: 7.06 us -> 11.6 us  [gather_call(): pl.pallas_call(kernel, out_shape=[jax.ShapeDtypeStruct((n, 2 * rank + 16,...]
    ppermute x0 -> x3, starting transfers between devices: none -> 3.84 us  [low_rank_doubling(): lax.ppermute(partial, 'tp', [(i, partner(i)) for i in range(tp_count)])]
  transfers between devices with their start and end apart: 24 -> 31, of which waited for: 18 -> 12; matrix products, arithmetic and copies ran while one was open for 1% -> 0% of each run, Pallas kernels for 33% -> 8%
where the time goes in v4:
time: 280 us; the launch traced here: 278 us
  waiting for transfers between devices  142 us (51%)
  starting transfers between devices  57.7 us (21%)
  Pallas kernels  31.1 us (11%)
  local copies, waits for them, and re-layouts  20.9 us (7%)
  between operations  14.1 us (5%)
  matrix products  8.27 us (3%)
  loops' own time  3.11 us (1%)
    ppermute x18, waiting for transfers between devices, shift(): return lax.ppermute(value, 'dp', pairs)  138 us
    ppermute x18, starting transfers between devices, shift(): return lax.ppermute(value, 'dp', pairs)  24 us
    cond x54, local copies, waits for them, and re-layouts  18.2 us
    all_to_all x1, starting transfers between devices, narrow(): main = lax.all_to_all(main_sent, 'dp', 0, 0, tiled=True)  13.3 us
    pallas_call x3, Pallas kernels, gather_call(): pl.pallas_call(kernel, out_shape=[jax.ShapeDtypeStruct((n, 2 * rank + 16,...  11.6 us
    dot_general x1, matrix products, narrow(): jnp.dot(base_hidden, value_weight, preferred_element_type=jnp.float32)  8.27 us
    pallas_call x2, Pallas kernels, low_partial(): pl.pallas_call(kernel, out_shape=jax.ShapeDtypeStruct((pairs * cap, 2 * r...  8.27 us
    ppermute x3, starting transfers between devices, low_rank_rounds(): lax.ppermute(cut(total, (z + d) % chips * piece, piece), 'tp', turn(d))  5.71 us
  transfers between devices with their start and end apart: 31, of which 12 were waited for; matrix products, arithmetic and copies ran while one was open for 0% of the time, Pallas kernels for 8%

profile of v4, /device:TPU:1, one launch (start us, length us, event | category | flops | bytes accessed | tf_op | source)
XLA Modules:
  0.0 277.7 jit_solution(16669827687054679774)
XLA Ops:
  8.1 1.8 shard_map.75
  11.2 259.6 %conditional.1 = (bf16[2048,128]{1,0:T(8,128)(2,1)}) conditional(s32[]{:T(128)} %bitcast.20, (s32[32]{0:T(128)S(1)}, bf16[2048,1024]{1,0:T(8,128)(2,1)}, bf16[1024,1024]{1,0:T(8,128)(2,1)}, s32[512]{0:T(512)}, s32[2048]{0:T(1024)}, /*index=5*/s32[]{:T(128)}, bf16[128,64,1024]{2,1,0:T(8,128)(2,1)}, bf16[128,64,128]{2,1,0:T(8,128)(2,1)}) %tuple.19, ...), branch_computations={%region_0.5_spmd, %region_5.7_spmd} | conditional | flops 4601487360 | bytes 304742112 | solution.py:648
  14.6 2.0 collective-permute-start
  16.6 2.3 collective-permute-start.1
  31.7 8.5 %branch_1_fun.13 = bf16[16,144,1024]{2,1,0:T(8,128)(2,1)S(1)} custom-call(s32[16,128]{1,0:T(8,128)S(1)} %copy-done.26, bf16[128,64,1024]{2,1,0:T(8,128)(2,1)S(1)} %copy-done.21, bf16[128,64,128]{2,1,0:T(8,128)(2,1)S(1)} %copy-done.24), custom_call_target="tpu_custom_call" | custom-call | bytes 9437184 | tf_op jit(solution)/shard_map/cond/branch_1_fun/pallas_call | solution.py:193
  40.2 2.2 copy-done
  42.6 55.3 %collective-permute-done.3.refs_3_ = bf16[2,144,1024]{2,1,0:T(8,128)(2,1)} collective-permute-done((bf16[2,144,1024]{2,1,0:T(8,128)(2,1)}, bf16[2,144,1024]{2,1,0:T(8,128)(2,1)}, u32[]{:S(2)}, u32[]{:S(2)}) %collective-permute-start.3) | collective-permute-done | bytes 589856 | tf_op jit(solution)/shard_map/cond/branch_1_fun/ppermute | solution.py:52
  107.1 8.3 %fusion.8 = f32[2048,1024]{1,0:T(8,128)} fusion(bf16[2048,1024]{1,0:T(8,128)(2,1)S(1)} %copy-done.22, bf16[1024,1024]{1,0:T(8,128)(2,1)} %get-tuple-element.92), kind=kOutput, calls=%fused_computation.42 | convolution fusion | flops 4294967296 | bytes 14680064 | tf_op jit(solution)/shard_map/cond/branch_1_fun/dot_general | solution.py:596
  115.5 13.3 %all-to-all-start.3 = ((bf16[16,144,1024]{2,1,0:T(8,128)(2,1)}), bf16[16,144,1024]{2,1,0:T(8,128)(2,1)}, u32[]{:S(2)}, u32[]{:S(2)}) async-start(bf16[16,144,1024]{2,1,0:T(8,128)(2,1)} %copy-done), calls=%async_computation.5 | async-start | bytes 9437184 | tf_op jit(solution)/shard_map/cond/branch_1_fun/all_to_all | solution.py:594
  134.3 61.1 %collective-permute-done.10.refs_8_ = bf16[2,144,1024]{2,1,0:T(8,128)(2,1)S(1)} collective-permute-done((bf16[2,144,1024]{2,1,0:T(8,128)(2,1)}, bf16[2,144,1024]{2,1,0:T(8,128)(2,1)S(1)}, u32[]{:S(2)}, u32[]{:S(2)}) %collective-permute-start.10) | collective-permute-done | bytes 589856 | tf_op jit(solution)/shard_map/cond/branch_1_fun/ppermute | solution.py:52
  195.4 2.5 collective-permute-start.5
  197.9 2.7 collective-permute-start.7
  200.6 9.5 %collective-permute-done.4.refs_1_ = bf16[2,144,1024]{2,1,0:T(8,128)(2,1)S(1)} collective-permute-done((bf16[2,144,1024]{2,1,0:T(8,128)(2,1)}, bf16[2,144,1024]{2,1,0:T(8,128)(2,1)S(1)}, u32[]{:S(2)}, u32[]{:S(2)}) %collective-permute-start.4) | collective-permute-done | bytes 589856 | tf_op jit(solution)/shard_map/cond/branch_1_fun/ppermute | solution.py:52
  210.2 2.9 %collective-permute-done.6.refs_6_ = bf16[2,144,1024]{2,1,0:T(8,128)(2,1)S(1)} collective-permute-done((bf16[2,144,1024]{2,1,0:T(8,128)(2,1)}, bf16[2,144,1024]{2,1,0:T(8,128)(2,1)S(1)}, u32[]{:S(2)}, u32[]{:S(2)}) %collective-permute-start.6) | collective-permute-done | bytes 589856 | tf_op jit(solution)/shard_map/cond/branch_1_fun/ppermute | solution.py:52
  213.1 1.9 branch_1_fun.15
  215.0 2.7 collective-permute-start.13
  217.6 2.8 %collective-permute-start.14 = (bf16[144,1024]{1,0:T(8,128)(2,1)}, bf16[144,1024]{1,0:T(8,128)(2,1)S(1)}, u32[]{:S(2)}, u32[]{:S(2)}) collective-permute-start(bf16[144,1024]{1,0:T(8,128)(2,1)} %get-tuple-element.104), channel_id=1, source_target_pairs={{0,32},{8,40},{16,48},{24,56},{32,64},{40,72},{48,80},{56,88},{64,... | collective-permute-start | bytes 884744 | tf_op jit(solution)/shard_map/cond/branch_1_fun/ppermute | solution.py:52
  220.4 2.4 collective-permute-done.12.refs_0_
  222.8 2.5 collective-permute-done.14.refs_1_
  225.3 1.8 collective-permute-done.15.refs_4_
  227.8 5.8 %branch_1_fun.19 = f32[896,128]{1,0:T(8,128)S(1)} custom-call(s32[8,128]{1,0:T(8,128)S(1)} %get-tuple-element.50.mine, bf16[2048,1024]{1,0:T(8,128)(2,1)} %get-tuple-element.91.hidden, bf16[16,144,1024]{2,1,0:T(8,128)(2,1)} %all-to-all-done.3.main), custom_call_target="tpu_custom_call" | custom-call | flops 234881024 | bytes 4718592 | tf_op jit(solution)/shard_map/cond/branch_1_fun/pallas_call | solution.py:337
  233.6 3.0 %collective-permute-start.21 = (f32[448,128]{1,0:T(8,128)S(1)}, f32[448,128]{1,0:T(8,128)S(1)}, u32[]{:S(2)}, u32[]{:S(2)}) collective-permute-start(f32[448,128]{1,0:T(8,128)S(1)} %constant_dynamic-slice_fusion.3), channel_id=1, source_target_pairs={{0,1},{1,0},{2,3},{3,2},{4,5},{5,4},{6,7},{7,6},{8,9},{9,8},{10,11... | collective-permute-start | bytes 688136 | tf_op jit(solution)/shard_map/cond/branch_1_fun/ppermute | solution.py:361
  237.8 1.7 collective-permute-start.22
  239.5 3.3 %collective-permute-start.23 = (f32[112,128]{1,0:T(8,128)S(1)}, f32[112,128]{1,0:T(8,128)S(1)}, u32[]{:S(2)}, u32[]{:S(2)}) collective-permute-start(f32[112,128]{1,0:T(8,128)S(1)} %get-tuple-element.128), channel_id=1, source_target_pairs={{0,4},{1,5},{2,6},{3,7},{4,0},{5,1},{6,2},{7,3},{8,12},{9,13},{10,... | collective-permute-start | bytes 172040 | tf_op jit(solution)/shard_map/cond/branch_1_fun/ppermute | solution.py:365
  243.5 2.5 collective-permute-done.16.refs_2_
  246.6 2.5 branch_1_fun.18
  250.5 1.7 collective-permute-start.25
  252.2 3.3 %collective-permute-start.26 = (bf16[112,128]{1,0:T(8,128)(2,1)S(1)}, bf16[112,128]{1,0:T(8,128)(2,1)S(1)}, u32[]{:S(2)}, u32[]{:S(2)}) collective-permute-start(bf16[112,128]{1,0:T(8,128)(2,1)S(1)} %add_convert_fusion), channel_id=1, source_target_pairs={{0,4},{1,5},{2,6},{3,7},{4,0},{5,1},{6,2},{7,3},{8,12},{9,13},{10,... | collective-permute-start | bytes 86024 | tf_op jit(solution)/shard_map/cond/branch_1_fun/ppermute | solution.py:369
  258.2 2.1 collective-permute-start.28
  260.4 1.7 collective-permute-start.20
  262.1 2.6 collective-permute-done.20
  266.1 3.1 %branch_1_fun.20._ = bf16[2048,128]{1,0:T(8,128)(2,1)} custom-call(s32[2]{0:T(128)S(1)} %pad_add_fusion.1.where, s32[8,128]{1,0:T(8,128)S(1)} %get-tuple-element.50.mine, s32[32]{0:T(128)S(1)} %copy-done.29, f32[2048,128]{1,0:T(8,128)S(1)} %copy-done.1, bf16[4,112,128]{2,1,0:T(8,128)(2,1)S(1)} %pad_maximum_fusion.own, ...), custom_call_target="tpu_custom_call" | custom-call | flops 33554432 | bytes 2097152 | tf_op jit(solution)/shard_map/cond/branch_1_fun/pallas_call | solution.py:472
  (113 shorter events, 40.6 us)
Async XLA Ops:
  11.4 253.4 %reduce-scatter.5.cloned.1.call-start = ((), (), s32[]{:S(2)}) async-start(), calls=%async_computation.7 | async-start | bytes 9437184 | tf_op jit(solution)/shard_map/cond/branch_1_fun/reduce_scatter | solution.py:597
  14.6 28.0 %collective-permute-start = (bf16[2,144,1024]{2,1,0:T(8,128)(2,1)}, bf16[2,144,1024]{2,1,0:T(8,128)(2,1)S(1)}, u32[]{:S(2)}, u32[]{:S(2)}) collective-permute-start(bf16[2,144,1024]{2,1,0:T(8,128)(2,1)} %get-tuple-element.57), channel_id=1, source_target_pairs={{0,32},{8,40},{16,48},{24,56},{32,64},{40,72},{48,80},{56,88},{64,... | collective-permute-start | bytes 1769480 | tf_op jit(solution)/shard_map/cond/branch_1_fun/ppermute | solution.py:52
  16.6 25.9 %collective-permute-start.1 = (bf16[2,144,1024]{2,1,0:T(8,128)(2,1)}, bf16[2,144,1024]{2,1,0:T(8,128)(2,1)S(1)}, u32[]{:S(2)}, u32[]{:S(2)}) collective-permute-start(bf16[2,144,1024]{2,1,0:T(8,128)(2,1)} %get-tuple-element.58), channel_id=1, source_target_pairs={{0,96},{8,104},{16,112},{24,120},{32,0},{40,8},{48,16},{56,24},{64... | collective-permute-start | bytes 1769480 | tf_op jit(solution)/shard_map/cond/branch_1_fun/ppermute | solution.py:52
  18.9 23.6 %collective-permute-start.2 = (bf16[2,144,1024]{2,1,0:T(8,128)(2,1)}, bf16[2,144,1024]{2,1,0:T(8,128)(2,1)}, u32[]{:S(2)}, u32[]{:S(2)}) collective-permute-start(bf16[2,144,1024]{2,1,0:T(8,128)(2,1)} %get-tuple-element.59), channel_id=1, source_target_pairs={{0,8},{8,16},{16,24},{24,0},{32,40},{40,48},{48,56},{56,32},{64,72... | collective-permute-start | bytes 1769480 | tf_op jit(solution)/shard_map/cond/branch_1_fun/ppermute | solution.py:52
  20.2 77.6 %collective-permute-start.3 = (bf16[2,144,1024]{2,1,0:T(8,128)(2,1)}, bf16[2,144,1024]{2,1,0:T(8,128)(2,1)}, u32[]{:S(2)}, u32[]{:S(2)}) collective-permute-start(bf16[2,144,1024]{2,1,0:T(8,128)(2,1)} %get-tuple-element.60), channel_id=1, source_target_pairs={{0,24},{8,0},{16,8},{24,16},{32,56},{40,32},{48,40},{56,48},{64,88... | collective-permute-start | bytes 1769480 | tf_op jit(solution)/shard_map/cond/branch_1_fun/ppermute | solution.py:52
  115.5 112.3 %all-to-all-start.3 = ((bf16[16,144,1024]{2,1,0:T(8,128)(2,1)}), bf16[16,144,1024]{2,1,0:T(8,128)(2,1)}, u32[]{:S(2)}, u32[]{:S(2)}) async-start(bf16[16,144,1024]{2,1,0:T(8,128)(2,1)} %copy-done), calls=%async_computation.5 | async-start | bytes 9437184 | tf_op jit(solution)/shard_map/cond/branch_1_fun/all_to_all | solution.py:594
  128.8 66.6 %collective-permute-start.10 = (bf16[2,144,1024]{2,1,0:T(8,128)(2,1)}, bf16[2,144,1024]{2,1,0:T(8,128)(2,1)S(1)}, u32[]{:S(2)}, u32[]{:S(2)}) collective-permute-start(bf16[2,144,1024]{2,1,0:T(8,128)(2,1)} %copy-done.15), channel_id=1, source_target_pairs={{0,8},{8,16},{16,24},{24,0},{32,40},{40,48},{48,56},{56,32},{64,72... | collective-permute-start | bytes 1769480 | tf_op jit(solution)/shard_map/cond/branch_1_fun/ppermute | solution.py:52
  130.1 67.8 %collective-permute-start.11 = (bf16[2,144,1024]{2,1,0:T(8,128)(2,1)}, bf16[2,144,1024]{2,1,0:T(8,128)(2,1)S(1)}, u32[]{:S(2)}, u32[]{:S(2)}) collective-permute-start(bf16[2,144,1024]{2,1,0:T(8,128)(2,1)} %copy-done.14), channel_id=1, source_target_pairs={{0,24},{8,0},{16,8},{24,16},{32,56},{40,32},{48,40},{56,48},{64,88... | collective-permute-start | bytes 1769480 | tf_op jit(solution)/shard_map/cond/branch_1_fun/ppermute | solution.py:52
  131.6 66.4 %collective-permute-start.8 = (bf16[2,144,1024]{2,1,0:T(8,128)(2,1)S(1)}, bf16[2,144,1024]{2,1,0:T(8,128)(2,1)S(1)}, u32[]{:S(2)}, u32[]{:S(2)}) collective-permute-start(bf16[2,144,1024]{2,1,0:T(8,128)(2,1)S(1)} %copy-done.13), channel_id=1, source_target_pairs={{0,32},{8,40},{16,48},{24,56},{32,64},{40,72},{48,80},{56,88},{64,... | collective-permute-start | bytes 1769480 | tf_op jit(solution)/shard_map/cond/branch_1_fun/ppermute | solution.py:52
  132.8 67.8 %collective-permute-start.9 = (bf16[2,144,1024]{2,1,0:T(8,128)(2,1)S(1)}, bf16[2,144,1024]{2,1,0:T(8,128)(2,1)S(1)}, u32[]{:S(2)}, u32[]{:S(2)}) collective-permute-start(bf16[2,144,1024]{2,1,0:T(8,128)(2,1)S(1)} %copy-done.11), channel_id=1, source_target_pairs={{0,96},{8,104},{16,112},{24,120},{32,0},{40,8},{48,16},{56,24},{64... | collective-permute-start | bytes 1769480 | tf_op jit(solution)/shard_map/cond/branch_1_fun/ppermute | solution.py:52
  134.2 75.9 %collective-permute-start.4 = (bf16[2,144,1024]{2,1,0:T(8,128)(2,1)}, bf16[2,144,1024]{2,1,0:T(8,128)(2,1)S(1)}, u32[]{:S(2)}, u32[]{:S(2)}) collective-permute-start(bf16[2,144,1024]{2,1,0:T(8,128)(2,1)} %copy-done.19), channel_id=1, source_target_pairs={{0,32},{8,40},{16,48},{24,56},{32,64},{40,72},{48,80},{56,88},{64,... | collective-permute-start | bytes 1769480 | tf_op jit(solution)/shard_map/cond/branch_1_fun/ppermute | solution.py:52
  195.4 14.7 %collective-permute-start.5 = (bf16[2,144,1024]{2,1,0:T(8,128)(2,1)}, bf16[2,144,1024]{2,1,0:T(8,128)(2,1)S(1)}, u32[]{:S(2)}, u32[]{:S(2)}) collective-permute-start(bf16[2,144,1024]{2,1,0:T(8,128)(2,1)} %copy-done.18), channel_id=1, source_target_pairs={{0,96},{8,104},{16,112},{24,120},{32,0},{40,8},{48,16},{56,24},{64... | collective-permute-start | bytes 1769480 | tf_op jit(solution)/shard_map/cond/branch_1_fun/ppermute | solution.py:52
  197.9 15.1 %collective-permute-start.6 = (bf16[2,144,1024]{2,1,0:T(8,128)(2,1)}, bf16[2,144,1024]{2,1,0:T(8,128)(2,1)S(1)}, u32[]{:S(2)}, u32[]{:S(2)}) collective-permute-start(bf16[2,144,1024]{2,1,0:T(8,128)(2,1)} %copy-done.17), channel_id=1, source_target_pairs={{0,8},{8,16},{16,24},{24,0},{32,40},{40,48},{48,56},{56,32},{64,72... | collective-permute-start | bytes 1769480 | tf_op jit(solution)/shard_map/cond/branch_1_fun/ppermute | solution.py:52
  197.9 15.1 %collective-permute-start.7 = (bf16[2,144,1024]{2,1,0:T(8,128)(2,1)}, bf16[2,144,1024]{2,1,0:T(8,128)(2,1)S(1)}, u32[]{:S(2)}, u32[]{:S(2)}) collective-permute-start(bf16[2,144,1024]{2,1,0:T(8,128)(2,1)} %copy-done.16), channel_id=1, source_target_pairs={{0,24},{8,0},{16,8},{24,16},{32,56},{40,32},{48,40},{56,48},{64,88... | collective-permute-start | bytes 1769480 | tf_op jit(solution)/shard_map/cond/branch_1_fun/ppermute | solution.py:52
  214.9 7.9 %collective-permute-start.12 = (bf16[144,1024]{1,0:T(8,128)(2,1)}, bf16[144,1024]{1,0:T(8,128)(2,1)S(1)}, u32[]{:S(2)}, u32[]{:S(2)}) collective-permute-start(bf16[144,1024]{1,0:T(8,128)(2,1)} %get-tuple-element.102), channel_id=1, source_target_pairs={{0,8},{8,16},{16,24},{24,0},{32,40},{40,48},{48,56},{56,32},{64,72... | collective-permute-start | bytes 884744 | tf_op jit(solution)/shard_map/cond/branch_1_fun/ppermute | solution.py:52
  215.0 7.9 %collective-permute-start.13 = (bf16[144,1024]{1,0:T(8,128)(2,1)}, bf16[144,1024]{1,0:T(8,128)(2,1)S(1)}, u32[]{:S(2)}, u32[]{:S(2)}) collective-permute-start(bf16[144,1024]{1,0:T(8,128)(2,1)} %get-tuple-element.103), channel_id=1, source_target_pairs={{0,24},{8,0},{16,8},{24,16},{32,56},{40,32},{48,40},{56,48},{64,88... | collective-permute-start | bytes 884744 | tf_op jit(solution)/shard_map/cond/branch_1_fun/ppermute | solution.py:52
  217.6 7.7 %collective-permute-start.14 = (bf16[144,1024]{1,0:T(8,128)(2,1)}, bf16[144,1024]{1,0:T(8,128)(2,1)S(1)}, u32[]{:S(2)}, u32[]{:S(2)}) collective-permute-start(bf16[144,1024]{1,0:T(8,128)(2,1)} %get-tuple-element.104), channel_id=1, source_target_pairs={{0,32},{8,40},{16,48},{24,56},{32,64},{40,72},{48,80},{56,88},{64,... | collective-permute-start | bytes 884744 | tf_op jit(solution)/shard_map/cond/branch_1_fun/ppermute | solution.py:52
  220.4 6.7 %collective-permute-start.15 = (bf16[144,1024]{1,0:T(8,128)(2,1)}, bf16[144,1024]{1,0:T(8,128)(2,1)S(1)}, u32[]{:S(2)}, u32[]{:S(2)}) collective-permute-start(bf16[144,1024]{1,0:T(8,128)(2,1)} %get-tuple-element.105), channel_id=1, source_target_pairs={{0,96},{8,104},{16,112},{24,120},{32,0},{40,8},{48,16},{56,24},{64... | collective-permute-start | bytes 884744 | tf_op jit(solution)/shard_map/cond/branch_1_fun/ppermute | solution.py:52
  233.6 4.1 %collective-permute-start.21 = (f32[448,128]{1,0:T(8,128)S(1)}, f32[448,128]{1,0:T(8,128)S(1)}, u32[]{:S(2)}, u32[]{:S(2)}) collective-permute-start(f32[448,128]{1,0:T(8,128)S(1)} %constant_dynamic-slice_fusion.3), channel_id=1, source_target_pairs={{0,1},{1,0},{2,3},{3,2},{4,5},{5,4},{6,7},{7,6},{8,9},{9,8},{10,11... | collective-permute-start | bytes 688136 | tf_op jit(solution)/shard_map/cond/branch_1_fun/ppermute | solution.py:361
  236.6 9.4 %collective-permute-start.16 = (bf16[144,1024]{1,0:T(8,128)(2,1)S(1)}, bf16[144,1024]{1,0:T(8,128)(2,1)S(1)}, u32[]{:S(2)}, u32[]{:S(2)}) collective-permute-start(bf16[144,1024]{1,0:T(8,128)(2,1)S(1)} %get-tuple-element.114), channel_id=1, source_target_pairs={{0,8},{8,16},{16,24},{24,0},{32,40},{40,48},{48,56},{56,32},{64,72... | collective-permute-start | bytes 884744 | tf_op jit(solution)/shard_map/cond/branch_1_fun/ppermute | solution.py:52
  236.6 9.4 %collective-permute-start.17 = (bf16[144,1024]{1,0:T(8,128)(2,1)S(1)}, bf16[144,1024]{1,0:T(8,128)(2,1)S(1)}, u32[]{:S(2)}, u32[]{:S(2)}) collective-permute-start(bf16[144,1024]{1,0:T(8,128)(2,1)S(1)} %get-tuple-element.117), channel_id=1, source_target_pairs={{0,32},{8,40},{16,48},{24,56},{32,64},{40,72},{48,80},{56,88},{64,... | collective-permute-start | bytes 884744 | tf_op jit(solution)/shard_map/cond/branch_1_fun/ppermute | solution.py:52
  237.7 27.1 %copy-start.29 = (s32[32]{0:T(128)S(1)}, s32[32]{0:T(128)}, u32[]{:S(2)}) copy-start(s32[32]{0:T(128)} %copy-done.28) | copy-start | bytes 388 | tf_op jit(solution)/shard_map/cond
  237.8 12.7 %collective-permute-start.22 = (f32[112,128]{1,0:T(8,128)S(1)}, f32[112,128]{1,0:T(8,128)S(1)}, u32[]{:S(2)}, u32[]{:S(2)}) collective-permute-start(f32[112,128]{1,0:T(8,128)S(1)} %get-tuple-element.130), channel_id=1, source_target_pairs={{0,2},{1,3},{2,4},{3,5},{4,6},{5,7},{6,0},{7,1},{8,10},{9,11},{10,... | collective-permute-start | bytes 172040 | tf_op jit(solution)/shard_map/cond/branch_1_fun/ppermute | solution.py:365
  239.5 11.0 %collective-permute-start.23 = (f32[112,128]{1,0:T(8,128)S(1)}, f32[112,128]{1,0:T(8,128)S(1)}, u32[]{:S(2)}, u32[]{:S(2)}) collective-permute-start(f32[112,128]{1,0:T(8,128)S(1)} %get-tuple-element.128), channel_id=1, source_target_pairs={{0,4},{1,5},{2,6},{3,7},{4,0},{5,1},{6,2},{7,3},{8,12},{9,13},{10,... | collective-permute-start | bytes 172040 | tf_op jit(solution)/shard_map/cond/branch_1_fun/ppermute | solution.py:365
  242.8 7.7 %collective-permute-start.24 = (f32[112,128]{1,0:T(8,128)S(1)}, f32[112,128]{1,0:T(8,128)S(1)}, u32[]{:S(2)}, u32[]{:S(2)}) collective-permute-start(f32[112,128]{1,0:T(8,128)S(1)} %get-tuple-element.129), channel_id=1, source_target_pairs={{0,6},{1,7},{2,0},{3,1},{4,2},{5,3},{6,4},{7,5},{8,14},{9,15},{10,... | collective-permute-start | bytes 172040 | tf_op jit(solution)/shard_map/cond/branch_1_fun/ppermute | solution.py:365
  249.1 7.1 %collective-permute-start.18 = (f32[128,128]{1,0:T(8,128)S(1)}, f32[128,128]{1,0:T(8,128)S(1)}, u32[]{:S(2)}, u32[]{:S(2)}) collective-permute-start(f32[128,128]{1,0:T(8,128)S(1)} %branch_1_fun.18), channel_id=1, source_target_pairs={{0,1},{1,0},{2,3},{3,2},{4,5},{5,4},{6,7},{7,6},{8,9},{9,8},{10,11... | collective-permute-start | bytes 196616 | tf_op jit(solution)/shard_map/cond/branch_1_fun/ppermute | solution.py:382
  250.5 6.5 %collective-permute-start.25 = (bf16[112,128]{1,0:T(8,128)(2,1)S(1)}, bf16[112,128]{1,0:T(8,128)(2,1)S(1)}, u32[]{:S(2)}, u32[]{:S(2)}) collective-permute-start(bf16[112,128]{1,0:T(8,128)(2,1)S(1)} %add_convert_fusion), channel_id=1, source_target_pairs={{0,2},{1,3},{2,4},{3,5},{4,6},{5,7},{6,0},{7,1},{8,10},{9,11},{10,... | collective-permute-start | bytes 86024 | tf_op jit(solution)/shard_map/cond/branch_1_fun/ppermute | solution.py:369
  252.2 5.0 %collective-permute-start.26 = (bf16[112,128]{1,0:T(8,128)(2,1)S(1)}, bf16[112,128]{1,0:T(8,128)(2,1)S(1)}, u32[]{:S(2)}, u32[]{:S(2)}) collective-permute-start(bf16[112,128]{1,0:T(8,128)(2,1)S(1)} %add_convert_fusion), channel_id=1, source_target_pairs={{0,4},{1,5},{2,6},{3,7},{4,0},{5,1},{6,2},{7,3},{8,12},{9,13},{10,... | collective-permute-start | bytes 86024 | tf_op jit(solution)/shard_map/cond/branch_1_fun/ppermute | solution.py:369
  255.5 2.7 collective-permute-start.27
  256.2 4.1 %collective-permute-start.19 = (f32[128,128]{1,0:T(8,128)S(1)}, f32[128,128]{1,0:T(8,128)S(1)}, u32[]{:S(2)}, u32[]{:S(2)}) collective-permute-start(f32[128,128]{1,0:T(8,128)S(1)} %add.132), channel_id=1, source_target_pairs={{0,2},{1,3},{2,0},{3,1},{4,6},{5,7},{6,4},{7,5},{8,10},{9,11},{10,... | collective-permute-start | bytes 196616 | tf_op jit(solution)/shard_map/cond/branch_1_fun/ppermute | solution.py:382
  258.2 6.6 %collective-permute-start.28 = (bf16[4,112,128]{2,1,0:T(8,128)(2,1)S(1)}, bf16[4,112,128]{2,1,0:T(8,128)(2,1)S(1)}, u32[]{:S(2)}, u32[]{:S(2)}) collective-permute-start(bf16[4,112,128]{2,1,0:T(8,128)(2,1)S(1)} %pad_maximum_fusion.own), channel_id=1, source_target_pairs={{0,1},{1,0},{2,3},{3,2},{4,5},{5,4},{6,7},{7,6},{8,9},{9,8},{10,11... | collective-permute-start | bytes 344072 | tf_op jit(solution)/shard_map/cond/branch_1_fun/ppermute | solution.py:370
  260.4 4.4 %collective-permute-start.20 = (f32[128,128]{1,0:T(8,128)S(1)}, f32[128,128]{1,0:T(8,128)S(1)}, u32[]{:S(2)}, u32[]{:S(2)}) collective-permute-start(f32[128,128]{1,0:T(8,128)S(1)} %add.133), channel_id=1, source_target_pairs={{0,6},{1,7},{2,4},{3,5},{4,2},{5,3},{6,0},{7,1},{8,14},{9,15},{10,... | collective-permute-start | bytes 196616 | tf_op jit(solution)/shard_map/cond/branch_1_fun/ppermute | solution.py:382
  (26 other events, 82.7 us)
Sparse Core Ops, SparseCore 0:
  115.6 61.8 reduce-scatter.4

commit v5 on v4

--- a/solution.py
+++ b/solution.py
@@ -36,7 +36,7 @@
 
 SMEM = pl.BlockSpec(memory_space=pltpu.SMEM)
 VMEM = pl.BlockSpec(memory_space=pltpu.VMEM)
-HBM = pl.BlockSpec(memory_space=pl.ANY)
+HBM = pl.BlockSpec(memory_space=pltpu.HBM)
 LANES = 128
 ORDER, PLACE, FLAGS = 0, 1, 2
 HOT, FITS = 0, 1
@@ -129,37 +129,32 @@
     )(me, ids.reshape(total, 1), table.reshape(-1, LANES))
 
 
-def copy_units(wanted, down, up, up_in, up_out, down_sem, up_sem, out_sem):
+def copy_units(wanted, down, up, up_in, down_sem, up_sem):
     rank = down.shape[1]
     lanes = up.shape[2]
     steps = rank // 16
-    waits = []
-    ups = []
+    downs, ups = [], []
     for i, (dest, index, rows) in enumerate(wanted):
         for half in range(2):
             n = 2 * i + half
             ups.append(pltpu.make_async_copy(up.at[rows[half]], up_in.at[n], up_sem.at[n]))
             ups[-1].start()
-            waits.append(
+            downs.append(
                 pltpu.make_async_copy(
                     down.at[rows[half]], dest.at[index, pl.ds(half * rank, rank)], down_sem.at[n]
                 )
             )
-            waits[-1].start()
+            downs[-1].start()
     for i, (dest, index, rows) in enumerate(wanted):
         for half in range(2):
             n = 2 * i + half
             ups[n].wait()
             for part in range(steps):
                 at = (half * steps + part) * lanes
-                up_out[i, :, at : at + lanes] = up_in[n, part * 16 : part * 16 + 16, :]
-        waits.append(
-            pltpu.make_async_copy(
-                up_out.at[i], dest.at[index, pl.ds(2 * rank, 16)], out_sem.at[i]
-            )
-        )
-        waits[-1].start()
-    for copy in waits:
+                dest[index, 2 * rank : 2 * rank + 16, at : at + lanes] = up_in[
+                    n, part * 16 : part * 16 + 16, :
+                ]
+    for copy in downs:
         copy.wait()
 
 
@@ -178,8 +173,8 @@
     def _():
         hot_x, hot_y = lax.div(hot, side), lax.rem(hot, side)
         wanted = []
-        for out, (x_first, a, units) in zip(outs, lines):
-            for i, b in enumerate(units):
+        for out, (x_first, units) in zip(outs, lines):
+            for i, (a, b) in enumerate(units):
                 dx, dy = (a, b) if x_first else (b, a)
                 peer = lax.rem(hot_x + dx, side) * side + lax.rem(hot_y + dy, side)
                 first = MAIN if x_first else MAIN + 2
@@ -194,22 +189,20 @@
         kernel,
         out_shape=[jax.ShapeDtypeStruct((n, 2 * rank + 16, width), down.dtype) for n in shapes],
         in_specs=[SMEM] * len(scalars) + [HBM, HBM],
-        out_specs=[HBM] * len(shapes),
+        out_specs=[VMEM] * len(shapes),
         scratch_shapes=[
             pltpu.VMEM((2 * count, rank, lanes), up.dtype),
-            pltpu.VMEM((count, 16, width), up.dtype),
             pltpu.SemaphoreType.DMA((2 * count,)),
             pltpu.SemaphoreType.DMA((2 * count,)),
-            pltpu.SemaphoreType.DMA((count,)),
         ],
-        compiler_params=pltpu.CompilerParams(vmem_limit_bytes=12 << 20),
+        compiler_params=pltpu.CompilerParams(vmem_limit_bytes=8 << 20),
         cost_estimate=pl.CostEstimate(
             flops=0, bytes_accessed=count * rank * (width + lanes) * 8, transcendentals=0
         ),
     )(*scalars, down, up)
 
 
-def vmem_call(kernel, shapes, dtype, scalars, arrays, limit=32):
+def vmem_call(kernel, shapes, dtype, scalars, arrays, limit=10):
     return pl.pallas_call(
         kernel,
         out_shape=[jax.ShapeDtypeStruct(shape, dtype) for shape in shapes],
@@ -255,6 +248,7 @@
         out = outs[4 * h : 4 * h + 4]
         at = offsets[h]
         low, high = own.at[pl.ds(0, 2)], own.at[pl.ds(2, 2)]
+        plus_b, minus_b = plus_b.at[pl.ds(2, 2)], minus_b.at[pl.ds(2, 2)]
         picks = ((low, high), (plus_a, plus_b), (plus_a, minus_a), (minus_a, minus_b))
         for offset, (first, second) in enumerate(picks):
 
@@ -339,7 +333,7 @@
         out_shape=jax.ShapeDtypeStruct((pairs * cap, 2 * rank), jnp.float32),
         in_specs=[SMEM] + [VMEM] * (1 + len(weights)),
         out_specs=VMEM,
-        compiler_params=pltpu.CompilerParams(vmem_limit_bytes=24 << 20),
+        compiler_params=pltpu.CompilerParams(vmem_limit_bytes=10 << 20),
         cost_estimate=pl.CostEstimate(
             flops=pairs * cap * rank * 4 * hidden.shape[1],
             bytes_accessed=sum(w.size for w in weights) * 2,
@@ -478,7 +472,7 @@
         scratch_shapes=[
             pltpu.VMEM((2 * own.shape[0] * own.shape[1], own.shape[2]), jnp.bfloat16)
         ],
-        compiler_params=pltpu.CompilerParams(vmem_limit_bytes=12 << 20),
+        compiler_params=pltpu.CompilerParams(vmem_limit_bytes=6 << 20),
         cost_estimate=pl.CostEstimate(
             flops=base.size * rank * 2, bytes_accessed=base.size * 8, transcendentals=0
         ),
@@ -499,7 +493,7 @@
             pltpu.VMEM((EXTRA, cap, base.shape[1]), jnp.bfloat16),
             pltpu.SemaphoreType.DMA((EXTRA,)),
         ],
-        compiler_params=pltpu.CompilerParams(vmem_limit_bytes=8 << 20),
+        compiler_params=pltpu.CompilerParams(vmem_limit_bytes=4 << 20),
         cost_estimate=pl.CostEstimate(
             flops=base.size * rank // 4, bytes_accessed=base.size * 4, transcendentals=0
         ),
@@ -556,20 +550,22 @@
         b = (me % side - hot % side) % side
         offsets = jnp.stack([a, b]).astype(jnp.int32)
         trees = (True, False)
-        soon = [(tree, 2, part) for tree in trees for part in ((0, 1), (2, 3))]
-        soon += [(tree, near, (2, 3)) for tree in trees for near in (1, 3)]
-        late = [(tree, near, (0, 1)) for tree in trees for near in (1, 3)]
-        late += [(tree, 0, (0, 1, 2, 3)) for tree in trees]
+        soon = [
+            (tree, ((2, part[0]), (2, part[1]), (near, 2), (near, 3)))
+            for tree in trees
+            for near, part in ((1, (0, 1)), (3, (2, 3)))
+        ]
+        late = [(tree, ((near, 0), (near, 1))) for tree in trees for near in (1, 3)]
+        late += [(tree, ((0, 0), (0, 1), (0, 2), (0, 3))) for tree in trees]
         moves = ((1, 0), (-1, 0), (0, 1), (0, -1))
         turned = ((0, 1), (0, -1), (1, 0), (-1, 0))
         send = lambda values, ways: [shift(v, *way) for v, way in zip(values, ways)]
         barrier = lax.optimization_barrier
         scalars = (me_row, served, mine)
         gathered = gather_call(
-            functools.partial(extra_kernel, soon), (2,) * 8, 16, scalars, down_weights, up_weights
-        )
-        fresh = send(gathered[:4], moves)
-        near_b = send(gathered[4:], moves)
+            functools.partial(extra_kernel, soon), (4,) * 4, 16, scalars, down_weights, up_weights
+        )
+        fresh = send(gathered, moves)
         later_served, _ = barrier((served, gathered))
         later = gather_call(
             functools.partial(extra_kernel, late),
@@ -589,15 +585,15 @@
         relayed = vmem_call(
             relay_kernel, (two,) * 4, main_sent.dtype, (offsets,), (*fresh, *near)
         )
-        main_sent, relayed = barrier((main_sent, relayed))
         near_a = send(relayed, moves)
-        main = lax.all_to_all(main_sent, "dp", 0, 0, tiled=True)
         base_hidden, _ = barrier((hidden, relayed))
         base_terms = jnp.dot(base_hidden, value_weight, preferred_element_type=jnp.float32)
+        base_terms, main_sent = barrier((base_terms, main_sent))
+        main = lax.all_to_all(main_sent, "dp", 0, 0, tiled=True)
         base = lax.psum_scatter(base_terms, "tp", scatter_dimension=1, tiled=True)
-        near_a, near_b, base_terms = barrier((near_a, near_b, base_terms))
+        near_a, base_terms = barrier((near_a, base_terms))
         tree_arrays = [
-            (later[4 + h], near_a[2 * h], near_a[2 * h + 1], near_b[2 * h], near_b[2 * h + 1])
+            (later[4 + h], near_a[2 * h], near_a[2 * h + 1], fresh[2 * h], fresh[2 * h + 1])
             for h in range(2)
         ]
         lines = vmem_call(

time: 280 us -> 214 us (0.76)
  waiting for transfers between devices: 142 us -> 79.7 us
  starting transfers between devices: 57.7 us -> 46.2 us
  local copies, waits for them, and re-layouts: 20.9 us -> 27.7 us
    ppermute x18 -> x14, waiting for transfers between devices: 138 us -> 75.9 us  [shift(): return lax.ppermute(value, 'dp', pairs)]
    all_to_all x1, starting transfers between devices: 13.3 us -> 4.81 us  [narrow(): main = lax.all_to_all(main_sent, 'dp', 0, 0, tiled=True)]
    cond x54 -> x68, local copies, waits for them, and re-layouts: 18.2 us -> 24.9 us
    ppermute x18 -> x14, starting transfers between devices: 24 us -> 21.8 us  [shift(): return lax.ppermute(value, 'dp', pairs)]
  transfers between devices with their start and end apart: 31 -> 27, of which waited for: 12 -> 12; matrix products, arithmetic and copies ran while one was open for 0% -> 0% of each run, Pallas kernels for 8% -> 10%
where the time goes in v5:
time: 214 us; the launch traced here: 211 us
  waiting for transfers between devices  79.7 us (37%)
  starting transfers between devices  46.2 us (22%)
  Pallas kernels  33.1 us (15%)
  local copies, waits for them, and re-layouts  27.7 us (13%)
  between operations  14.1 us (7%)
  matrix products  6.68 us (3%)
  loops' own time  3.4 us (2%)
    ppermute x14, waiting for transfers between devices, shift(): return lax.ppermute(value, 'dp', pairs)  75.9 us
    cond x68, local copies, waits for them, and re-layouts  24.9 us
    ppermute x14, starting transfers between devices, shift(): return lax.ppermute(value, 'dp', pairs)  21.8 us
    pallas_call x3, Pallas kernels, gather_call(): pl.pallas_call(kernel, out_shape=[jax.ShapeDtypeStruct((n, 2 * rank + 16,...  12.6 us
    pallas_call x2, Pallas kernels, low_partial(): pl.pallas_call(kernel, out_shape=jax.ShapeDtypeStruct((pairs * cap, 2 * r...  8.31 us
    dot_general x1, matrix products, narrow(): jnp.dot(base_hidden, value_weight, preferred_element_type=jnp.float32)  6.68 us
    pallas_call x4, Pallas kernels, vmem_call(): pl.pallas_call(kernel, out_shape=[jax.ShapeDtypeStruct(shape, dtype) for...  5.79 us
    ppermute x3, starting transfers between devices, low_rank_rounds(): lax.ppermute(cut(total, (z + d) % chips * piece, piece), 'tp', turn(d))  5.69 us
  transfers between devices with their start and end apart: 27, of which 12 were waited for; matrix products, arithmetic and copies ran while one was open for 0% of the time, Pallas kernels for 10%

profile of v5, /device:TPU:1, one launch (start us, length us, event | category | flops | bytes accessed | tf_op | source)
XLA Modules:
  0.0 211.1 jit_solution(4997764873859378851)
XLA Ops:
  8.1 1.8 shard_map.75
  11.2 193.0 %conditional.1 = (bf16[2048,128]{1,0:T(8,128)(2,1)}) conditional(s32[]{:T(128)} %bitcast.20, (s32[32]{0:T(128)S(1)}, bf16[2048,1024]{1,0:T(8,128)(2,1)}, bf16[1024,1024]{1,0:T(8,128)(2,1)}, s32[512]{0:T(512)}, s32[2048]{0:T(1024)}, /*index=5*/s32[]{:T(128)}, bf16[128,64,1024]{2,1,0:T(8,128)(2,1)}, bf16[128,64,128]{2,1,0:T(8,128)(2,1)}) %tuple.19, ...), branch_computations={%region_0.5_spmd, %region_5.7_spmd} | conditional | flops 4601487360 | bytes 327286624 | solution.py:644
  11.5 3.5 %branch_1_fun.11 = (bf16[4,144,1024]{2,1,0:T(8,128)(2,1)}, bf16[4,144,1024]{2,1,0:T(8,128)(2,1)}, bf16[4,144,1024]{2,1,0:T(8,128)(2,1)}, bf16[4,144,1024]{2,1,0:T(8,128)(2,1)}) custom-call(s32[1]{0:T(128)} %get-tuple-element.54.me, s32[16,128]{1,0:T(8,128)S(1)} %get-tuple-element.69.served, s32[8,128]{1,0:T(8,128)S(1)} %get-tuple-element.50.mine, ...), custom_call_target="tpu_custom_call" | custom-call | bytes 9437184 | tf_op jit(solution)/shard_map/cond/branch_1_fun/pallas_call | solution.py:188
  15.0 2.1 collective-permute-start
  19.8 1.4 collective-permute-start.3
  24.5 1.5 branch_1_fun.12
  32.5 7.7 %branch_1_fun.13 = bf16[16,144,1024]{2,1,0:T(8,128)(2,1)S(1)} custom-call(s32[16,128]{1,0:T(8,128)S(1)} %copy-done.32, bf16[128,64,1024]{2,1,0:T(8,128)(2,1)S(1)} %copy-done.27, bf16[128,64,128]{2,1,0:T(8,128)(2,1)S(1)} %copy-done.30), custom_call_target="tpu_custom_call" | custom-call | bytes 9437184 | tf_op jit(solution)/shard_map/cond/branch_1_fun/pallas_call | solution.py:188
  40.2 2.2 %copy-done = bf16[16,144,1024]{2,1,0:T(8,128)(2,1)} copy-done((bf16[16,144,1024]{2,1,0:T(8,128)(2,1)}, bf16[16,144,1024]{2,1,0:T(8,128)(2,1)S(1)}, u32[]{:S(2)}) %copy-start) | copy-done | bytes 4718616 | tf_op jit(solution)/shard_map/cond
  43.9 2.5 %collective-permute-done.2.refs_2_.refs_8_ = bf16[4,144,1024]{2,1,0:T(8,128)(2,1)S(1)} collective-permute-done((bf16[4,144,1024]{2,1,0:T(8,128)(2,1)}, bf16[4,144,1024]{2,1,0:T(8,128)(2,1)S(1)}, u32[]{:S(2)}, u32[]{:S(2)}) %collective-permute-start.2) | collective-permute-done | bytes 1179680 | tf_op jit(solution)/shard_map/cond/branch_1_fun/ppermute | solution.py:52
  51.7 1.7 branch_1_fun.14
  56.9 6.7 %fusion.8 = f32[2048,1024]{1,0:T(8,128)} fusion(bf16[2048,1024]{1,0:T(8,128)(2,1)S(1)} %copy-done.28, bf16[1024,1024]{1,0:T(8,128)(2,1)S(1)} %copy-done.36), kind=kOutput, calls=%fused_computation.42 | convolution fusion | flops 4294967296 | bytes 14680064 | tf_op jit(solution)/shard_map/cond/branch_1_fun/dot_general | solution.py:590
  63.6 4.8 %all-to-all-start.3 = ((bf16[16,144,1024]{2,1,0:T(8,128)(2,1)}), bf16[16,144,1024]{2,1,0:T(8,128)(2,1)}, u32[]{:S(2)}, u32[]{:S(2)}) async-start(bf16[16,144,1024]{2,1,0:T(8,128)(2,1)} %copy-done), calls=%async_computation.5 | async-start | bytes 9437184 | tf_op jit(solution)/shard_map/cond/branch_1_fun/all_to_all | solution.py:592
  72.4 1.4 collective-permute-start.7
  73.8 62.6 %collective-permute-done.4.refs_1_ = bf16[2,144,1024]{2,1,0:T(8,128)(2,1)S(1)} collective-permute-done((bf16[2,144,1024]{2,1,0:T(8,128)(2,1)}, bf16[2,144,1024]{2,1,0:T(8,128)(2,1)S(1)}, u32[]{:S(2)}, u32[]{:S(2)}) %collective-permute-start.4) | collective-permute-done | bytes 589856 | tf_op jit(solution)/shard_map/cond/branch_1_fun/ppermute | solution.py:52
  139.0 2.6 %branch_1_fun.15 = (bf16[144,1024]{1,0:T(8,128)(2,1)S(1)}, bf16[144,1024]{1,0:T(8,128)(2,1)S(1)}, bf16[144,1024]{1,0:T(8,128)(2,1)}, bf16[144,1024]{1,0:T(8,128)...) custom-call(s32[2]{0:T(128)S(1)} %pad_add_fusion.offsets, ...), custom_call_target="tpu_custom_call" | custom-call | bytes 4718592 | tf_op jit(solution)/shard_map/cond/branch_1_fun/pallas_call | solution.py:206
  144.4 5.9 %collective-permute-start.10 = (bf16[144,1024]{1,0:T(8,128)(2,1)}, bf16[144,1024]{1,0:T(8,128)(2,1)S(1)}, u32[]{:S(2)}, u32[]{:S(2)}) collective-permute-start(bf16[144,1024]{1,0:T(8,128)(2,1)} %get-tuple-element.93), channel_id=1, source_target_pairs={{0,32},{8,40},{16,48},{24,56},{32,64},{40,72},{48,80},{56,88},{64,... | collective-permute-start | bytes 884744 | tf_op jit(solution)/shard_map/cond/branch_1_fun/ppermute | solution.py:52
  150.9 2.1 %collective-permute-start.9 = (bf16[144,1024]{1,0:T(8,128)(2,1)}, bf16[144,1024]{1,0:T(8,128)(2,1)S(1)}, u32[]{:S(2)}, u32[]{:S(2)}) collective-permute-start(bf16[144,1024]{1,0:T(8,128)(2,1)} %get-tuple-element.92), channel_id=1, source_target_pairs={{0,24},{8,0},{16,8},{24,16},{32,56},{40,32},{48,40},{56,48},{64,88... | collective-permute-start | bytes 884744 | tf_op jit(solution)/shard_map/cond/branch_1_fun/ppermute | solution.py:52
  153.0 2.8 %collective-permute-done.10.refs_1_ = bf16[144,1024]{1,0:T(8,128)(2,1)S(1)} collective-permute-done((bf16[144,1024]{1,0:T(8,128)(2,1)}, bf16[144,1024]{1,0:T(8,128)(2,1)S(1)}, u32[]{:S(2)}, u32[]{:S(2)}) %collective-permute-start.10) | collective-permute-done | bytes 294944 | tf_op jit(solution)/shard_map/cond/branch_1_fun/ppermute | solution.py:52
  155.8 1.8 collective-permute-done.11.refs_4_
  161.4 5.8 %branch_1_fun.19 = f32[896,128]{1,0:T(8,128)S(1)} custom-call(s32[8,128]{1,0:T(8,128)S(1)} %get-tuple-element.50.mine, bf16[2048,1024]{1,0:T(8,128)(2,1)} %get-tuple-element.82.hidden, bf16[16,144,1024]{2,1,0:T(8,128)(2,1)} %all-to-all-done.3.main), custom_call_target="tpu_custom_call" | custom-call | flops 234881024 | bytes 4718592 | tf_op jit(solution)/shard_map/cond/branch_1_fun/pallas_call | solution.py:331
  167.3 2.5 %collective-permute-start.17 = (f32[448,128]{1,0:T(8,128)S(1)}, f32[448,128]{1,0:T(8,128)S(1)}, u32[]{:S(2)}, u32[]{:S(2)}) collective-permute-start(f32[448,128]{1,0:T(8,128)S(1)} %constant_dynamic-slice_fusion.3), channel_id=1, source_target_pairs={{0,1},{1,0},{2,3},{3,2},{4,5},{5,4},{6,7},{7,6},{8,9},{9,8},{10,11... | collective-permute-start | bytes 688136 | tf_op jit(solution)/shard_map/cond/branch_1_fun/ppermute | solution.py:355
  169.7 1.5 collective-permute-start.13
  171.3 1.7 collective-permute-start.18
  173.0 3.3 %collective-permute-start.19 = (f32[112,128]{1,0:T(8,128)S(1)}, f32[112,128]{1,0:T(8,128)S(1)}, u32[]{:S(2)}, u32[]{:S(2)}) collective-permute-start(f32[112,128]{1,0:T(8,128)S(1)} %get-tuple-element.117), channel_id=1, source_target_pairs={{0,4},{1,5},{2,6},{3,7},{4,0},{5,1},{6,2},{7,3},{8,12},{9,13},{10,... | collective-permute-start | bytes 172040 | tf_op jit(solution)/shard_map/cond/branch_1_fun/ppermute | solution.py:359
  177.0 2.4 %collective-permute-done.12.refs_2_ = bf16[144,1024]{1,0:T(8,128)(2,1)S(1)} collective-permute-done((bf16[144,1024]{1,0:T(8,128)(2,1)S(1)}, bf16[144,1024]{1,0:T(8,128)(2,1)S(1)}, u32[]{:S(2)}, u32[]{:S(2)}) %collective-permute-start.12) | collective-permute-done | bytes 294944 | tf_op jit(solution)/shard_map/cond/branch_1_fun/ppermute | solution.py:52
  180.3 2.5 %branch_1_fun.18 = f32[128,128]{1,0:T(8,128)S(1)} custom-call(s32[8,128]{1,0:T(8,128)S(1)} %get-tuple-element.50.mine, bf16[2048,1024]{1,0:T(8,128)(2,1)} %get-tuple-element.82.hidden, bf16[144,1024]{1,0:T(8,128)(2,1)S(1)} %get-tuple-element.107.refs_0_.first_pack, bf16[144,1024]{1,0:T(8,128)(2,1)S(1)} %get-tuple-element.108.refs_1_.second_pack), custom_call_target="tpu_custom_call" | custom-call | flops 33554432 | bytes 589824 | tf_op jit(solution)/shard_map/cond/branch_1_fun/pallas_call | solution.py:331
  183.9 1.7 collective-permute-start.21
  185.6 3.3 %collective-permute-start.22 = (bf16[112,128]{1,0:T(8,128)(2,1)S(1)}, bf16[112,128]{1,0:T(8,128)(2,1)S(1)}, u32[]{:S(2)}, u32[]{:S(2)}) collective-permute-start(bf16[112,128]{1,0:T(8,128)(2,1)S(1)} %add_convert_fusion), channel_id=1, source_target_pairs={{0,4},{1,5},{2,6},{3,7},{4,0},{5,1},{6,2},{7,3},{8,12},{9,13},{10,... | collective-permute-start | bytes 86024 | tf_op jit(solution)/shard_map/cond/branch_1_fun/ppermute | solution.py:363
  191.6 2.1 %collective-permute-start.24 = (bf16[4,112,128]{2,1,0:T(8,128)(2,1)S(1)}, bf16[4,112,128]{2,1,0:T(8,128)(2,1)S(1)}, u32[]{:S(2)}, u32[]{:S(2)}) collective-permute-start(bf16[4,112,128]{2,1,0:T(8,128)(2,1)S(1)} %pad_maximum_fusion.own), channel_id=1, source_target_pairs={{0,1},{1,0},{2,3},{3,2},{4,5},{5,4},{6,7},{7,6},{8,9},{9,8},{10,11... | collective-permute-start | bytes 344072 | tf_op jit(solution)/shard_map/cond/branch_1_fun/ppermute | solution.py:364
  193.7 1.7 collective-permute-start.16
  195.5 2.6 %collective-permute-done.16 = f32[128,128]{1,0:T(8,128)S(1)} collective-permute-done((f32[128,128]{1,0:T(8,128)S(1)}, f32[128,128]{1,0:T(8,128)S(1)}, u32[]{:S(2)}, u32[]{:S(2)}) %collective-permute-start.16) | collective-permute-done | bytes 65568 | tf_op jit(solution)/shard_map/cond/branch_1_fun/ppermute | solution.py:376
  199.4 3.1 %branch_1_fun.20._ = bf16[2048,128]{1,0:T(8,128)(2,1)} custom-call(s32[2]{0:T(128)S(1)} %pad_add_fusion.1.where, s32[8,128]{1,0:T(8,128)S(1)} %get-tuple-element.50.mine, s32[32]{0:T(128)S(1)} %copy-done.35, f32[2048,128]{1,0:T(8,128)S(1)} %copy-done.1, bf16[4,112,128]{2,1,0:T(8,128)(2,1)S(1)} %pad_maximum_fusion.own, ...), custom_call_target="tpu_custom_call" | custom-call | flops 33554432 | bytes 2097152 | tf_op jit(solution)/shard_map/cond/branch_1_fun/pallas_call | solution.py:466
  (119 shorter events, 44.2 us)
Async XLA Ops:
  11.4 186.8 %reduce-scatter.5.cloned.1.call-start = ((), (), s32[]{:S(2)}) async-start(), calls=%async_computation.7 | async-start | bytes 9437184 | tf_op jit(solution)/shard_map/cond/branch_1_fun/reduce_scatter | solution.py:593
  15.0 28.8 %collective-permute-start = (bf16[4,144,1024]{2,1,0:T(8,128)(2,1)}, bf16[4,144,1024]{2,1,0:T(8,128)(2,1)S(1)}, u32[]{:S(2)}, u32[]{:S(2)}) collective-permute-start(bf16[4,144,1024]{2,1,0:T(8,128)(2,1)} %get-tuple-element.58), channel_id=1, source_target_pairs={{0,32},{8,40},{16,48},{24,56},{32,64},{40,72},{48,80},{56,88},{64,... | collective-permute-start | bytes 3538952 | tf_op jit(solution)/shard_map/cond/branch_1_fun/ppermute | solution.py:52
  17.1 26.8 %collective-permute-start.1 = (bf16[4,144,1024]{2,1,0:T(8,128)(2,1)}, bf16[4,144,1024]{2,1,0:T(8,128)(2,1)S(1)}, u32[]{:S(2)}, u32[]{:S(2)}) collective-permute-start(bf16[4,144,1024]{2,1,0:T(8,128)(2,1)} %get-tuple-element.59), channel_id=1, source_target_pairs={{0,96},{8,104},{16,112},{24,120},{32,0},{40,8},{48,16},{56,24},{64... | collective-permute-start | bytes 3538952 | tf_op jit(solution)/shard_map/cond/branch_1_fun/ppermute | solution.py:52
  18.4 28.0 %collective-permute-start.2 = (bf16[4,144,1024]{2,1,0:T(8,128)(2,1)}, bf16[4,144,1024]{2,1,0:T(8,128)(2,1)S(1)}, u32[]{:S(2)}, u32[]{:S(2)}) collective-permute-start(bf16[4,144,1024]{2,1,0:T(8,128)(2,1)} %get-tuple-element.60), channel_id=1, source_target_pairs={{0,8},{8,16},{16,24},{24,0},{32,40},{40,48},{48,56},{56,32},{64,72... | collective-permute-start | bytes 3538952 | tf_op jit(solution)/shard_map/cond/branch_1_fun/ppermute | solution.py:52
  19.8 27.7 %collective-permute-start.3 = (bf16[4,144,1024]{2,1,0:T(8,128)(2,1)}, bf16[4,144,1024]{2,1,0:T(8,128)(2,1)}, u32[]{:S(2)}, u32[]{:S(2)}) collective-permute-start(bf16[4,144,1024]{2,1,0:T(8,128)(2,1)} %get-tuple-element.61), channel_id=1, source_target_pairs={{0,24},{8,0},{16,8},{24,16},{32,56},{40,32},{48,40},{56,48},{64,88... | collective-permute-start | bytes 3538952 | tf_op jit(solution)/shard_map/cond/branch_1_fun/ppermute | solution.py:52
  24.5 8.1 %copy-start.30 = (bf16[128,64,128]{2,1,0:T(8,128)(2,1)S(1)}, bf16[128,64,128]{2,1,0:T(8,128)(2,1)}, u32[]{:S(2)}) copy-start(bf16[128,64,128]{2,1,0:T(8,128)(2,1)} %get-tuple-element.57.up) | copy-start | bytes 6291460 | tf_op jit(solution)/shard_map/cond
  24.5 8.0 %copy-start.32 = (s32[16,128]{1,0:T(8,128)S(1)}, s32[16,128]{1,0:T(8,128)}, u32[]{:S(2)}) copy-start(s32[16,128]{1,0:T(8,128)} %copy-done.31) | copy-start | bytes 24580 | tf_op jit(solution)/shard_map/cond
  63.6 97.8 %all-to-all-start.3 = ((bf16[16,144,1024]{2,1,0:T(8,128)(2,1)}), bf16[16,144,1024]{2,1,0:T(8,128)(2,1)}, u32[]{:S(2)}, u32[]{:S(2)}) async-start(bf16[16,144,1024]{2,1,0:T(8,128)(2,1)} %copy-done), calls=%async_computation.5 | async-start | bytes 9437184 | tf_op jit(solution)/shard_map/cond/branch_1_fun/all_to_all | solution.py:592
  68.4 68.1 %collective-permute-start.4 = (bf16[2,144,1024]{2,1,0:T(8,128)(2,1)}, bf16[2,144,1024]{2,1,0:T(8,128)(2,1)S(1)}, u32[]{:S(2)}, u32[]{:S(2)}) collective-permute-start(bf16[2,144,1024]{2,1,0:T(8,128)(2,1)} %copy-done.25), channel_id=1, source_target_pairs={{0,32},{8,40},{16,48},{24,56},{32,64},{40,72},{48,80},{56,88},{64,... | collective-permute-start | bytes 1769480 | tf_op jit(solution)/shard_map/cond/branch_1_fun/ppermute | solution.py:52
  69.7 66.7 %collective-permute-start.5 = (bf16[2,144,1024]{2,1,0:T(8,128)(2,1)}, bf16[2,144,1024]{2,1,0:T(8,128)(2,1)S(1)}, u32[]{:S(2)}, u32[]{:S(2)}) collective-permute-start(bf16[2,144,1024]{2,1,0:T(8,128)(2,1)} %copy-done.24), channel_id=1, source_target_pairs={{0,96},{8,104},{16,112},{24,120},{32,0},{40,8},{48,16},{56,24},{64... | collective-permute-start | bytes 1769480 | tf_op jit(solution)/shard_map/cond/branch_1_fun/ppermute | solution.py:52
  71.1 65.3 %collective-permute-start.6 = (bf16[2,144,1024]{2,1,0:T(8,128)(2,1)}, bf16[2,144,1024]{2,1,0:T(8,128)(2,1)S(1)}, u32[]{:S(2)}, u32[]{:S(2)}) collective-permute-start(bf16[2,144,1024]{2,1,0:T(8,128)(2,1)} %copy-done.23), channel_id=1, source_target_pairs={{0,8},{8,16},{16,24},{24,0},{32,40},{40,48},{48,56},{56,32},{64,72... | collective-permute-start | bytes 1769480 | tf_op jit(solution)/shard_map/cond/branch_1_fun/ppermute | solution.py:52
  72.4 64.1 %collective-permute-start.7 = (bf16[2,144,1024]{2,1,0:T(8,128)(2,1)}, bf16[2,144,1024]{2,1,0:T(8,128)(2,1)S(1)}, u32[]{:S(2)}, u32[]{:S(2)}) collective-permute-start(bf16[2,144,1024]{2,1,0:T(8,128)(2,1)} %copy-done.22), channel_id=1, source_target_pairs={{0,24},{8,0},{16,8},{24,16},{32,56},{40,32},{48,40},{56,48},{64,88... | collective-permute-start | bytes 1769480 | tf_op jit(solution)/shard_map/cond/branch_1_fun/ppermute | solution.py:52
  144.4 11.4 %collective-permute-start.10 = (bf16[144,1024]{1,0:T(8,128)(2,1)}, bf16[144,1024]{1,0:T(8,128)(2,1)S(1)}, u32[]{:S(2)}, u32[]{:S(2)}) collective-permute-start(bf16[144,1024]{1,0:T(8,128)(2,1)} %get-tuple-element.93), channel_id=1, source_target_pairs={{0,32},{8,40},{16,48},{24,56},{32,64},{40,72},{48,80},{56,88},{64,... | collective-permute-start | bytes 884744 | tf_op jit(solution)/shard_map/cond/branch_1_fun/ppermute | solution.py:52
  150.4 7.3 %collective-permute-start.11 = (bf16[144,1024]{1,0:T(8,128)(2,1)}, bf16[144,1024]{1,0:T(8,128)(2,1)S(1)}, u32[]{:S(2)}, u32[]{:S(2)}) collective-permute-start(bf16[144,1024]{1,0:T(8,128)(2,1)} %get-tuple-element.94), channel_id=1, source_target_pairs={{0,96},{8,104},{16,112},{24,120},{32,0},{40,8},{48,16},{56,24},{64... | collective-permute-start | bytes 884744 | tf_op jit(solution)/shard_map/cond/branch_1_fun/ppermute | solution.py:52
  150.4 8.5 %collective-permute-start.8 = (bf16[144,1024]{1,0:T(8,128)(2,1)}, bf16[144,1024]{1,0:T(8,128)(2,1)S(1)}, u32[]{:S(2)}, u32[]{:S(2)}) collective-permute-start(bf16[144,1024]{1,0:T(8,128)(2,1)} %get-tuple-element.91), channel_id=1, source_target_pairs={{0,8},{8,16},{16,24},{24,0},{32,40},{40,48},{48,56},{56,32},{64,72... | collective-permute-start | bytes 884744 | tf_op jit(solution)/shard_map/cond/branch_1_fun/ppermute | solution.py:52
  150.9 7.9 %collective-permute-start.9 = (bf16[144,1024]{1,0:T(8,128)(2,1)}, bf16[144,1024]{1,0:T(8,128)(2,1)S(1)}, u32[]{:S(2)}, u32[]{:S(2)}) collective-permute-start(bf16[144,1024]{1,0:T(8,128)(2,1)} %get-tuple-element.92), channel_id=1, source_target_pairs={{0,24},{8,0},{16,8},{24,16},{32,56},{40,32},{48,40},{56,48},{64,88... | collective-permute-start | bytes 884744 | tf_op jit(solution)/shard_map/cond/branch_1_fun/ppermute | solution.py:52
  161.4 18.0 %copy-start.15 = (bf16[144,1024]{1,0:T(8,128)(2,1)S(1)}, bf16[144,1024]{1,0:T(8,128)(2,1)}, u32[]{:S(2)}) copy-start(bf16[144,1024]{1,0:T(8,128)(2,1)} %copy-done.14) | copy-start | bytes 884740 | tf_op jit(solution)/shard_map/cond
  161.4 18.0 %copy-start.17 = (bf16[144,1024]{1,0:T(8,128)(2,1)S(1)}, bf16[144,1024]{1,0:T(8,128)(2,1)}, u32[]{:S(2)}) copy-start(bf16[144,1024]{1,0:T(8,128)(2,1)} %copy-done.16) | copy-start | bytes 884740 | tf_op jit(solution)/shard_map/cond
  167.3 3.9 %collective-permute-start.17 = (f32[448,128]{1,0:T(8,128)S(1)}, f32[448,128]{1,0:T(8,128)S(1)}, u32[]{:S(2)}, u32[]{:S(2)}) collective-permute-start(f32[448,128]{1,0:T(8,128)S(1)} %constant_dynamic-slice_fusion.3), channel_id=1, source_target_pairs={{0,1},{1,0},{2,3},{3,2},{4,5},{5,4},{6,7},{7,6},{8,9},{9,8},{10,11... | collective-permute-start | bytes 688136 | tf_op jit(solution)/shard_map/cond/branch_1_fun/ppermute | solution.py:355
  169.7 9.7 %collective-permute-start.12 = (bf16[144,1024]{1,0:T(8,128)(2,1)S(1)}, bf16[144,1024]{1,0:T(8,128)(2,1)S(1)}, u32[]{:S(2)}, u32[]{:S(2)}) collective-permute-start(bf16[144,1024]{1,0:T(8,128)(2,1)S(1)} %get-tuple-element.103), channel_id=1, source_target_pairs={{0,8},{8,16},{16,24},{24,0},{32,40},{40,48},{48,56},{56,32},{64,72... | collective-permute-start | bytes 884744 | tf_op jit(solution)/shard_map/cond/branch_1_fun/ppermute | solution.py:52
  169.7 9.7 %collective-permute-start.13 = (bf16[144,1024]{1,0:T(8,128)(2,1)S(1)}, bf16[144,1024]{1,0:T(8,128)(2,1)S(1)}, u32[]{:S(2)}, u32[]{:S(2)}) collective-permute-start(bf16[144,1024]{1,0:T(8,128)(2,1)S(1)} %get-tuple-element.106), channel_id=1, source_target_pairs={{0,32},{8,40},{16,48},{24,56},{32,64},{40,72},{48,80},{56,88},{64,... | collective-permute-start | bytes 884744 | tf_op jit(solution)/shard_map/cond/branch_1_fun/ppermute | solution.py:52
  171.2 27.0 %copy-start.35 = (s32[32]{0:T(128)S(1)}, s32[32]{0:T(128)}, u32[]{:S(2)}) copy-start(s32[32]{0:T(128)} %copy-done.34) | copy-start | bytes 388 | tf_op jit(solution)/shard_map/cond
  171.3 12.6 %collective-permute-start.18 = (f32[112,128]{1,0:T(8,128)S(1)}, f32[112,128]{1,0:T(8,128)S(1)}, u32[]{:S(2)}, u32[]{:S(2)}) collective-permute-start(f32[112,128]{1,0:T(8,128)S(1)} %get-tuple-element.119), channel_id=1, source_target_pairs={{0,2},{1,3},{2,4},{3,5},{4,6},{5,7},{6,0},{7,1},{8,10},{9,11},{10,... | collective-permute-start | bytes 172040 | tf_op jit(solution)/shard_map/cond/branch_1_fun/ppermute | solution.py:359
  173.0 10.9 %collective-permute-start.19 = (f32[112,128]{1,0:T(8,128)S(1)}, f32[112,128]{1,0:T(8,128)S(1)}, u32[]{:S(2)}, u32[]{:S(2)}) collective-permute-start(f32[112,128]{1,0:T(8,128)S(1)} %get-tuple-element.117), channel_id=1, source_target_pairs={{0,4},{1,5},{2,6},{3,7},{4,0},{5,1},{6,2},{7,3},{8,12},{9,13},{10,... | collective-permute-start | bytes 172040 | tf_op jit(solution)/shard_map/cond/branch_1_fun/ppermute | solution.py:359
  176.3 7.6 %collective-permute-start.20 = (f32[112,128]{1,0:T(8,128)S(1)}, f32[112,128]{1,0:T(8,128)S(1)}, u32[]{:S(2)}, u32[]{:S(2)}) collective-permute-start(f32[112,128]{1,0:T(8,128)S(1)} %get-tuple-element.118), channel_id=1, source_target_pairs={{0,6},{1,7},{2,0},{3,1},{4,2},{5,3},{6,4},{7,5},{8,14},{9,15},{10,... | collective-permute-start | bytes 172040 | tf_op jit(solution)/shard_map/cond/branch_1_fun/ppermute | solution.py:359
  182.8 6.8 %collective-permute-start.14 = (f32[128,128]{1,0:T(8,128)S(1)}, f32[128,128]{1,0:T(8,128)S(1)}, u32[]{:S(2)}, u32[]{:S(2)}) collective-permute-start(f32[128,128]{1,0:T(8,128)S(1)} %branch_1_fun.18), channel_id=1, source_target_pairs={{0,1},{1,0},{2,3},{3,2},{4,5},{5,4},{6,7},{7,6},{8,9},{9,8},{10,11... | collective-permute-start | bytes 196616 | tf_op jit(solution)/shard_map/cond/branch_1_fun/ppermute | solution.py:376
  183.9 6.6 %collective-permute-start.21 = (bf16[112,128]{1,0:T(8,128)(2,1)S(1)}, bf16[112,128]{1,0:T(8,128)(2,1)S(1)}, u32[]{:S(2)}, u32[]{:S(2)}) collective-permute-start(bf16[112,128]{1,0:T(8,128)(2,1)S(1)} %add_convert_fusion), channel_id=1, source_target_pairs={{0,2},{1,3},{2,4},{3,5},{4,6},{5,7},{6,0},{7,1},{8,10},{9,11},{10,... | collective-permute-start | bytes 86024 | tf_op jit(solution)/shard_map/cond/branch_1_fun/ppermute | solution.py:363
  185.6 5.0 %collective-permute-start.22 = (bf16[112,128]{1,0:T(8,128)(2,1)S(1)}, bf16[112,128]{1,0:T(8,128)(2,1)S(1)}, u32[]{:S(2)}, u32[]{:S(2)}) collective-permute-start(bf16[112,128]{1,0:T(8,128)(2,1)S(1)} %add_convert_fusion), channel_id=1, source_target_pairs={{0,4},{1,5},{2,6},{3,7},{4,0},{5,1},{6,2},{7,3},{8,12},{9,13},{10,... | collective-permute-start | bytes 86024 | tf_op jit(solution)/shard_map/cond/branch_1_fun/ppermute | solution.py:363
  188.9 2.7 %collective-permute-start.23 = (bf16[112,128]{1,0:T(8,128)(2,1)S(1)}, bf16[112,128]{1,0:T(8,128)(2,1)S(1)}, u32[]{:S(2)}, u32[]{:S(2)}) collective-permute-start(bf16[112,128]{1,0:T(8,128)(2,1)S(1)} %add_convert_fusion), channel_id=1, source_target_pairs={{0,6},{1,7},{2,0},{3,1},{4,2},{5,3},{6,4},{7,5},{8,14},{9,15},{10,... | collective-permute-start | bytes 86024 | tf_op jit(solution)/shard_map/cond/branch_1_fun/ppermute | solution.py:363
  189.6 4.2 %collective-permute-start.15 = (f32[128,128]{1,0:T(8,128)S(1)}, f32[128,128]{1,0:T(8,128)S(1)}, u32[]{:S(2)}, u32[]{:S(2)}) collective-permute-start(f32[128,128]{1,0:T(8,128)S(1)} %add.132), channel_id=1, source_target_pairs={{0,2},{1,3},{2,0},{3,1},{4,6},{5,7},{6,4},{7,5},{8,10},{9,11},{10,... | collective-permute-start | bytes 196616 | tf_op jit(solution)/shard_map/cond/branch_1_fun/ppermute | solution.py:376
  191.6 6.6 %collective-permute-start.24 = (bf16[4,112,128]{2,1,0:T(8,128)(2,1)S(1)}, bf16[4,112,128]{2,1,0:T(8,128)(2,1)S(1)}, u32[]{:S(2)}, u32[]{:S(2)}) collective-permute-start(bf16[4,112,128]{2,1,0:T(8,128)(2,1)S(1)} %pad_maximum_fusion.own), channel_id=1, source_target_pairs={{0,1},{1,0},{2,3},{3,2},{4,5},{5,4},{6,7},{7,6},{8,9},{9,8},{10,11... | collective-permute-start | bytes 344072 | tf_op jit(solution)/shard_map/cond/branch_1_fun/ppermute | solution.py:364
  193.7 4.4 %collective-permute-start.16 = (f32[128,128]{1,0:T(8,128)S(1)}, f32[128,128]{1,0:T(8,128)S(1)}, u32[]{:S(2)}, u32[]{:S(2)}) collective-permute-start(f32[128,128]{1,0:T(8,128)S(1)} %add.133), channel_id=1, source_target_pairs={{0,6},{1,7},{2,4},{3,5},{4,2},{5,3},{6,0},{7,1},{8,14},{9,15},{10,... | collective-permute-start | bytes 196616 | tf_op jit(solution)/shard_map/cond/branch_1_fun/ppermute | solution.py:376
  (29 other events, 48.6 us)
Sparse Core Ops, SparseCore 0:
  63.7 53.5 reduce-scatter.4

commit v6 on v5

--- a/solution.py
+++ b/solution.py
@@ -259,24 +259,13 @@
                     move(out[2 + u], second.at[u])
 
 
-def pass_kernel(offsets, *refs):
-    for h in range(2):
-        at = offsets[1 - h]
-        for source, when in ((refs[2 + h], at != 1), (refs[h], at == 1)):
-
-            @pl.when(when)
-            def _(source=source, out=refs[4 + h]):
-                move(out, source)
-
-
 def pick_kernel(offsets, *refs):
     for h in range(2):
         at = offsets[1 - h]
-        own, back, ahead = refs[3 * h : 3 * h + 3]
-        for source, when in ((own, at == 0), (back, at == 3), (ahead, (at == 1) | (at == 2))):
-
-            @pl.when(when)
-            def _(source=source, out=refs[6 + h]):
+        for offset, source in enumerate(refs[4 * h : 4 * h + 4]):
+
+            @pl.when(at == offset)
+            def _(source=source, out=refs[8 + h]):
                 move(out, source)
 
 
@@ -558,15 +547,26 @@
         late = [(tree, ((near, 0), (near, 1))) for tree in trees for near in (1, 3)]
         late += [(tree, ((0, 0), (0, 1), (0, 2), (0, 3))) for tree in trees]
         moves = ((1, 0), (-1, 0), (0, 1), (0, -1))
-        turned = ((0, 1), (0, -1), (1, 0), (-1, 0))
+        turned = ((0, 1), (0, 2), (0, -1), (1, 0), (2, 0), (-1, 0))
         send = lambda values, ways: [shift(v, *way) for v, way in zip(values, ways)]
         barrier = lax.optimization_barrier
-        scalars = (me_row, served, mine)
+        (main_sent,) = gather_call(
+            main_kernel, (dp_count,), dp_count, (served,), down_weights, up_weights
+        )
+        main = lax.all_to_all(main_sent, "dp", 0, 0, tiled=True)
+        unit = main_sent.shape[1:]
+        dtype = main_sent.dtype
+        soon_served, _ = barrier((served, main_sent))
         gathered = gather_call(
-            functools.partial(extra_kernel, soon), (4,) * 4, 16, scalars, down_weights, up_weights
+            functools.partial(extra_kernel, soon),
+            (4,) * 4,
+            16,
+            (me_row, soon_served, mine),
+            down_weights,
+            up_weights,
         )
         fresh = send(gathered, moves)
-        later_served, _ = barrier((served, gathered))
+        later_served, _ = barrier((soon_served, gathered))
         later = gather_call(
             functools.partial(extra_kernel, late),
             (2,) * 4 + (4,) * 2,
@@ -575,56 +575,38 @@
             down_weights,
             up_weights,
         )
-        main_served, _ = barrier((served, later))
-        (main_sent,) = gather_call(
-            main_kernel, (dp_count,), dp_count, (main_served,), down_weights, up_weights
-        )
-        fresh, near, main_sent = barrier((fresh, later[:4], main_sent))
-        unit = main_sent.shape[1:]
-        two = (2,) + unit
+        base_hidden, _ = barrier((hidden, later))
+        base_terms = jnp.dot(base_hidden, value_weight, preferred_element_type=jnp.float32)
+        base = lax.psum_scatter(base_terms, "tp", scatter_dimension=1, tiled=True)
+        main, _ = barrier((main, base_terms))
+        pairs = (groups - EXTRA) // 2
+        partial = low_partial(
+            functools.partial(low_main_kernel, cap), pairs, cap, rank, mine, hidden, (main,)
+        )
+        own, other = low_rank_rounds(partial)
+        t = lax.axis_index("tp")
+        where = jnp.stack([t // 2, t % 2]).astype(jnp.int32)
+        out = combine_main(where, mine, counts, base, own, other, main, rank)
+        fresh, near, _ = barrier((fresh, later[:4], partial))
         relayed = vmem_call(
-            relay_kernel, (two,) * 4, main_sent.dtype, (offsets,), (*fresh, *near)
-        )
-        near_a = send(relayed, moves)
-        base_hidden, _ = barrier((hidden, relayed))
-        base_terms = jnp.dot(base_hidden, value_weight, preferred_element_type=jnp.float32)
-        base_terms, main_sent = barrier((base_terms, main_sent))
-        main = lax.all_to_all(main_sent, "dp", 0, 0, tiled=True)
-        base = lax.psum_scatter(base_terms, "tp", scatter_dimension=1, tiled=True)
-        near_a, base_terms = barrier((near_a, base_terms))
+            relay_kernel, ((2,) + unit,) * 4, dtype, (offsets,), (*fresh, *near)
+        )
+        near_a = barrier(send(relayed, moves))
         tree_arrays = [
             (later[4 + h], near_a[2 * h], near_a[2 * h + 1], fresh[2 * h], fresh[2 * h + 1])
             for h in range(2)
         ]
         lines = vmem_call(
-            line_kernel,
-            (unit,) * 8,
-            main_sent.dtype,
-            (offsets,),
-            tree_arrays[0] + tree_arrays[1],
-        )
-        x0, x1, x2, x3, y0, y1, y2, y3 = lines
-        x_ahead, x_back, y_ahead, y_back = barrier(send((x2, x3, y2, y3), turned))
-        passed = vmem_call(
-            pass_kernel,
-            (unit,) * 2,
-            main_sent.dtype,
-            (offsets,),
-            (x_ahead, y_ahead, x1, y1),
-        )
-        passed, main = barrier((passed, main))
-        x_next, y_next = send(passed, (turned[0], turned[2]))
-        pairs = (groups - EXTRA) // 2
-        partial = low_partial(
-            functools.partial(low_main_kernel, cap), pairs, cap, rank, mine, hidden, (main,)
-        )
-        own, other = low_rank_rounds(partial)
+            line_kernel, (unit,) * 8, dtype, (offsets,), tree_arrays[0] + tree_arrays[1]
+        )
+        got = send(lines[1:4] + lines[5:8], turned)
+        got, out = barrier((got, out))
         extras = vmem_call(
             pick_kernel,
             (unit,) * 2,
-            main_sent.dtype,
+            dtype,
             (offsets,),
-            (x0, x_back, x_next, y0, y_back, y_next),
+            (lines[0], *got[:3], lines[4], *got[3:]),
         )
         extra_partial = low_partial(
             functools.partial(low_extra_kernel, groups - EXTRA, cap),
@@ -636,9 +618,6 @@
             extras,
         )
         extra_low = low_rank_doubling(extra_partial)
-        t = lax.axis_index("tp")
-        where = jnp.stack([t // 2, t % 2]).astype(jnp.int32)
-        out = combine_main(where, mine, counts, base, own, other, main, rank)
         return combine_extra(mine, counts, base, extra_low, extras, out, rank)
 
     return lax.cond(

time: 214 us -> 243 us (1.14)
  waiting for transfers between devices: 79.7 us -> 105 us
  starting transfers between devices: 46.2 us -> 58.8 us
  local copies, waits for them, and re-layouts: 27.7 us -> 22.4 us
  Pallas kernels: 33.1 us -> 28.3 us
    all_to_all x1, waiting for transfers between devices: 0.01 us -> 63.2 us  [narrow(): main = lax.all_to_all(main_sent, 'dp', 0, 0, tiled=True)]
    ppermute x14, waiting for transfers between devices: 75.9 us -> 30.3 us  [shift(): return lax.ppermute(value, 'dp', pairs)]
    all_to_all x1, starting transfers between devices: 4.81 us -> 20.5 us  [narrow(): main = lax.all_to_all(main_sent, 'dp', 0, 0, tiled=True)]
    cond x68 -> x60, local copies, waits for them, and re-layouts: 24.9 us -> 18.3 us
    ppermute x3, waiting for transfers between devices: 2.65 us -> 7.85 us  [low_rank_doubling(): lax.ppermute(partial, 'tp', [(i, partner(i)) for i in range(tp_count)])]
    pallas_call x3, Pallas kernels: 12.6 us -> 8.01 us  [gather_call(): pl.pallas_call(kernel, out_shape=[jax.ShapeDtypeStruct((n, 2 * rank + 16,...]
    pallas_call x4 -> x3, Pallas kernels: 5.79 us -> 7.02 us  [vmem_call(): pl.pallas_call(kernel, out_shape=[jax.ShapeDtypeStruct(shape, dtype) for...]
  transfers between devices with their start and end apart: 27 -> 27, of which waited for: 12 -> 13; matrix products, arithmetic and copies ran while one was open for 0% -> 2% of each run, Pallas kernels for 10% -> 6%
where the time goes in v6:
time: 243 us; the launch traced here: 241 us
  waiting for transfers between devices  105 us (43%)
  starting transfers between devices  58.8 us (24%)
  Pallas kernels  28.3 us (12%)
  local copies, waits for them, and re-layouts  22.4 us (9%)
  between operations  14.1 us (6%)
  matrix products  6.67 us (3%)
  loops' own time  3.42 us (1%)
    all_to_all x1, waiting for transfers between devices, narrow(): main = lax.all_to_all(main_sent, 'dp', 0, 0, tiled=True)  63.2 us
    ppermute x14, waiting for transfers between devices, shift(): return lax.ppermute(value, 'dp', pairs)  30.3 us
    all_to_all x1, starting transfers between devices, narrow(): main = lax.all_to_all(main_sent, 'dp', 0, 0, tiled=True)  20.5 us
    ppermute x14, starting transfers between devices, shift(): return lax.ppermute(value, 'dp', pairs)  19.4 us
    cond x60, local copies, waits for them, and re-layouts  18.3 us
    pallas_call x3, Pallas kernels, gather_call(): pl.pallas_call(kernel, out_shape=[jax.ShapeDtypeStruct((n, 2 * rank + 16,...  8.01 us
    ppermute x3, waiting for transfers between devices, low_rank_doubling(): lax.ppermute(partial, 'tp', [(i, partner(i)) for i in range(tp_count)])  7.85 us
    ppermute x3, starting transfers between devices, low_rank_rounds(): lax.ppermute(cut(total, (z + d) % chips * piece, piece), 'tp', turn(d))  7.55 us
  transfers between devices with their start and end apart: 27, of which 13 were waited for; matrix products, arithmetic and copies ran while one was open for 2% of the time, Pallas kernels for 6%

profile of v6, /device:TPU:1, one launch (start us, length us, event | category | flops | bytes accessed | tf_op | source)
XLA Modules:
  0.0 240.8 jit_solution(9649402337286701519)
XLA Ops:
  8.1 1.8 shard_map.75
  11.2 222.8 %conditional.1 = (bf16[2048,128]{1,0:T(8,128)(2,1)}) conditional(s32[]{:T(128)} %bitcast.20, (s32[32]{0:T(128)S(1)}, bf16[2048,1024]{1,0:T(8,128)(2,1)}, bf16[1024,1024]{1,0:T(8,128)(2,1)}, s32[512]{0:T(512)}, s32[2048]{0:T(1024)}, /*index=5*/s32[]{:T(128)}, bf16[128,64,1024]{2,1,0:T(8,128)(2,1)}, bf16[128,64,128]{2,1,0:T(8,128)(2,1)}) %tuple.18, ...), branch_computations={%region_0.5_spmd, %region_5.7_spmd} | conditional | flops 4601487360 | bytes 345046432 | solution.py:623
  11.5 3.9 %branch_1_fun.10 = bf16[16,144,1024]{2,1,0:T(8,128)(2,1)S(1)} custom-call(s32[16,128]{1,0:T(8,128)S(1)} %get-tuple-element.62.served, bf16[128,64,1024]{2,1,0:T(8,128)(2,1)} %get-tuple-element.55.down, bf16[128,64,128]{2,1,0:T(8,128)(2,1)} %get-tuple-element.56.up), custom_call_target="tpu_custom_call" | custom-call | bytes 9437184 | tf_op jit(solution)/shard_map/cond/branch_1_fun/pallas_call | solution.py:188
  15.4 2.4 copy-done
  17.8 2.6 %copy-done.23 = bf16[128,64,1024]{2,1,0:T(8,128)(2,1)S(1)} copy-done((bf16[128,64,1024]{2,1,0:T(8,128)(2,1)S(1)}, bf16[128,64,1024]{2,1,0:T(8,128)(2,1)}, u32[]{:S(2)}) %copy-start.23) | copy-done | bytes 16777240 | tf_op jit(solution)/shard_map/cond
  21.0 2.8 %branch_1_fun.11 = (bf16[4,144,1024]{2,1,0:T(8,128)(2,1)}, bf16[4,144,1024]{2,1,0:T(8,128)(2,1)}, bf16[4,144,1024]{2,1,0:T(8,128)(2,1)S(1)}, bf16[4,144,1024]{2,1,0:T(8,128)(2,1)S(1)}) custom-call(s32[1]{0:T(128)} %get-tuple-element.53.me, s32[16,128]{1,0:T(8,128)S(1)} %get-tuple-element.62.served, s32[8,128]{1,0:T(8,128)S(1)} %get-tuple-element.50.mine, ...), custom_call_target="tpu_custom_call" | custom-call | bytes 9437184 | tf_op jit(solution)/shard_map/cond/branch_1_fun/pallas_call | solution.py:188
  32.6 6.7 %fusion.8 = f32[2048,1024]{1,0:T(8,128)} fusion(bf16[2048,1024]{1,0:T(8,128)(2,1)S(1)} %copy-done.24, bf16[1024,1024]{1,0:T(8,128)(2,1)S(1)} %copy-done.32), kind=kOutput, calls=%fused_computation.42 | convolution fusion | flops 4294967296 | bytes 14680064 | tf_op jit(solution)/shard_map/cond/branch_1_fun/dot_general | solution.py:579
  39.3 20.5 %all-to-all-start.3 = ((bf16[16,144,1024]{2,1,0:T(8,128)(2,1)}), bf16[16,144,1024]{2,1,0:T(8,128)(2,1)}, u32[]{:S(2)}, u32[]{:S(2)}) async-start(bf16[16,144,1024]{2,1,0:T(8,128)(2,1)} %copy-done), calls=%async_computation.5 | async-start | bytes 9437184 | tf_op jit(solution)/shard_map/cond/branch_1_fun/all_to_all | solution.py:556
  63.8 1.4 collective-permute-start.3
  68.5 63.2 %all-to-all-done.3.main = bf16[16,144,1024]{2,1,0:T(8,128)(2,1)} async-done(((bf16[16,144,1024]{2,1,0:T(8,128)(2,1)}), bf16[16,144,1024]{2,1,0:T(8,128)(2,1)}, u32[]{:S(2)}, u32[]{:S(2)}) %all-to-all-start.3) | async-done | bytes 4718624 | tf_op jit(solution)/shard_map/cond/branch_1_fun/all_to_all | solution.py:556
  131.8 5.9 %branch_1_fun.13 = f32[896,128]{1,0:T(8,128)S(1)} custom-call(s32[8,128]{1,0:T(8,128)S(1)} %get-tuple-element.50.mine, bf16[2048,1024]{1,0:T(8,128)(2,1)} %get-tuple-element.69.hidden, bf16[16,144,1024]{2,1,0:T(8,128)(2,1)} %all-to-all-done.3.main), custom_call_target="tpu_custom_call" | custom-call | flops 234881024 | bytes 4718592 | tf_op jit(solution)/shard_map/cond/branch_1_fun/pallas_call | solution.py:320
  137.7 19.3 %collective-permute-done.refs_0_.refs_3_ = bf16[4,144,1024]{2,1,0:T(8,128)(2,1)S(1)} collective-permute-done((bf16[4,144,1024]{2,1,0:T(8,128)(2,1)}, bf16[4,144,1024]{2,1,0:T(8,128)(2,1)S(1)}, u32[]{:S(2)}, u32[]{:S(2)}) %collective-permute-start) | collective-permute-done | bytes 1179680 | tf_op jit(solution)/shard_map/cond/branch_1_fun/ppermute | solution.py:52
  157.1 3.0 %branch_1_fun.14 = (bf16[2,144,1024]{2,1,0:T(8,128)(2,1)}, bf16[2,144,1024]{2,1,0:T(8,128)(2,1)}, bf16[2,144,1024]{2,1,0:T(8,128)(2,1)}, bf16[2,144,1024]{2,1,0:T(8,128)(2,1)}) custom-call(s32[2]{0:T(128)S(1)} %pad_add_fusion.offsets, bf16[4,144,1024]{2,1,0:T(8,128)(2,1)S(1)} %collective-permute-done.refs_0_.refs_3_, ...), custom_call_target="tpu_custom_call" | custom-call | bytes 4718592 | tf_op jit(solution)/shard_map/cond/branch_1_fun/pallas_call | solution.py:206
  160.1 2.1 collective-permute-start.4
  163.5 2.1 collective-permute-start.14
  165.6 2.0 collective-permute-start.6
  170.7 3.8 %collective-permute-start.16 = (f32[112,128]{1,0:T(8,128)}, f32[112,128]{1,0:T(8,128)}, u32[]{:S(2)}, u32[]{:S(2)}) collective-permute-start(f32[112,128]{1,0:T(8,128)} %get-tuple-element.113), channel_id=1, source_target_pairs={{0,4},{1,5},{2,6},{3,7},{4,0},{5,1},{6,2},{7,3},{8,12},{9,13},{10,... | collective-permute-start | bytes 172040 | tf_op jit(solution)/shard_map/cond/branch_1_fun/ppermute | solution.py:348
  174.9 3.8 %collective-permute-start.17 = (f32[112,128]{1,0:T(8,128)}, f32[112,128]{1,0:T(8,128)}, u32[]{:S(2)}, u32[]{:S(2)}) collective-permute-start(f32[112,128]{1,0:T(8,128)} %get-tuple-element.114), channel_id=1, source_target_pairs={{0,6},{1,7},{2,0},{3,1},{4,2},{5,3},{6,4},{7,5},{8,14},{9,15},{10,... | collective-permute-start | bytes 172040 | tf_op jit(solution)/shard_map/cond/branch_1_fun/ppermute | solution.py:348
  178.7 3.4 %collective-permute-done.6.refs_6_ = bf16[2,144,1024]{2,1,0:T(8,128)(2,1)} collective-permute-done((bf16[2,144,1024]{2,1,0:T(8,128)(2,1)}, bf16[2,144,1024]{2,1,0:T(8,128)(2,1)}, u32[]{:S(2)}, u32[]{:S(2)}) %collective-permute-start.6) | collective-permute-done | bytes 589856 | tf_op jit(solution)/shard_map/cond/branch_1_fun/ppermute | solution.py:52
  185.1 3.4 %branch_1_fun.15 = (bf16[144,1024]{1,0:T(8,128)(2,1)S(1)}, bf16[144,1024]{1,0:T(8,128)(2,1)S(1)}, bf16[144,1024]{1,0:T(8,128)(2,1)}, bf16[144,1024]{1,0:T(8,128)...) custom-call(s32[2]{0:T(128)S(1)} %pad_add_fusion.offsets, ...), custom_call_target="tpu_custom_call" | custom-call | bytes 4718592 | tf_op jit(solution)/shard_map/cond/branch_1_fun/pallas_call | solution.py:206
  190.4 3.8 %collective-permute-start.20 = (bf16[112,128]{1,0:T(8,128)(2,1)S(1)}, bf16[112,128]{1,0:T(8,128)(2,1)S(1)}, u32[]{:S(2)}, u32[]{:S(2)}) collective-permute-start(bf16[112,128]{1,0:T(8,128)(2,1)S(1)} %add_convert_fusion), channel_id=1, source_target_pairs={{0,6},{1,7},{2,0},{3,1},{4,2},{5,3},{6,4},{7,5},{8,14},{9,15},{10,... | collective-permute-start | bytes 86024 | tf_op jit(solution)/shard_map/cond/branch_1_fun/ppermute | solution.py:352
  195.2 3.3 %collective-permute-done.19 = bf16[112,128]{1,0:T(8,128)(2,1)S(1)} collective-permute-done((bf16[112,128]{1,0:T(8,128)(2,1)S(1)}, bf16[112,128]{1,0:T(8,128)(2,1)S(1)}, u32[]{:S(2)}, u32[]{:S(2)}) %collective-permute-start.19) | collective-permute-done | bytes 28704 | tf_op jit(solution)/shard_map/cond/branch_1_fun/ppermute | solution.py:352
  198.5 2.6 %collective-permute-start.21 = (bf16[4,112,128]{2,1,0:T(8,128)(2,1)S(1)}, bf16[4,112,128]{2,1,0:T(8,128)(2,1)S(1)}, u32[]{:S(2)}, u32[]{:S(2)}) collective-permute-start(bf16[4,112,128]{2,1,0:T(8,128)(2,1)S(1)} %pad_maximum_fusion.own), channel_id=1, source_target_pairs={{0,1},{1,0},{2,3},{3,2},{4,5},{5,4},{6,7},{7,6},{8,9},{9,8},{10,11... | collective-permute-start | bytes 344072 | tf_op jit(solution)/shard_map/cond/branch_1_fun/ppermute | solution.py:353
  201.1 3.2 %collective-permute-start.9 = (bf16[144,1024]{1,0:T(8,128)(2,1)}, bf16[144,1024]{1,0:T(8,128)(2,1)S(1)}, u32[]{:S(2)}, u32[]{:S(2)}) collective-permute-start(bf16[144,1024]{1,0:T(8,128)(2,1)} %get-tuple-element.91), channel_id=1, source_target_pairs={{0,16},{8,24},{16,0},{24,8},{32,48},{40,56},{48,32},{56,40},{64,80... | collective-permute-start | bytes 884744 | tf_op jit(solution)/shard_map/cond/branch_1_fun/ppermute | solution.py:52
  205.3 2.1 collective-permute-start.12
  207.4 2.0 collective-permute-start.13
  210.7 3.3 %branch_1_fun.16._ = bf16[2048,128]{1,0:T(8,128)(2,1)} custom-call(s32[2]{0:T(128)S(1)} %pad_add_fusion.1.where, s32[8,128]{1,0:T(8,128)S(1)} %get-tuple-element.50.mine, s32[32]{0:T(128)S(1)} %copy-done.31, f32[2048,128]{1,0:T(8,128)S(1)} %copy-done.1, bf16[4,112,128]{2,1,0:T(8,128)(2,1)S(1)} %pad_maximum_fusion.own, ...), custom_call_target="tpu_custom_call" | custom-call | flops 33554432 | bytes 2097152 | tf_op jit(solution)/shard_map/cond/branch_1_fun/pallas_call | solution.py:455
  214.0 4.0 %collective-permute-done.10.refs_3_ = bf16[144,1024]{1,0:T(8,128)(2,1)S(1)} collective-permute-done((bf16[144,1024]{1,0:T(8,128)(2,1)}, bf16[144,1024]{1,0:T(8,128)(2,1)S(1)}, u32[]{:S(2)}, u32[]{:S(2)}) %collective-permute-start.10) | collective-permute-done | bytes 294944 | tf_op jit(solution)/shard_map/cond/branch_1_fun/ppermute | solution.py:52
  218.0 2.6 %collective-permute-done.12.refs_6_ = bf16[144,1024]{1,0:T(8,128)(2,1)S(1)} collective-permute-done((bf16[144,1024]{1,0:T(8,128)(2,1)}, bf16[144,1024]{1,0:T(8,128)(2,1)S(1)}, u32[]{:S(2)}, u32[]{:S(2)}) %collective-permute-start.12) | collective-permute-done | bytes 294944 | tf_op jit(solution)/shard_map/cond/branch_1_fun/ppermute | solution.py:52
  222.2 1.5 collective-permute-start.22
  224.8 3.1 %collective-permute-done.23 = f32[128,128]{1,0:T(8,128)S(1)} collective-permute-done((f32[128,128]{1,0:T(8,128)S(1)}, f32[128,128]{1,0:T(8,128)S(1)}, u32[]{:S(2)}, u32[]{:S(2)}) %collective-permute-start.23) | collective-permute-done | bytes 65568 | tf_op jit(solution)/shard_map/cond/branch_1_fun/ppermute | solution.py:365
  228.4 3.8 %collective-permute-done.24 = f32[128,128]{1,0:T(8,128)S(1)} collective-permute-done((f32[128,128]{1,0:T(8,128)S(1)}, f32[128,128]{1,0:T(8,128)S(1)}, u32[]{:S(2)}, u32[]{:S(2)}) %collective-permute-start.24) | collective-permute-done | bytes 65568 | tf_op jit(solution)/shard_map/cond/branch_1_fun/ppermute | solution.py:365
  (110 shorter events, 33.9 us)
Async XLA Ops:
  11.4 198.1 %reduce-scatter.5.cloned.1.call-start = ((), (), s32[]{:S(2)}) async-start(), calls=%async_computation.7 | async-start | bytes 9437184 | tf_op jit(solution)/shard_map/cond/branch_1_fun/reduce_scatter | solution.py:580
  39.3 92.4 %all-to-all-start.3 = ((bf16[16,144,1024]{2,1,0:T(8,128)(2,1)}), bf16[16,144,1024]{2,1,0:T(8,128)(2,1)}, u32[]{:S(2)}, u32[]{:S(2)}) async-start(bf16[16,144,1024]{2,1,0:T(8,128)(2,1)} %copy-done), calls=%async_computation.5 | async-start | bytes 9437184 | tf_op jit(solution)/shard_map/cond/branch_1_fun/all_to_all | solution.py:556
  59.8 97.2 %collective-permute-start = (bf16[4,144,1024]{2,1,0:T(8,128)(2,1)}, bf16[4,144,1024]{2,1,0:T(8,128)(2,1)S(1)}, u32[]{:S(2)}, u32[]{:S(2)}) collective-permute-start(bf16[4,144,1024]{2,1,0:T(8,128)(2,1)} %get-tuple-element.58), channel_id=1, source_target_pairs={{0,32},{8,40},{16,48},{24,56},{32,64},{40,72},{48,80},{56,88},{64,... | collective-permute-start | bytes 3538952 | tf_op jit(solution)/shard_map/cond/branch_1_fun/ppermute | solution.py:52
  61.1 95.9 %collective-permute-start.1 = (bf16[4,144,1024]{2,1,0:T(8,128)(2,1)}, bf16[4,144,1024]{2,1,0:T(8,128)(2,1)S(1)}, u32[]{:S(2)}, u32[]{:S(2)}) collective-permute-start(bf16[4,144,1024]{2,1,0:T(8,128)(2,1)} %get-tuple-element.59), channel_id=1, source_target_pairs={{0,96},{8,104},{16,112},{24,120},{32,0},{40,8},{48,16},{56,24},{64... | collective-permute-start | bytes 3538952 | tf_op jit(solution)/shard_map/cond/branch_1_fun/ppermute | solution.py:52
  62.6 94.5 %collective-permute-start.2 = (bf16[4,144,1024]{2,1,0:T(8,128)(2,1)}, bf16[4,144,1024]{2,1,0:T(8,128)(2,1)S(1)}, u32[]{:S(2)}, u32[]{:S(2)}) collective-permute-start(bf16[4,144,1024]{2,1,0:T(8,128)(2,1)} %copy-done.21), channel_id=1, source_target_pairs={{0,8},{8,16},{16,24},{24,0},{32,40},{40,48},{48,56},{56,32},{64,72... | collective-permute-start | bytes 3538952 | tf_op jit(solution)/shard_map/cond/branch_1_fun/ppermute | solution.py:52
  63.8 93.2 %collective-permute-start.3 = (bf16[4,144,1024]{2,1,0:T(8,128)(2,1)}, bf16[4,144,1024]{2,1,0:T(8,128)(2,1)}, u32[]{:S(2)}, u32[]{:S(2)}) collective-permute-start(bf16[4,144,1024]{2,1,0:T(8,128)(2,1)} %copy-done.20), channel_id=1, source_target_pairs={{0,24},{8,0},{16,8},{24,16},{32,56},{40,32},{48,40},{56,48},{64,88... | collective-permute-start | bytes 3538952 | tf_op jit(solution)/shard_map/cond/branch_1_fun/ppermute | solution.py:52
  131.7 25.3 %copy-start.11 = (bf16[2,144,1024]{2,1,0:T(8,128)(2,1)S(1)}, bf16[2,144,1024]{2,1,0:T(8,128)(2,1)}, u32[]{:S(2)}) copy-start(bf16[2,144,1024]{2,1,0:T(8,128)(2,1)} %copy-done.10) | copy-start | bytes 1769476 | tf_op jit(solution)/shard_map/cond
  131.8 25.3 %copy-start.13 = (bf16[2,144,1024]{2,1,0:T(8,128)(2,1)S(1)}, bf16[2,144,1024]{2,1,0:T(8,128)(2,1)}, u32[]{:S(2)}) copy-start(bf16[2,144,1024]{2,1,0:T(8,128)(2,1)} %copy-done.12) | copy-start | bytes 1769476 | tf_op jit(solution)/shard_map/cond
  131.8 25.3 %copy-start.15 = (bf16[2,144,1024]{2,1,0:T(8,128)(2,1)S(1)}, bf16[2,144,1024]{2,1,0:T(8,128)(2,1)}, u32[]{:S(2)}) copy-start(bf16[2,144,1024]{2,1,0:T(8,128)(2,1)} %copy-done.14) | copy-start | bytes 1769476 | tf_op jit(solution)/shard_map/cond
  160.1 14.8 %collective-permute-start.4 = (bf16[2,144,1024]{2,1,0:T(8,128)(2,1)}, bf16[2,144,1024]{2,1,0:T(8,128)(2,1)}, u32[]{:S(2)}, u32[]{:S(2)}) collective-permute-start(bf16[2,144,1024]{2,1,0:T(8,128)(2,1)} %get-tuple-element.81), channel_id=1, source_target_pairs={{0,32},{8,40},{16,48},{24,56},{32,64},{40,72},{48,80},{56,88},{64,... | collective-permute-start | bytes 1769480 | tf_op jit(solution)/shard_map/cond/branch_1_fun/ppermute | solution.py:52
  162.2 16.5 %collective-permute-start.5 = (bf16[2,144,1024]{2,1,0:T(8,128)(2,1)}, bf16[2,144,1024]{2,1,0:T(8,128)(2,1)}, u32[]{:S(2)}, u32[]{:S(2)}) collective-permute-start(bf16[2,144,1024]{2,1,0:T(8,128)(2,1)} %get-tuple-element.82), channel_id=1, source_target_pairs={{0,96},{8,104},{16,112},{24,120},{32,0},{40,8},{48,16},{56,24},{64... | collective-permute-start | bytes 1769480 | tf_op jit(solution)/shard_map/cond/branch_1_fun/ppermute | solution.py:52
  163.5 4.8 %collective-permute-start.14 = (f32[448,128]{1,0:T(8,128)}, f32[448,128]{1,0:T(8,128)}, u32[]{:S(2)}, u32[]{:S(2)}) collective-permute-start(f32[448,128]{1,0:T(8,128)} %constant_dynamic-slice_fusion.3), channel_id=1, source_target_pairs={{0,1},{1,0},{2,3},{3,2},{4,5},{5,4},{6,7},{7,6},{8,9},{9,8},{10,11... | collective-permute-start | bytes 688136 | tf_op jit(solution)/shard_map/cond/branch_1_fun/ppermute | solution.py:344
  165.6 16.5 %collective-permute-start.6 = (bf16[2,144,1024]{2,1,0:T(8,128)(2,1)}, bf16[2,144,1024]{2,1,0:T(8,128)(2,1)}, u32[]{:S(2)}, u32[]{:S(2)}) collective-permute-start(bf16[2,144,1024]{2,1,0:T(8,128)(2,1)} %get-tuple-element.83), channel_id=1, source_target_pairs={{0,8},{8,16},{16,24},{24,0},{32,40},{40,48},{48,56},{56,32},{64,72... | collective-permute-start | bytes 1769480 | tf_op jit(solution)/shard_map/cond/branch_1_fun/ppermute | solution.py:52
  167.6 15.0 %collective-permute-start.7 = (bf16[2,144,1024]{2,1,0:T(8,128)(2,1)}, bf16[2,144,1024]{2,1,0:T(8,128)(2,1)}, u32[]{:S(2)}, u32[]{:S(2)}) collective-permute-start(bf16[2,144,1024]{2,1,0:T(8,128)(2,1)} %get-tuple-element.84), channel_id=1, source_target_pairs={{0,24},{8,0},{16,8},{24,16},{32,56},{40,32},{48,40},{56,48},{64,88... | collective-permute-start | bytes 1769480 | tf_op jit(solution)/shard_map/cond/branch_1_fun/ppermute | solution.py:52
  170.7 18.8 %collective-permute-start.16 = (f32[112,128]{1,0:T(8,128)}, f32[112,128]{1,0:T(8,128)}, u32[]{:S(2)}, u32[]{:S(2)}) collective-permute-start(f32[112,128]{1,0:T(8,128)} %get-tuple-element.113), channel_id=1, source_target_pairs={{0,4},{1,5},{2,6},{3,7},{4,0},{5,1},{6,2},{7,3},{8,12},{9,13},{10,... | collective-permute-start | bytes 172040 | tf_op jit(solution)/shard_map/cond/branch_1_fun/ppermute | solution.py:348
  174.9 14.6 %collective-permute-start.17 = (f32[112,128]{1,0:T(8,128)}, f32[112,128]{1,0:T(8,128)}, u32[]{:S(2)}, u32[]{:S(2)}) collective-permute-start(f32[112,128]{1,0:T(8,128)} %get-tuple-element.114), channel_id=1, source_target_pairs={{0,6},{1,7},{2,0},{3,1},{4,2},{5,3},{6,4},{7,5},{8,14},{9,15},{10,... | collective-permute-start | bytes 172040 | tf_op jit(solution)/shard_map/cond/branch_1_fun/ppermute | solution.py:348
  178.6 10.9 %collective-permute-start.15 = (f32[112,128]{1,0:T(8,128)}, f32[112,128]{1,0:T(8,128)}, u32[]{:S(2)}, u32[]{:S(2)}) collective-permute-start(f32[112,128]{1,0:T(8,128)} %get-tuple-element.115), channel_id=1, source_target_pairs={{0,2},{1,3},{2,4},{3,5},{4,6},{5,7},{6,0},{7,1},{8,10},{9,11},{10,... | collective-permute-start | bytes 172040 | tf_op jit(solution)/shard_map/cond/branch_1_fun/ppermute | solution.py:348
  178.6 30.8 %copy-start.31 = (s32[32]{0:T(128)S(1)}, s32[32]{0:T(128)}, u32[]{:S(2)}) copy-start(s32[32]{0:T(128)} %copy-done.30) | copy-start | bytes 388 | tf_op jit(solution)/shard_map/cond
  189.2 31.5 %copy-start.19 = (bf16[144,1024]{1,0:T(8,128)(2,1)S(1)}, bf16[144,1024]{1,0:T(8,128)(2,1)}, u32[]{:S(2)}) copy-start(bf16[144,1024]{1,0:T(8,128)(2,1)} %copy-done.18) | copy-start | bytes 884740 | tf_op jit(solution)/shard_map/cond
  189.2 18.2 %collective-permute-start.8 = (bf16[144,1024]{1,0:T(8,128)(2,1)S(1)}, bf16[144,1024]{1,0:T(8,128)(2,1)S(1)}, u32[]{:S(2)}, u32[]{:S(2)}) collective-permute-start(bf16[144,1024]{1,0:T(8,128)(2,1)S(1)} %get-tuple-element.90), channel_id=1, source_target_pairs={{0,8},{8,16},{16,24},{24,0},{32,40},{40,48},{48,56},{56,32},{64,72... | collective-permute-start | bytes 884744 | tf_op jit(solution)/shard_map/cond/branch_1_fun/ppermute | solution.py:52
  190.4 4.8 %collective-permute-start.20 = (bf16[112,128]{1,0:T(8,128)(2,1)S(1)}, bf16[112,128]{1,0:T(8,128)(2,1)S(1)}, u32[]{:S(2)}, u32[]{:S(2)}) collective-permute-start(bf16[112,128]{1,0:T(8,128)(2,1)S(1)} %add_convert_fusion), channel_id=1, source_target_pairs={{0,6},{1,7},{2,0},{3,1},{4,2},{5,3},{6,4},{7,5},{8,14},{9,15},{10,... | collective-permute-start | bytes 86024 | tf_op jit(solution)/shard_map/cond/branch_1_fun/ppermute | solution.py:352
  194.2 4.2 %collective-permute-start.19 = (bf16[112,128]{1,0:T(8,128)(2,1)S(1)}, bf16[112,128]{1,0:T(8,128)(2,1)S(1)}, u32[]{:S(2)}, u32[]{:S(2)}) collective-permute-start(bf16[112,128]{1,0:T(8,128)(2,1)S(1)} %add_convert_fusion), channel_id=1, source_target_pairs={{0,4},{1,5},{2,6},{3,7},{4,0},{5,1},{6,2},{7,3},{8,12},{9,13},{10,... | collective-permute-start | bytes 86024 | tf_op jit(solution)/shard_map/cond/branch_1_fun/ppermute | solution.py:352
  194.2 4.2 %collective-permute-start.18 = (bf16[112,128]{1,0:T(8,128)(2,1)S(1)}, bf16[112,128]{1,0:T(8,128)(2,1)S(1)}, u32[]{:S(2)}, u32[]{:S(2)}) collective-permute-start(bf16[112,128]{1,0:T(8,128)(2,1)S(1)} %add_convert_fusion), channel_id=1, source_target_pairs={{0,2},{1,3},{2,4},{3,5},{4,6},{5,7},{6,0},{7,1},{8,10},{9,11},{10,... | collective-permute-start | bytes 86024 | tf_op jit(solution)/shard_map/cond/branch_1_fun/ppermute | solution.py:352
  198.5 6.8 %collective-permute-start.21 = (bf16[4,112,128]{2,1,0:T(8,128)(2,1)S(1)}, bf16[4,112,128]{2,1,0:T(8,128)(2,1)S(1)}, u32[]{:S(2)}, u32[]{:S(2)}) collective-permute-start(bf16[4,112,128]{2,1,0:T(8,128)(2,1)S(1)} %pad_maximum_fusion.own), channel_id=1, source_target_pairs={{0,1},{1,0},{2,3},{3,2},{4,5},{5,4},{6,7},{7,6},{8,9},{9,8},{10,11... | collective-permute-start | bytes 344072 | tf_op jit(solution)/shard_map/cond/branch_1_fun/ppermute | solution.py:353
  201.1 12.9 %collective-permute-start.9 = (bf16[144,1024]{1,0:T(8,128)(2,1)}, bf16[144,1024]{1,0:T(8,128)(2,1)S(1)}, u32[]{:S(2)}, u32[]{:S(2)}) collective-permute-start(bf16[144,1024]{1,0:T(8,128)(2,1)} %get-tuple-element.91), channel_id=1, source_target_pairs={{0,16},{8,24},{16,0},{24,8},{32,48},{40,56},{48,32},{56,40},{64,80... | collective-permute-start | bytes 884744 | tf_op jit(solution)/shard_map/cond/branch_1_fun/ppermute | solution.py:52
  204.3 13.7 %collective-permute-start.10 = (bf16[144,1024]{1,0:T(8,128)(2,1)}, bf16[144,1024]{1,0:T(8,128)(2,1)S(1)}, u32[]{:S(2)}, u32[]{:S(2)}) collective-permute-start(bf16[144,1024]{1,0:T(8,128)(2,1)} %get-tuple-element.92), channel_id=1, source_target_pairs={{0,24},{8,0},{16,8},{24,16},{32,56},{40,32},{48,40},{56,48},{64,88... | collective-permute-start | bytes 884744 | tf_op jit(solution)/shard_map/cond/branch_1_fun/ppermute | solution.py:52
  204.3 13.7 %collective-permute-start.11 = (bf16[144,1024]{1,0:T(8,128)(2,1)}, bf16[144,1024]{1,0:T(8,128)(2,1)S(1)}, u32[]{:S(2)}, u32[]{:S(2)}) collective-permute-start(bf16[144,1024]{1,0:T(8,128)(2,1)} %get-tuple-element.93), channel_id=1, source_target_pairs={{0,32},{8,40},{16,48},{24,56},{32,64},{40,72},{48,80},{56,88},{64,... | collective-permute-start | bytes 884744 | tf_op jit(solution)/shard_map/cond/branch_1_fun/ppermute | solution.py:52
  205.3 15.3 %collective-permute-start.12 = (bf16[144,1024]{1,0:T(8,128)(2,1)}, bf16[144,1024]{1,0:T(8,128)(2,1)S(1)}, u32[]{:S(2)}, u32[]{:S(2)}) collective-permute-start(bf16[144,1024]{1,0:T(8,128)(2,1)} %get-tuple-element.94), channel_id=1, source_target_pairs={{0,64},{8,72},{16,80},{24,88},{32,96},{40,104},{48,112},{56,120},{... | collective-permute-start | bytes 884744 | tf_op jit(solution)/shard_map/cond/branch_1_fun/ppermute | solution.py:52
  207.4 13.2 %collective-permute-start.13 = (bf16[144,1024]{1,0:T(8,128)(2,1)}, bf16[144,1024]{1,0:T(8,128)(2,1)S(1)}, u32[]{:S(2)}, u32[]{:S(2)}) collective-permute-start(bf16[144,1024]{1,0:T(8,128)(2,1)} %get-tuple-element.95), channel_id=1, source_target_pairs={{0,96},{8,104},{16,112},{24,120},{32,0},{40,8},{48,16},{56,24},{64... | collective-permute-start | bytes 884744 | tf_op jit(solution)/shard_map/cond/branch_1_fun/ppermute | solution.py:52
  222.2 2.4 %collective-permute-start.22 = (f32[128,128]{1,0:T(8,128)S(1)}, f32[128,128]{1,0:T(8,128)S(1)}, u32[]{:S(2)}, u32[]{:S(2)}) collective-permute-start(f32[128,128]{1,0:T(8,128)S(1)} %branch_1_fun.18), channel_id=1, source_target_pairs={{0,1},{1,0},{2,3},{3,2},{4,5},{5,4},{6,7},{7,6},{8,9},{9,8},{10,11... | collective-permute-start | bytes 196616 | tf_op jit(solution)/shard_map/cond/branch_1_fun/ppermute | solution.py:365
  224.7 3.2 %collective-permute-start.23 = (f32[128,128]{1,0:T(8,128)S(1)}, f32[128,128]{1,0:T(8,128)S(1)}, u32[]{:S(2)}, u32[]{:S(2)}) collective-permute-start(f32[128,128]{1,0:T(8,128)S(1)} %add.149), channel_id=1, source_target_pairs={{0,2},{1,3},{2,0},{3,1},{4,6},{5,7},{6,4},{7,5},{8,10},{9,11},{10,... | collective-permute-start | bytes 196616 | tf_op jit(solution)/shard_map/cond/branch_1_fun/ppermute | solution.py:365
  227.9 4.4 %collective-permute-start.24 = (f32[128,128]{1,0:T(8,128)S(1)}, f32[128,128]{1,0:T(8,128)S(1)}, u32[]{:S(2)}, u32[]{:S(2)}) collective-permute-start(f32[128,128]{1,0:T(8,128)S(1)} %add.150), channel_id=1, source_target_pairs={{0,6},{1,7},{2,4},{3,5},{4,2},{5,3},{6,0},{7,1},{8,14},{9,15},{10,... | collective-permute-start | bytes 196616 | tf_op jit(solution)/shard_map/cond/branch_1_fun/ppermute | solution.py:365
  (25 other events, 156.3 us)
Sparse Core Ops, SparseCore 0:
  39.4 67.9 reduce-scatter.4

commit v7 on v6

--- a/solution.py
+++ b/solution.py
@@ -182,7 +182,7 @@
         copy_units(wanted, down, up, *scratch)
 
 
-def gather_call(kernel, shapes, count, scalars, down, up):
+def gather_call(kernel, shapes, count, scalars, down, up, limit=8):
     _, rank, width = down.shape
     lanes = up.shape[2]
     return pl.pallas_call(
@@ -195,7 +195,7 @@
             pltpu.SemaphoreType.DMA((2 * count,)),
             pltpu.SemaphoreType.DMA((2 * count,)),
         ],
-        compiler_params=pltpu.CompilerParams(vmem_limit_bytes=8 << 20),
+        compiler_params=pltpu.CompilerParams(vmem_limit_bytes=limit << 20),
         cost_estimate=pl.CostEstimate(
             flops=0, bytes_accessed=count * rank * (width + lanes) * 8, transcendentals=0
         ),
@@ -556,17 +556,16 @@
         main = lax.all_to_all(main_sent, "dp", 0, 0, tiled=True)
         unit = main_sent.shape[1:]
         dtype = main_sent.dtype
-        soon_served, _ = barrier((served, main_sent))
         gathered = gather_call(
             functools.partial(extra_kernel, soon),
             (4,) * 4,
             16,
-            (me_row, soon_served, mine),
+            (me_row, served, mine),
             down_weights,
             up_weights,
-        )
-        fresh = send(gathered, moves)
-        later_served, _ = barrier((soon_served, gathered))
+            40,
+        )
+        later_served, _ = barrier((served, gathered))
         later = gather_call(
             functools.partial(extra_kernel, late),
             (2,) * 4 + (4,) * 2,
@@ -574,11 +573,12 @@
             (me_row, later_served, mine),
             down_weights,
             up_weights,
-        )
-        base_hidden, _ = barrier((hidden, later))
-        base_terms = jnp.dot(base_hidden, value_weight, preferred_element_type=jnp.float32)
+            40,
+        )
+        base_terms = jnp.dot(hidden, value_weight, preferred_element_type=jnp.float32)
+        main, gathered, later, base_terms = barrier((main, gathered, later, base_terms))
+        fresh = send(gathered, moves)
         base = lax.psum_scatter(base_terms, "tp", scatter_dimension=1, tiled=True)
-        main, _ = barrier((main, base_terms))
         pairs = (groups - EXTRA) // 2
         partial = low_partial(
             functools.partial(low_main_kernel, cap), pairs, cap, rank, mine, hidden, (main,)

time: 243 us -> 216 us (0.89)
  waiting for transfers between devices: 105 us -> 84.8 us
  starting transfers between devices: 58.8 us -> 49.5 us
  matrix products: 6.67 us -> 10.7 us
    all_to_all x1, waiting for transfers between devices: 63.2 us -> 46.8 us  [narrow(): main = lax.all_to_all(main_sent, 'dp', 0, 0, tiled=True)]
    all_to_all x1, starting transfers between devices: 20.5 us -> 7.76 us  [narrow(): main = lax.all_to_all(main_sent, 'dp', 0, 0, tiled=True)]
    dot_general x1, matrix products: 6.67 us -> 10.7 us  [narrow(): jnp.dot(hidden, value_weight, preferred_element_type=jnp.float32)]
    ppermute x3, starting transfers between devices: 2.18 us -> 5.33 us  [low_rank_doubling(): lax.ppermute(partial, 'tp', [(i, partner(i)) for i in range(tp_count)])]
    cond x60 -> x56, local copies, waits for them, and re-layouts: 18.3 us -> 17.5 us
  transfers between devices with their start and end apart: 27 -> 27, of which waited for: 13 -> 13; matrix products, arithmetic and copies ran while one was open for 2% -> 7% of each run, Pallas kernels for 6% -> 9%
where the time goes in v7:
time: 216 us; the launch traced here: 214 us
  waiting for transfers between devices  84.8 us (39%)
  starting transfers between devices  49.5 us (23%)
  Pallas kernels  28.2 us (13%)
  local copies, waits for them, and re-layouts  21.6 us (10%)
  between operations  14.1 us (7%)
  matrix products  10.7 us (5%)
  loops' own time  3.41 us (2%)
  other arithmetic  2.22 us (1%)
    all_to_all x1, waiting for transfers between devices, narrow(): main = lax.all_to_all(main_sent, 'dp', 0, 0, tiled=True)  46.8 us
    ppermute x14, waiting for transfers between devices, shift(): return lax.ppermute(value, 'dp', pairs)  29.2 us
    ppermute x14, starting transfers between devices, shift(): return lax.ppermute(value, 'dp', pairs)  18.3 us
    cond x56, local copies, waits for them, and re-layouts  17.5 us
    dot_general x1, matrix products, narrow(): jnp.dot(hidden, value_weight, preferred_element_type=jnp.float32)  10.7 us
    all_to_all x1, starting transfers between devices, narrow(): main = lax.all_to_all(main_sent, 'dp', 0, 0, tiled=True)  7.76 us
    pallas_call x3, Pallas kernels, gather_call(): pl.pallas_call(kernel, out_shape=[jax.ShapeDtypeStruct((n, 2 * rank + 16,...  7.7 us
    pallas_call x3, Pallas kernels, vmem_call(): pl.pallas_call(kernel, out_shape=[jax.ShapeDtypeStruct(shape, dtype) for...  7.14 us
  transfers between devices with their start and end apart: 27, of which 13 were waited for; matrix products, arithmetic and copies ran while one was open for 7% of the time, Pallas kernels for 9%

profile of v7, /device:TPU:1, one launch (start us, length us, event | category | flops | bytes accessed | tf_op | source)
XLA Modules:
  0.0 214.4 jit_solution(85086560052743365)
XLA Ops:
  8.1 1.8 shard_map.75
  11.2 196.4 %conditional.1 = (bf16[2048,128]{1,0:T(8,128)(2,1)}) conditional(s32[]{:T(128)} %bitcast.20, (s32[32]{0:T(128)S(1)}, bf16[2048,1024]{1,0:T(8,128)(2,1)}, bf16[1024,1024]{1,0:T(8,128)(2,1)}, s32[512]{0:T(512)}, s32[2048]{0:T(1024)}, /*index=5*/s32[]{:T(128)}, bf16[128,64,1024]{2,1,0:T(8,128)(2,1)}, bf16[128,64,128]{2,1,0:T(8,128)(2,1)}) %tuple.16, ...), branch_computations={%region_0.5_spmd, %region_5.7_spmd} | conditional | flops 4601487360 | bytes 319880800 | solution.py:623
  11.4 3.7 %branch_1_fun.10 = bf16[16,144,1024]{2,1,0:T(8,128)(2,1)S(1)} custom-call(s32[16,128]{1,0:T(8,128)S(1)} %get-tuple-element.60.served, bf16[128,64,1024]{2,1,0:T(8,128)(2,1)} %get-tuple-element.53.down, bf16[128,64,128]{2,1,0:T(8,128)(2,1)} %get-tuple-element.54.up), custom_call_target="tpu_custom_call" | custom-call | bytes 9437184 | tf_op jit(solution)/shard_map/cond/branch_1_fun/pallas_call | solution.py:188
  15.1 2.1 copy-done
  17.2 7.8 %all-to-all-start.3 = ((bf16[16,144,1024]{2,1,0:T(8,128)(2,1)}), bf16[16,144,1024]{2,1,0:T(8,128)(2,1)}, u32[]{:S(2)}, u32[]{:S(2)}) async-start(bf16[16,144,1024]{2,1,0:T(8,128)(2,1)} %copy-done), calls=%async_computation.4 | async-start | bytes 9437184 | tf_op jit(solution)/shard_map/cond/branch_1_fun/all_to_all | solution.py:556
  25.1 2.7 %branch_1_fun.11 = (bf16[4,144,1024]{2,1,0:T(8,128)(2,1)}, bf16[4,144,1024]{2,1,0:T(8,128)(2,1)}, bf16[4,144,1024]{2,1,0:T(8,128)(2,1)S(1)}, bf16[4,144,1024]{2,1,0:T(8,128)(2,1)S(1)}) custom-call(s32[1]{0:T(128)} %get-tuple-element.55.me, s32[16,128]{1,0:T(8,128)S(1)} %get-tuple-element.60.served, s32[8,128]{1,0:T(8,128)S(1)} %get-tuple-element.50.mine, ...), custom_call_target="tpu_custom_call" | custom-call | bytes 9437184 | tf_op jit(solution)/shard_map/cond/branch_1_fun/pallas_call | solution.py:188
  29.9 2.6 %copy-done.23 = bf16[128,64,1024]{2,1,0:T(8,128)(2,1)S(1)} copy-done((bf16[128,64,1024]{2,1,0:T(8,128)(2,1)S(1)}, bf16[128,64,1024]{2,1,0:T(8,128)(2,1)}, u32[]{:S(2)}) %copy-start.23) | copy-done | bytes 16777240 | tf_op jit(solution)/shard_map/cond
  39.2 10.7 %fusion.8 = f32[2048,1024]{1,0:T(8,128)} fusion(bf16[2048,1024]{1,0:T(8,128)(2,1)} %get-tuple-element.67.hidden, bf16[1024,1024]{1,0:T(8,128)(2,1)} %get-tuple-element.68), kind=kOutput, calls=%fused_computation.42 | convolution fusion | flops 4294967296 | bytes 14680064 | tf_op jit(solution)/shard_map/cond/branch_1_fun/dot_general | solution.py:578
  50.0 46.8 %all-to-all-done.3.main = bf16[16,144,1024]{2,1,0:T(8,128)(2,1)} async-done(((bf16[16,144,1024]{2,1,0:T(8,128)(2,1)}), bf16[16,144,1024]{2,1,0:T(8,128)(2,1)}, u32[]{:S(2)}, u32[]{:S(2)}) %all-to-all-start.3) | async-done | bytes 4718624 | tf_op jit(solution)/shard_map/cond/branch_1_fun/all_to_all | solution.py:556
  96.9 2.7 %collective-permute-start.1 = (bf16[4,144,1024]{2,1,0:T(8,128)(2,1)}, bf16[4,144,1024]{2,1,0:T(8,128)(2,1)S(1)}, u32[]{:S(2)}, u32[]{:S(2)}) collective-permute-start(bf16[4,144,1024]{2,1,0:T(8,128)(2,1)} %get-tuple-element.73), channel_id=1, source_target_pairs={{0,96},{8,104},{16,112},{24,120},{32,0},{40,8},{48,16},{56,24},{64... | collective-permute-start | bytes 3538952 | tf_op jit(solution)/shard_map/cond/branch_1_fun/ppermute | solution.py:52
  99.6 1.9 collective-permute-start.2
  105.5 5.9 %branch_1_fun.13 = f32[896,128]{1,0:T(8,128)S(1)} custom-call(s32[8,128]{1,0:T(8,128)S(1)} %get-tuple-element.50.mine, bf16[2048,1024]{1,0:T(8,128)(2,1)} %get-tuple-element.67.hidden, bf16[16,144,1024]{2,1,0:T(8,128)(2,1)} %all-to-all-done.3.main), custom_call_target="tpu_custom_call" | custom-call | flops 234881024 | bytes 4718592 | tf_op jit(solution)/shard_map/cond/branch_1_fun/pallas_call | solution.py:320
  111.4 11.8 %collective-permute-done.refs_0_.refs_3_ = bf16[4,144,1024]{2,1,0:T(8,128)(2,1)S(1)} collective-permute-done((bf16[4,144,1024]{2,1,0:T(8,128)(2,1)}, bf16[4,144,1024]{2,1,0:T(8,128)(2,1)S(1)}, u32[]{:S(2)}, u32[]{:S(2)}) %collective-permute-start) | collective-permute-done | bytes 1179680 | tf_op jit(solution)/shard_map/cond/branch_1_fun/ppermute | solution.py:52
  123.2 2.0 collective-permute-done.2.refs_2_.refs_8_
  126.9 3.0 %branch_1_fun.14 = (bf16[2,144,1024]{2,1,0:T(8,128)(2,1)}, bf16[2,144,1024]{2,1,0:T(8,128)(2,1)}, bf16[2,144,1024]{2,1,0:T(8,128)(2,1)}, bf16[2,144,1024]{2,1,0:T(8,128)(2,1)}) custom-call(s32[2]{0:T(128)S(1)} %pad_add_fusion.offsets, bf16[4,144,1024]{2,1,0:T(8,128)(2,1)S(1)} %collective-permute-done.refs_0_.refs_3_, ...), custom_call_target="tpu_custom_call" | custom-call | bytes 4718592 | tf_op jit(solution)/shard_map/cond/branch_1_fun/pallas_call | solution.py:206
  133.3 3.8 %collective-permute-start.14 = (f32[448,128]{1,0:T(8,128)}, f32[448,128]{1,0:T(8,128)}, u32[]{:S(2)}, u32[]{:S(2)}) collective-permute-start(f32[448,128]{1,0:T(8,128)} %constant_dynamic-slice_fusion.3), channel_id=1, source_target_pairs={{0,1},{1,0},{2,3},{3,2},{4,5},{5,4},{6,7},{7,6},{8,9},{9,8},{10,11... | collective-permute-start | bytes 688136 | tf_op jit(solution)/shard_map/cond/branch_1_fun/ppermute | solution.py:344
  137.6 2.2 %collective-permute-start.7 = (bf16[2,144,1024]{2,1,0:T(8,128)(2,1)}, bf16[2,144,1024]{2,1,0:T(8,128)(2,1)}, u32[]{:S(2)}, u32[]{:S(2)}) collective-permute-start(bf16[2,144,1024]{2,1,0:T(8,128)(2,1)} %get-tuple-element.92), channel_id=1, source_target_pairs={{0,24},{8,0},{16,8},{24,16},{32,56},{40,32},{48,40},{56,48},{64,88... | collective-permute-start | bytes 1769480 | tf_op jit(solution)/shard_map/cond/branch_1_fun/ppermute | solution.py:52
  144.0 3.3 %collective-permute-start.16 = (f32[112,128]{1,0:T(8,128)}, f32[112,128]{1,0:T(8,128)}, u32[]{:S(2)}, u32[]{:S(2)}) collective-permute-start(f32[112,128]{1,0:T(8,128)} %get-tuple-element.122), channel_id=1, source_target_pairs={{0,4},{1,5},{2,6},{3,7},{4,0},{5,1},{6,2},{7,3},{8,12},{9,13},{10,... | collective-permute-start | bytes 172040 | tf_op jit(solution)/shard_map/cond/branch_1_fun/ppermute | solution.py:348
  148.0 5.7 %collective-permute-done.6.refs_6_ = bf16[2,144,1024]{2,1,0:T(8,128)(2,1)} collective-permute-done((bf16[2,144,1024]{2,1,0:T(8,128)(2,1)}, bf16[2,144,1024]{2,1,0:T(8,128)(2,1)}, u32[]{:S(2)}, u32[]{:S(2)}) %collective-permute-start.6) | collective-permute-done | bytes 589856 | tf_op jit(solution)/shard_map/cond/branch_1_fun/ppermute | solution.py:52
  156.2 3.5 %branch_1_fun.15 = (bf16[144,1024]{1,0:T(8,128)(2,1)S(1)}, bf16[144,1024]{1,0:T(8,128)(2,1)}, bf16[144,1024]{1,0:T(8,128)(2,1)}, bf16[144,1024]{1,0:T(8,128)(2,1...) custom-call(s32[2]{0:T(128)S(1)} %pad_add_fusion.offsets, ...), custom_call_target="tpu_custom_call" | custom-call | bytes 4718592 | tf_op jit(solution)/shard_map/cond/branch_1_fun/pallas_call | solution.py:206
  160.4 2.3 %collective-permute-start.10 = (bf16[144,1024]{1,0:T(8,128)(2,1)S(1)}, bf16[144,1024]{1,0:T(8,128)(2,1)S(1)}, u32[]{:S(2)}, u32[]{:S(2)}) collective-permute-start(bf16[144,1024]{1,0:T(8,128)(2,1)S(1)} %get-tuple-element.101), channel_id=1, source_target_pairs={{0,24},{8,0},{16,8},{24,16},{32,56},{40,32},{48,40},{56,48},{64,88... | collective-permute-start | bytes 884744 | tf_op jit(solution)/shard_map/cond/branch_1_fun/ppermute | solution.py:52
  163.7 1.7 collective-permute-start.18
  165.4 3.3 %collective-permute-start.19 = (bf16[112,128]{1,0:T(8,128)(2,1)S(1)}, bf16[112,128]{1,0:T(8,128)(2,1)S(1)}, u32[]{:S(2)}, u32[]{:S(2)}) collective-permute-start(bf16[112,128]{1,0:T(8,128)(2,1)S(1)} %add_convert_fusion), channel_id=1, source_target_pairs={{0,4},{1,5},{2,6},{3,7},{4,0},{5,1},{6,2},{7,3},{8,12},{9,13},{10,... | collective-permute-start | bytes 86024 | tf_op jit(solution)/shard_map/cond/branch_1_fun/ppermute | solution.py:352
  171.8 2.7 %collective-permute-start.21 = (bf16[4,112,128]{2,1,0:T(8,128)(2,1)S(1)}, bf16[4,112,128]{2,1,0:T(8,128)(2,1)S(1)}, u32[]{:S(2)}, u32[]{:S(2)}) collective-permute-start(bf16[4,112,128]{2,1,0:T(8,128)(2,1)S(1)} %pad_maximum_fusion.own), channel_id=1, source_target_pairs={{0,1},{1,0},{2,3},{3,2},{4,5},{5,4},{6,7},{7,6},{8,9},{9,8},{10,11... | collective-permute-start | bytes 344072 | tf_op jit(solution)/shard_map/cond/branch_1_fun/ppermute | solution.py:353
  174.6 2.0 collective-permute-start.12
  176.5 2.0 collective-permute-start.13
  181.1 3.3 %branch_1_fun.16._ = bf16[2048,128]{1,0:T(8,128)(2,1)} custom-call(s32[2]{0:T(128)S(1)} %pad_add_fusion.1.where, s32[8,128]{1,0:T(8,128)S(1)} %get-tuple-element.50.mine, s32[32]{0:T(128)S(1)} %copy-done.30, f32[2048,128]{1,0:T(8,128)S(1)} %copy-done.1, bf16[4,112,128]{2,1,0:T(8,128)(2,1)S(1)} %pad_maximum_fusion.own, ...), custom_call_target="tpu_custom_call" | custom-call | flops 33554432 | bytes 2097152 | tf_op jit(solution)/shard_map/cond/branch_1_fun/pallas_call | solution.py:455
  184.4 6.5 %collective-permute-done.11.refs_5_ = bf16[144,1024]{1,0:T(8,128)(2,1)S(1)} collective-permute-done((bf16[144,1024]{1,0:T(8,128)(2,1)}, bf16[144,1024]{1,0:T(8,128)(2,1)S(1)}, u32[]{:S(2)}, u32[]{:S(2)}) %collective-permute-start.11) | collective-permute-done | bytes 294944 | tf_op jit(solution)/shard_map/cond/branch_1_fun/ppermute | solution.py:52
  194.1 3.3 %collective-permute-start.22 = (f32[128,128]{1,0:T(8,128)S(1)}, f32[128,128]{1,0:T(8,128)S(1)}, u32[]{:S(2)}, u32[]{:S(2)}) collective-permute-start(f32[128,128]{1,0:T(8,128)S(1)} %branch_1_fun.18), channel_id=1, source_target_pairs={{0,1},{1,0},{2,3},{3,2},{4,5},{5,4},{6,7},{7,6},{8,9},{9,8},{10,11... | collective-permute-start | bytes 196616 | tf_op jit(solution)/shard_map/cond/branch_1_fun/ppermute | solution.py:365
  198.3 3.1 %collective-permute-done.23 = f32[128,128]{1,0:T(8,128)S(1)} collective-permute-done((f32[128,128]{1,0:T(8,128)S(1)}, f32[128,128]{1,0:T(8,128)S(1)}, u32[]{:S(2)}, u32[]{:S(2)}) %collective-permute-start.23) | collective-permute-done | bytes 65568 | tf_op jit(solution)/shard_map/cond/branch_1_fun/ppermute | solution.py:365
  201.5 2.0 collective-permute-start.24
  203.4 2.4 %collective-permute-done.24 = f32[128,128]{1,0:T(8,128)S(1)} collective-permute-done((f32[128,128]{1,0:T(8,128)S(1)}, f32[128,128]{1,0:T(8,128)S(1)}, u32[]{:S(2)}, u32[]{:S(2)}) %collective-permute-start.24) | collective-permute-done | bytes 65568 | tf_op jit(solution)/shard_map/cond/branch_1_fun/ppermute | solution.py:365
  (106 shorter events, 38.4 us)
Async XLA Ops:
  17.2 79.6 %all-to-all-start.3 = ((bf16[16,144,1024]{2,1,0:T(8,128)(2,1)}), bf16[16,144,1024]{2,1,0:T(8,128)(2,1)}, u32[]{:S(2)}, u32[]{:S(2)}) async-start(bf16[16,144,1024]{2,1,0:T(8,128)(2,1)} %copy-done), calls=%async_computation.4 | async-start | bytes 9437184 | tf_op jit(solution)/shard_map/cond/branch_1_fun/all_to_all | solution.py:556
  25.0 154.9 %reduce-scatter.5.cloned.1.call-start = ((), (), s32[]{:S(2)}) async-start(), calls=%async_computation.7 | async-start | bytes 9437184 | tf_op jit(solution)/shard_map/cond/branch_1_fun/reduce_scatter | solution.py:581
  96.8 26.4 %collective-permute-start = (bf16[4,144,1024]{2,1,0:T(8,128)(2,1)}, bf16[4,144,1024]{2,1,0:T(8,128)(2,1)S(1)}, u32[]{:S(2)}, u32[]{:S(2)}) collective-permute-start(bf16[4,144,1024]{2,1,0:T(8,128)(2,1)} %get-tuple-element.72), channel_id=1, source_target_pairs={{0,32},{8,40},{16,48},{24,56},{32,64},{40,72},{48,80},{56,88},{64,... | collective-permute-start | bytes 3538952 | tf_op jit(solution)/shard_map/cond/branch_1_fun/ppermute | solution.py:52
  96.9 26.3 %collective-permute-start.1 = (bf16[4,144,1024]{2,1,0:T(8,128)(2,1)}, bf16[4,144,1024]{2,1,0:T(8,128)(2,1)S(1)}, u32[]{:S(2)}, u32[]{:S(2)}) collective-permute-start(bf16[4,144,1024]{2,1,0:T(8,128)(2,1)} %get-tuple-element.73), channel_id=1, source_target_pairs={{0,96},{8,104},{16,112},{24,120},{32,0},{40,8},{48,16},{56,24},{64... | collective-permute-start | bytes 3538952 | tf_op jit(solution)/shard_map/cond/branch_1_fun/ppermute | solution.py:52
  99.6 25.7 %collective-permute-start.2 = (bf16[4,144,1024]{2,1,0:T(8,128)(2,1)}, bf16[4,144,1024]{2,1,0:T(8,128)(2,1)S(1)}, u32[]{:S(2)}, u32[]{:S(2)}) collective-permute-start(bf16[4,144,1024]{2,1,0:T(8,128)(2,1)} %copy-done.21), channel_id=1, source_target_pairs={{0,8},{8,16},{16,24},{24,0},{32,40},{40,48},{48,56},{56,32},{64,72... | collective-permute-start | bytes 3538952 | tf_op jit(solution)/shard_map/cond/branch_1_fun/ppermute | solution.py:52
  101.4 25.4 %collective-permute-start.3 = (bf16[4,144,1024]{2,1,0:T(8,128)(2,1)}, bf16[4,144,1024]{2,1,0:T(8,128)(2,1)}, u32[]{:S(2)}, u32[]{:S(2)}) collective-permute-start(bf16[4,144,1024]{2,1,0:T(8,128)(2,1)} %copy-done.20), channel_id=1, source_target_pairs={{0,24},{8,0},{16,8},{24,16},{32,56},{40,32},{48,40},{56,48},{64,88... | collective-permute-start | bytes 3538952 | tf_op jit(solution)/shard_map/cond/branch_1_fun/ppermute | solution.py:52
  105.5 21.3 %copy-start.13 = (bf16[2,144,1024]{2,1,0:T(8,128)(2,1)S(1)}, bf16[2,144,1024]{2,1,0:T(8,128)(2,1)}, u32[]{:S(2)}) copy-start(bf16[2,144,1024]{2,1,0:T(8,128)(2,1)} %copy-done.12) | copy-start | bytes 1769476 | tf_op jit(solution)/shard_map/cond
  105.5 21.3 %copy-start.15 = (bf16[2,144,1024]{2,1,0:T(8,128)(2,1)S(1)}, bf16[2,144,1024]{2,1,0:T(8,128)(2,1)}, u32[]{:S(2)}) copy-start(bf16[2,144,1024]{2,1,0:T(8,128)(2,1)} %copy-done.14) | copy-start | bytes 1769476 | tf_op jit(solution)/shard_map/cond
  129.9 14.1 %collective-permute-start.4 = (bf16[2,144,1024]{2,1,0:T(8,128)(2,1)}, bf16[2,144,1024]{2,1,0:T(8,128)(2,1)}, u32[]{:S(2)}, u32[]{:S(2)}) collective-permute-start(bf16[2,144,1024]{2,1,0:T(8,128)(2,1)} %get-tuple-element.89), channel_id=1, source_target_pairs={{0,32},{8,40},{16,48},{24,56},{32,64},{40,72},{48,80},{56,88},{64,... | collective-permute-start | bytes 1769480 | tf_op jit(solution)/shard_map/cond/branch_1_fun/ppermute | solution.py:52
  131.4 15.9 %collective-permute-start.5 = (bf16[2,144,1024]{2,1,0:T(8,128)(2,1)}, bf16[2,144,1024]{2,1,0:T(8,128)(2,1)}, u32[]{:S(2)}, u32[]{:S(2)}) collective-permute-start(bf16[2,144,1024]{2,1,0:T(8,128)(2,1)} %get-tuple-element.90), channel_id=1, source_target_pairs={{0,96},{8,104},{16,112},{24,120},{32,0},{40,8},{48,16},{56,24},{64... | collective-permute-start | bytes 1769480 | tf_op jit(solution)/shard_map/cond/branch_1_fun/ppermute | solution.py:52
  133.3 6.5 %collective-permute-start.14 = (f32[448,128]{1,0:T(8,128)}, f32[448,128]{1,0:T(8,128)}, u32[]{:S(2)}, u32[]{:S(2)}) collective-permute-start(f32[448,128]{1,0:T(8,128)} %constant_dynamic-slice_fusion.3), channel_id=1, source_target_pairs={{0,1},{1,0},{2,3},{3,2},{4,5},{5,4},{6,7},{7,6},{8,9},{9,8},{10,11... | collective-permute-start | bytes 688136 | tf_op jit(solution)/shard_map/cond/branch_1_fun/ppermute | solution.py:344
  137.2 16.5 %collective-permute-start.6 = (bf16[2,144,1024]{2,1,0:T(8,128)(2,1)}, bf16[2,144,1024]{2,1,0:T(8,128)(2,1)}, u32[]{:S(2)}, u32[]{:S(2)}) collective-permute-start(bf16[2,144,1024]{2,1,0:T(8,128)(2,1)} %get-tuple-element.91), channel_id=1, source_target_pairs={{0,8},{8,16},{16,24},{24,0},{32,40},{40,48},{48,56},{56,32},{64,72... | collective-permute-start | bytes 1769480 | tf_op jit(solution)/shard_map/cond/branch_1_fun/ppermute | solution.py:52
  137.6 16.0 %collective-permute-start.7 = (bf16[2,144,1024]{2,1,0:T(8,128)(2,1)}, bf16[2,144,1024]{2,1,0:T(8,128)(2,1)}, u32[]{:S(2)}, u32[]{:S(2)}) collective-permute-start(bf16[2,144,1024]{2,1,0:T(8,128)(2,1)} %get-tuple-element.92), channel_id=1, source_target_pairs={{0,24},{8,0},{16,8},{24,16},{32,56},{40,32},{48,40},{56,48},{64,88... | collective-permute-start | bytes 1769480 | tf_op jit(solution)/shard_map/cond/branch_1_fun/ppermute | solution.py:52
  142.3 20.4 %collective-permute-start.15 = (f32[112,128]{1,0:T(8,128)}, f32[112,128]{1,0:T(8,128)}, u32[]{:S(2)}, u32[]{:S(2)}) collective-permute-start(f32[112,128]{1,0:T(8,128)} %get-tuple-element.124), channel_id=1, source_target_pairs={{0,2},{1,3},{2,4},{3,5},{4,6},{5,7},{6,0},{7,1},{8,10},{9,11},{10,... | collective-permute-start | bytes 172040 | tf_op jit(solution)/shard_map/cond/branch_1_fun/ppermute | solution.py:348
  144.0 18.8 %collective-permute-start.16 = (f32[112,128]{1,0:T(8,128)}, f32[112,128]{1,0:T(8,128)}, u32[]{:S(2)}, u32[]{:S(2)}) collective-permute-start(f32[112,128]{1,0:T(8,128)} %get-tuple-element.122), channel_id=1, source_target_pairs={{0,4},{1,5},{2,6},{3,7},{4,0},{5,1},{6,2},{7,3},{8,12},{9,13},{10,... | collective-permute-start | bytes 172040 | tf_op jit(solution)/shard_map/cond/branch_1_fun/ppermute | solution.py:348
  147.2 15.5 %collective-permute-start.17 = (f32[112,128]{1,0:T(8,128)}, f32[112,128]{1,0:T(8,128)}, u32[]{:S(2)}, u32[]{:S(2)}) collective-permute-start(f32[112,128]{1,0:T(8,128)} %get-tuple-element.123), channel_id=1, source_target_pairs={{0,6},{1,7},{2,0},{3,1},{4,2},{5,3},{6,4},{7,5},{8,14},{9,15},{10,... | collective-permute-start | bytes 172040 | tf_op jit(solution)/shard_map/cond/branch_1_fun/ppermute | solution.py:348
  148.0 31.9 %copy-start.30 = (s32[32]{0:T(128)S(1)}, s32[32]{0:T(128)}, u32[]{:S(2)}) copy-start(s32[32]{0:T(128)} %copy-done.29) | copy-start | bytes 388 | tf_op jit(solution)/shard_map/cond
  160.4 32.1 %copy-start.19 = (bf16[144,1024]{1,0:T(8,128)(2,1)S(1)}, bf16[144,1024]{1,0:T(8,128)(2,1)}, u32[]{:S(2)}) copy-start(bf16[144,1024]{1,0:T(8,128)(2,1)} %copy-done.18) | copy-start | bytes 884740 | tf_op jit(solution)/shard_map/cond
  160.4 18.1 %collective-permute-start.10 = (bf16[144,1024]{1,0:T(8,128)(2,1)S(1)}, bf16[144,1024]{1,0:T(8,128)(2,1)S(1)}, u32[]{:S(2)}, u32[]{:S(2)}) collective-permute-start(bf16[144,1024]{1,0:T(8,128)(2,1)S(1)} %get-tuple-element.101), channel_id=1, source_target_pairs={{0,24},{8,0},{16,8},{24,16},{32,56},{40,32},{48,40},{56,48},{64,88... | collective-permute-start | bytes 884744 | tf_op jit(solution)/shard_map/cond/branch_1_fun/ppermute | solution.py:52
  163.7 5.8 %collective-permute-start.18 = (bf16[112,128]{1,0:T(8,128)(2,1)S(1)}, bf16[112,128]{1,0:T(8,128)(2,1)S(1)}, u32[]{:S(2)}, u32[]{:S(2)}) collective-permute-start(bf16[112,128]{1,0:T(8,128)(2,1)S(1)} %add_convert_fusion), channel_id=1, source_target_pairs={{0,2},{1,3},{2,4},{3,5},{4,6},{5,7},{6,0},{7,1},{8,10},{9,11},{10,... | collective-permute-start | bytes 86024 | tf_op jit(solution)/shard_map/cond/branch_1_fun/ppermute | solution.py:352
  165.4 4.9 %collective-permute-start.19 = (bf16[112,128]{1,0:T(8,128)(2,1)S(1)}, bf16[112,128]{1,0:T(8,128)(2,1)S(1)}, u32[]{:S(2)}, u32[]{:S(2)}) collective-permute-start(bf16[112,128]{1,0:T(8,128)(2,1)S(1)} %add_convert_fusion), channel_id=1, source_target_pairs={{0,4},{1,5},{2,6},{3,7},{4,0},{5,1},{6,2},{7,3},{8,12},{9,13},{10,... | collective-permute-start | bytes 86024 | tf_op jit(solution)/shard_map/cond/branch_1_fun/ppermute | solution.py:352
  168.7 3.1 %collective-permute-start.20 = (bf16[112,128]{1,0:T(8,128)(2,1)S(1)}, bf16[112,128]{1,0:T(8,128)(2,1)S(1)}, u32[]{:S(2)}, u32[]{:S(2)}) collective-permute-start(bf16[112,128]{1,0:T(8,128)(2,1)S(1)} %add_convert_fusion), channel_id=1, source_target_pairs={{0,6},{1,7},{2,0},{3,1},{4,2},{5,3},{6,4},{7,5},{8,14},{9,15},{10,... | collective-permute-start | bytes 86024 | tf_op jit(solution)/shard_map/cond/branch_1_fun/ppermute | solution.py:352
  171.8 6.7 %collective-permute-start.21 = (bf16[4,112,128]{2,1,0:T(8,128)(2,1)S(1)}, bf16[4,112,128]{2,1,0:T(8,128)(2,1)S(1)}, u32[]{:S(2)}, u32[]{:S(2)}) collective-permute-start(bf16[4,112,128]{2,1,0:T(8,128)(2,1)S(1)} %pad_maximum_fusion.own), channel_id=1, source_target_pairs={{0,1},{1,0},{2,3},{3,2},{4,5},{5,4},{6,7},{7,6},{8,9},{9,8},{10,11... | collective-permute-start | bytes 344072 | tf_op jit(solution)/shard_map/cond/branch_1_fun/ppermute | solution.py:353
  174.5 16.3 %collective-permute-start.11 = (bf16[144,1024]{1,0:T(8,128)(2,1)}, bf16[144,1024]{1,0:T(8,128)(2,1)S(1)}, u32[]{:S(2)}, u32[]{:S(2)}) collective-permute-start(bf16[144,1024]{1,0:T(8,128)(2,1)} %get-tuple-element.102), channel_id=1, source_target_pairs={{0,32},{8,40},{16,48},{24,56},{32,64},{40,72},{48,80},{56,88},{64,... | collective-permute-start | bytes 884744 | tf_op jit(solution)/shard_map/cond/branch_1_fun/ppermute | solution.py:52
  174.6 16.3 %collective-permute-start.12 = (bf16[144,1024]{1,0:T(8,128)(2,1)}, bf16[144,1024]{1,0:T(8,128)(2,1)S(1)}, u32[]{:S(2)}, u32[]{:S(2)}) collective-permute-start(bf16[144,1024]{1,0:T(8,128)(2,1)} %get-tuple-element.103), channel_id=1, source_target_pairs={{0,64},{8,72},{16,80},{24,88},{32,96},{40,104},{48,112},{56,120},{... | collective-permute-start | bytes 884744 | tf_op jit(solution)/shard_map/cond/branch_1_fun/ppermute | solution.py:52
  176.5 14.6 %collective-permute-start.13 = (bf16[144,1024]{1,0:T(8,128)(2,1)}, bf16[144,1024]{1,0:T(8,128)(2,1)S(1)}, u32[]{:S(2)}, u32[]{:S(2)}) collective-permute-start(bf16[144,1024]{1,0:T(8,128)(2,1)} %get-tuple-element.104), channel_id=1, source_target_pairs={{0,96},{8,104},{16,112},{24,120},{32,0},{40,8},{48,16},{56,24},{64... | collective-permute-start | bytes 884744 | tf_op jit(solution)/shard_map/cond/branch_1_fun/ppermute | solution.py:52
  178.5 12.7 %collective-permute-start.8 = (bf16[144,1024]{1,0:T(8,128)(2,1)}, bf16[144,1024]{1,0:T(8,128)(2,1)S(1)}, u32[]{:S(2)}, u32[]{:S(2)}) collective-permute-start(bf16[144,1024]{1,0:T(8,128)(2,1)} %get-tuple-element.99), channel_id=1, source_target_pairs={{0,8},{8,16},{16,24},{24,0},{32,40},{40,48},{48,56},{56,32},{64,72... | collective-permute-start | bytes 884744 | tf_op jit(solution)/shard_map/cond/branch_1_fun/ppermute | solution.py:52
  178.5 14.0 %collective-permute-start.9 = (bf16[144,1024]{1,0:T(8,128)(2,1)}, bf16[144,1024]{1,0:T(8,128)(2,1)S(1)}, u32[]{:S(2)}, u32[]{:S(2)}) collective-permute-start(bf16[144,1024]{1,0:T(8,128)(2,1)} %get-tuple-element.100), channel_id=1, source_target_pairs={{0,16},{8,24},{16,0},{24,8},{32,48},{40,56},{48,32},{56,40},{64,80... | collective-permute-start | bytes 884744 | tf_op jit(solution)/shard_map/cond/branch_1_fun/ppermute | solution.py:52
  184.3 21.5 %copy-start.2 = (f32[2048,128]{1,0:T(8,128)S(1)}, f32[2048,128]{1,0:T(8,128)}, u32[]{:S(2)}) copy-start(f32[2048,128]{1,0:T(8,128)} %reduce-scatter.5.cloned.1.call-done.base) | copy-start | bytes 3145732 | tf_op jit(solution)/shard_map/cond
  194.1 4.2 %collective-permute-start.22 = (f32[128,128]{1,0:T(8,128)S(1)}, f32[128,128]{1,0:T(8,128)S(1)}, u32[]{:S(2)}, u32[]{:S(2)}) collective-permute-start(f32[128,128]{1,0:T(8,128)S(1)} %branch_1_fun.18), channel_id=1, source_target_pairs={{0,1},{1,0},{2,3},{3,2},{4,5},{5,4},{6,7},{7,6},{8,9},{9,8},{10,11... | collective-permute-start | bytes 196616 | tf_op jit(solution)/shard_map/cond/branch_1_fun/ppermute | solution.py:365
  198.3 3.2 %collective-permute-start.23 = (f32[128,128]{1,0:T(8,128)S(1)}, f32[128,128]{1,0:T(8,128)S(1)}, u32[]{:S(2)}, u32[]{:S(2)}) collective-permute-start(f32[128,128]{1,0:T(8,128)S(1)} %add.149), channel_id=1, source_target_pairs={{0,2},{1,3},{2,0},{3,1},{4,6},{5,7},{6,4},{7,5},{8,10},{9,11},{10,... | collective-permute-start | bytes 196616 | tf_op jit(solution)/shard_map/cond/branch_1_fun/ppermute | solution.py:365
  201.5 4.4 %collective-permute-start.24 = (f32[128,128]{1,0:T(8,128)S(1)}, f32[128,128]{1,0:T(8,128)S(1)}, u32[]{:S(2)}, u32[]{:S(2)}) collective-permute-start(f32[128,128]{1,0:T(8,128)S(1)} %add.150), channel_id=1, source_target_pairs={{0,6},{1,7},{2,4},{3,5},{4,2},{5,3},{6,0},{7,1},{8,14},{9,15},{10,... | collective-permute-start | bytes 196616 | tf_op jit(solution)/shard_map/cond/branch_1_fun/ppermute | solution.py:365
  (23 other events, 139.3 us)
Sparse Core Ops, SparseCore 0:
  96.9 61.0 reduce-scatter.4

commit v8 on v7

--- a/solution.py
+++ b/solution.py
@@ -331,26 +331,36 @@
     )(mine, hidden, *weights)
 
 
-def low_rank_rounds(partial):
+def turn(step):
     tp_count = lax.axis_size("tp")
-    chips = tp_count // 2
+    return [(i, (i + 2 * step) % tp_count) for i in range(tp_count)]
+
+
+def swap():
+    return [(i, i ^ 1) for i in range(lax.axis_size("tp"))]
+
+
+def low_rank_down(partial):
+    chips = lax.axis_size("tp") // 2
     t = lax.axis_index("tp")
     z, core = t // 2, t % 2
     half = partial.shape[0] // 2
     piece = half // chips
-    swap = [(i, i ^ 1) for i in range(tp_count)]
-    turn = lambda d: [(i, (i + 2 * d) % tp_count) for i in range(tp_count)]
     cut = lambda array, start, size: lax.dynamic_slice_in_dim(array, start, size, 0)
     total = cut(partial, core * half, half) + lax.ppermute(
-        cut(partial, (1 - core) * half, half), "tp", swap
+        cut(partial, (1 - core) * half, half), "tp", swap()
     )
     pieces = [
         lax.ppermute(cut(total, (z + d) % chips * piece, piece), "tp", turn(d))
         for d in range(1, chips)
     ]
-    summed = (cut(total, z * piece, piece) + sum(pieces)).astype(jnp.bfloat16)
+    return (cut(total, z * piece, piece) + sum(pieces)).astype(jnp.bfloat16)
+
+
+def low_rank_up(summed):
+    chips = lax.axis_size("tp") // 2
     own = jnp.stack([summed] + [lax.ppermute(summed, "tp", turn(d)) for d in range(1, chips)])
-    return own, lax.ppermute(own, "tp", swap)
+    return own, lax.ppermute(own, "tp", swap())
 
 
 def low_rank_doubling(partial):
@@ -563,7 +573,7 @@
             (me_row, served, mine),
             down_weights,
             up_weights,
-            40,
+            50,
         )
         later_served, _ = barrier((served, gathered))
         later = gather_call(
@@ -573,7 +583,7 @@
             (me_row, later_served, mine),
             down_weights,
             up_weights,
-            40,
+            50,
         )
         base_terms = jnp.dot(hidden, value_weight, preferred_element_type=jnp.float32)
         main, gathered, later, base_terms = barrier((main, gathered, later, base_terms))
@@ -583,15 +593,11 @@
         partial = low_partial(
             functools.partial(low_main_kernel, cap), pairs, cap, rank, mine, hidden, (main,)
         )
-        own, other = low_rank_rounds(partial)
-        t = lax.axis_index("tp")
-        where = jnp.stack([t // 2, t % 2]).astype(jnp.int32)
-        out = combine_main(where, mine, counts, base, own, other, main, rank)
-        fresh, near, _ = barrier((fresh, later[:4], partial))
+        fresh, near, summed = barrier((fresh, later[:4], low_rank_down(partial)))
         relayed = vmem_call(
             relay_kernel, ((2,) + unit,) * 4, dtype, (offsets,), (*fresh, *near)
         )
-        near_a = barrier(send(relayed, moves))
+        near_a, (own, other) = barrier((send(relayed, moves), low_rank_up(summed)))
         tree_arrays = [
             (later[4 + h], near_a[2 * h], near_a[2 * h + 1], fresh[2 * h], fresh[2 * h + 1])
             for h in range(2)
@@ -600,6 +606,10 @@
             line_kernel, (unit,) * 8, dtype, (offsets,), tree_arrays[0] + tree_arrays[1]
         )
         got = send(lines[1:4] + lines[5:8], turned)
+        t = lax.axis_index("tp")
+        where = jnp.stack([t // 2, t % 2]).astype(jnp.int32)
+        own, _ = barrier((own, lines))
+        out = combine_main(where, mine, counts, base, own, other, main, rank)
         got, out = barrier((got, out))
         extras = vmem_call(
             pick_kernel,

time: 216 us -> 217 us (level)
  waiting for transfers between devices: 84.8 us -> 97.9 us
  starting transfers between devices: 49.5 us -> 44.1 us
  matrix products: 10.7 us -> 6.67 us
  local copies, waits for them, and re-layouts: 21.6 us -> 19.2 us
    ppermute x8, waiting for transfers between devices: 2.34 us -> 23 us  [the longest x3 11.4 us: low_rank_up(): lax.ppermute(summed, 'tp', turn(d))]
    ppermute x14, waiting for transfers between devices: 29.2 us -> 11.7 us  [shift(): return lax.ppermute(value, 'dp', pairs)]
    all_to_all x1, waiting for transfers between devices: 46.8 us -> 57.6 us  [narrow(): main = lax.all_to_all(main_sent, 'dp', 0, 0, tiled=True)]
    dot_general x1, matrix products: 10.7 us -> 6.67 us  [narrow(): jnp.dot(hidden, value_weight, preferred_element_type=jnp.float32)]
    ppermute x8, starting transfers between devices: 18 us -> 15.3 us  [the longest x1 6.23 us: low_rank_up(): return (own, lax.ppermute(own, 'tp', swap()))]
    cond x56 -> x66, local copies, waits for them, and re-layouts: 17.5 us -> 15.1 us
    ppermute x14, starting transfers between devices: 18.3 us -> 16 us  [shift(): return lax.ppermute(value, 'dp', pairs)]
  transfers between devices with their start and end apart: 27 -> 27, of which waited for: 13 -> 14; matrix products, arithmetic and copies ran while one was open for 7% -> 5% of each run, Pallas kernels for 9% -> 9%
where the time goes in v8:
time: 217 us; the launch traced here: 215 us
  waiting for transfers between devices  97.9 us (45%)
  starting transfers between devices  44.1 us (20%)
  Pallas kernels  27.3 us (13%)
  local copies, waits for them, and re-layouts  19.2 us (9%)
  between operations  14.1 us (6%)
  matrix products  6.67 us (3%)
  loops' own time  3.39 us (2%)
  other arithmetic  2.17 us (1%)
    all_to_all x1, waiting for transfers between devices, narrow(): main = lax.all_to_all(main_sent, 'dp', 0, 0, tiled=True)  57.6 us
    ppermute x14, starting transfers between devices, shift(): return lax.ppermute(value, 'dp', pairs)  16 us
    cond x66, local copies, waits for them, and re-layouts  15.1 us
    ppermute x14, waiting for transfers between devices, shift(): return lax.ppermute(value, 'dp', pairs)  11.7 us
    ppermute x3, waiting for transfers between devices, low_rank_up(): lax.ppermute(summed, 'tp', turn(d))  11.4 us
    ppermute x3, waiting for transfers between devices, low_rank_down(): lax.ppermute(cut(total, (z + d) % chips * piece, piece), 'tp', turn(d))  9.13 us
    pallas_call x3, Pallas kernels, gather_call(): pl.pallas_call(kernel, out_shape=[jax.ShapeDtypeStruct((n, 2 * rank + 16,...  9.08 us
    all_to_all x1, starting transfers between devices, narrow(): main = lax.all_to_all(main_sent, 'dp', 0, 0, tiled=True)  7.69 us
  transfers between devices with their start and end apart: 27, of which 14 were waited for; matrix products, arithmetic and copies ran while one was open for 5% of the time, Pallas kernels for 9%

profile of v8, /device:TPU:1, one launch (start us, length us, event | category | flops | bytes accessed | tf_op | source)
XLA Modules:
  0.0 214.7 jit_solution(862880915388781017)
XLA Ops:
  8.1 1.8 shard_map.75
  11.2 196.7 %conditional.1 = (bf16[2048,128]{1,0:T(8,128)(2,1)}) conditional(s32[]{:T(128)} %bitcast.20, (s32[32]{0:T(128)S(1)}, bf16[2048,1024]{1,0:T(8,128)(2,1)}, bf16[1024,1024]{1,0:T(8,128)(2,1)}, s32[512]{0:T(512)}, s32[2048]{0:T(1024)}, /*index=5*/s32[]{:T(128)}, bf16[128,64,1024]{2,1,0:T(8,128)(2,1)}, bf16[128,64,128]{2,1,0:T(8,128)(2,1)}) %tuple.17, ...), branch_computations={%region_0.5_spmd, %region_5.7_spmd} | conditional | flops 4601487360 | bytes 272695968 | solution.py:633
  11.4 3.7 %branch_1_fun.10 = bf16[16,144,1024]{2,1,0:T(8,128)(2,1)S(1)} custom-call(s32[16,128]{1,0:T(8,128)S(1)} %get-tuple-element.60.served, bf16[128,64,1024]{2,1,0:T(8,128)(2,1)} %get-tuple-element.53.down, bf16[128,64,128]{2,1,0:T(8,128)(2,1)} %get-tuple-element.54.up), custom_call_target="tpu_custom_call" | custom-call | bytes 9437184 | tf_op jit(solution)/shard_map/cond/branch_1_fun/pallas_call | solution.py:188
  15.1 2.1 copy-done
  17.2 7.7 %all-to-all-start.3 = ((bf16[16,144,1024]{2,1,0:T(8,128)(2,1)}), bf16[16,144,1024]{2,1,0:T(8,128)(2,1)}, u32[]{:S(2)}, u32[]{:S(2)}) async-start(bf16[16,144,1024]{2,1,0:T(8,128)(2,1)} %copy-done), calls=%async_computation.4 | async-start | bytes 9437184 | tf_op jit(solution)/shard_map/cond/branch_1_fun/all_to_all | solution.py:566
  25.0 3.1 %branch_1_fun.11 = (bf16[4,144,1024]{2,1,0:T(8,128)(2,1)}, bf16[4,144,1024]{2,1,0:T(8,128)(2,1)}, bf16[4,144,1024]{2,1,0:T(8,128)(2,1)S(1)}, bf16[4,144,1024]{2,1,0:T(8,128)(2,1)}) custom-call(s32[1]{0:T(128)} %get-tuple-element.55.me, s32[16,128]{1,0:T(8,128)S(1)} %get-tuple-element.60.served, s32[8,128]{1,0:T(8,128)S(1)} %get-tuple-element.50.mine, ...), custom_call_target="tpu_custom_call" | custom-call | bytes 9437184 | tf_op jit(solution)/shard_map/cond/branch_1_fun/pallas_call | solution.py:188
  29.2 2.3 %branch_1_fun.12 = (bf16[2,144,1024]{2,1,0:T(8,128)(2,1)S(1)}, bf16[2,144,1024]{2,1,0:T(8,128)(2,1)S(1)}, bf16[2,144,1024]{2,1,0:T(8,128)(2,1)S(1)}, bf16[2,144,...) custom-call(s32[1]{0:T(128)} %get-tuple-element.55.me, ...), custom_call_target="tpu_custom_call" | custom-call | bytes 9437184 | tf_op jit(solution)/shard_map/cond/branch_1_fun/pallas_call | solution.py:188
  32.4 6.7 %fusion.8 = f32[2048,1024]{1,0:T(8,128)} fusion(bf16[2048,1024]{1,0:T(8,128)(2,1)S(1)} %copy-done.27, bf16[1024,1024]{1,0:T(8,128)(2,1)S(1)} %copy-done.35), kind=kOutput, calls=%fused_computation.42 | convolution fusion | flops 4294967296 | bytes 14680064 | tf_op jit(solution)/shard_map/cond/branch_1_fun/dot_general | solution.py:588
  39.2 57.6 %all-to-all-done.3.main = bf16[16,144,1024]{2,1,0:T(8,128)(2,1)} async-done(((bf16[16,144,1024]{2,1,0:T(8,128)(2,1)}), bf16[16,144,1024]{2,1,0:T(8,128)(2,1)}, u32[]{:S(2)}, u32[]{:S(2)}) %all-to-all-start.3) | async-done | bytes 4718624 | tf_op jit(solution)/shard_map/cond/branch_1_fun/all_to_all | solution.py:566
  96.8 2.7 %collective-permute-start.1 = (bf16[4,144,1024]{2,1,0:T(8,128)(2,1)}, bf16[4,144,1024]{2,1,0:T(8,128)(2,1)S(1)}, u32[]{:S(2)}, u32[]{:S(2)}) collective-permute-start(bf16[4,144,1024]{2,1,0:T(8,128)(2,1)} %get-tuple-element.73), channel_id=1, source_target_pairs={{0,96},{8,104},{16,112},{24,120},{32,0},{40,8},{48,16},{56,24},{64... | collective-permute-start | bytes 3538952 | tf_op jit(solution)/shard_map/cond/branch_1_fun/ppermute | solution.py:52
  99.5 1.9 collective-permute-start.2
  102.2 5.8 %branch_1_fun.13 = f32[896,128]{1,0:T(8,128)S(1)} custom-call(s32[8,128]{1,0:T(8,128)S(1)} %get-tuple-element.50.mine, bf16[2048,1024]{1,0:T(8,128)(2,1)} %get-tuple-element.67.hidden, bf16[16,144,1024]{2,1,0:T(8,128)(2,1)} %all-to-all-done.3.main), custom_call_target="tpu_custom_call" | custom-call | flops 234881024 | bytes 4718592 | tf_op jit(solution)/shard_map/cond/branch_1_fun/pallas_call | solution.py:320
  109.4 3.9 %collective-permute-start.4 = (f32[448,128]{1,0:T(8,128)}, f32[448,128]{1,0:T(8,128)}, u32[]{:S(2)}, u32[]{:S(2)}) collective-permute-start(f32[448,128]{1,0:T(8,128)} %constant_dynamic-slice_fusion.3), channel_id=1, source_target_pairs={{0,1},{1,0},{2,3},{3,2},{4,5},{5,4},{6,7},{7,6},{8,9},{9,8},{10,11... | collective-permute-start | bytes 688136 | tf_op jit(solution)/shard_map/cond/branch_1_fun/ppermute | solution.py:350
  113.3 1.5 collective-permute-done.4
  117.2 1.6 collective-permute-start.5
  118.8 5.2 %collective-permute-done.5 = f32[112,128]{1,0:T(8,128)} collective-permute-done((f32[112,128]{1,0:T(8,128)S(1)}, f32[112,128]{1,0:T(8,128)}, u32[]{:S(2)}, u32[]{:S(2)}) %collective-permute-start.5) | collective-permute-done | bytes 57376 | tf_op jit(solution)/shard_map/cond/branch_1_fun/ppermute | solution.py:354
  131.0 2.9 %collective-permute-done.7 = f32[112,128]{1,0:T(8,128)S(1)} collective-permute-done((f32[112,128]{1,0:T(8,128)}, f32[112,128]{1,0:T(8,128)S(1)}, u32[]{:S(2)}, u32[]{:S(2)}) %collective-permute-start.7) | collective-permute-done | bytes 57376 | tf_op jit(solution)/shard_map/cond/branch_1_fun/ppermute | solution.py:354
  139.1 1.6 branch_1_fun.14
  140.8 2.7 %collective-permute-start.11 = (bf16[2,144,1024]{2,1,0:T(8,128)(2,1)S(1)}, bf16[2,144,1024]{2,1,0:T(8,128)(2,1)S(1)}, u32[]{:S(2)}, u32[]{:S(2)}) collective-permute-start(bf16[2,144,1024]{2,1,0:T(8,128)(2,1)S(1)} %get-tuple-element.92), channel_id=1, source_target_pairs={{0,24},{8,0},{16,8},{24,16},{32,56},{40,32},{48,40},{56,48},{64,88... | collective-permute-start | bytes 1769480 | tf_op jit(solution)/shard_map/cond/branch_1_fun/ppermute | solution.py:52
  143.5 1.6 collective-permute-start.8
  146.2 4.7 %collective-permute-done.12 = bf16[112,128]{1,0:T(8,128)(2,1)S(1)} collective-permute-done((bf16[112,128]{1,0:T(8,128)(2,1)S(1)}, bf16[112,128]{1,0:T(8,128)(2,1)S(1)}, u32[]{:S(2)}, u32[]{:S(2)}) %collective-permute-start.12) | collective-permute-done | bytes 28704 | tf_op jit(solution)/shard_map/cond/branch_1_fun/ppermute | solution.py:362
  151.0 4.5 %collective-permute-done.13 = bf16[112,128]{1,0:T(8,128)(2,1)S(1)} collective-permute-done((bf16[112,128]{1,0:T(8,128)(2,1)S(1)}, bf16[112,128]{1,0:T(8,128)(2,1)S(1)}, u32[]{:S(2)}, u32[]{:S(2)}) %collective-permute-start.13) | collective-permute-done | bytes 28704 | tf_op jit(solution)/shard_map/cond/branch_1_fun/ppermute | solution.py:362
  156.5 2.2 %collective-permute-done.14 = bf16[112,128]{1,0:T(8,128)(2,1)S(1)} collective-permute-done((bf16[112,128]{1,0:T(8,128)(2,1)S(1)}, bf16[112,128]{1,0:T(8,128)(2,1)S(1)}, u32[]{:S(2)}, u32[]{:S(2)}) %collective-permute-start.14) | collective-permute-done | bytes 28704 | tf_op jit(solution)/shard_map/cond/branch_1_fun/ppermute | solution.py:362
  158.7 6.2 %collective-permute-start.15 = (bf16[4,112,128]{2,1,0:T(8,128)(2,1)S(1)}, bf16[4,112,128]{2,1,0:T(8,128)(2,1)S(1)}, u32[]{:S(2)}, u32[]{:S(2)}) collective-permute-start(bf16[4,112,128]{2,1,0:T(8,128)(2,1)S(1)} %pad_maximum_fusion.own), channel_id=1, source_target_pairs={{0,1},{1,0},{2,3},{3,2},{4,5},{5,4},{6,7},{7,6},{8,9},{9,8},{10,11... | collective-permute-start | bytes 344072 | tf_op jit(solution)/shard_map/cond/branch_1_fun/ppermute | solution.py:363
  165.9 2.7 %branch_1_fun.15 = (bf16[144,1024]{1,0:T(8,128)(2,1)S(1)}, bf16[144,1024]{1,0:T(8,128)(2,1)S(1)}, bf16[144,1024]{1,0:T(8,128)(2,1)}, bf16[144,1024]{1,0:T(8,128)...) custom-call(s32[2]{0:T(128)S(1)} %pad_add_fusion.offsets, ...), custom_call_target="tpu_custom_call" | custom-call | bytes 4718592 | tf_op jit(solution)/shard_map/cond/branch_1_fun/pallas_call | solution.py:206
  173.2 2.0 collective-permute-start.20
  175.2 10.6 %collective-permute-done.16.refs_1_ = bf16[144,1024]{1,0:T(8,128)(2,1)S(1)} collective-permute-done((bf16[144,1024]{1,0:T(8,128)(2,1)S(1)}, bf16[144,1024]{1,0:T(8,128)(2,1)S(1)}, u32[]{:S(2)}, u32[]{:S(2)}) %collective-permute-start.16) | collective-permute-done | bytes 294944 | tf_op jit(solution)/shard_map/cond/branch_1_fun/ppermute | solution.py:52
  189.7 3.3 %branch_1_fun.16._ = bf16[2048,128]{1,0:T(8,128)(2,1)} custom-call(s32[2]{0:T(128)S(1)} %pad_add_fusion.1.where, s32[8,128]{1,0:T(8,128)S(1)} %get-tuple-element.50.mine, s32[32]{0:T(128)S(1)} %copy-done.34, f32[2048,128]{1,0:T(8,128)S(1)} %copy-done.1, bf16[4,112,128]{2,1,0:T(8,128)(2,1)S(1)} %copy-done.16, bf16[4,112,128]{2,1,0:T(8,128)(2,1)S(1)} %copy-done.24, ...), custom_call_target="tpu_custom_call" | custom-call | flops 33554432 | bytes 2097152 | tf_op jit(solution)/shard_map/cond/branch_1_fun/pallas_call | solution.py:465
  195.7 2.2 %collective-permute-start.22 = (f32[128,128]{1,0:T(8,128)S(1)}, f32[128,128]{1,0:T(8,128)S(1)}, u32[]{:S(2)}, u32[]{:S(2)}) collective-permute-start(f32[128,128]{1,0:T(8,128)S(1)} %branch_1_fun.18), channel_id=1, source_target_pairs={{0,1},{1,0},{2,3},{3,2},{4,5},{5,4},{6,7},{7,6},{8,9},{9,8},{10,11... | collective-permute-start | bytes 196616 | tf_op jit(solution)/shard_map/cond/branch_1_fun/ppermute | solution.py:375
  198.9 3.1 %collective-permute-done.23 = f32[128,128]{1,0:T(8,128)S(1)} collective-permute-done((f32[128,128]{1,0:T(8,128)S(1)}, f32[128,128]{1,0:T(8,128)S(1)}, u32[]{:S(2)}, u32[]{:S(2)}) %collective-permute-start.23) | collective-permute-done | bytes 65568 | tf_op jit(solution)/shard_map/cond/branch_1_fun/ppermute | solution.py:375
  202.0 2.8 %collective-permute-start.24 = (f32[128,128]{1,0:T(8,128)S(1)}, f32[128,128]{1,0:T(8,128)S(1)}, u32[]{:S(2)}, u32[]{:S(2)}) collective-permute-start(f32[128,128]{1,0:T(8,128)S(1)} %add.150), channel_id=1, source_target_pairs={{0,6},{1,7},{2,4},{3,5},{4,2},{5,3},{6,0},{7,1},{8,14},{9,15},{10,... | collective-permute-start | bytes 196616 | tf_op jit(solution)/shard_map/cond/branch_1_fun/ppermute | solution.py:375
  204.8 1.7 collective-permute-done.24
  (116 shorter events, 35.0 us)
Async XLA Ops:
  17.2 79.5 %all-to-all-start.3 = ((bf16[16,144,1024]{2,1,0:T(8,128)(2,1)}), bf16[16,144,1024]{2,1,0:T(8,128)(2,1)}, u32[]{:S(2)}, u32[]{:S(2)}) async-start(bf16[16,144,1024]{2,1,0:T(8,128)(2,1)} %copy-done), calls=%async_computation.4 | async-start | bytes 9437184 | tf_op jit(solution)/shard_map/cond/branch_1_fun/all_to_all | solution.py:566
  24.9 161.7 %reduce-scatter.5.cloned.1.call-start = ((), (), s32[]{:S(2)}) async-start(), calls=%async_computation.7 | async-start | bytes 9437184 | tf_op jit(solution)/shard_map/cond/branch_1_fun/reduce_scatter | solution.py:591
  96.7 38.0 %collective-permute-start = (bf16[4,144,1024]{2,1,0:T(8,128)(2,1)}, bf16[4,144,1024]{2,1,0:T(8,128)(2,1)S(1)}, u32[]{:S(2)}, u32[]{:S(2)}) collective-permute-start(bf16[4,144,1024]{2,1,0:T(8,128)(2,1)} %get-tuple-element.72), channel_id=1, source_target_pairs={{0,32},{8,40},{16,48},{24,56},{32,64},{40,72},{48,80},{56,88},{64,... | collective-permute-start | bytes 3538952 | tf_op jit(solution)/shard_map/cond/branch_1_fun/ppermute | solution.py:52
  96.8 38.0 %collective-permute-start.1 = (bf16[4,144,1024]{2,1,0:T(8,128)(2,1)}, bf16[4,144,1024]{2,1,0:T(8,128)(2,1)S(1)}, u32[]{:S(2)}, u32[]{:S(2)}) collective-permute-start(bf16[4,144,1024]{2,1,0:T(8,128)(2,1)} %get-tuple-element.73), channel_id=1, source_target_pairs={{0,96},{8,104},{16,112},{24,120},{32,0},{40,8},{48,16},{56,24},{64... | collective-permute-start | bytes 3538952 | tf_op jit(solution)/shard_map/cond/branch_1_fun/ppermute | solution.py:52
  99.5 35.3 %collective-permute-start.2 = (bf16[4,144,1024]{2,1,0:T(8,128)(2,1)}, bf16[4,144,1024]{2,1,0:T(8,128)(2,1)S(1)}, u32[]{:S(2)}, u32[]{:S(2)}) collective-permute-start(bf16[4,144,1024]{2,1,0:T(8,128)(2,1)} %copy-done.25), channel_id=1, source_target_pairs={{0,8},{8,16},{16,24},{24,0},{32,40},{40,48},{48,56},{56,32},{64,72... | collective-permute-start | bytes 3538952 | tf_op jit(solution)/shard_map/cond/branch_1_fun/ppermute | solution.py:52
  101.4 33.4 %collective-permute-start.3 = (bf16[4,144,1024]{2,1,0:T(8,128)(2,1)}, bf16[4,144,1024]{2,1,0:T(8,128)(2,1)}, u32[]{:S(2)}, u32[]{:S(2)}) collective-permute-start(bf16[4,144,1024]{2,1,0:T(8,128)(2,1)} %get-tuple-element.75), channel_id=1, source_target_pairs={{0,24},{8,0},{16,8},{24,16},{32,56},{40,32},{48,40},{56,48},{64,88... | collective-permute-start | bytes 3538952 | tf_op jit(solution)/shard_map/cond/branch_1_fun/ppermute | solution.py:52
  109.4 5.3 %collective-permute-start.4 = (f32[448,128]{1,0:T(8,128)}, f32[448,128]{1,0:T(8,128)}, u32[]{:S(2)}, u32[]{:S(2)}) collective-permute-start(f32[448,128]{1,0:T(8,128)} %constant_dynamic-slice_fusion.3), channel_id=1, source_target_pairs={{0,1},{1,0},{2,3},{3,2},{4,5},{5,4},{6,7},{7,6},{8,9},{9,8},{10,11... | collective-permute-start | bytes 688136 | tf_op jit(solution)/shard_map/cond/branch_1_fun/ppermute | solution.py:350
  117.2 6.8 %collective-permute-start.5 = (f32[112,128]{1,0:T(8,128)S(1)}, f32[112,128]{1,0:T(8,128)}, u32[]{:S(2)}, u32[]{:S(2)}) collective-permute-start(f32[112,128]{1,0:T(8,128)S(1)} %get-tuple-element.128), channel_id=1, source_target_pairs={{0,2},{1,3},{2,4},{3,5},{4,6},{5,7},{6,0},{7,1},{8,10},{9,11},{10,... | collective-permute-start | bytes 172040 | tf_op jit(solution)/shard_map/cond/branch_1_fun/ppermute | solution.py:354
  124.0 5.5 %collective-permute-start.6 = (f32[112,128]{1,0:T(8,128)}, f32[112,128]{1,0:T(8,128)}, u32[]{:S(2)}, u32[]{:S(2)}) collective-permute-start(f32[112,128]{1,0:T(8,128)} %get-tuple-element.126), channel_id=1, source_target_pairs={{0,4},{1,5},{2,6},{3,7},{4,0},{5,1},{6,2},{7,3},{8,12},{9,13},{10,... | collective-permute-start | bytes 172040 | tf_op jit(solution)/shard_map/cond/branch_1_fun/ppermute | solution.py:354
  128.5 37.4 %copy-start.5 = (bf16[4,144,1024]{2,1,0:T(8,128)(2,1)S(1)}, bf16[4,144,1024]{2,1,0:T(8,128)(2,1)}, u32[]{:S(2)}) copy-start(bf16[4,144,1024]{2,1,0:T(8,128)(2,1)} %copy-done.4) | copy-start | bytes 3538948 | tf_op jit(solution)/shard_map/cond
  128.5 37.4 %copy-start.6 = (bf16[4,144,1024]{2,1,0:T(8,128)(2,1)S(1)}, bf16[4,144,1024]{2,1,0:T(8,128)(2,1)}, u32[]{:S(2)}) copy-start(bf16[4,144,1024]{2,1,0:T(8,128)(2,1)} %get-tuple-element.96.refs_5_) | copy-start | bytes 3538948 | tf_op jit(solution)/shard_map/cond
  129.5 4.3 %collective-permute-start.7 = (f32[112,128]{1,0:T(8,128)}, f32[112,128]{1,0:T(8,128)S(1)}, u32[]{:S(2)}, u32[]{:S(2)}) collective-permute-start(f32[112,128]{1,0:T(8,128)} %get-tuple-element.127), channel_id=1, source_target_pairs={{0,6},{1,7},{2,0},{3,1},{4,2},{5,3},{6,4},{7,5},{8,14},{9,15},{10,... | collective-permute-start | bytes 172040 | tf_op jit(solution)/shard_map/cond/branch_1_fun/ppermute | solution.py:354
  140.7 25.1 %collective-permute-start.10 = (bf16[2,144,1024]{2,1,0:T(8,128)(2,1)S(1)}, bf16[2,144,1024]{2,1,0:T(8,128)(2,1)S(1)}, u32[]{:S(2)}, u32[]{:S(2)}) collective-permute-start(bf16[2,144,1024]{2,1,0:T(8,128)(2,1)S(1)} %get-tuple-element.91), channel_id=1, source_target_pairs={{0,8},{8,16},{16,24},{24,0},{32,40},{40,48},{48,56},{56,32},{64,72... | collective-permute-start | bytes 1769480 | tf_op jit(solution)/shard_map/cond/branch_1_fun/ppermute | solution.py:52
  140.8 25.1 %collective-permute-start.11 = (bf16[2,144,1024]{2,1,0:T(8,128)(2,1)S(1)}, bf16[2,144,1024]{2,1,0:T(8,128)(2,1)S(1)}, u32[]{:S(2)}, u32[]{:S(2)}) collective-permute-start(bf16[2,144,1024]{2,1,0:T(8,128)(2,1)S(1)} %get-tuple-element.92), channel_id=1, source_target_pairs={{0,24},{8,0},{16,8},{24,16},{32,56},{40,32},{48,40},{56,48},{64,88... | collective-permute-start | bytes 1769480 | tf_op jit(solution)/shard_map/cond/branch_1_fun/ppermute | solution.py:52
  143.5 22.4 %collective-permute-start.8 = (bf16[2,144,1024]{2,1,0:T(8,128)(2,1)S(1)}, bf16[2,144,1024]{2,1,0:T(8,128)(2,1)S(1)}, u32[]{:S(2)}, u32[]{:S(2)}) collective-permute-start(bf16[2,144,1024]{2,1,0:T(8,128)(2,1)S(1)} %get-tuple-element.89), channel_id=1, source_target_pairs={{0,32},{8,40},{16,48},{24,56},{32,64},{40,72},{48,80},{56,88},{64,... | collective-permute-start | bytes 1769480 | tf_op jit(solution)/shard_map/cond/branch_1_fun/ppermute | solution.py:52
  145.1 20.8 %collective-permute-start.9 = (bf16[2,144,1024]{2,1,0:T(8,128)(2,1)S(1)}, bf16[2,144,1024]{2,1,0:T(8,128)(2,1)S(1)}, u32[]{:S(2)}, u32[]{:S(2)}) collective-permute-start(bf16[2,144,1024]{2,1,0:T(8,128)(2,1)S(1)} %get-tuple-element.90), channel_id=1, source_target_pairs={{0,96},{8,104},{16,112},{24,120},{32,0},{40,8},{48,16},{56,24},{64... | collective-permute-start | bytes 1769480 | tf_op jit(solution)/shard_map/cond/branch_1_fun/ppermute | solution.py:52
  146.2 4.7 %collective-permute-start.12 = (bf16[112,128]{1,0:T(8,128)(2,1)S(1)}, bf16[112,128]{1,0:T(8,128)(2,1)S(1)}, u32[]{:S(2)}, u32[]{:S(2)}) collective-permute-start(bf16[112,128]{1,0:T(8,128)(2,1)S(1)} %add_convert_fusion), channel_id=1, source_target_pairs={{0,2},{1,3},{2,4},{3,5},{4,6},{5,7},{6,0},{7,1},{8,10},{9,11},{10,... | collective-permute-start | bytes 86024 | tf_op jit(solution)/shard_map/cond/branch_1_fun/ppermute | solution.py:362
  150.9 4.7 %collective-permute-start.13 = (bf16[112,128]{1,0:T(8,128)(2,1)S(1)}, bf16[112,128]{1,0:T(8,128)(2,1)S(1)}, u32[]{:S(2)}, u32[]{:S(2)}) collective-permute-start(bf16[112,128]{1,0:T(8,128)(2,1)S(1)} %add_convert_fusion), channel_id=1, source_target_pairs={{0,4},{1,5},{2,6},{3,7},{4,0},{5,1},{6,2},{7,3},{8,12},{9,13},{10,... | collective-permute-start | bytes 86024 | tf_op jit(solution)/shard_map/cond/branch_1_fun/ppermute | solution.py:362
  155.6 3.1 %collective-permute-start.14 = (bf16[112,128]{1,0:T(8,128)(2,1)S(1)}, bf16[112,128]{1,0:T(8,128)(2,1)S(1)}, u32[]{:S(2)}, u32[]{:S(2)}) collective-permute-start(bf16[112,128]{1,0:T(8,128)(2,1)S(1)} %add_convert_fusion), channel_id=1, source_target_pairs={{0,6},{1,7},{2,0},{3,1},{4,2},{5,3},{6,4},{7,5},{8,14},{9,15},{10,... | collective-permute-start | bytes 86024 | tf_op jit(solution)/shard_map/cond/branch_1_fun/ppermute | solution.py:362
  158.7 10.0 %copy-start.15 = (bf16[4,112,128]{2,1,0:T(8,128)(2,1)}, bf16[4,112,128]{2,1,0:T(8,128)(2,1)S(1)}, u32[]{:S(2)}) copy-start(bf16[4,112,128]{2,1,0:T(8,128)(2,1)S(1)} %pad_maximum_fusion.own) | copy-start | bytes 344068 | tf_op jit(solution)/shard_map/cond
  158.7 28.0 %copy-start.34 = (s32[32]{0:T(128)S(1)}, s32[32]{0:T(128)}, u32[]{:S(2)}) copy-start(s32[32]{0:T(128)} %copy-done.33) | copy-start | bytes 388 | tf_op jit(solution)/shard_map/cond
  158.7 7.2 %collective-permute-start.15 = (bf16[4,112,128]{2,1,0:T(8,128)(2,1)S(1)}, bf16[4,112,128]{2,1,0:T(8,128)(2,1)S(1)}, u32[]{:S(2)}, u32[]{:S(2)}) collective-permute-start(bf16[4,112,128]{2,1,0:T(8,128)(2,1)S(1)} %pad_maximum_fusion.own), channel_id=1, source_target_pairs={{0,1},{1,0},{2,3},{3,2},{4,5},{5,4},{6,7},{7,6},{8,9},{9,8},{10,11... | collective-permute-start | bytes 344072 | tf_op jit(solution)/shard_map/cond/branch_1_fun/ppermute | solution.py:363
  170.1 15.8 %collective-permute-start.16 = (bf16[144,1024]{1,0:T(8,128)(2,1)S(1)}, bf16[144,1024]{1,0:T(8,128)(2,1)S(1)}, u32[]{:S(2)}, u32[]{:S(2)}) collective-permute-start(bf16[144,1024]{1,0:T(8,128)(2,1)S(1)} %get-tuple-element.100), channel_id=1, source_target_pairs={{0,8},{8,16},{16,24},{24,0},{32,40},{40,48},{48,56},{56,32},{64,72... | collective-permute-start | bytes 884744 | tf_op jit(solution)/shard_map/cond/branch_1_fun/ppermute | solution.py:52
  170.1 22.9 %collective-permute-start.17 = (bf16[144,1024]{1,0:T(8,128)(2,1)}, bf16[144,1024]{1,0:T(8,128)(2,1)S(1)}, u32[]{:S(2)}, u32[]{:S(2)}) collective-permute-start(bf16[144,1024]{1,0:T(8,128)(2,1)} %get-tuple-element.101), channel_id=1, source_target_pairs={{0,16},{8,24},{16,0},{24,8},{32,48},{40,56},{48,32},{56,40},{64,80... | collective-permute-start | bytes 884744 | tf_op jit(solution)/shard_map/cond/branch_1_fun/ppermute | solution.py:52
  171.5 21.5 %collective-permute-start.18 = (bf16[144,1024]{1,0:T(8,128)(2,1)}, bf16[144,1024]{1,0:T(8,128)(2,1)S(1)}, u32[]{:S(2)}, u32[]{:S(2)}) collective-permute-start(bf16[144,1024]{1,0:T(8,128)(2,1)} %get-tuple-element.102), channel_id=1, source_target_pairs={{0,24},{8,0},{16,8},{24,16},{32,56},{40,32},{48,40},{56,48},{64,88... | collective-permute-start | bytes 884744 | tf_op jit(solution)/shard_map/cond/branch_1_fun/ppermute | solution.py:52
  172.8 20.2 %collective-permute-start.19 = (bf16[144,1024]{1,0:T(8,128)(2,1)}, bf16[144,1024]{1,0:T(8,128)(2,1)S(1)}, u32[]{:S(2)}, u32[]{:S(2)}) collective-permute-start(bf16[144,1024]{1,0:T(8,128)(2,1)} %get-tuple-element.103), channel_id=1, source_target_pairs={{0,32},{8,40},{16,48},{24,56},{32,64},{40,72},{48,80},{56,88},{64,... | collective-permute-start | bytes 884744 | tf_op jit(solution)/shard_map/cond/branch_1_fun/ppermute | solution.py:52
  173.2 19.8 %collective-permute-start.20 = (bf16[144,1024]{1,0:T(8,128)(2,1)}, bf16[144,1024]{1,0:T(8,128)(2,1)S(1)}, u32[]{:S(2)}, u32[]{:S(2)}) collective-permute-start(bf16[144,1024]{1,0:T(8,128)(2,1)} %get-tuple-element.104), channel_id=1, source_target_pairs={{0,64},{8,72},{16,80},{24,88},{32,96},{40,104},{48,112},{56,120},{... | collective-permute-start | bytes 884744 | tf_op jit(solution)/shard_map/cond/branch_1_fun/ppermute | solution.py:52
  186.6 7.5 %collective-permute-start.21 = (bf16[144,1024]{1,0:T(8,128)(2,1)}, bf16[144,1024]{1,0:T(8,128)(2,1)S(1)}, u32[]{:S(2)}, u32[]{:S(2)}) collective-permute-start(bf16[144,1024]{1,0:T(8,128)(2,1)} %get-tuple-element.105), channel_id=1, source_target_pairs={{0,96},{8,104},{16,112},{24,120},{32,0},{40,8},{48,16},{56,24},{64... | collective-permute-start | bytes 884744 | tf_op jit(solution)/shard_map/cond/branch_1_fun/ppermute | solution.py:52
  192.9 13.5 %copy-start.2 = (f32[2048,128]{1,0:T(8,128)S(1)}, f32[2048,128]{1,0:T(8,128)}, u32[]{:S(2)}) copy-start(f32[2048,128]{1,0:T(8,128)} %reduce-scatter.5.cloned.1.call-done.base) | copy-start | bytes 3145732 | tf_op jit(solution)/shard_map/cond
  195.7 3.1 %collective-permute-start.22 = (f32[128,128]{1,0:T(8,128)S(1)}, f32[128,128]{1,0:T(8,128)S(1)}, u32[]{:S(2)}, u32[]{:S(2)}) collective-permute-start(f32[128,128]{1,0:T(8,128)S(1)} %branch_1_fun.18), channel_id=1, source_target_pairs={{0,1},{1,0},{2,3},{3,2},{4,5},{5,4},{6,7},{7,6},{8,9},{9,8},{10,11... | collective-permute-start | bytes 196616 | tf_op jit(solution)/shard_map/cond/branch_1_fun/ppermute | solution.py:375
  198.8 3.2 %collective-permute-start.23 = (f32[128,128]{1,0:T(8,128)S(1)}, f32[128,128]{1,0:T(8,128)S(1)}, u32[]{:S(2)}, u32[]{:S(2)}) collective-permute-start(f32[128,128]{1,0:T(8,128)S(1)} %add.149), channel_id=1, source_target_pairs={{0,2},{1,3},{2,0},{3,1},{4,6},{5,7},{6,4},{7,5},{8,10},{9,11},{10,... | collective-permute-start | bytes 196616 | tf_op jit(solution)/shard_map/cond/branch_1_fun/ppermute | solution.py:375
  202.0 4.5 %collective-permute-start.24 = (f32[128,128]{1,0:T(8,128)S(1)}, f32[128,128]{1,0:T(8,128)S(1)}, u32[]{:S(2)}, u32[]{:S(2)}) collective-permute-start(f32[128,128]{1,0:T(8,128)S(1)} %add.150), channel_id=1, source_target_pairs={{0,6},{1,7},{2,4},{3,5},{4,2},{5,3},{6,0},{7,1},{8,14},{9,15},{10,... | collective-permute-start | bytes 196616 | tf_op jit(solution)/shard_map/cond/branch_1_fun/ppermute | solution.py:375
  (28 other events, 87.1 us)
Sparse Core Ops, SparseCore 0:
  96.9 61.4 reduce-scatter.4

commit v9 on v8

--- a/solution.py
+++ b/solution.py
@@ -269,6 +269,31 @@
                 move(out, source)
 
 
+def base_kernel(hidden, weight, out):
+    out[...] = jnp.dot(hidden[...], weight[...], preferred_element_type=jnp.float32)
+
+
+def base_product(hidden, weight, block=256):
+    rows, width = hidden.shape
+    columns = weight.shape[1]
+    return pl.pallas_call(
+        base_kernel,
+        grid=(rows // block,),
+        out_shape=jax.ShapeDtypeStruct((rows, columns), jnp.float32),
+        in_specs=[
+            pl.BlockSpec((block, width), lambda i: (i, 0)),
+            pl.BlockSpec((width, columns), lambda i: (0, 0)),
+        ],
+        out_specs=pl.BlockSpec((block, columns), lambda i: (i, 0)),
+        compiler_params=pltpu.CompilerParams(vmem_limit_bytes=14 << 20),
+        cost_estimate=pl.CostEstimate(
+            flops=2 * rows * width * columns,
+            bytes_accessed=hidden.size * 2 + weight.size * 2 + rows * columns * 4,
+            transcendentals=0,
+        ),
+    )(hidden, weight)
+
+
 def paired(hidden, mine, i, pairs, cap, first, second):
     spots = [pl.multiple_of(mine[ORDER, j] * cap, cap) for j in (i, i + pairs)]
     rows = jnp.concatenate([hidden[pl.ds(spot, cap), :] for spot in spots], axis=0)
@@ -282,9 +307,11 @@
     return jnp.where(lane < first.shape[0], product[:cap], product[cap:])
 
 
-def low_main_kernel(cap, mine, hidden, main, out):
+def low_kernel(cap, mine, hidden, main, *refs):
+    extras, out = refs[:-1], refs[-1]
     rank = out.shape[1] // 2
     pairs = out.shape[0] // cap
+    full = pairs - EXTRA
 
     def weights(j):
         place = mine[PLACE, j]
@@ -296,39 +323,27 @@
         out[at, :] = paired(hidden, mine, i, pairs, cap, weights(i), weights(i + pairs))
         return carry
 
-    lax.fori_loop(0, pairs, body, 0, unroll=2)
-
-
-def low_extra_kernel(first, cap, mine, hidden, *refs):
-    extras, out = refs[:-1], refs[-1]
-    rank = out.shape[1] // 2
-    for i in range(2):
-        spots = [pl.multiple_of(mine[ORDER, first + 2 * u + i] * cap, cap) for u in range(2)]
-        rows = jnp.concatenate([hidden[pl.ds(spot, cap), :] for spot in spots], axis=0)
-        part = slice(i * rank, (i + 1) * rank)
-        product = lax.dot_general(
-            rows,
-            jnp.concatenate([extras[0][part, :], extras[1][part, :]], axis=0),
-            (((1,), (1,)), ((), ())),
-            preferred_element_type=jnp.float32,
-        )
-        lane = lax.broadcasted_iota(jnp.int32, (cap, 2 * rank), 1)
-        out[i * cap : (i + 1) * cap, :] = jnp.where(lane < rank, product[:cap], product[cap:])
-
-
-def low_partial(kernel, pairs, cap, rank, mine, hidden, weights):
+    lax.fori_loop(0, full, body, 0, unroll=2)
+    for e in range(EXTRA):
+        i = full + e
+        late = extras[e // 2][e % 2 * rank : (e % 2 + 1) * rank, :]
+        out[i * cap : (i + 1) * cap, :] = paired(hidden, mine, i, pairs, cap, weights(i), late)
+
+
+def low_partial(mine, hidden, main, extras, cap, rank):
+    pairs = hidden.shape[0] // cap // 2
     return pl.pallas_call(
-        kernel,
+        functools.partial(low_kernel, cap),
         out_shape=jax.ShapeDtypeStruct((pairs * cap, 2 * rank), jnp.float32),
-        in_specs=[SMEM] + [VMEM] * (1 + len(weights)),
+        in_specs=[SMEM] + [VMEM] * (2 + len(extras)),
         out_specs=VMEM,
-        compiler_params=pltpu.CompilerParams(vmem_limit_bytes=10 << 20),
+        compiler_params=pltpu.CompilerParams(vmem_limit_bytes=12 << 20),
         cost_estimate=pl.CostEstimate(
             flops=pairs * cap * rank * 4 * hidden.shape[1],
-            bytes_accessed=sum(w.size for w in weights) * 2,
+            bytes_accessed=(hidden.size + main.size) * 2,
             transcendentals=0,
         ),
-    )(mine, hidden, *weights)
+    )(mine, hidden, main, *extras)
 
 
 def turn(step):
@@ -363,19 +378,6 @@
     return own, lax.ppermute(own, "tp", swap())
 
 
-def low_rank_doubling(partial):
-    tp_count = lax.axis_size("tp")
-    last = tp_count // 2 - 1
-    z_of = lambda i: i // 2
-    for partner in (
-        lambda i: i ^ 1,
-        lambda i: (z_of(i) ^ 1) * 2 + i % 2,
-        lambda i: (last - z_of(i)) * 2 + i % 2,
-    ):
-        partial += lax.ppermute(partial, "tp", [(i, partner(i)) for i in range(tp_count)])
-    return partial
-
-
 def blend(base, out, counts, mine, j, both, ups, cap):
     rank = both.shape[1] // 2
     lane = lax.broadcasted_iota(jnp.int32, both.shape, 1)
@@ -389,21 +391,23 @@
         g = mine[ORDER, j[n]]
         here = pl.ds(pl.multiple_of(g * cap, cap), cap)
         merged = base[here, :] + ADAPTER_SCALE * delta[n * cap : (n + 1) * cap]
-        out(n, here, jnp.where(rows < counts[g], merged, 0.0).astype(jnp.bfloat16))
-
-
-def out_main_kernel(where, mine, counts, base, own, other, main, out, low):
+        out[here, :] = jnp.where(rows < counts[g], merged, 0.0).astype(out.dtype)
+
+
+def out_kernel(where, mine, counts, base, own, other, main, *refs):
+    extras, out, low = refs[:2], refs[2], refs[3]
     groups = counts.shape[0]
     cap = base.shape[0] // groups
     chips, piece, rank = own.shape[0], own.shape[1], own.shape[2] // 2
     lanes = base.shape[1]
     z, core = where[0], where[1]
     steps = rank // 16
-    pairs = low.shape[0] // cap
+    pairs = groups // 2
+    full = pairs - EXTRA
     for d in range(chips):
         quarter = lax.rem(z - d + chips, chips)
         for ref, half in ((own, core), (other, 1 - core)):
-            at = pl.multiple_of((half * chips + quarter) * piece, 16)
+            at = pl.multiple_of((half * chips + quarter) * piece, piece)
             low[pl.ds(at, piece), :] = ref[d]
 
     def up(j):
@@ -415,88 +419,44 @@
             for part in range(steps)
         ]
 
-    def store(n, here, value):
-        out[here, :] = value
-
     def body(i, carry):
         both = low[pl.ds(pl.multiple_of(i * cap, cap), cap), :]
-        spots = (i, i + pairs)
-        blend(base, store, counts, mine, spots, both, up(i) + up(i + pairs), cap)
+        blend(base, out, counts, mine, (i, i + pairs), both, up(i) + up(i + pairs), cap)
         return carry
 
-    lax.fori_loop(0, pairs, body, 0, unroll=2)
-
-
-def out_extra_kernel(mine, counts, base, low, first_pack, second_pack, _, out, blocks, sems):
-    groups = counts.shape[0]
-    cap = base.shape[0] // groups
-    rank = low.shape[1] // 2
-    lanes = base.shape[1]
-    steps = rank // 16
-    first = groups - EXTRA
-    copies = []
-    for i in range(2):
-        both = low[i * cap : (i + 1) * cap, :].astype(jnp.bfloat16)
-        ups = [
-            pack[:, (i * steps + part) * lanes : (i * steps + part + 1) * lanes]
-            for pack in (first_pack, second_pack)
+    lax.fori_loop(0, full, body, 0, unroll=2)
+    for e in range(EXTRA):
+        i = full + e
+        pack = extras[e // 2]
+        late = [
+            pack[:, (e % 2 * steps + part) * lanes : (e % 2 * steps + part + 1) * lanes]
             for part in range(steps)
         ]
-
-        def store(n, here, value, i=i):
-            blocks[2 * i + n] = value
-            copy = pltpu.make_async_copy(
-                blocks.at[2 * i + n], out.at[here, :], sems.at[2 * i + n]
-            )
-            copy.start()
-            copies.append(copy)
-
-        blend(base, store, counts, mine, (first + i, first + 2 + i), both, ups, cap)
-    for copy in copies:
-        copy.wait()
+        both = low[i * cap : (i + 1) * cap, :]
+        blend(base, out, counts, mine, (i, i + pairs), both, up(i) + late, cap)
 
 
 def whole(array):
     return pl.BlockSpec(array.shape, lambda i: (0,) * array.ndim)
 
 
-def combine_main(where, mine, counts, base, own, other, main, rank):
+def combine(where, mine, counts, base, own, other, main, extras, rank):
     packs = pl.BlockSpec((main.shape[0], 16, main.shape[2]), lambda i: (0, rank // 8, 0))
+    pack = pl.BlockSpec((16, main.shape[2]), lambda i: (rank // 8, 0))
     return pl.pallas_call(
-        out_main_kernel,
+        out_kernel,
         grid=(1,),
         out_shape=jax.ShapeDtypeStruct(base.shape, jnp.bfloat16),
-        in_specs=[SMEM, SMEM, SMEM, whole(base), whole(own), whole(other), packs],
+        in_specs=[SMEM, SMEM, SMEM, whole(base), whole(own), whole(other), packs, pack, pack],
         out_specs=whole(base),
         scratch_shapes=[
             pltpu.VMEM((2 * own.shape[0] * own.shape[1], own.shape[2]), jnp.bfloat16)
         ],
-        compiler_params=pltpu.CompilerParams(vmem_limit_bytes=6 << 20),
+        compiler_params=pltpu.CompilerParams(vmem_limit_bytes=8 << 20),
         cost_estimate=pl.CostEstimate(
             flops=base.size * rank * 2, bytes_accessed=base.size * 8, transcendentals=0
         ),
-    )(where, mine, counts, base, own, other, main)
-
-
-def combine_extra(mine, counts, base, low, extras, out, rank):
-    pack = pl.BlockSpec((16, extras[0].shape[1]), lambda i: (rank // 8, 0))
-    cap = base.shape[0] // counts.shape[0]
-    return pl.pallas_call(
-        out_extra_kernel,
-        grid=(1,),
-        out_shape=jax.ShapeDtypeStruct(out.shape, out.dtype),
-        in_specs=[SMEM, SMEM, whole(base), whole(low), pack, pack, HBM],
-        out_specs=HBM,
-        input_output_aliases={6: 0},
-        scratch_shapes=[
-            pltpu.VMEM((EXTRA, cap, base.shape[1]), jnp.bfloat16),
-            pltpu.SemaphoreType.DMA((EXTRA,)),
-        ],
-        compiler_params=pltpu.CompilerParams(vmem_limit_bytes=4 << 20),
-        cost_estimate=pl.CostEstimate(
-            flops=base.size * rank // 4, bytes_accessed=base.size * 4, transcendentals=0
-        ),
-    )(mine, counts, base, low, *extras, out)
+    )(where, mine, counts, base, own, other, main, *extras)
 
 
 def on_device(
@@ -560,21 +520,11 @@
         turned = ((0, 1), (0, 2), (0, -1), (1, 0), (2, 0), (-1, 0))
         send = lambda values, ways: [shift(v, *way) for v, way in zip(values, ways)]
         barrier = lax.optimization_barrier
-        (main_sent,) = gather_call(
-            main_kernel, (dp_count,), dp_count, (served,), down_weights, up_weights
-        )
-        main = lax.all_to_all(main_sent, "dp", 0, 0, tiled=True)
-        unit = main_sent.shape[1:]
-        dtype = main_sent.dtype
+        scalars = (me_row, served, mine)
         gathered = gather_call(
-            functools.partial(extra_kernel, soon),
-            (4,) * 4,
-            16,
-            (me_row, served, mine),
-            down_weights,
-            up_weights,
-            50,
-        )
+            functools.partial(extra_kernel, soon), (4,) * 4, 16, scalars, down_weights, up_weights
+        )
+        fresh = send(gathered, moves)
         later_served, _ = barrier((served, gathered))
         later = gather_call(
             functools.partial(extra_kernel, late),
@@ -583,21 +533,22 @@
             (me_row, later_served, mine),
             down_weights,
             up_weights,
-            50,
-        )
-        base_terms = jnp.dot(hidden, value_weight, preferred_element_type=jnp.float32)
-        main, gathered, later, base_terms = barrier((main, gathered, later, base_terms))
-        fresh = send(gathered, moves)
+        )
+        main_served, _ = barrier((served, later))
+        (main_sent,) = gather_call(
+            main_kernel, (dp_count,), dp_count, (main_served,), down_weights, up_weights
+        )
+        base_hidden, _ = barrier((hidden, main_sent))
+        base_terms = base_product(base_hidden, value_weight)
         base = lax.psum_scatter(base_terms, "tp", scatter_dimension=1, tiled=True)
-        pairs = (groups - EXTRA) // 2
-        partial = low_partial(
-            functools.partial(low_main_kernel, cap), pairs, cap, rank, mine, hidden, (main,)
-        )
-        fresh, near, summed = barrier((fresh, later[:4], low_rank_down(partial)))
+        unit = main_sent.shape[1:]
+        dtype = main_sent.dtype
+        fresh, near, main_sent, _ = barrier((fresh, later[:4], main_sent, base_terms))
         relayed = vmem_call(
             relay_kernel, ((2,) + unit,) * 4, dtype, (offsets,), (*fresh, *near)
         )
-        near_a, (own, other) = barrier((send(relayed, moves), low_rank_up(summed)))
+        near_a, main_sent = barrier((send(relayed, moves), main_sent))
+        main = lax.all_to_all(main_sent, "dp", 0, 0, tiled=True)
         tree_arrays = [
             (later[4 + h], near_a[2 * h], near_a[2 * h + 1], fresh[2 * h], fresh[2 * h + 1])
             for h in range(2)
@@ -606,11 +557,6 @@
             line_kernel, (unit,) * 8, dtype, (offsets,), tree_arrays[0] + tree_arrays[1]
         )
         got = send(lines[1:4] + lines[5:8], turned)
-        t = lax.axis_index("tp")
-        where = jnp.stack([t // 2, t % 2]).astype(jnp.int32)
-        own, _ = barrier((own, lines))
-        out = combine_main(where, mine, counts, base, own, other, main, rank)
-        got, out = barrier((got, out))
         extras = vmem_call(
             pick_kernel,
             (unit,) * 2,
@@ -618,17 +564,11 @@
             (offsets,),
             (lines[0], *got[:3], lines[4], *got[3:]),
         )
-        extra_partial = low_partial(
-            functools.partial(low_extra_kernel, groups - EXTRA, cap),
-            EXTRA // 2,
-            cap,
-            rank,
-            mine,
-            hidden,
-            extras,
-        )
-        extra_low = low_rank_doubling(extra_partial)
-        return combine_extra(mine, counts, base, extra_low, extras, out, rank)
+        partial = low_partial(mine, hidden, main, extras, cap, rank)
+        own, other = low_rank_up(low_rank_down(partial))
+        t = lax.axis_index("tp")
+        where = jnp.stack([t // 2, t % 2]).astype(jnp.int32)
+        return combine(where, mine, counts, base, own, other, main, extras, rank)
 
     return lax.cond(
         mine[FLAGS, FITS] == 1, narrow, wide, hidden, value_weight, down_weights, up_weights

time: 217 us -> 231 us (1.065)
  local copies, waits for them, and re-layouts: 19.2 us -> 38.9 us
  waiting for transfers between devices: 97.9 us -> 84.9 us
  starting transfers between devices: 44.1 us -> 56.9 us
  matrix products: 6.67 us -> 0 us
  Pallas kernels: 27.3 us -> 32.3 us
    ppermute x14, waiting for transfers between devices: 11.7 us -> 77.8 us  [shift(): return lax.ppermute(value, 'dp', pairs)]
    all_to_all x1, waiting for transfers between devices: 57.6 us -> 0.01 us  [narrow(): main = lax.all_to_all(main_sent, 'dp', 0, 0, tiled=True)]
    cond x66 -> x70, local copies, waits for them, and re-layouts: 15.1 us -> 35.3 us
    ppermute x14, starting transfers between devices: 16 us -> 27.9 us  [shift(): return lax.ppermute(value, 'dp', pairs)]
    ppermute x3, waiting for transfers between devices: 11.4 us -> 2.32 us  [low_rank_up(): lax.ppermute(summed, 'tp', turn(d))]
    ppermute x1, starting transfers between devices: 3.86 us -> 10.8 us  [low_rank_down(): lax.ppermute(cut(partial, (1 - core) * half, half), 'tp', swap())]
    dot_general x1 -> x0, matrix products: 6.67 us -> none  [narrow(): jnp.dot(hidden, value_weight, preferred_element_type=jnp.float32)]
    ppermute x3, waiting for transfers between devices: 9.13 us -> 2.71 us  [low_rank_down(): lax.ppermute(cut(total, (z + d) % chips * piece, piece), 'tp', turn(d))]
  transfers between devices with their start and end apart: 27 -> 24, of which waited for: 14 -> 16; matrix products, arithmetic and copies ran while one was open for 5% -> 0% of each run, Pallas kernels for 9% -> 5%
where the time goes in v9:
time: 231 us; the launch traced here: 230 us
  waiting for transfers between devices  84.9 us (37%)
  starting transfers between devices  56.9 us (25%)
  local copies, waits for them, and re-layouts  38.9 us (17%)
  Pallas kernels  32.3 us (14%)
  between operations  14.1 us (6%)
  loops' own time  3.13 us (1%)
    ppermute x14, waiting for transfers between devices, shift(): return lax.ppermute(value, 'dp', pairs)  77.8 us
    cond x70, local copies, waits for them, and re-layouts  35.3 us
    ppermute x14, starting transfers between devices, shift(): return lax.ppermute(value, 'dp', pairs)  27.9 us
    pallas_call x3, Pallas kernels, gather_call(): pl.pallas_call(kernel, out_shape=[jax.ShapeDtypeStruct((n, 2 * rank + 16,...  11.7 us
    ppermute x1, starting transfers between devices, low_rank_down(): lax.ppermute(cut(partial, (1 - core) * half, half), 'tp', swap())  10.8 us
    ppermute x3, starting transfers between devices, low_rank_down(): lax.ppermute(cut(total, (z + d) % chips * piece, piece), 'tp', turn(d))  6.35 us
    pallas_call x1, Pallas kernels, low_partial(): pl.pallas_call(functools.partial(low_kernel, cap), out_shape=jax.ShapeDty...  5.9 us
    pallas_call x1, Pallas kernels, base_product(): pl.pallas_call(base_kernel, grid=(rows // block,), out_shape=jax.ShapeDty...  5.68 us
  transfers between devices with their start and end apart: 24, of which 16 were waited for; matrix products, arithmetic and copies ran while one was open for 0% of the time, Pallas kernels for 5%

profile of v9, /device:TPU:1, one launch (start us, length us, event | category | flops | bytes accessed | tf_op | source)
XLA Modules:
  0.0 230.4 jit_solution(1380501762461486016)
XLA Ops:
  8.1 1.8 shard_map.75
  11.2 211.6 %conditional.1 = (bf16[2048,128]{1,0:T(8,128)(2,1)S(1)}) conditional(s32[]{:T(128)} %bitcast.20, (s32[32]{0:T(128)S(1)}, bf16[2048,1024]{1,0:T(8,128)(2,1)}, bf16[1024,1024]{1,0:T(8,128)(2,1)}, s32[512]{0:T(512)}, s32[2048]{0:T(1024)}, /*index=5*/s32[]{:T(128)}, bf16[128,64,1024]{2,1,0:T(8,128)(2,1)}, bf16[128,64,128]{2,1,0:T(8,128)(2,1)}) %tuple.16, ...), branch_computations={%region_0.5_spmd, %region_5.7_spmd} | conditional | flops 4598219776 | bytes 375557984 | solution.py:573
  11.5 2.7 %branch_1_fun.9 = (bf16[4,144,1024]{2,1,0:T(8,128)(2,1)}, bf16[4,144,1024]{2,1,0:T(8,128)(2,1)}, bf16[4,144,1024]{2,1,0:T(8,128)(2,1)S(1)}, bf16[4,144,1024]{2,1,0:T(8,128)(2,1)S(1)}) custom-call(s32[1]{0:T(128)} %get-tuple-element.54.me, s32[16,128]{1,0:T(8,128)S(1)} %get-tuple-element.68.served, s32[8,128]{1,0:T(8,128)S(1)} %get-tuple-element.50.mine, ...), custom_call_target="tpu_custom_call" | custom-call | bytes 9437184 | tf_op jit(solution)/shard_map/cond/branch_1_fun/pallas_call | solution.py:188
  16.3 2.6 %copy-done.30 = bf16[128,64,1024]{2,1,0:T(8,128)(2,1)S(1)} copy-done((bf16[128,64,1024]{2,1,0:T(8,128)(2,1)S(1)}, bf16[128,64,1024]{2,1,0:T(8,128)(2,1)}, u32[]{:S(2)}) %copy-start.30) | copy-done | bytes 16777240 | tf_op jit(solution)/shard_map/cond
  19.5 1.3 branch_1_fun.10
  26.3 7.7 %branch_1_fun.11 = bf16[16,144,1024]{2,1,0:T(8,128)(2,1)S(1)} custom-call(s32[16,128]{1,0:T(8,128)S(1)} %get-tuple-element.68.served, bf16[128,64,1024]{2,1,0:T(8,128)(2,1)S(1)} %copy-done.30, bf16[128,64,128]{2,1,0:T(8,128)(2,1)S(1)} %copy-done.32), custom_call_target="tpu_custom_call" | custom-call | bytes 9437184 | tf_op jit(solution)/shard_map/cond/branch_1_fun/pallas_call | solution.py:188
  34.0 2.2 copy-done
  36.2 5.7 %branch_1_fun.12 = f32[2048,1024]{1,0:T(8,128)S(1)} custom-call(bf16[2048,1024]{1,0:T(8,128)(2,1)S(1)} %copy-done.33, bf16[1024,1024]{1,0:T(8,128)(2,1)S(1)} %copy-done.38), custom_call_target="tpu_custom_call" | custom-call | flops 4294967296 | bytes 14680064 | tf_op jit(solution)/shard_map/cond/branch_1_fun/pallas_call | solution.py:279
  41.9 3.3 %copy-done.1 = f32[2048,1024]{1,0:T(8,128)} copy-done((f32[2048,1024]{1,0:T(8,128)}, f32[2048,1024]{1,0:T(8,128)S(1)}, u32[]{:S(2)}) %copy-start.1) | copy-done | bytes 8388632 | tf_op jit(solution)/shard_map/cond
  45.2 2.1 collective-permute-start
  47.3 10.3 %collective-permute-start.1 = (bf16[4,144,1024]{2,1,0:T(8,128)(2,1)}, bf16[4,144,1024]{2,1,0:T(8,128)(2,1)S(1)}, u32[]{:S(2)}, u32[]{:S(2)}) collective-permute-start(bf16[4,144,1024]{2,1,0:T(8,128)(2,1)} %get-tuple-element.58), channel_id=1, source_target_pairs={{0,96},{8,104},{16,112},{24,120},{32,0},{40,8},{48,16},{56,24},{64... | collective-permute-start | bytes 3538952 | tf_op jit(solution)/shard_map/cond/branch_1_fun/ppermute | solution.py:52
  57.6 2.7 %collective-permute-start.3 = (bf16[4,144,1024]{2,1,0:T(8,128)(2,1)}, bf16[4,144,1024]{2,1,0:T(8,128)(2,1)}, u32[]{:S(2)}, u32[]{:S(2)}) collective-permute-start(bf16[4,144,1024]{2,1,0:T(8,128)(2,1)} %copy-done.27), channel_id=1, source_target_pairs={{0,24},{8,0},{16,8},{24,16},{32,56},{40,32},{48,40},{56,48},{64,88... | collective-permute-start | bytes 3538952 | tf_op jit(solution)/shard_map/cond/branch_1_fun/ppermute | solution.py:52
  63.6 20.0 %collective-permute-done.refs_0_.refs_3_ = bf16[4,144,1024]{2,1,0:T(8,128)(2,1)S(1)} collective-permute-done((bf16[4,144,1024]{2,1,0:T(8,128)(2,1)}, bf16[4,144,1024]{2,1,0:T(8,128)(2,1)S(1)}, u32[]{:S(2)}, u32[]{:S(2)}) %collective-permute-start) | collective-permute-done | bytes 1179680 | tf_op jit(solution)/shard_map/cond/branch_1_fun/ppermute | solution.py:52
  83.6 2.1 collective-permute-done.2.refs_2_.refs_8_
  90.0 1.6 branch_1_fun.13
  91.7 2.7 %collective-permute-start.5 = (bf16[2,144,1024]{2,1,0:T(8,128)(2,1)S(1)}, bf16[2,144,1024]{2,1,0:T(8,128)(2,1)S(1)}, u32[]{:S(2)}, u32[]{:S(2)}) collective-permute-start(bf16[2,144,1024]{2,1,0:T(8,128)(2,1)S(1)} %get-tuple-element.81), channel_id=1, source_target_pairs={{0,96},{8,104},{16,112},{24,120},{32,0},{40,8},{48,16},{56,24},{64... | collective-permute-start | bytes 1769480 | tf_op jit(solution)/shard_map/cond/branch_1_fun/ppermute | solution.py:52
  94.3 2.7 %collective-permute-start.7 = (bf16[2,144,1024]{2,1,0:T(8,128)(2,1)S(1)}, bf16[2,144,1024]{2,1,0:T(8,128)(2,1)S(1)}, u32[]{:S(2)}, u32[]{:S(2)}) collective-permute-start(bf16[2,144,1024]{2,1,0:T(8,128)(2,1)S(1)} %get-tuple-element.83), channel_id=1, source_target_pairs={{0,24},{8,0},{16,8},{24,16},{32,56},{40,32},{48,40},{56,48},{64,88... | collective-permute-start | bytes 1769480 | tf_op jit(solution)/shard_map/cond/branch_1_fun/ppermute | solution.py:52
  97.0 9.0 %collective-permute-done.4.refs_1_ = bf16[2,144,1024]{2,1,0:T(8,128)(2,1)S(1)} collective-permute-done((bf16[2,144,1024]{2,1,0:T(8,128)(2,1)S(1)}, bf16[2,144,1024]{2,1,0:T(8,128)(2,1)S(1)}, u32[]{:S(2)}, u32[]{:S(2)}) %collective-permute-start.4) | collective-permute-done | bytes 589856 | tf_op jit(solution)/shard_map/cond/branch_1_fun/ppermute | solution.py:52
  109.7 4.5 %all-to-all-start = ((bf16[16,144,1024]{2,1,0:T(8,128)(2,1)}), bf16[16,144,1024]{2,1,0:T(8,128)(2,1)}, u32[]{:S(2)}, u32[]{:S(2)}) async-start(bf16[16,144,1024]{2,1,0:T(8,128)(2,1)} %copy-done), calls=%async_computation.1 | async-start | bytes 9437184 | tf_op jit(solution)/shard_map/cond/branch_1_fun/all_to_all | solution.py:551
  121.1 2.7 %branch_1_fun.14 = (bf16[144,1024]{1,0:T(8,128)(2,1)S(1)}, bf16[144,1024]{1,0:T(8,128)(2,1)}, bf16[144,1024]{1,0:T(8,128)(2,1)}, bf16[144,1024]{1,0:T(8,128)(2,1...) custom-call(s32[2]{0:T(128)S(1)} %pad_add_fusion.1.offsets, ...), custom_call_target="tpu_custom_call" | custom-call | bytes 4718592 | tf_op jit(solution)/shard_map/cond/branch_1_fun/pallas_call | solution.py:206
  125.2 2.4 %collective-permute-start.10 = (bf16[144,1024]{1,0:T(8,128)(2,1)S(1)}, bf16[144,1024]{1,0:T(8,128)(2,1)S(1)}, u32[]{:S(2)}, u32[]{:S(2)}) collective-permute-start(bf16[144,1024]{1,0:T(8,128)(2,1)S(1)} %get-tuple-element.93), channel_id=1, source_target_pairs={{0,24},{8,0},{16,8},{24,16},{32,56},{40,32},{48,40},{56,48},{64,88... | collective-permute-start | bytes 884744 | tf_op jit(solution)/shard_map/cond/branch_1_fun/ppermute | solution.py:52
  128.8 2.5 %collective-permute-start.12 = (bf16[144,1024]{1,0:T(8,128)(2,1)}, bf16[144,1024]{1,0:T(8,128)(2,1)S(1)}, u32[]{:S(2)}, u32[]{:S(2)}) collective-permute-start(bf16[144,1024]{1,0:T(8,128)(2,1)} %get-tuple-element.96), channel_id=1, source_target_pairs={{0,64},{8,72},{16,80},{24,88},{32,96},{40,104},{48,112},{56,120},{... | collective-permute-start | bytes 884744 | tf_op jit(solution)/shard_map/cond/branch_1_fun/ppermute | solution.py:52
  132.4 38.0 %collective-permute-done.10.refs_3_ = bf16[144,1024]{1,0:T(8,128)(2,1)S(1)} collective-permute-done((bf16[144,1024]{1,0:T(8,128)(2,1)S(1)}, bf16[144,1024]{1,0:T(8,128)(2,1)S(1)}, u32[]{:S(2)}, u32[]{:S(2)}) %collective-permute-start.10) | collective-permute-done | bytes 294944 | tf_op jit(solution)/shard_map/cond/branch_1_fun/ppermute | solution.py:52
  171.0 7.7 %collective-permute-done.12.refs_6_ = bf16[144,1024]{1,0:T(8,128)(2,1)S(1)} collective-permute-done((bf16[144,1024]{1,0:T(8,128)(2,1)}, bf16[144,1024]{1,0:T(8,128)(2,1)S(1)}, u32[]{:S(2)}, u32[]{:S(2)}) %collective-permute-start.12) | collective-permute-done | bytes 294944 | tf_op jit(solution)/shard_map/cond/branch_1_fun/ppermute | solution.py:52
  181.6 5.9 %branch_1_fun.16 = f32[1024,128]{1,0:T(8,128)S(1)} custom-call(s32[8,128]{1,0:T(8,128)S(1)} %get-tuple-element.50.mine, bf16[2048,1024]{1,0:T(8,128)(2,1)} %get-tuple-element.69.hidden, bf16[16,144,1024]{2,1,0:T(8,128)(2,1)} %all-to-all-done.main, bf16[144,1024]{1,0:T(8,128)(2,1)S(1)} %get-tuple-element.98.refs_0_, ...), custom_call_target="tpu_custom_call" | custom-call | flops 268435456 | bytes 8912896 | tf_op jit(solution)/shard_map/cond/branch_1_fun/pallas_call | solution.py:335
  187.5 10.8 %collective-permute-start.14 = (f32[512,128]{1,0:T(8,128)S(1)}, f32[512,128]{1,0:T(8,128)S(1)}, u32[]{:S(2)}, u32[]{:S(2)}) collective-permute-start(f32[512,128]{1,0:T(8,128)S(1)} %constant_dynamic-slice_fusion.3), channel_id=1, source_target_pairs={{0,1},{1,0},{2,3},{3,2},{4,5},{5,4},{6,7},{7,6},{8,9},{9,8},{10,11... | collective-permute-start | bytes 786440 | tf_op jit(solution)/shard_map/cond/branch_1_fun/ppermute | solution.py:365
  199.6 2.3 %collective-permute-start.15 = (f32[128,128]{1,0:T(8,128)S(1)}, f32[128,128]{1,0:T(8,128)S(1)}, u32[]{:S(2)}, u32[]{:S(2)}) collective-permute-start(f32[128,128]{1,0:T(8,128)S(1)} %get-tuple-element.109), channel_id=1, source_target_pairs={{0,2},{1,3},{2,4},{3,5},{4,6},{5,7},{6,0},{7,1},{8,10},{9,11},{10,... | collective-permute-start | bytes 196616 | tf_op jit(solution)/shard_map/cond/branch_1_fun/ppermute | solution.py:369
  201.9 3.3 %collective-permute-start.16 = (f32[128,128]{1,0:T(8,128)S(1)}, f32[128,128]{1,0:T(8,128)S(1)}, u32[]{:S(2)}, u32[]{:S(2)}) collective-permute-start(f32[128,128]{1,0:T(8,128)S(1)} %get-tuple-element.107), channel_id=1, source_target_pairs={{0,4},{1,5},{2,6},{3,7},{4,0},{5,1},{6,2},{7,3},{8,12},{9,13},{10,... | collective-permute-start | bytes 196616 | tf_op jit(solution)/shard_map/cond/branch_1_fun/ppermute | solution.py:369
  206.2 2.0 collective-permute-done.16
  209.4 2.2 collective-permute-start.19
  214.4 3.8 %collective-permute-start.21 = (bf16[4,128,128]{2,1,0:T(8,128)(2,1)S(1)}, bf16[4,128,128]{2,1,0:T(8,128)(2,1)S(1)}, u32[]{:S(2)}, u32[]{:S(2)}) collective-permute-start(bf16[4,128,128]{2,1,0:T(8,128)(2,1)S(1)} %pad_maximum_fusion.own), channel_id=1, source_target_pairs={{0,1},{1,0},{2,3},{3,2},{4,5},{5,4},{6,7},{7,6},{8,9},{9,8},{10,11... | collective-permute-start | bytes 393224 | tf_op jit(solution)/shard_map/cond/branch_1_fun/ppermute | solution.py:378
  220.4 2.3 %branch_1_fun.17 = bf16[2048,128]{1,0:T(8,128)(2,1)S(1)} custom-call(s32[2]{0:T(128)S(1)} %pad_add_fusion.where, s32[8,128]{1,0:T(8,128)S(1)} %get-tuple-element.50.mine, s32[32]{0:T(128)S(1)} %copy-done.37, f32[2048,128]{1,0:T(8,128)S(1)} %copy-done.6, bf16[4,128,128]{2,1,0:T(8,128)(2,1)S(1)} %pad_maximum_fusion.own, ...), custom_call_target="tpu_custom_call" | custom-call | flops 33554432 | bytes 2097152 | tf_op jit(solution)/shard_map/cond/branch_1_fun/pallas_call | solution.py:446
  (111 shorter events, 42.3 us)
Async XLA Ops:
  11.4 2.8 %copy-start.36 = (s32[32]{0:T(128)}, s32[32]{0:T(128)S(1)}, u32[]{:S(2)}) copy-start(s32[32]{0:T(128)S(1)} %get-tuple-element.51.counts) | copy-start | bytes 388 | tf_op jit(solution)/shard_map/cond
  11.4 207.8 %reduce-scatter.5.cloned.1.call-start = ((), (), s32[]{:S(2)}) async-start(), calls=%async_computation.7 | async-start | bytes 9437184 | tf_op jit(solution)/shard_map/cond/branch_1_fun/reduce_scatter | solution.py:543
  11.4 7.5 %copy-start.30 = (bf16[128,64,1024]{2,1,0:T(8,128)(2,1)S(1)}, bf16[128,64,1024]{2,1,0:T(8,128)(2,1)}, u32[]{:S(2)}) copy-start(bf16[128,64,1024]{2,1,0:T(8,128)(2,1)} %get-tuple-element.55.down) | copy-start | bytes 50331652 | tf_op jit(solution)/shard_map/cond
  11.5 8.1 %copy-start.32 = (bf16[128,64,128]{2,1,0:T(8,128)(2,1)S(1)}, bf16[128,64,128]{2,1,0:T(8,128)(2,1)}, u32[]{:S(2)}) copy-start(bf16[128,64,128]{2,1,0:T(8,128)(2,1)} %get-tuple-element.56.up) | copy-start | bytes 6291460 | tf_op jit(solution)/shard_map/cond
  26.3 9.9 %copy-start.33 = (bf16[2048,1024]{1,0:T(8,128)(2,1)S(1)}, bf16[2048,1024]{1,0:T(8,128)(2,1)}, u32[]{:S(2)}) copy-start(bf16[2048,1024]{1,0:T(8,128)(2,1)} %get-tuple-element.69.hidden) | copy-start | bytes 12582916 | tf_op jit(solution)/shard_map/cond
  26.3 9.9 %copy-start.38 = (bf16[1024,1024]{1,0:T(8,128)(2,1)S(1)}, bf16[1024,1024]{1,0:T(8,128)(2,1)}, u32[]{:S(2)}) copy-start(bf16[1024,1024]{1,0:T(8,128)(2,1)} %get-tuple-element.70.weight) | copy-start | bytes 6291460 | tf_op jit(solution)/shard_map/cond
  34.0 2.2 copy-start
  41.9 3.3 %copy-start.1 = (f32[2048,1024]{1,0:T(8,128)}, f32[2048,1024]{1,0:T(8,128)S(1)}, u32[]{:S(2)}) copy-start(f32[2048,1024]{1,0:T(8,128)S(1)} %branch_1_fun.12) | copy-start | bytes 25165828 | tf_op jit(solution)/shard_map/cond
  45.2 38.3 %collective-permute-start = (bf16[4,144,1024]{2,1,0:T(8,128)(2,1)}, bf16[4,144,1024]{2,1,0:T(8,128)(2,1)S(1)}, u32[]{:S(2)}, u32[]{:S(2)}) collective-permute-start(bf16[4,144,1024]{2,1,0:T(8,128)(2,1)} %get-tuple-element.57), channel_id=1, source_target_pairs={{0,32},{8,40},{16,48},{24,56},{32,64},{40,72},{48,80},{56,88},{64,... | collective-permute-start | bytes 3538952 | tf_op jit(solution)/shard_map/cond/branch_1_fun/ppermute | solution.py:52
  47.3 36.2 %collective-permute-start.1 = (bf16[4,144,1024]{2,1,0:T(8,128)(2,1)}, bf16[4,144,1024]{2,1,0:T(8,128)(2,1)S(1)}, u32[]{:S(2)}, u32[]{:S(2)}) collective-permute-start(bf16[4,144,1024]{2,1,0:T(8,128)(2,1)} %get-tuple-element.58), channel_id=1, source_target_pairs={{0,96},{8,104},{16,112},{24,120},{32,0},{40,8},{48,16},{56,24},{64... | collective-permute-start | bytes 3538952 | tf_op jit(solution)/shard_map/cond/branch_1_fun/ppermute | solution.py:52
  57.6 28.0 %collective-permute-start.2 = (bf16[4,144,1024]{2,1,0:T(8,128)(2,1)}, bf16[4,144,1024]{2,1,0:T(8,128)(2,1)S(1)}, u32[]{:S(2)}, u32[]{:S(2)}) collective-permute-start(bf16[4,144,1024]{2,1,0:T(8,128)(2,1)} %copy-done.28), channel_id=1, source_target_pairs={{0,8},{8,16},{16,24},{24,0},{32,40},{40,48},{48,56},{56,32},{64,72... | collective-permute-start | bytes 3538952 | tf_op jit(solution)/shard_map/cond/branch_1_fun/ppermute | solution.py:52
  57.6 28.0 %collective-permute-start.3 = (bf16[4,144,1024]{2,1,0:T(8,128)(2,1)}, bf16[4,144,1024]{2,1,0:T(8,128)(2,1)}, u32[]{:S(2)}, u32[]{:S(2)}) collective-permute-start(bf16[4,144,1024]{2,1,0:T(8,128)(2,1)} %copy-done.27), channel_id=1, source_target_pairs={{0,24},{8,0},{16,8},{24,16},{32,56},{40,32},{48,40},{56,48},{64,88... | collective-permute-start | bytes 3538952 | tf_op jit(solution)/shard_map/cond/branch_1_fun/ppermute | solution.py:52
  91.6 14.4 %collective-permute-start.4 = (bf16[2,144,1024]{2,1,0:T(8,128)(2,1)S(1)}, bf16[2,144,1024]{2,1,0:T(8,128)(2,1)S(1)}, u32[]{:S(2)}, u32[]{:S(2)}) collective-permute-start(bf16[2,144,1024]{2,1,0:T(8,128)(2,1)S(1)} %get-tuple-element.80), channel_id=1, source_target_pairs={{0,32},{8,40},{16,48},{24,56},{32,64},{40,72},{48,80},{56,88},{64,... | collective-permute-start | bytes 1769480 | tf_op jit(solution)/shard_map/cond/branch_1_fun/ppermute | solution.py:52
  91.7 15.2 %collective-permute-start.5 = (bf16[2,144,1024]{2,1,0:T(8,128)(2,1)S(1)}, bf16[2,144,1024]{2,1,0:T(8,128)(2,1)S(1)}, u32[]{:S(2)}, u32[]{:S(2)}) collective-permute-start(bf16[2,144,1024]{2,1,0:T(8,128)(2,1)S(1)} %get-tuple-element.81), channel_id=1, source_target_pairs={{0,96},{8,104},{16,112},{24,120},{32,0},{40,8},{48,16},{56,24},{64... | collective-permute-start | bytes 1769480 | tf_op jit(solution)/shard_map/cond/branch_1_fun/ppermute | solution.py:52
  94.3 13.7 %collective-permute-start.6 = (bf16[2,144,1024]{2,1,0:T(8,128)(2,1)S(1)}, bf16[2,144,1024]{2,1,0:T(8,128)(2,1)S(1)}, u32[]{:S(2)}, u32[]{:S(2)}) collective-permute-start(bf16[2,144,1024]{2,1,0:T(8,128)(2,1)S(1)} %get-tuple-element.82), channel_id=1, source_target_pairs={{0,8},{8,16},{16,24},{24,0},{32,40},{40,48},{48,56},{56,32},{64,72... | collective-permute-start | bytes 1769480 | tf_op jit(solution)/shard_map/cond/branch_1_fun/ppermute | solution.py:52
  94.3 14.6 %collective-permute-start.7 = (bf16[2,144,1024]{2,1,0:T(8,128)(2,1)S(1)}, bf16[2,144,1024]{2,1,0:T(8,128)(2,1)S(1)}, u32[]{:S(2)}, u32[]{:S(2)}) collective-permute-start(bf16[2,144,1024]{2,1,0:T(8,128)(2,1)S(1)} %get-tuple-element.83), channel_id=1, source_target_pairs={{0,24},{8,0},{16,8},{24,16},{32,56},{40,32},{48,40},{56,48},{64,88... | collective-permute-start | bytes 1769480 | tf_op jit(solution)/shard_map/cond/branch_1_fun/ppermute | solution.py:52
  109.7 71.8 %all-to-all-start = ((bf16[16,144,1024]{2,1,0:T(8,128)(2,1)}), bf16[16,144,1024]{2,1,0:T(8,128)(2,1)}, u32[]{:S(2)}, u32[]{:S(2)}) async-start(bf16[16,144,1024]{2,1,0:T(8,128)(2,1)} %copy-done), calls=%async_computation.1 | async-start | bytes 9437184 | tf_op jit(solution)/shard_map/cond/branch_1_fun/all_to_all | solution.py:551
  125.2 45.2 %collective-permute-start.10 = (bf16[144,1024]{1,0:T(8,128)(2,1)S(1)}, bf16[144,1024]{1,0:T(8,128)(2,1)S(1)}, u32[]{:S(2)}, u32[]{:S(2)}) collective-permute-start(bf16[144,1024]{1,0:T(8,128)(2,1)S(1)} %get-tuple-element.93), channel_id=1, source_target_pairs={{0,24},{8,0},{16,8},{24,16},{32,56},{40,32},{48,40},{56,48},{64,88... | collective-permute-start | bytes 884744 | tf_op jit(solution)/shard_map/cond/branch_1_fun/ppermute | solution.py:52
  127.6 43.4 %collective-permute-start.11 = (bf16[144,1024]{1,0:T(8,128)(2,1)}, bf16[144,1024]{1,0:T(8,128)(2,1)S(1)}, u32[]{:S(2)}, u32[]{:S(2)}) collective-permute-start(bf16[144,1024]{1,0:T(8,128)(2,1)} %get-tuple-element.95), channel_id=1, source_target_pairs={{0,32},{8,40},{16,48},{24,56},{32,64},{40,72},{48,80},{56,88},{64,... | collective-permute-start | bytes 884744 | tf_op jit(solution)/shard_map/cond/branch_1_fun/ppermute | solution.py:52
  128.8 49.9 %collective-permute-start.12 = (bf16[144,1024]{1,0:T(8,128)(2,1)}, bf16[144,1024]{1,0:T(8,128)(2,1)S(1)}, u32[]{:S(2)}, u32[]{:S(2)}) collective-permute-start(bf16[144,1024]{1,0:T(8,128)(2,1)} %get-tuple-element.96), channel_id=1, source_target_pairs={{0,64},{8,72},{16,80},{24,88},{32,96},{40,104},{48,112},{56,120},{... | collective-permute-start | bytes 884744 | tf_op jit(solution)/shard_map/cond/branch_1_fun/ppermute | solution.py:52
  131.3 47.4 %collective-permute-start.13 = (bf16[144,1024]{1,0:T(8,128)(2,1)}, bf16[144,1024]{1,0:T(8,128)(2,1)S(1)}, u32[]{:S(2)}, u32[]{:S(2)}) collective-permute-start(bf16[144,1024]{1,0:T(8,128)(2,1)} %get-tuple-element.97), channel_id=1, source_target_pairs={{0,96},{8,104},{16,112},{24,120},{32,0},{40,8},{48,16},{56,24},{64... | collective-permute-start | bytes 884744 | tf_op jit(solution)/shard_map/cond/branch_1_fun/ppermute | solution.py:52
  132.4 46.3 %collective-permute-start.8 = (bf16[144,1024]{1,0:T(8,128)(2,1)}, bf16[144,1024]{1,0:T(8,128)(2,1)S(1)}, u32[]{:S(2)}, u32[]{:S(2)}) collective-permute-start(bf16[144,1024]{1,0:T(8,128)(2,1)} %get-tuple-element.91), channel_id=1, source_target_pairs={{0,8},{8,16},{16,24},{24,0},{32,40},{40,48},{48,56},{56,32},{64,72... | collective-permute-start | bytes 884744 | tf_op jit(solution)/shard_map/cond/branch_1_fun/ppermute | solution.py:52
  170.4 8.6 %collective-permute-start.9 = (bf16[144,1024]{1,0:T(8,128)(2,1)}, bf16[144,1024]{1,0:T(8,128)(2,1)S(1)}, u32[]{:S(2)}, u32[]{:S(2)}) collective-permute-start(bf16[144,1024]{1,0:T(8,128)(2,1)} %get-tuple-element.92), channel_id=1, source_target_pairs={{0,16},{8,24},{16,0},{24,8},{32,48},{40,56},{48,32},{56,40},{64,80... | collective-permute-start | bytes 884744 | tf_op jit(solution)/shard_map/cond/branch_1_fun/ppermute | solution.py:52
  181.6 37.6 %copy-start.37 = (s32[32]{0:T(128)S(1)}, s32[32]{0:T(128)}, u32[]{:S(2)}) copy-start(s32[32]{0:T(128)} %copy-done.36) | copy-start | bytes 388 | tf_op jit(solution)/shard_map/cond
  187.5 12.0 %collective-permute-start.14 = (f32[512,128]{1,0:T(8,128)S(1)}, f32[512,128]{1,0:T(8,128)S(1)}, u32[]{:S(2)}, u32[]{:S(2)}) collective-permute-start(f32[512,128]{1,0:T(8,128)S(1)} %constant_dynamic-slice_fusion.3), channel_id=1, source_target_pairs={{0,1},{1,0},{2,3},{3,2},{4,5},{5,4},{6,7},{7,6},{8,9},{9,8},{10,11... | collective-permute-start | bytes 786440 | tf_op jit(solution)/shard_map/cond/branch_1_fun/ppermute | solution.py:365
  199.6 6.6 %collective-permute-start.15 = (f32[128,128]{1,0:T(8,128)S(1)}, f32[128,128]{1,0:T(8,128)S(1)}, u32[]{:S(2)}, u32[]{:S(2)}) collective-permute-start(f32[128,128]{1,0:T(8,128)S(1)} %get-tuple-element.109), channel_id=1, source_target_pairs={{0,2},{1,3},{2,4},{3,5},{4,6},{5,7},{6,0},{7,1},{8,10},{9,11},{10,... | collective-permute-start | bytes 196616 | tf_op jit(solution)/shard_map/cond/branch_1_fun/ppermute | solution.py:369
  201.9 6.3 %collective-permute-start.16 = (f32[128,128]{1,0:T(8,128)S(1)}, f32[128,128]{1,0:T(8,128)S(1)}, u32[]{:S(2)}, u32[]{:S(2)}) collective-permute-start(f32[128,128]{1,0:T(8,128)S(1)} %get-tuple-element.107), channel_id=1, source_target_pairs={{0,4},{1,5},{2,6},{3,7},{4,0},{5,1},{6,2},{7,3},{8,12},{9,13},{10,... | collective-permute-start | bytes 196616 | tf_op jit(solution)/shard_map/cond/branch_1_fun/ppermute | solution.py:369
  205.2 3.4 %collective-permute-start.17 = (f32[128,128]{1,0:T(8,128)S(1)}, f32[128,128]{1,0:T(8,128)S(1)}, u32[]{:S(2)}, u32[]{:S(2)}) collective-permute-start(f32[128,128]{1,0:T(8,128)S(1)} %get-tuple-element.108), channel_id=1, source_target_pairs={{0,6},{1,7},{2,0},{3,1},{4,2},{5,3},{6,4},{7,5},{8,14},{9,15},{10,... | collective-permute-start | bytes 196616 | tf_op jit(solution)/shard_map/cond/branch_1_fun/ppermute | solution.py:369
  208.7 4.0 %collective-permute-start.18 = (bf16[128,128]{1,0:T(8,128)(2,1)S(1)}, bf16[128,128]{1,0:T(8,128)(2,1)S(1)}, u32[]{:S(2)}, u32[]{:S(2)}) collective-permute-start(bf16[128,128]{1,0:T(8,128)(2,1)S(1)} %add_convert_fusion), channel_id=1, source_target_pairs={{0,2},{1,3},{2,4},{3,5},{4,6},{5,7},{6,0},{7,1},{8,10},{9,11},{10,... | collective-permute-start | bytes 98312 | tf_op jit(solution)/shard_map/cond/branch_1_fun/ppermute | solution.py:377
  209.4 4.3 %collective-permute-start.19 = (bf16[128,128]{1,0:T(8,128)(2,1)S(1)}, bf16[128,128]{1,0:T(8,128)(2,1)S(1)}, u32[]{:S(2)}, u32[]{:S(2)}) collective-permute-start(bf16[128,128]{1,0:T(8,128)(2,1)S(1)} %add_convert_fusion), channel_id=1, source_target_pairs={{0,4},{1,5},{2,6},{3,7},{4,0},{5,1},{6,2},{7,3},{8,12},{9,13},{10,... | collective-permute-start | bytes 98312 | tf_op jit(solution)/shard_map/cond/branch_1_fun/ppermute | solution.py:377
  211.6 2.8 %collective-permute-start.20 = (bf16[128,128]{1,0:T(8,128)(2,1)S(1)}, bf16[128,128]{1,0:T(8,128)(2,1)S(1)}, u32[]{:S(2)}, u32[]{:S(2)}) collective-permute-start(bf16[128,128]{1,0:T(8,128)(2,1)S(1)} %add_convert_fusion), channel_id=1, source_target_pairs={{0,6},{1,7},{2,0},{3,1},{4,2},{5,3},{6,4},{7,5},{8,14},{9,15},{10,... | collective-permute-start | bytes 98312 | tf_op jit(solution)/shard_map/cond/branch_1_fun/ppermute | solution.py:377
  214.4 4.8 %collective-permute-start.21 = (bf16[4,128,128]{2,1,0:T(8,128)(2,1)S(1)}, bf16[4,128,128]{2,1,0:T(8,128)(2,1)S(1)}, u32[]{:S(2)}, u32[]{:S(2)}) collective-permute-start(bf16[4,128,128]{2,1,0:T(8,128)(2,1)S(1)} %pad_maximum_fusion.own), channel_id=1, source_target_pairs={{0,1},{1,0},{2,3},{3,2},{4,5},{5,4},{6,7},{7,6},{8,9},{9,8},{10,11... | collective-permute-start | bytes 393224 | tf_op jit(solution)/shard_map/cond/branch_1_fun/ppermute | solution.py:378
  (28 other events, 27.4 us)
Sparse Core Ops, SparseCore 0:
  45.3 61.1 reduce-scatter.4

commit v10 on v9

--- a/solution.py
+++ b/solution.py
@@ -39,7 +39,7 @@
 HBM = pl.BlockSpec(memory_space=pltpu.HBM)
 LANES = 128
 ORDER, PLACE, FLAGS = 0, 1, 2
-HOT, FITS = 0, 1
+HOT, FITS, AT, CHIP, CORE = 0, 1, 2, 4, 5
 
 
 def shift(value, dx, dy):
@@ -52,13 +52,13 @@
     return lax.ppermute(value, "dp", pairs)
 
 
-def index_kernel(me_ref, ids_ref, table_ref, served_ref, mine_ref, owner_ref, rank_ref):
+def index_kernel(spot_ref, ids_ref, table_ref, served_ref, mine_ref, owner_ref, rank_ref):
     total = ids_ref.shape[0]
     dp_count = served_ref.shape[0]
     groups = total // dp_count
     chunks = table_ref.shape[0]
     owned = chunks * LANES // dp_count
-    me = me_ref[0]
+    me = spot_ref[0]
     f32, bf16 = jnp.float32, jnp.bfloat16
     ids = ids_ref[...]
     lane = lax.broadcasted_iota(jnp.int32, (total, LANES), 1)
@@ -109,12 +109,23 @@
     mine_ref[...] = jnp.zeros(mine_ref.shape, jnp.int32)
     mine_ref[ORDER : ORDER + 1, :] = jnp.sum(jnp.where(here, group, 0), axis=0, keepdims=True)
     mine_ref[PLACE : PLACE + 1, :] = jnp.sum(jnp.where(here, place, 0), axis=0, keepdims=True)
-    mine_ref[FLAGS : FLAGS + 1, :] = jnp.where(
-        row_lane == HOT, hot, jnp.where(row_lane == FITS, fits, 0)
-    )
-
-
-def index_tables(me, ids, table, dp_count):
+    side = math.isqrt(dp_count)
+    x, y = lax.div(me, side), lax.rem(me, side)
+    flags = (
+        (HOT, hot),
+        (FITS, fits),
+        (AT, lax.rem(x - lax.div(hot, side) + side, side)),
+        (AT + 1, lax.rem(y - lax.rem(hot, side) + side, side)),
+        (CHIP, lax.div(spot_ref[1], 2)),
+        (CORE, lax.rem(spot_ref[1], 2)),
+    )
+    row = jnp.zeros((1, LANES), jnp.int32)
+    for at, value in flags:
+        row = jnp.where(row_lane == at, value, row)
+    mine_ref[FLAGS : FLAGS + 1, :] = row
+
+
+def index_tables(spot, ids, table, dp_count):
     total = ids.shape[0]
     return pl.pallas_call(
         index_kernel,
@@ -126,7 +137,7 @@
         out_specs=(VMEM, VMEM),
         scratch_shapes=[pltpu.VMEM((total, LANES), jnp.int32)] * 2,
         compiler_params=pltpu.CompilerParams(vmem_limit_bytes=8 << 20),
-    )(me, ids.reshape(total, 1), table.reshape(-1, LANES))
+    )(spot, ids.reshape(total, 1), table.reshape(-1, LANES))
 
 
 def copy_units(wanted, down, up, up_in, down_sem, up_sem):
@@ -158,18 +169,13 @@
         copy.wait()
 
 
-def main_kernel(served, down, up, out, *scratch):
-    wanted = [(out, p, (served[p, 0], served[p, 1])) for p in range(out.shape[0])]
-    copy_units(wanted, down, up, *scratch)
-
-
-def extra_kernel(lines, me, served, mine, down, up, *refs):
-    outs, scratch = refs[: len(lines)], refs[len(lines) :]
+def gather_kernel(lines, served, mine, down, up, *refs):
+    main, outs, scratch = refs[0], refs[1 : 1 + len(lines)], refs[1 + len(lines) :]
     dp_count = served.shape[0]
     side = math.isqrt(dp_count)
     hot = mine[FLAGS, HOT]
 
-    @pl.when(hot == me[0])
+    @pl.when((mine[FLAGS, AT] == 0) & (mine[FLAGS, AT + 1] == 0))
     def _():
         hot_x, hot_y = lax.div(hot, side), lax.rem(hot, side)
         wanted = []
@@ -181,25 +187,32 @@
                 wanted.append((out, i, (served[peer, first], served[peer, first + 1])))
         copy_units(wanted, down, up, *scratch)
 
-
-def gather_call(kernel, shapes, count, scalars, down, up, limit=8):
+    copy_units(
+        [(main, p, (served[p, 0], served[p, 1])) for p in range(dp_count)], down, up, *scratch
+    )
+
+
+def gather_units(lines, served, mine, down, up):
     _, rank, width = down.shape
     lanes = up.shape[2]
+    dp_count = served.shape[0]
+    shapes = [dp_count] + [len(units) for _, units in lines]
+    count = max(dp_count, sum(shapes[1:]))
     return pl.pallas_call(
-        kernel,
+        functools.partial(gather_kernel, lines),
         out_shape=[jax.ShapeDtypeStruct((n, 2 * rank + 16, width), down.dtype) for n in shapes],
-        in_specs=[SMEM] * len(scalars) + [HBM, HBM],
+        in_specs=[SMEM, SMEM, HBM, HBM],
         out_specs=[VMEM] * len(shapes),
         scratch_shapes=[
             pltpu.VMEM((2 * count, rank, lanes), up.dtype),
             pltpu.SemaphoreType.DMA((2 * count,)),
             pltpu.SemaphoreType.DMA((2 * count,)),
         ],
-        compiler_params=pltpu.CompilerParams(vmem_limit_bytes=limit << 20),
+        compiler_params=pltpu.CompilerParams(vmem_limit_bytes=18 << 20),
         cost_estimate=pl.CostEstimate(
             flops=0, bytes_accessed=count * rank * (width + lanes) * 8, transcendentals=0
         ),
-    )(*scalars, down, up)
+    )(served, mine, down, up)
 
 
 def vmem_call(kernel, shapes, dtype, scalars, arrays, limit=10):
@@ -228,10 +241,10 @@
     lax.fori_loop(0, rows // 16, body, 0, unroll=3)
 
 
-def relay_kernel(offsets, *refs):
+def relay_kernel(mine, *refs):
     fresh, near, outs = refs[:4], refs[4:8], refs[8:]
     for i in range(4):
-        at = offsets[i // 2]
+        at = mine[FLAGS, AT + i // 2]
         close = 1 if i % 2 == 0 else 3
         for source, when in ((near[i], at != close), (fresh[i], at == close)):
 
@@ -241,12 +254,12 @@
                     move(out.at[u], source.at[u])
 
 
-def line_kernel(offsets, *refs):
+def line_kernel(mine, *refs):
     outs = refs[10:]
     for h in range(2):
         own, plus_a, minus_a, plus_b, minus_b = refs[5 * h : 5 * h + 5]
         out = outs[4 * h : 4 * h + 4]
-        at = offsets[h]
+        at = mine[FLAGS, AT + h]
         low, high = own.at[pl.ds(0, 2)], own.at[pl.ds(2, 2)]
         plus_b, minus_b = plus_b.at[pl.ds(2, 2)], minus_b.at[pl.ds(2, 2)]
         picks = ((low, high), (plus_a, plus_b), (plus_a, minus_a), (minus_a, minus_b))
@@ -259,9 +272,9 @@
                     move(out[2 + u], second.at[u])
 
 
-def pick_kernel(offsets, *refs):
+def pick_kernel(mine, *refs):
     for h in range(2):
-        at = offsets[1 - h]
+        at = mine[FLAGS, AT + 1 - h]
         for offset, source in enumerate(refs[4 * h : 4 * h + 4]):
 
             @pl.when(at == offset)
@@ -394,13 +407,13 @@
         out[here, :] = jnp.where(rows < counts[g], merged, 0.0).astype(out.dtype)
 
 
-def out_kernel(where, mine, counts, base, own, other, main, *refs):
+def out_kernel(mine, counts, base, own, other, main, *refs):
     extras, out, low = refs[:2], refs[2], refs[3]
     groups = counts.shape[0]
     cap = base.shape[0] // groups
     chips, piece, rank = own.shape[0], own.shape[1], own.shape[2] // 2
     lanes = base.shape[1]
-    z, core = where[0], where[1]
+    z, core = mine[FLAGS, CHIP], mine[FLAGS, CORE]
     steps = rank // 16
     pairs = groups // 2
     full = pairs - EXTRA
@@ -440,14 +453,14 @@
     return pl.BlockSpec(array.shape, lambda i: (0,) * array.ndim)
 
 
-def combine(where, mine, counts, base, own, other, main, extras, rank):
+def combine(mine, counts, base, own, other, main, extras, rank):
     packs = pl.BlockSpec((main.shape[0], 16, main.shape[2]), lambda i: (0, rank // 8, 0))
     pack = pl.BlockSpec((16, main.shape[2]), lambda i: (rank // 8, 0))
     return pl.pallas_call(
         out_kernel,
         grid=(1,),
         out_shape=jax.ShapeDtypeStruct(base.shape, jnp.bfloat16),
-        in_specs=[SMEM, SMEM, SMEM, whole(base), whole(own), whole(other), packs, pack, pack],
+        in_specs=[SMEM, SMEM, whole(base), whole(own), whole(other), packs, pack, pack],
         out_specs=whole(base),
         scratch_shapes=[
             pltpu.VMEM((2 * own.shape[0] * own.shape[1], own.shape[2]), jnp.bfloat16)
@@ -456,7 +469,7 @@
         cost_estimate=pl.CostEstimate(
             flops=base.size * rank * 2, bytes_accessed=base.size * 8, transcendentals=0
         ),
-    )(where, mine, counts, base, own, other, main, *extras)
+    )(mine, counts, base, own, other, main, *extras)
 
 
 def on_device(
@@ -473,8 +486,8 @@
     owned, rank, width = down_weights.shape
     groups = group_adapter_id.shape[0] // dp_count
     cap = hidden.shape[0] // groups
-    me_row = me.astype(jnp.int32).reshape(1)
-    served, mine = index_tables(me_row, group_adapter_id, adapter_storage_row, dp_count)
+    spot = jnp.stack([me, lax.axis_index("tp")]).astype(jnp.int32)
+    served, mine = index_tables(spot, group_adapter_id, adapter_storage_row, dp_count)
     counts = lax.dynamic_slice_in_dim(group_live_count, me * groups, groups)
 
     def wide(hidden, value_weight, down_weights, up_weights):
@@ -503,11 +516,6 @@
         return finish(base, low, ups[picked], counts)
 
     def narrow(hidden, value_weight, down_weights, up_weights):
-        side = math.isqrt(dp_count)
-        hot = mine[FLAGS, HOT]
-        a = (me // side - hot // side) % side
-        b = (me % side - hot % side) % side
-        offsets = jnp.stack([a, b]).astype(jnp.int32)
         trees = (True, False)
         soon = [
             (tree, ((2, part[0]), (2, part[1]), (near, 2), (near, 3)))
@@ -520,55 +528,32 @@
         turned = ((0, 1), (0, 2), (0, -1), (1, 0), (2, 0), (-1, 0))
         send = lambda values, ways: [shift(v, *way) for v, way in zip(values, ways)]
         barrier = lax.optimization_barrier
-        scalars = (me_row, served, mine)
-        gathered = gather_call(
-            functools.partial(extra_kernel, soon), (4,) * 4, 16, scalars, down_weights, up_weights
+        main_sent, *gathered = gather_units(soon + late, served, mine, down_weights, up_weights)
+        unit, dtype = main_sent.shape[1:], main_sent.dtype
+        near, homes = gathered[4:8], gathered[8:]
+        fresh = barrier(send(gathered[:4], moves))
+        relayed = vmem_call(
+            relay_kernel, ((2,) + unit,) * 4, dtype, (mine,), (*fresh, *near)
         )
-        fresh = send(gathered, moves)
-        later_served, _ = barrier((served, gathered))
-        later = gather_call(
-            functools.partial(extra_kernel, late),
-            (2,) * 4 + (4,) * 2,
-            16,
-            (me_row, later_served, mine),
-            down_weights,
-            up_weights,
-        )
-        main_served, _ = barrier((served, later))
-        (main_sent,) = gather_call(
-            main_kernel, (dp_count,), dp_count, (main_served,), down_weights, up_weights
-        )
-        base_hidden, _ = barrier((hidden, main_sent))
+        base_hidden, _ = barrier((hidden, relayed))
         base_terms = base_product(base_hidden, value_weight)
         base = lax.psum_scatter(base_terms, "tp", scatter_dimension=1, tiled=True)
-        unit = main_sent.shape[1:]
-        dtype = main_sent.dtype
-        fresh, near, main_sent, _ = barrier((fresh, later[:4], main_sent, base_terms))
-        relayed = vmem_call(
-            relay_kernel, ((2,) + unit,) * 4, dtype, (offsets,), (*fresh, *near)
-        )
         near_a, main_sent = barrier((send(relayed, moves), main_sent))
         main = lax.all_to_all(main_sent, "dp", 0, 0, tiled=True)
         tree_arrays = [
-            (later[4 + h], near_a[2 * h], near_a[2 * h + 1], fresh[2 * h], fresh[2 * h + 1])
+            (homes[h], near_a[2 * h], near_a[2 * h + 1], fresh[2 * h], fresh[2 * h + 1])
             for h in range(2)
         ]
         lines = vmem_call(
-            line_kernel, (unit,) * 8, dtype, (offsets,), tree_arrays[0] + tree_arrays[1]
+            line_kernel, (unit,) * 8, dtype, (mine,), tree_arrays[0] + tree_arrays[1]
         )
         got = send(lines[1:4] + lines[5:8], turned)
         extras = vmem_call(
-            pick_kernel,
-            (unit,) * 2,
-            dtype,
-            (offsets,),
-            (lines[0], *got[:3], lines[4], *got[3:]),
+            pick_kernel, (unit,) * 2, dtype, (mine,), (lines[0], *got[:3], lines[4], *got[3:])
         )
         partial = low_partial(mine, hidden, main, extras, cap, rank)
         own, other = low_rank_up(low_rank_down(partial))
-        t = lax.axis_index("tp")
-        where = jnp.stack([t // 2, t % 2]).astype(jnp.int32)
-        return combine(where, mine, counts, base, own, other, main, extras, rank)
+        return combine(mine, counts, base, own, other, main, extras, rank)
 
     return lax.cond(
         mine[FLAGS, FITS] == 1, narrow, wide, hidden, value_weight, down_weights, up_weights

time: 231 us -> 204 us (0.88)
  starting transfers between devices: 56.9 us -> 45.3 us
  local copies, waits for them, and re-layouts: 38.9 us -> 28 us
  Pallas kernels: 32.3 us -> 23.8 us
  waiting for transfers between devices: 84.9 us -> 91.9 us
  loops' own time: 3.13 us -> 0.42 us
    cond x70 -> x58, local copies, waits for them, and re-layouts: 35.3 us -> 25 us
    ppermute x14, starting transfers between devices: 27.9 us -> 19 us  [shift(): return lax.ppermute(value, 'dp', pairs)]
    pallas_call x3 -> x1, Pallas kernels: 11.7 us -> 4.39 us  [gather_units(): pl.pallas_call(functools.partial(gather_kernel, lines), out_shape=[jax.Sh...]
    ppermute x14, waiting for transfers between devices: 77.8 us -> 83 us  [shift(): return lax.ppermute(value, 'dp', pairs)]
    another operation x1, loops' own time: 3.13 us -> 0.42 us  [on_device(): lax.cond(mine[FLAGS, FITS] == 1, narrow, wide, hidden, value_weight, down...]
  transfers between devices with their start and end apart: 24 -> 24, of which waited for: 16 -> 17; matrix products, arithmetic and copies ran while one was open for 0% -> 0% of each run, Pallas kernels for 5% -> 4%
where the time goes in v10:
time: 204 us
  waiting for transfers between devices  91.9 us (45%)
  starting transfers between devices  45.3 us (22%)
  local copies, waits for them, and re-layouts  28 us (14%)
  Pallas kernels  23.8 us (12%)
  between operations  14.1 us (7%)
    ppermute x14, waiting for transfers between devices, shift(): return lax.ppermute(value, 'dp', pairs)  83 us
    cond x58, local copies, waits for them, and re-layouts  25 us
    ppermute x14, starting transfers between devices, shift(): return lax.ppermute(value, 'dp', pairs)  19 us
    ppermute x1, starting transfers between devices, low_rank_down(): lax.ppermute(cut(partial, (1 - core) * half, half), 'tp', swap())  8.8 us
    ppermute x3, starting transfers between devices, low_rank_down(): lax.ppermute(cut(total, (z + d) % chips * piece, piece), 'tp', turn(d))  6.6 us
    pallas_call x1, Pallas kernels, low_partial(): pl.pallas_call(functools.partial(low_kernel, cap), out_shape=jax.ShapeDty...  5.91 us
    pallas_call x1, Pallas kernels, base_product(): pl.pallas_call(base_kernel, grid=(rows // block,), out_shape=jax.ShapeDty...  5.7 us
    all_to_all x1, starting transfers between devices, narrow(): main = lax.all_to_all(main_sent, 'dp', 0, 0, tiled=True)  4.57 us
  transfers between devices with their start and end apart: 24, of which 17 were waited for; matrix products, arithmetic and copies ran while one was open for 0% of the time, Pallas kernels for 4%

profile of v10, /device:TPU:1, one launch (start us, length us, event | category | flops | bytes accessed | tf_op | source)
XLA Modules:
  0.0 203.5 jit_solution(17977661792957783803)
XLA Ops:
  8.2 1.8 shard_map.75
  11.3 184.6 %conditional.1 = (bf16[2048,128]{1,0:T(8,128)(2,1)S(1)}) conditional(s32[]{:T(128)} %bitcast.16, (s32[32]{0:T(128)S(1)}, bf16[2048,1024]{1,0:T(8,128)(2,1)}, bf16[1024,1024]{1,0:T(8,128)(2,1)}, s32[512]{0:T(512)}, s32[2048]{0:T(1024)}, /*index=5*/s32[]{:T(128)}, bf16[128,64,1024]{2,1,0:T(8,128)(2,1)}, bf16[128,64,128]{2,1,0:T(8,128)(2,1)}) %tuple.14, ...), branch_computations={%region_0.5_spmd, %region_5.7_spmd} | conditional | flops 4598219776 | bytes 281184896 | solution.py:558
  11.5 4.4 %branch_1_fun.7 = (bf16[16,144,1024]{2,1,0:T(8,128)(2,1)S(1)}, bf16[4,144,1024]{2,1,0:T(8,128)(2,1)S(1)}, bf16[4,144,1024]{2,1,0:T(8,128)(2,1)S(1)}, bf16[4,144,...) custom-call(s32[16,128]{1,0:T(8,128)S(1)} %get-tuple-element.49.serv, ...), custom_call_target="tpu_custom_call" | custom-call | bytes 18874368 | tf_op jit(solution)/shard_map/cond/branch_1_fun/pallas_call | solution.py:201
  15.9 2.2 %copy-done.1 = bf16[16,144,1024]{2,1,0:T(8,128)(2,1)} copy-done((bf16[16,144,1024]{2,1,0:T(8,128)(2,1)}, bf16[16,144,1024]{2,1,0:T(8,128)(2,1)S(1)}, u32[]{:S(2)}) %copy-start.1) | copy-done | bytes 4718616 | tf_op jit(solution)/shard_map/cond
  18.2 2.0 %collective-permute-start = (bf16[4,144,1024]{2,1,0:T(8,128)(2,1)S(1)}, bf16[4,144,1024]{2,1,0:T(8,128)(2,1)S(1)}, u32[]{:S(2)}, u32[]{:S(2)}) collective-permute-start(bf16[4,144,1024]{2,1,0:T(8,128)(2,1)S(1)} %get-tuple-element.52), channel_id=1, source_target_pairs={{0,32},{8,40},{16,48},{24,56},{32,64},{40,72},{48,80},{56,88},{64,... | collective-permute-start | bytes 3538952 | tf_op jit(solution)/shard_map/cond/branch_1_fun/ppermute | solution.py:52
  20.2 1.3 collective-permute-start.1
  21.6 1.4 collective-permute-start.2
  23.0 1.4 collective-permute-start.3
  24.4 22.2 %collective-permute-done.refs_0_.refs_3_ = bf16[4,144,1024]{2,1,0:T(8,128)(2,1)S(1)} collective-permute-done((bf16[4,144,1024]{2,1,0:T(8,128)(2,1)S(1)}, bf16[4,144,1024]{2,1,0:T(8,128)(2,1)S(1)}, u32[]{:S(2)}, u32[]{:S(2)}) %collective-permute-start) | collective-permute-done | bytes 1179680 | tf_op jit(solution)/shard_map/cond/branch_1_fun/ppermute | solution.py:52
  46.8 2.5 %collective-permute-done.2.refs_2_.refs_8_ = bf16[4,144,1024]{2,1,0:T(8,128)(2,1)S(1)} collective-permute-done((bf16[4,144,1024]{2,1,0:T(8,128)(2,1)S(1)}, bf16[4,144,1024]{2,1,0:T(8,128)(2,1)S(1)}, u32[]{:S(2)}, u32[]{:S(2)}) %collective-permute-start.2) | collective-permute-done | bytes 1179680 | tf_op jit(solution)/shard_map/cond/branch_1_fun/ppermute | solution.py:52
  49.3 2.5 %collective-permute-done.3.refs_3_.refs_9_ = bf16[4,144,1024]{2,1,0:T(8,128)(2,1)S(1)} collective-permute-done((bf16[4,144,1024]{2,1,0:T(8,128)(2,1)S(1)}, bf16[4,144,1024]{2,1,0:T(8,128)(2,1)S(1)}, u32[]{:S(2)}, u32[]{:S(2)}) %collective-permute-start.3) | collective-permute-done | bytes 1179680 | tf_op jit(solution)/shard_map/cond/branch_1_fun/ppermute | solution.py:52
  56.0 5.7 %branch_1_fun.9 = f32[2048,1024]{1,0:T(8,128)S(1)} custom-call(bf16[2048,1024]{1,0:T(8,128)(2,1)S(1)} %copy-done.26, bf16[1024,1024]{1,0:T(8,128)(2,1)S(1)} %copy-done.32), custom_call_target="tpu_custom_call" | custom-call | flops 4294967296 | bytes 14680064 | tf_op jit(solution)/shard_map/cond/branch_1_fun/pallas_call | solution.py:292
  61.7 3.3 %copy-done = f32[2048,1024]{1,0:T(8,128)} copy-done((f32[2048,1024]{1,0:T(8,128)}, f32[2048,1024]{1,0:T(8,128)S(1)}, u32[]{:S(2)}) %copy-start) | copy-done | bytes 8388632 | tf_op jit(solution)/shard_map/cond
  66.3 1.5 collective-permute-start.5
  69.0 1.5 collective-permute-start.7
  70.5 9.1 %collective-permute-done.4.refs_1_ = bf16[2,144,1024]{2,1,0:T(8,128)(2,1)S(1)} collective-permute-done((bf16[2,144,1024]{2,1,0:T(8,128)(2,1)}, bf16[2,144,1024]{2,1,0:T(8,128)(2,1)S(1)}, u32[]{:S(2)}, u32[]{:S(2)}) %collective-permute-start.4) | collective-permute-done | bytes 589856 | tf_op jit(solution)/shard_map/cond/branch_1_fun/ppermute | solution.py:52
  83.4 4.6 %all-to-all-start = ((bf16[16,144,1024]{2,1,0:T(8,128)(2,1)}), bf16[16,144,1024]{2,1,0:T(8,128)(2,1)}, u32[]{:S(2)}, u32[]{:S(2)}) async-start(bf16[16,144,1024]{2,1,0:T(8,128)(2,1)} %copy-done.1), calls=%async_computation.1 | async-start | bytes 9437184 | tf_op jit(solution)/shard_map/cond/branch_1_fun/all_to_all | solution.py:542
  96.2 2.0 branch_1_fun.10
  99.6 2.4 %collective-permute-start.10 = (bf16[144,1024]{1,0:T(8,128)(2,1)S(1)}, bf16[144,1024]{1,0:T(8,128)(2,1)S(1)}, u32[]{:S(2)}, u32[]{:S(2)}) collective-permute-start(bf16[144,1024]{1,0:T(8,128)(2,1)S(1)} %get-tuple-element.81), channel_id=1, source_target_pairs={{0,24},{8,0},{16,8},{24,16},{32,56},{40,32},{48,40},{56,48},{64,88... | collective-permute-start | bytes 884744 | tf_op jit(solution)/shard_map/cond/branch_1_fun/ppermute | solution.py:52
  103.3 2.4 %collective-permute-start.12 = (bf16[144,1024]{1,0:T(8,128)(2,1)}, bf16[144,1024]{1,0:T(8,128)(2,1)S(1)}, u32[]{:S(2)}, u32[]{:S(2)}) collective-permute-start(bf16[144,1024]{1,0:T(8,128)(2,1)} %get-tuple-element.84), channel_id=1, source_target_pairs={{0,64},{8,72},{16,80},{24,88},{32,96},{40,104},{48,112},{56,120},{... | collective-permute-start | bytes 884744 | tf_op jit(solution)/shard_map/cond/branch_1_fun/ppermute | solution.py:52
  106.9 37.3 %collective-permute-done.10.refs_3_ = bf16[144,1024]{1,0:T(8,128)(2,1)S(1)} collective-permute-done((bf16[144,1024]{1,0:T(8,128)(2,1)S(1)}, bf16[144,1024]{1,0:T(8,128)(2,1)S(1)}, u32[]{:S(2)}, u32[]{:S(2)}) %collective-permute-start.10) | collective-permute-done | bytes 294944 | tf_op jit(solution)/shard_map/cond/branch_1_fun/ppermute | solution.py:52
  144.3 3.9 %collective-permute-done.11.refs_5_ = bf16[144,1024]{1,0:T(8,128)(2,1)S(1)} collective-permute-done((bf16[144,1024]{1,0:T(8,128)(2,1)}, bf16[144,1024]{1,0:T(8,128)(2,1)S(1)}, u32[]{:S(2)}, u32[]{:S(2)}) %collective-permute-start.11) | collective-permute-done | bytes 294944 | tf_op jit(solution)/shard_map/cond/branch_1_fun/ppermute | solution.py:52
  148.1 4.4 %collective-permute-done.12.refs_6_ = bf16[144,1024]{1,0:T(8,128)(2,1)S(1)} collective-permute-done((bf16[144,1024]{1,0:T(8,128)(2,1)}, bf16[144,1024]{1,0:T(8,128)(2,1)S(1)}, u32[]{:S(2)}, u32[]{:S(2)}) %collective-permute-start.12) | collective-permute-done | bytes 294944 | tf_op jit(solution)/shard_map/cond/branch_1_fun/ppermute | solution.py:52
  155.8 5.9 %branch_1_fun.12 = f32[1024,128]{1,0:T(8,128)S(1)} custom-call(s32[8,128]{1,0:T(8,128)S(1)} %get-tuple-element.46.mine, bf16[2048,1024]{1,0:T(8,128)(2,1)} %get-tuple-element.68.hidden, bf16[16,144,1024]{2,1,0:T(8,128)(2,1)} %all-to-all-done.main, bf16[144,1024]{1,0:T(8,128)(2,1)S(1)} %get-tuple-element.86.refs_0_, ...), custom_call_target="tpu_custom_call" | custom-call | flops 268435456 | bytes 8912896 | tf_op jit(solution)/shard_map/cond/branch_1_fun/pallas_call | solution.py:348
  161.8 8.8 %collective-permute-start.14 = (f32[512,128]{1,0:T(8,128)S(1)}, f32[512,128]{1,0:T(8,128)S(1)}, u32[]{:S(2)}, u32[]{:S(2)}) collective-permute-start(f32[512,128]{1,0:T(8,128)S(1)} %constant_dynamic-slice_fusion.3), channel_id=1, source_target_pairs={{0,1},{1,0},{2,3},{3,2},{4,5},{5,4},{6,7},{7,6},{8,9},{9,8},{10,11... | collective-permute-start | bytes 786440 | tf_op jit(solution)/shard_map/cond/branch_1_fun/ppermute | solution.py:378
  171.8 2.6 %collective-permute-start.15 = (f32[128,128]{1,0:T(8,128)S(1)}, f32[128,128]{1,0:T(8,128)S(1)}, u32[]{:S(2)}, u32[]{:S(2)}) collective-permute-start(f32[128,128]{1,0:T(8,128)S(1)} %get-tuple-element.97), channel_id=1, source_target_pairs={{0,2},{1,3},{2,4},{3,5},{4,6},{5,7},{6,0},{7,1},{8,10},{9,11},{10,... | collective-permute-start | bytes 196616 | tf_op jit(solution)/shard_map/cond/branch_1_fun/ppermute | solution.py:382
  174.4 3.3 %collective-permute-start.16 = (f32[128,128]{1,0:T(8,128)S(1)}, f32[128,128]{1,0:T(8,128)S(1)}, u32[]{:S(2)}, u32[]{:S(2)}) collective-permute-start(f32[128,128]{1,0:T(8,128)S(1)} %get-tuple-element.95), channel_id=1, source_target_pairs={{0,4},{1,5},{2,6},{3,7},{4,0},{5,1},{6,2},{7,3},{8,12},{9,13},{10,... | collective-permute-start | bytes 196616 | tf_op jit(solution)/shard_map/cond/branch_1_fun/ppermute | solution.py:382
  178.6 2.0 collective-permute-done.16
  182.4 1.8 collective-permute-start.20
  185.4 2.7 %collective-permute-done.18 = bf16[128,128]{1,0:T(8,128)(2,1)S(1)} collective-permute-done((bf16[128,128]{1,0:T(8,128)(2,1)S(1)}, bf16[128,128]{1,0:T(8,128)(2,1)S(1)}, u32[]{:S(2)}, u32[]{:S(2)}) %collective-permute-start.18) | collective-permute-done | bytes 32800 | tf_op jit(solution)/shard_map/cond/branch_1_fun/ppermute | solution.py:390
  188.1 3.2 %collective-permute-start.21 = (bf16[4,128,128]{2,1,0:T(8,128)(2,1)S(1)}, bf16[4,128,128]{2,1,0:T(8,128)(2,1)S(1)}, u32[]{:S(2)}, u32[]{:S(2)}) collective-permute-start(bf16[4,128,128]{2,1,0:T(8,128)(2,1)S(1)} %pad_maximum_fusion.own), channel_id=1, source_target_pairs={{0,1},{1,0},{2,3},{3,2},{4,5},{5,4},{6,7},{7,6},{8,9},{9,8},{10,11... | collective-permute-start | bytes 393224 | tf_op jit(solution)/shard_map/cond/branch_1_fun/ppermute | solution.py:391
  193.6 2.3 %branch_1_fun.13 = bf16[2048,128]{1,0:T(8,128)(2,1)S(1)} custom-call(s32[8,128]{1,0:T(8,128)S(1)} %get-tuple-element.46.mine, s32[32]{0:T(128)S(1)} %copy-done.31, f32[2048,128]{1,0:T(8,128)S(1)} %copy-done.8, bf16[4,128,128]{2,1,0:T(8,128)(2,1)S(1)} %pad_maximum_fusion.own, bf16[4,128,128]{2,1,0:T(8,128)(2,1)S(1)} %collective-permute-done.21.other, ...), custom_call_target="tpu_custom_call" | custom-call | flops 33554432 | bytes 2097152 | tf_op jit(solution)/shard_map/cond/branch_1_fun/pallas_call | solution.py:459
  (95 shorter events, 36.5 us)
Async XLA Ops:
  11.5 4.5 %copy-start.30 = (s32[32]{0:T(128)}, s32[32]{0:T(128)S(1)}, u32[]{:S(2)}) copy-start(s32[32]{0:T(128)S(1)} %get-tuple-element.47.counts) | copy-start | bytes 388 | tf_op jit(solution)/shard_map/cond
  11.5 180.8 %reduce-scatter.5.cloned.1.call-start = ((), (), s32[]{:S(2)}) async-start(), calls=%async_computation.7 | async-start | bytes 9437184 | tf_op jit(solution)/shard_map/cond/branch_1_fun/reduce_scatter | solution.py:540
  18.2 37.8 %copy-start.4 = (bf16[4,144,1024]{2,1,0:T(8,128)(2,1)}, bf16[4,144,1024]{2,1,0:T(8,128)(2,1)S(1)}, u32[]{:S(2)}) copy-start(bf16[4,144,1024]{2,1,0:T(8,128)(2,1)S(1)} %get-tuple-element.72.refs_0_) | copy-start | bytes 3538948 | tf_op jit(solution)/shard_map/cond
  18.2 37.8 %copy-start.6 = (bf16[4,144,1024]{2,1,0:T(8,128)(2,1)}, bf16[4,144,1024]{2,1,0:T(8,128)(2,1)S(1)}, u32[]{:S(2)}) copy-start(bf16[4,144,1024]{2,1,0:T(8,128)(2,1)S(1)} %get-tuple-element.75.refs_5_) | copy-start | bytes 3538948 | tf_op jit(solution)/shard_map/cond
  18.2 37.8 %copy-start.26 = (bf16[2048,1024]{1,0:T(8,128)(2,1)S(1)}, bf16[2048,1024]{1,0:T(8,128)(2,1)}, u32[]{:S(2)}) copy-start(bf16[2048,1024]{1,0:T(8,128)(2,1)} %get-tuple-element.68.hidden) | copy-start | bytes 12582916 | tf_op jit(solution)/shard_map/cond
  18.2 37.8 %copy-start.32 = (bf16[1024,1024]{1,0:T(8,128)(2,1)S(1)}, bf16[1024,1024]{1,0:T(8,128)(2,1)}, u32[]{:S(2)}) copy-start(bf16[1024,1024]{1,0:T(8,128)(2,1)} %get-tuple-element.69.weight) | copy-start | bytes 6291460 | tf_op jit(solution)/shard_map/cond
  18.2 28.5 %collective-permute-start = (bf16[4,144,1024]{2,1,0:T(8,128)(2,1)S(1)}, bf16[4,144,1024]{2,1,0:T(8,128)(2,1)S(1)}, u32[]{:S(2)}, u32[]{:S(2)}) collective-permute-start(bf16[4,144,1024]{2,1,0:T(8,128)(2,1)S(1)} %get-tuple-element.52), channel_id=1, source_target_pairs={{0,32},{8,40},{16,48},{24,56},{32,64},{40,72},{48,80},{56,88},{64,... | collective-permute-start | bytes 3538952 | tf_op jit(solution)/shard_map/cond/branch_1_fun/ppermute | solution.py:52
  20.2 26.5 %collective-permute-start.1 = (bf16[4,144,1024]{2,1,0:T(8,128)(2,1)S(1)}, bf16[4,144,1024]{2,1,0:T(8,128)(2,1)S(1)}, u32[]{:S(2)}, u32[]{:S(2)}) collective-permute-start(bf16[4,144,1024]{2,1,0:T(8,128)(2,1)S(1)} %get-tuple-element.53), channel_id=1, source_target_pairs={{0,96},{8,104},{16,112},{24,120},{32,0},{40,8},{48,16},{56,24},{64... | collective-permute-start | bytes 3538952 | tf_op jit(solution)/shard_map/cond/branch_1_fun/ppermute | solution.py:52
  21.6 27.7 %collective-permute-start.2 = (bf16[4,144,1024]{2,1,0:T(8,128)(2,1)S(1)}, bf16[4,144,1024]{2,1,0:T(8,128)(2,1)S(1)}, u32[]{:S(2)}, u32[]{:S(2)}) collective-permute-start(bf16[4,144,1024]{2,1,0:T(8,128)(2,1)S(1)} %get-tuple-element.54), channel_id=1, source_target_pairs={{0,8},{8,16},{16,24},{24,0},{32,40},{40,48},{48,56},{56,32},{64,72... | collective-permute-start | bytes 3538952 | tf_op jit(solution)/shard_map/cond/branch_1_fun/ppermute | solution.py:52
  23.0 28.7 %collective-permute-start.3 = (bf16[4,144,1024]{2,1,0:T(8,128)(2,1)S(1)}, bf16[4,144,1024]{2,1,0:T(8,128)(2,1)S(1)}, u32[]{:S(2)}, u32[]{:S(2)}) collective-permute-start(bf16[4,144,1024]{2,1,0:T(8,128)(2,1)S(1)} %get-tuple-element.55), channel_id=1, source_target_pairs={{0,24},{8,0},{16,8},{24,16},{32,56},{40,32},{48,40},{56,48},{64,88... | collective-permute-start | bytes 3538952 | tf_op jit(solution)/shard_map/cond/branch_1_fun/ppermute | solution.py:52
  51.7 4.2 %copy-start.2 = (bf16[4,144,1024]{2,1,0:T(8,128)(2,1)}, bf16[4,144,1024]{2,1,0:T(8,128)(2,1)S(1)}, u32[]{:S(2)}) copy-start(bf16[4,144,1024]{2,1,0:T(8,128)(2,1)S(1)} %collective-permute-done.3.refs_3_.refs_9_) | copy-start | bytes 3538948 | tf_op jit(solution)/shard_map/cond
  61.7 3.3 %copy-start = (f32[2048,1024]{1,0:T(8,128)}, f32[2048,1024]{1,0:T(8,128)S(1)}, u32[]{:S(2)}) copy-start(f32[2048,1024]{1,0:T(8,128)S(1)} %branch_1_fun.9) | copy-start | bytes 25165828 | tf_op jit(solution)/shard_map/cond
  65.0 14.5 %collective-permute-start.4 = (bf16[2,144,1024]{2,1,0:T(8,128)(2,1)}, bf16[2,144,1024]{2,1,0:T(8,128)(2,1)S(1)}, u32[]{:S(2)}, u32[]{:S(2)}) collective-permute-start(bf16[2,144,1024]{2,1,0:T(8,128)(2,1)} %copy-done.24), channel_id=1, source_target_pairs={{0,32},{8,40},{16,48},{24,56},{32,64},{40,72},{48,80},{56,88},{64,... | collective-permute-start | bytes 1769480 | tf_op jit(solution)/shard_map/cond/branch_1_fun/ppermute | solution.py:52
  66.3 14.2 %collective-permute-start.5 = (bf16[2,144,1024]{2,1,0:T(8,128)(2,1)}, bf16[2,144,1024]{2,1,0:T(8,128)(2,1)S(1)}, u32[]{:S(2)}, u32[]{:S(2)}) collective-permute-start(bf16[2,144,1024]{2,1,0:T(8,128)(2,1)} %copy-done.23), channel_id=1, source_target_pairs={{0,96},{8,104},{16,112},{24,120},{32,0},{40,8},{48,16},{56,24},{64... | collective-permute-start | bytes 1769480 | tf_op jit(solution)/shard_map/cond/branch_1_fun/ppermute | solution.py:52
  67.8 13.9 %collective-permute-start.6 = (bf16[2,144,1024]{2,1,0:T(8,128)(2,1)}, bf16[2,144,1024]{2,1,0:T(8,128)(2,1)S(1)}, u32[]{:S(2)}, u32[]{:S(2)}) collective-permute-start(bf16[2,144,1024]{2,1,0:T(8,128)(2,1)} %copy-done.22), channel_id=1, source_target_pairs={{0,8},{8,16},{16,24},{24,0},{32,40},{40,48},{48,56},{56,32},{64,72... | collective-permute-start | bytes 1769480 | tf_op jit(solution)/shard_map/cond/branch_1_fun/ppermute | solution.py:52
  69.0 13.6 %collective-permute-start.7 = (bf16[2,144,1024]{2,1,0:T(8,128)(2,1)}, bf16[2,144,1024]{2,1,0:T(8,128)(2,1)S(1)}, u32[]{:S(2)}, u32[]{:S(2)}) collective-permute-start(bf16[2,144,1024]{2,1,0:T(8,128)(2,1)} %copy-done.21), channel_id=1, source_target_pairs={{0,24},{8,0},{16,8},{24,16},{32,56},{40,32},{48,40},{56,48},{64,88... | collective-permute-start | bytes 1769480 | tf_op jit(solution)/shard_map/cond/branch_1_fun/ppermute | solution.py:52
  83.4 72.3 %all-to-all-start = ((bf16[16,144,1024]{2,1,0:T(8,128)(2,1)}), bf16[16,144,1024]{2,1,0:T(8,128)(2,1)}, u32[]{:S(2)}, u32[]{:S(2)}) async-start(bf16[16,144,1024]{2,1,0:T(8,128)(2,1)} %copy-done.1), calls=%async_computation.1 | async-start | bytes 9437184 | tf_op jit(solution)/shard_map/cond/branch_1_fun/all_to_all | solution.py:542
  99.6 44.5 %collective-permute-start.10 = (bf16[144,1024]{1,0:T(8,128)(2,1)S(1)}, bf16[144,1024]{1,0:T(8,128)(2,1)S(1)}, u32[]{:S(2)}, u32[]{:S(2)}) collective-permute-start(bf16[144,1024]{1,0:T(8,128)(2,1)S(1)} %get-tuple-element.81), channel_id=1, source_target_pairs={{0,24},{8,0},{16,8},{24,16},{32,56},{40,32},{48,40},{56,48},{64,88... | collective-permute-start | bytes 884744 | tf_op jit(solution)/shard_map/cond/branch_1_fun/ppermute | solution.py:52
  102.1 46.1 %collective-permute-start.11 = (bf16[144,1024]{1,0:T(8,128)(2,1)}, bf16[144,1024]{1,0:T(8,128)(2,1)S(1)}, u32[]{:S(2)}, u32[]{:S(2)}) collective-permute-start(bf16[144,1024]{1,0:T(8,128)(2,1)} %get-tuple-element.83), channel_id=1, source_target_pairs={{0,32},{8,40},{16,48},{24,56},{32,64},{40,72},{48,80},{56,88},{64,... | collective-permute-start | bytes 884744 | tf_op jit(solution)/shard_map/cond/branch_1_fun/ppermute | solution.py:52
  103.3 49.2 %collective-permute-start.12 = (bf16[144,1024]{1,0:T(8,128)(2,1)}, bf16[144,1024]{1,0:T(8,128)(2,1)S(1)}, u32[]{:S(2)}, u32[]{:S(2)}) collective-permute-start(bf16[144,1024]{1,0:T(8,128)(2,1)} %get-tuple-element.84), channel_id=1, source_target_pairs={{0,64},{8,72},{16,80},{24,88},{32,96},{40,104},{48,112},{56,120},{... | collective-permute-start | bytes 884744 | tf_op jit(solution)/shard_map/cond/branch_1_fun/ppermute | solution.py:52
  105.7 46.8 %collective-permute-start.13 = (bf16[144,1024]{1,0:T(8,128)(2,1)}, bf16[144,1024]{1,0:T(8,128)(2,1)S(1)}, u32[]{:S(2)}, u32[]{:S(2)}) collective-permute-start(bf16[144,1024]{1,0:T(8,128)(2,1)} %get-tuple-element.85), channel_id=1, source_target_pairs={{0,96},{8,104},{16,112},{24,120},{32,0},{40,8},{48,16},{56,24},{64... | collective-permute-start | bytes 884744 | tf_op jit(solution)/shard_map/cond/branch_1_fun/ppermute | solution.py:52
  106.9 45.6 %collective-permute-start.8 = (bf16[144,1024]{1,0:T(8,128)(2,1)}, bf16[144,1024]{1,0:T(8,128)(2,1)S(1)}, u32[]{:S(2)}, u32[]{:S(2)}) collective-permute-start(bf16[144,1024]{1,0:T(8,128)(2,1)} %get-tuple-element.79), channel_id=1, source_target_pairs={{0,8},{8,16},{16,24},{24,0},{32,40},{40,48},{48,56},{56,32},{64,72... | collective-permute-start | bytes 884744 | tf_op jit(solution)/shard_map/cond/branch_1_fun/ppermute | solution.py:52
  144.1 9.0 %collective-permute-start.9 = (bf16[144,1024]{1,0:T(8,128)(2,1)}, bf16[144,1024]{1,0:T(8,128)(2,1)S(1)}, u32[]{:S(2)}, u32[]{:S(2)}) collective-permute-start(bf16[144,1024]{1,0:T(8,128)(2,1)} %get-tuple-element.80), channel_id=1, source_target_pairs={{0,16},{8,24},{16,0},{24,8},{32,48},{40,56},{48,32},{56,40},{64,80... | collective-permute-start | bytes 884744 | tf_op jit(solution)/shard_map/cond/branch_1_fun/ppermute | solution.py:52
  155.8 36.5 %copy-start.31 = (s32[32]{0:T(128)S(1)}, s32[32]{0:T(128)}, u32[]{:S(2)}) copy-start(s32[32]{0:T(128)} %copy-done.30) | copy-start | bytes 388 | tf_op jit(solution)/shard_map/cond
  161.8 10.0 %collective-permute-start.14 = (f32[512,128]{1,0:T(8,128)S(1)}, f32[512,128]{1,0:T(8,128)S(1)}, u32[]{:S(2)}, u32[]{:S(2)}) collective-permute-start(f32[512,128]{1,0:T(8,128)S(1)} %constant_dynamic-slice_fusion.3), channel_id=1, source_target_pairs={{0,1},{1,0},{2,3},{3,2},{4,5},{5,4},{6,7},{7,6},{8,9},{9,8},{10,11... | collective-permute-start | bytes 786440 | tf_op jit(solution)/shard_map/cond/branch_1_fun/ppermute | solution.py:378
  171.8 6.9 %collective-permute-start.15 = (f32[128,128]{1,0:T(8,128)S(1)}, f32[128,128]{1,0:T(8,128)S(1)}, u32[]{:S(2)}, u32[]{:S(2)}) collective-permute-start(f32[128,128]{1,0:T(8,128)S(1)} %get-tuple-element.97), channel_id=1, source_target_pairs={{0,2},{1,3},{2,4},{3,5},{4,6},{5,7},{6,0},{7,1},{8,10},{9,11},{10,... | collective-permute-start | bytes 196616 | tf_op jit(solution)/shard_map/cond/branch_1_fun/ppermute | solution.py:382
  174.4 6.2 %collective-permute-start.16 = (f32[128,128]{1,0:T(8,128)S(1)}, f32[128,128]{1,0:T(8,128)S(1)}, u32[]{:S(2)}, u32[]{:S(2)}) collective-permute-start(f32[128,128]{1,0:T(8,128)S(1)} %get-tuple-element.95), channel_id=1, source_target_pairs={{0,4},{1,5},{2,6},{3,7},{4,0},{5,1},{6,2},{7,3},{8,12},{9,13},{10,... | collective-permute-start | bytes 196616 | tf_op jit(solution)/shard_map/cond/branch_1_fun/ppermute | solution.py:382
  177.7 3.4 %collective-permute-start.17 = (f32[128,128]{1,0:T(8,128)S(1)}, f32[128,128]{1,0:T(8,128)S(1)}, u32[]{:S(2)}, u32[]{:S(2)}) collective-permute-start(f32[128,128]{1,0:T(8,128)S(1)} %get-tuple-element.96), channel_id=1, source_target_pairs={{0,6},{1,7},{2,0},{3,1},{4,2},{5,3},{6,4},{7,5},{8,14},{9,15},{10,... | collective-permute-start | bytes 196616 | tf_op jit(solution)/shard_map/cond/branch_1_fun/ppermute | solution.py:382
  181.1 4.3 %collective-permute-start.19 = (bf16[128,128]{1,0:T(8,128)(2,1)S(1)}, bf16[128,128]{1,0:T(8,128)(2,1)S(1)}, u32[]{:S(2)}, u32[]{:S(2)}) collective-permute-start(bf16[128,128]{1,0:T(8,128)(2,1)S(1)} %add_convert_fusion), channel_id=1, source_target_pairs={{0,4},{1,5},{2,6},{3,7},{4,0},{5,1},{6,2},{7,3},{8,12},{9,13},{10,... | collective-permute-start | bytes 98312 | tf_op jit(solution)/shard_map/cond/branch_1_fun/ppermute | solution.py:390
  182.4 3.1 %collective-permute-start.20 = (bf16[128,128]{1,0:T(8,128)(2,1)S(1)}, bf16[128,128]{1,0:T(8,128)(2,1)S(1)}, u32[]{:S(2)}, u32[]{:S(2)}) collective-permute-start(bf16[128,128]{1,0:T(8,128)(2,1)S(1)} %add_convert_fusion), channel_id=1, source_target_pairs={{0,6},{1,7},{2,0},{3,1},{4,2},{5,3},{6,4},{7,5},{8,14},{9,15},{10,... | collective-permute-start | bytes 98312 | tf_op jit(solution)/shard_map/cond/branch_1_fun/ppermute | solution.py:390
  184.1 4.0 %collective-permute-start.18 = (bf16[128,128]{1,0:T(8,128)(2,1)S(1)}, bf16[128,128]{1,0:T(8,128)(2,1)S(1)}, u32[]{:S(2)}, u32[]{:S(2)}) collective-permute-start(bf16[128,128]{1,0:T(8,128)(2,1)S(1)} %add_convert_fusion), channel_id=1, source_target_pairs={{0,2},{1,3},{2,4},{3,5},{4,6},{5,7},{6,0},{7,1},{8,10},{9,11},{10,... | collective-permute-start | bytes 98312 | tf_op jit(solution)/shard_map/cond/branch_1_fun/ppermute | solution.py:390
  188.1 4.2 %collective-permute-start.21 = (bf16[4,128,128]{2,1,0:T(8,128)(2,1)S(1)}, bf16[4,128,128]{2,1,0:T(8,128)(2,1)S(1)}, u32[]{:S(2)}, u32[]{:S(2)}) collective-permute-start(bf16[4,128,128]{2,1,0:T(8,128)(2,1)S(1)} %pad_maximum_fusion.own), channel_id=1, source_target_pairs={{0,1},{1,0},{2,3},{3,2},{4,5},{5,4},{6,7},{7,6},{8,9},{9,8},{10,11... | collective-permute-start | bytes 393224 | tf_op jit(solution)/shard_map/cond/branch_1_fun/ppermute | solution.py:391
  (22 other events, 22.5 us)
Sparse Core Ops, SparseCore 0:
  65.2 53.5 reduce-scatter.4

commit v11 on v10

--- a/solution.py
+++ b/solution.py
@@ -169,8 +169,13 @@
         copy.wait()
 
 
-def gather_kernel(lines, served, mine, down, up, *refs):
-    main, outs, scratch = refs[0], refs[1 : 1 + len(lines)], refs[1 + len(lines) :]
+def main_kernel(served, mine, down, up, out, *scratch):
+    rows = [(served[p, 0], served[p, 1]) for p in range(out.shape[0])]
+    copy_units([(out, p, pair) for p, pair in enumerate(rows)], down, up, *scratch)
+
+
+def extra_kernel(lines, served, mine, down, up, *refs):
+    outs, scratch = refs[: len(lines)], refs[len(lines) :]
     dp_count = served.shape[0]
     side = math.isqrt(dp_count)
     hot = mine[FLAGS, HOT]
@@ -187,19 +192,13 @@
                 wanted.append((out, i, (served[peer, first], served[peer, first + 1])))
         copy_units(wanted, down, up, *scratch)
 
-    copy_units(
-        [(main, p, (served[p, 0], served[p, 1])) for p in range(dp_count)], down, up, *scratch
-    )
-
-
-def gather_units(lines, served, mine, down, up):
+
+def gather_units(kernel, shapes, served, mine, down, up):
     _, rank, width = down.shape
     lanes = up.shape[2]
-    dp_count = served.shape[0]
-    shapes = [dp_count] + [len(units) for _, units in lines]
-    count = max(dp_count, sum(shapes[1:]))
+    count = sum(shapes)
     return pl.pallas_call(
-        functools.partial(gather_kernel, lines),
+        kernel,
         out_shape=[jax.ShapeDtypeStruct((n, 2 * rank + 16, width), down.dtype) for n in shapes],
         in_specs=[SMEM, SMEM, HBM, HBM],
         out_specs=[VMEM] * len(shapes),
@@ -208,7 +207,7 @@
             pltpu.SemaphoreType.DMA((2 * count,)),
             pltpu.SemaphoreType.DMA((2 * count,)),
         ],
-        compiler_params=pltpu.CompilerParams(vmem_limit_bytes=18 << 20),
+        compiler_params=pltpu.CompilerParams(vmem_limit_bytes=(count // 2 << 20)),
         cost_estimate=pl.CostEstimate(
             flops=0, bytes_accessed=count * rank * (width + lanes) * 8, transcendentals=0
         ),
@@ -307,8 +306,8 @@
     )(hidden, weight)
 
 
-def paired(hidden, mine, i, pairs, cap, first, second):
-    spots = [pl.multiple_of(mine[ORDER, j] * cap, cap) for j in (i, i + pairs)]
+def paired(hidden, mine, groups, cap, first, second):
+    spots = [pl.multiple_of(mine[ORDER, j] * cap, cap) for j in groups]
     rows = jnp.concatenate([hidden[pl.ds(spot, cap), :] for spot in spots], axis=0)
     product = lax.dot_general(
         rows,
@@ -320,11 +319,9 @@
     return jnp.where(lane < first.shape[0], product[:cap], product[cap:])
 
 
-def low_kernel(cap, mine, hidden, main, *refs):
-    extras, out = refs[:-1], refs[-1]
+def low_main_kernel(cap, mine, hidden, main, out):
     rank = out.shape[1] // 2
-    pairs = out.shape[0] // cap
-    full = pairs - EXTRA
+    pairs = out.shape[0] // cap - EXTRA // 2
 
     def weights(j):
         place = mine[PLACE, j]
@@ -333,30 +330,40 @@
 
     def body(i, carry):
         at = pl.ds(pl.multiple_of(i * cap, cap), cap)
-        out[at, :] = paired(hidden, mine, i, pairs, cap, weights(i), weights(i + pairs))
+        spots = (i, i + pairs)
+        out[at, :] = paired(hidden, mine, spots, cap, weights(i), weights(i + pairs))
         return carry
 
-    lax.fori_loop(0, full, body, 0, unroll=2)
-    for e in range(EXTRA):
-        i = full + e
-        late = extras[e // 2][e % 2 * rank : (e % 2 + 1) * rank, :]
-        out[i * cap : (i + 1) * cap, :] = paired(hidden, mine, i, pairs, cap, weights(i), late)
-
-
-def low_partial(mine, hidden, main, extras, cap, rank):
+    lax.fori_loop(0, pairs, body, 0, unroll=2)
+
+
+def low_extra_kernel(cap, mine, hidden, first, second, _, out):
+    rank = out.shape[1] // 2
+    pairs = out.shape[0] // cap
+    for e in range(EXTRA // 2):
+        spots = (2 * pairs - EXTRA + e, 2 * pairs - EXTRA // 2 + e)
+        at = (pairs - EXTRA // 2 + e) * cap
+        part = slice(e * rank, (e + 1) * rank)
+        out[at : at + cap, :] = paired(
+            hidden, mine, spots, cap, first[part, :], second[part, :]
+        )
+
+
+def low_call(kernel, cap, rank, mine, hidden, arrays, aliases):
     pairs = hidden.shape[0] // cap // 2
     return pl.pallas_call(
-        functools.partial(low_kernel, cap),
+        functools.partial(kernel, cap),
         out_shape=jax.ShapeDtypeStruct((pairs * cap, 2 * rank), jnp.float32),
-        in_specs=[SMEM] + [VMEM] * (2 + len(extras)),
+        in_specs=[SMEM] + [VMEM] * (1 + len(arrays)),
         out_specs=VMEM,
+        input_output_aliases=aliases,
         compiler_params=pltpu.CompilerParams(vmem_limit_bytes=12 << 20),
         cost_estimate=pl.CostEstimate(
             flops=pairs * cap * rank * 4 * hidden.shape[1],
-            bytes_accessed=(hidden.size + main.size) * 2,
+            bytes_accessed=sum(array.size for array in arrays) * 2,
             transcendentals=0,
         ),
-    )(mine, hidden, main, *extras)
+    )(mine, hidden, *arrays)
 
 
 def turn(step):
@@ -415,8 +422,7 @@
     lanes = base.shape[1]
     z, core = mine[FLAGS, CHIP], mine[FLAGS, CORE]
     steps = rank // 16
-    pairs = groups // 2
-    full = pairs - EXTRA
+    pairs = (groups - EXTRA) // 2
     for d in range(chips):
         quarter = lax.rem(z - d + chips, chips)
         for ref, half in ((own, core), (other, 1 - core)):
@@ -437,16 +443,16 @@
         blend(base, out, counts, mine, (i, i + pairs), both, up(i) + up(i + pairs), cap)
         return carry
 
-    lax.fori_loop(0, full, body, 0, unroll=2)
-    for e in range(EXTRA):
-        i = full + e
-        pack = extras[e // 2]
-        late = [
-            pack[:, (e % 2 * steps + part) * lanes : (e % 2 * steps + part + 1) * lanes]
+    lax.fori_loop(0, pairs, body, 0, unroll=2)
+    for e in range(EXTRA // 2):
+        ups = [
+            pack[:, (e * steps + part) * lanes : (e * steps + part + 1) * lanes]
+            for pack in extras
             for part in range(steps)
         ]
-        both = low[i * cap : (i + 1) * cap, :]
-        blend(base, out, counts, mine, (i, i + pairs), both, up(i) + late, cap)
+        both = low[(pairs + e) * cap : (pairs + e + 1) * cap, :]
+        spots = (groups - EXTRA + e, groups - EXTRA // 2 + e)
+        blend(base, out, counts, mine, spots, both, ups, cap)
 
 
 def whole(array):
@@ -528,18 +534,32 @@
         turned = ((0, 1), (0, 2), (0, -1), (1, 0), (2, 0), (-1, 0))
         send = lambda values, ways: [shift(v, *way) for v, way in zip(values, ways)]
         barrier = lax.optimization_barrier
-        main_sent, *gathered = gather_units(soon + late, served, mine, down_weights, up_weights)
+        (main_sent,) = gather_units(
+            main_kernel, [dp_count], served, mine, down_weights, up_weights
+        )
+        main = lax.all_to_all(main_sent, "dp", 0, 0, tiled=True)
         unit, dtype = main_sent.shape[1:], main_sent.dtype
+        later_served, _ = barrier((served, main_sent))
+        wanted = soon + late
+        gathered = gather_units(
+            functools.partial(extra_kernel, wanted),
+            [len(units) for _, units in wanted],
+            later_served,
+            mine,
+            down_weights,
+            up_weights,
+        )
         near, homes = gathered[4:8], gathered[8:]
-        fresh = barrier(send(gathered[:4], moves))
+        fresh = send(gathered[:4], moves)
+        base_hidden, _ = barrier((hidden, gathered))
+        base_terms = base_product(base_hidden, value_weight)
+        main, fresh, base_terms = barrier((main, fresh, base_terms))
+        base = lax.psum_scatter(base_terms, "tp", scatter_dimension=1, tiled=True)
+        partial = low_call(low_main_kernel, cap, rank, mine, hidden, (main,), {})
         relayed = vmem_call(
             relay_kernel, ((2,) + unit,) * 4, dtype, (mine,), (*fresh, *near)
         )
-        base_hidden, _ = barrier((hidden, relayed))
-        base_terms = base_product(base_hidden, value_weight)
-        base = lax.psum_scatter(base_terms, "tp", scatter_dimension=1, tiled=True)
-        near_a, main_sent = barrier((send(relayed, moves), main_sent))
-        main = lax.all_to_all(main_sent, "dp", 0, 0, tiled=True)
+        near_a, partial = barrier((send(relayed, moves), partial))
         tree_arrays = [
             (homes[h], near_a[2 * h], near_a[2 * h + 1], fresh[2 * h], fresh[2 * h + 1])
             for h in range(2)
@@ -551,7 +571,9 @@
         extras = vmem_call(
             pick_kernel, (unit,) * 2, dtype, (mine,), (lines[0], *got[:3], lines[4], *got[3:])
         )
-        partial = low_partial(mine, hidden, main, extras, cap, rank)
+        partial = low_call(
+            low_extra_kernel, cap, rank, mine, hidden, (*extras, partial), {4: 0}
+        )
         own, other = low_rank_up(low_rank_down(partial))
         return combine(mine, counts, base, own, other, main, extras, rank)
 

time: 204 us -> 209 us (1.025)
  local copies, waits for them, and re-layouts: 28 us -> 17.4 us
  waiting for transfers between devices: 91.9 us -> 100 us
  Pallas kernels: 23.8 us -> 31 us
    cond x58 -> x34, local copies, waits for them, and re-layouts: 25 us -> 14.4 us
    ppermute x14, waiting for transfers between devices: 83 us -> 89.3 us  [shift(): return lax.ppermute(value, 'dp', pairs)]
    pallas_call x2 -> x4, Pallas kernels: 10.3 us -> 15.2 us  [the longest x2 8.03 us: gather_units(): pl.pallas_call(kernel, out_shape=[jax.ShapeDtypeStruct((n, 2 * rank + 16,...]
    all_to_all x1, starting transfers between devices: 4.57 us -> 7.76 us  [narrow(): main = lax.all_to_all(main_sent, 'dp', 0, 0, tiled=True)]
    pallas_call x3, Pallas kernels: 3.62 us -> 5.87 us  [vmem_call(): pl.pallas_call(kernel, out_shape=[jax.ShapeDtypeStruct(shape, dtype) for...]
    ppermute x3, waiting for transfers between devices: 2.68 us -> 4.9 us  [low_rank_down(): lax.ppermute(cut(total, (z + d) % chips * piece, piece), 'tp', turn(d))]
  transfers between devices with their start and end apart: 24 -> 24, of which waited for: 17 -> 15; matrix products, arithmetic and copies ran while one was open for 0% -> 0% of each run, Pallas kernels for 4% -> 11%
where the time goes in v11:
time: 209 us; the launch traced here: 208 us
  waiting for transfers between devices  100 us (48%)
  starting transfers between devices  45.1 us (22%)
  Pallas kernels  31 us (15%)
  local copies, waits for them, and re-layouts  17.4 us (8%)
  between operations  14.1 us (7%)
    ppermute x14, waiting for transfers between devices, shift(): return lax.ppermute(value, 'dp', pairs)  89.3 us
    ppermute x14, starting transfers between devices, shift(): return lax.ppermute(value, 'dp', pairs)  19.2 us
    cond x34, local copies, waits for them, and re-layouts  14.4 us
    pallas_call x2, Pallas kernels, gather_units(): pl.pallas_call(kernel, out_shape=[jax.ShapeDtypeStruct((n, 2 * rank + 16,...  8.03 us
    all_to_all x1, starting transfers between devices, narrow(): main = lax.all_to_all(main_sent, 'dp', 0, 0, tiled=True)  7.76 us
    ppermute x1, starting transfers between devices, low_rank_down(): lax.ppermute(cut(partial, (1 - core) * half, half), 'tp', swap())  7.56 us
    pallas_call x2, Pallas kernels, low_call(): pl.pallas_call(functools.partial(kernel, cap), out_shape=jax.ShapeDtypeSt...  7.14 us
    pallas_call x3, Pallas kernels, vmem_call(): pl.pallas_call(kernel, out_shape=[jax.ShapeDtypeStruct(shape, dtype) for...  5.87 us
  transfers between devices with their start and end apart: 24, of which 15 were waited for; matrix products, arithmetic and copies ran while one was open for 0% of the time, Pallas kernels for 11%

profile of v11, /device:TPU:1, one launch (start us, length us, event | category | flops | bytes accessed | tf_op | source)
XLA Modules:
  0.0 208.0 jit_solution(13904582551070465141)
XLA Ops:
  7.4 1.8 shard_map.75
  11.3 189.1 %conditional.1 = (bf16[2048,128]{1,0:T(8,128)(2,1)S(1)}) conditional(s32[]{:T(128)} %bitcast.16, (s32[32]{0:T(128)S(1)}, bf16[2048,1024]{1,0:T(8,128)(2,1)}, bf16[1024,1024]{1,0:T(8,128)(2,1)}, s32[512]{0:T(512)}, s32[2048]{0:T(1024)}, /*index=5*/s32[]{:T(128)}, bf16[128,64,1024]{2,1,0:T(8,128)(2,1)}, bf16[128,64,128]{2,1,0:T(8,128)(2,1)}) %tuple.15, ...), branch_computations={%region_0.5_spmd, %region_5.7_spmd} | conditional | flops 4865720320 | bytes 284132640 | solution.py:580
  11.3 3.7 %branch_1_fun.9 = bf16[16,144,1024]{2,1,0:T(8,128)(2,1)S(1)} custom-call(s32[16,128]{1,0:T(8,128)S(1)} %get-tuple-element.51.served, s32[8,128]{1,0:T(8,128)S(1)} %get-tuple-element.46.mine, bf16[128,64,1024]{2,1,0:T(8,128)(2,1)} %get-tuple-element.49.down, bf16[128,64,128]{2,1,0:T(8,128)(2,1)} %get-tuple-element.50.up), custom_call_target="tpu_custom_call" | custom-call | bytes 9437184 | tf_op jit(solution)/shard_map/cond/branch_1_fun/pallas_call | solution.py:200
  15.0 2.1 %copy-done = bf16[16,144,1024]{2,1,0:T(8,128)(2,1)} copy-done((bf16[16,144,1024]{2,1,0:T(8,128)(2,1)}, bf16[16,144,1024]{2,1,0:T(8,128)(2,1)S(1)}, u32[]{:S(2)}) %copy-start) | copy-done | bytes 4718616 | tf_op jit(solution)/shard_map/cond
  17.1 7.8 %all-to-all-start = ((bf16[16,144,1024]{2,1,0:T(8,128)(2,1)}), bf16[16,144,1024]{2,1,0:T(8,128)(2,1)}, u32[]{:S(2)}, u32[]{:S(2)}) async-start(bf16[16,144,1024]{2,1,0:T(8,128)(2,1)} %copy-done), calls=%async_computation | async-start | bytes 9437184 | tf_op jit(solution)/shard_map/cond/branch_1_fun/all_to_all | solution.py:540
  25.0 4.3 %branch_1_fun.10 = (bf16[4,144,1024]{2,1,0:T(8,128)(2,1)}, bf16[4,144,1024]{2,1,0:T(8,128)(2,1)}, bf16[4,144,1024]{2,1,0:T(8,128)(2,1)}, bf16[4,144,1024]{2,1,0:...) custom-call(s32[16,128]{1,0:T(8,128)S(1)} %get-tuple-element.51.serv, ...), custom_call_target="tpu_custom_call" | custom-call | bytes 18874368 | tf_op jit(solution)/shard_map/cond/branch_1_fun/pallas_call | solution.py:200
  33.9 1.3 collective-permute-start
  35.2 1.4 collective-permute-start.1
  37.9 1.4 collective-permute-start.3
  39.2 5.7 %branch_1_fun.11 = f32[2048,1024]{1,0:T(8,128)S(1)} custom-call(bf16[2048,1024]{1,0:T(8,128)(2,1)S(1)} %copy-done.14, bf16[1024,1024]{1,0:T(8,128)(2,1)S(1)} %copy-done.20), custom_call_target="tpu_custom_call" | custom-call | flops 4294967296 | bytes 14680064 | tf_op jit(solution)/shard_map/cond/branch_1_fun/pallas_call | solution.py:291
  44.9 3.3 %copy-done.1 = f32[2048,1024]{1,0:T(8,128)} copy-done((f32[2048,1024]{1,0:T(8,128)}, f32[2048,1024]{1,0:T(8,128)S(1)}, u32[]{:S(2)}) %copy-start.1) | copy-done | bytes 8388632 | tf_op jit(solution)/shard_map/cond
  48.2 74.0 %collective-permute-done.refs_0_.refs_3_ = bf16[4,144,1024]{2,1,0:T(8,128)(2,1)S(1)} collective-permute-done((bf16[4,144,1024]{2,1,0:T(8,128)(2,1)}, bf16[4,144,1024]{2,1,0:T(8,128)(2,1)S(1)}, u32[]{:S(2)}, u32[]{:S(2)}) %collective-permute-start) | collective-permute-done | bytes 1179680 | tf_op jit(solution)/shard_map/cond/branch_1_fun/ppermute | solution.py:52
  125.4 2.1 %branch_1_fun.12 = (bf16[2,144,1024]{2,1,0:T(8,128)(2,1)S(1)}, bf16[2,144,1024]{2,1,0:T(8,128)(2,1)S(1)}, bf16[2,144,1024]{2,1,0:T(8,128)(2,1)S(1)}, bf16[2,144,1024]{2,1,0:T(8,128)(2,1)S(1)}) custom-call(s32[8,128]{1,0:T(8,128)S(1)} %get-tuple-element.46.mine, bf16[4,144,1024]{2,1,0:T(8,128)(2,1)S(1)} %collective-permute-done.refs_0_.refs_3_, ...), custom_call_target="tpu_custom_call" | custom-call | bytes 4718592 | tf_op jit(solution)/shard_map/cond/branch_1_fun/pallas_call | solution.py:218
  127.5 2.2 %collective-permute-start.4 = (bf16[2,144,1024]{2,1,0:T(8,128)(2,1)S(1)}, bf16[2,144,1024]{2,1,0:T(8,128)(2,1)S(1)}, u32[]{:S(2)}, u32[]{:S(2)}) collective-permute-start(bf16[2,144,1024]{2,1,0:T(8,128)(2,1)S(1)} %get-tuple-element.70), channel_id=1, source_target_pairs={{0,32},{8,40},{16,48},{24,56},{32,64},{40,72},{48,80},{56,88},{64,... | collective-permute-start | bytes 1769480 | tf_op jit(solution)/shard_map/cond/branch_1_fun/ppermute | solution.py:52
  130.3 2.0 collective-permute-start.6
  132.9 4.6 %branch_1_fun.13._ = f32[1024,128]{1,0:T(8,128)S(1)} custom-call(s32[8,128]{1,0:T(8,128)S(1)} %get-tuple-element.46.mine, bf16[2048,1024]{1,0:T(8,128)(2,1)S(1)} %copy-done.15, bf16[16,144,1024]{2,1,0:T(8,128)(2,1)} %all-to-all-done.main), custom_call_target="tpu_custom_call" | custom-call | flops 268435456 | bytes 4718592 | tf_op jit(solution)/shard_map/cond/branch_1_fun/pallas_call | solution.py:354
  137.5 4.7 %collective-permute-done.4.refs_1_ = bf16[2,144,1024]{2,1,0:T(8,128)(2,1)S(1)} collective-permute-done((bf16[2,144,1024]{2,1,0:T(8,128)(2,1)S(1)}, bf16[2,144,1024]{2,1,0:T(8,128)(2,1)S(1)}, u32[]{:S(2)}, u32[]{:S(2)}) %collective-permute-start.4) | collective-permute-done | bytes 589856 | tf_op jit(solution)/shard_map/cond/branch_1_fun/ppermute | solution.py:52
  142.9 1.4 collective-permute-done.6.refs_6_
  144.8 3.1 %branch_1_fun.14 = (bf16[144,1024]{1,0:T(8,128)(2,1)S(1)}, bf16[144,1024]{1,0:T(8,128)(2,1)S(1)}, bf16[144,1024]{1,0:T(8,128)(2,1)}, bf16[144,1024]{1,0:T(8,128)...) custom-call(s32[8,128]{1,0:T(8,128)S(1)} %get-tuple-element.46.mine,, ...), custom_call_target="tpu_custom_call" | custom-call | bytes 4718592 | tf_op jit(solution)/shard_map/cond/branch_1_fun/pallas_call | solution.py:218
  148.5 2.5 %collective-permute-start.9 = (bf16[144,1024]{1,0:T(8,128)(2,1)}, bf16[144,1024]{1,0:T(8,128)(2,1)S(1)}, u32[]{:S(2)}, u32[]{:S(2)}) collective-permute-start(bf16[144,1024]{1,0:T(8,128)(2,1)} %get-tuple-element.81), channel_id=1, source_target_pairs={{0,16},{8,24},{16,0},{24,8},{32,48},{40,56},{48,32},{56,40},{64,80... | collective-permute-start | bytes 884744 | tf_op jit(solution)/shard_map/cond/branch_1_fun/ppermute | solution.py:52
  151.0 1.3 collective-permute-start.11
  152.3 1.9 collective-permute-start.12
  155.1 2.1 %collective-permute-start.13 = (bf16[144,1024]{1,0:T(8,128)(2,1)}, bf16[144,1024]{1,0:T(8,128)(2,1)S(1)}, u32[]{:S(2)}, u32[]{:S(2)}) collective-permute-start(bf16[144,1024]{1,0:T(8,128)(2,1)} %get-tuple-element.86), channel_id=1, source_target_pairs={{0,96},{8,104},{16,112},{24,120},{32,0},{40,8},{48,16},{56,24},{64... | collective-permute-start | bytes 884744 | tf_op jit(solution)/shard_map/cond/branch_1_fun/ppermute | solution.py:52
  157.3 3.6 %collective-permute-done.9.refs_2_ = bf16[144,1024]{1,0:T(8,128)(2,1)S(1)} collective-permute-done((bf16[144,1024]{1,0:T(8,128)(2,1)}, bf16[144,1024]{1,0:T(8,128)(2,1)S(1)}, u32[]{:S(2)}, u32[]{:S(2)}) %collective-permute-start.9) | collective-permute-done | bytes 294944 | tf_op jit(solution)/shard_map/cond/branch_1_fun/ppermute | solution.py:52
  160.9 2.5 %collective-permute-done.10.refs_3_ = bf16[144,1024]{1,0:T(8,128)(2,1)S(1)} collective-permute-done((bf16[144,1024]{1,0:T(8,128)(2,1)}, bf16[144,1024]{1,0:T(8,128)(2,1)S(1)}, u32[]{:S(2)}, u32[]{:S(2)}) %collective-permute-start.10) | collective-permute-done | bytes 294944 | tf_op jit(solution)/shard_map/cond/branch_1_fun/ppermute | solution.py:52
  165.0 2.6 %branch_1_fun.16 = f32[1024,128]{1,0:T(8,128)S(1)} custom-call(s32[8,128]{1,0:T(8,128)S(1)} %get-tuple-element.46.mine, bf16[2048,1024]{1,0:T(8,128)(2,1)} %get-tuple-element.63.hidden, bf16[144,1024]{1,0:T(8,128)(2,1)S(1)} %get-tuple-element.87.first.refs_0_, ...), custom_call_target="tpu_custom_call", output_to_operand_aliasing={{}: (4, {})} | custom-call | flops 268435456 | bytes 851968 | tf_op jit(solution)/shard_map/cond/branch_1_fun/pallas_call | solution.py:354
  167.7 7.6 %collective-permute-start.14 = (f32[512,128]{1,0:T(8,128)S(1)}, f32[512,128]{1,0:T(8,128)S(1)}, u32[]{:S(2)}, u32[]{:S(2)}) collective-permute-start(f32[512,128]{1,0:T(8,128)S(1)} %constant_dynamic-slice_fusion.3), channel_id=1, source_target_pairs={{0,1},{1,0},{2,3},{3,2},{4,5},{5,4},{6,7},{7,6},{8,9},{9,8},{10,11... | collective-permute-start | bytes 786440 | tf_op jit(solution)/shard_map/cond/branch_1_fun/ppermute | solution.py:385
  176.5 3.9 %collective-permute-start.17 = (f32[128,128]{1,0:T(8,128)S(1)}, f32[128,128]{1,0:T(8,128)S(1)}, u32[]{:S(2)}, u32[]{:S(2)}) collective-permute-start(f32[128,128]{1,0:T(8,128)S(1)} %get-tuple-element.98), channel_id=1, source_target_pairs={{0,6},{1,7},{2,0},{3,1},{4,2},{5,3},{6,4},{7,5},{8,14},{9,15},{10,... | collective-permute-start | bytes 196616 | tf_op jit(solution)/shard_map/cond/branch_1_fun/ppermute | solution.py:389
  181.7 4.9 %collective-permute-done.15 = f32[128,128]{1,0:T(8,128)S(1)} collective-permute-done((f32[128,128]{1,0:T(8,128)S(1)}, f32[128,128]{1,0:T(8,128)S(1)}, u32[]{:S(2)}, u32[]{:S(2)}) %collective-permute-start.15) | collective-permute-done | bytes 65568 | tf_op jit(solution)/shard_map/cond/branch_1_fun/ppermute | solution.py:389
  189.4 2.7 %collective-permute-done.19 = bf16[128,128]{1,0:T(8,128)(2,1)S(1)} collective-permute-done((bf16[128,128]{1,0:T(8,128)(2,1)S(1)}, bf16[128,128]{1,0:T(8,128)(2,1)S(1)}, u32[]{:S(2)}, u32[]{:S(2)}) %collective-permute-start.19) | collective-permute-done | bytes 32800 | tf_op jit(solution)/shard_map/cond/branch_1_fun/ppermute | solution.py:397
  192.2 3.5 %collective-permute-start.21 = (bf16[4,128,128]{2,1,0:T(8,128)(2,1)S(1)}, bf16[4,128,128]{2,1,0:T(8,128)(2,1)S(1)}, u32[]{:S(2)}, u32[]{:S(2)}) collective-permute-start(bf16[4,128,128]{2,1,0:T(8,128)(2,1)S(1)} %pad_maximum_fusion.own), channel_id=1, source_target_pairs={{0,1},{1,0},{2,3},{3,2},{4,5},{5,4},{6,7},{7,6},{8,9},{9,8},{10,11... | collective-permute-start | bytes 393224 | tf_op jit(solution)/shard_map/cond/branch_1_fun/ppermute | solution.py:398
  197.9 2.5 %branch_1_fun.17 = bf16[2048,128]{1,0:T(8,128)(2,1)S(1)} custom-call(s32[8,128]{1,0:T(8,128)S(1)} %get-tuple-element.46.mine, s32[32]{0:T(128)S(1)} %get-tuple-element.47.counts, f32[2048,128]{1,0:T(8,128)S(1)} %copy-done.6, bf16[4,128,128]{2,1,0:T(8,128)(2,1)S(1)} %pad_maximum_fusion.own, bf16[4,128,128]{2,1,0:T(8,128)(2,1)S(1)} %collective-permute-done.21.other, ...), custom_call_target="tpu_custom_call" | custom-call | flops 33554432 | bytes 2097152 | tf_op jit(solution)/shard_map/cond/branch_1_fun/pallas_call | solution.py:465
  (73 shorter events, 25.5 us)
Async XLA Ops:
  15.0 2.1 %copy-start = (bf16[16,144,1024]{2,1,0:T(8,128)(2,1)}, bf16[16,144,1024]{2,1,0:T(8,128)(2,1)S(1)}, u32[]{:S(2)}) copy-start(bf16[16,144,1024]{2,1,0:T(8,128)(2,1)S(1)} %branch_1_fun.9) | copy-start | bytes 14155780 | tf_op jit(solution)/shard_map/cond
  17.1 7.8 %copy-start.17 = (bf16[128,64,128]{2,1,0:T(8,128)(2,1)S(1)}, bf16[128,64,128]{2,1,0:T(8,128)(2,1)}, u32[]{:S(2)}) copy-start(bf16[128,64,128]{2,1,0:T(8,128)(2,1)} %get-tuple-element.50.up) | copy-start | bytes 6291460 | tf_op jit(solution)/shard_map/cond
  17.1 105.0 %all-to-all-start = ((bf16[16,144,1024]{2,1,0:T(8,128)(2,1)}), bf16[16,144,1024]{2,1,0:T(8,128)(2,1)}, u32[]{:S(2)}, u32[]{:S(2)}) async-start(bf16[16,144,1024]{2,1,0:T(8,128)(2,1)} %copy-done), calls=%async_computation | async-start | bytes 9437184 | tf_op jit(solution)/shard_map/cond/branch_1_fun/all_to_all | solution.py:540
  24.9 171.7 %reduce-scatter.5.cloned.1.call-start = ((), (), s32[]{:S(2)}) async-start(), calls=%async_computation.7 | async-start | bytes 9437184 | tf_op jit(solution)/shard_map/cond/branch_1_fun/reduce_scatter | solution.py:557
  25.0 14.2 %copy-start.14 = (bf16[2048,1024]{1,0:T(8,128)(2,1)S(1)}, bf16[2048,1024]{1,0:T(8,128)(2,1)}, u32[]{:S(2)}) copy-start(bf16[2048,1024]{1,0:T(8,128)(2,1)} %get-tuple-element.63.hidden) | copy-start | bytes 12582916 | tf_op jit(solution)/shard_map/cond
  25.0 14.2 %copy-start.20 = (bf16[1024,1024]{1,0:T(8,128)(2,1)S(1)}, bf16[1024,1024]{1,0:T(8,128)(2,1)}, u32[]{:S(2)}) copy-start(bf16[1024,1024]{1,0:T(8,128)(2,1)} %get-tuple-element.64.weight) | copy-start | bytes 6291460 | tf_op jit(solution)/shard_map/cond
  33.9 88.3 %collective-permute-start = (bf16[4,144,1024]{2,1,0:T(8,128)(2,1)}, bf16[4,144,1024]{2,1,0:T(8,128)(2,1)S(1)}, u32[]{:S(2)}, u32[]{:S(2)}) collective-permute-start(bf16[4,144,1024]{2,1,0:T(8,128)(2,1)} %get-tuple-element.52), channel_id=1, source_target_pairs={{0,32},{8,40},{16,48},{24,56},{32,64},{40,72},{48,80},{56,88},{64,... | collective-permute-start | bytes 3538952 | tf_op jit(solution)/shard_map/cond/branch_1_fun/ppermute | solution.py:52
  35.2 87.0 %collective-permute-start.1 = (bf16[4,144,1024]{2,1,0:T(8,128)(2,1)}, bf16[4,144,1024]{2,1,0:T(8,128)(2,1)S(1)}, u32[]{:S(2)}, u32[]{:S(2)}) collective-permute-start(bf16[4,144,1024]{2,1,0:T(8,128)(2,1)} %get-tuple-element.53), channel_id=1, source_target_pairs={{0,96},{8,104},{16,112},{24,120},{32,0},{40,8},{48,16},{56,24},{64... | collective-permute-start | bytes 3538952 | tf_op jit(solution)/shard_map/cond/branch_1_fun/ppermute | solution.py:52
  36.5 85.6 %collective-permute-start.2 = (bf16[4,144,1024]{2,1,0:T(8,128)(2,1)}, bf16[4,144,1024]{2,1,0:T(8,128)(2,1)}, u32[]{:S(2)}, u32[]{:S(2)}) collective-permute-start(bf16[4,144,1024]{2,1,0:T(8,128)(2,1)} %get-tuple-element.54), channel_id=1, source_target_pairs={{0,8},{8,16},{16,24},{24,0},{32,40},{40,48},{48,56},{56,32},{64,72... | collective-permute-start | bytes 3538952 | tf_op jit(solution)/shard_map/cond/branch_1_fun/ppermute | solution.py:52
  37.9 84.3 %collective-permute-start.3 = (bf16[4,144,1024]{2,1,0:T(8,128)(2,1)}, bf16[4,144,1024]{2,1,0:T(8,128)(2,1)}, u32[]{:S(2)}, u32[]{:S(2)}) collective-permute-start(bf16[4,144,1024]{2,1,0:T(8,128)(2,1)} %get-tuple-element.55), channel_id=1, source_target_pairs={{0,24},{8,0},{16,8},{24,16},{32,56},{40,32},{48,40},{56,48},{64,88... | collective-permute-start | bytes 3538952 | tf_op jit(solution)/shard_map/cond/branch_1_fun/ppermute | solution.py:52
  44.9 3.3 %copy-start.1 = (f32[2048,1024]{1,0:T(8,128)}, f32[2048,1024]{1,0:T(8,128)S(1)}, u32[]{:S(2)}) copy-start(f32[2048,1024]{1,0:T(8,128)S(1)} %branch_1_fun.11) | copy-start | bytes 25165828 | tf_op jit(solution)/shard_map/cond
  125.4 7.5 %copy-start.15 = (bf16[2048,1024]{1,0:T(8,128)(2,1)S(1)}, bf16[2048,1024]{1,0:T(8,128)(2,1)}, u32[]{:S(2)}) copy-start(bf16[2048,1024]{1,0:T(8,128)(2,1)} %get-tuple-element.63.hidden) | copy-start | bytes 12582916 | tf_op jit(solution)/shard_map/cond
  127.5 14.7 %collective-permute-start.4 = (bf16[2,144,1024]{2,1,0:T(8,128)(2,1)S(1)}, bf16[2,144,1024]{2,1,0:T(8,128)(2,1)S(1)}, u32[]{:S(2)}, u32[]{:S(2)}) collective-permute-start(bf16[2,144,1024]{2,1,0:T(8,128)(2,1)S(1)} %get-tuple-element.70), channel_id=1, source_target_pairs={{0,32},{8,40},{16,48},{24,56},{32,64},{40,72},{48,80},{56,88},{64,... | collective-permute-start | bytes 1769480 | tf_op jit(solution)/shard_map/cond/branch_1_fun/ppermute | solution.py:52
  129.7 13.2 %collective-permute-start.5 = (bf16[2,144,1024]{2,1,0:T(8,128)(2,1)S(1)}, bf16[2,144,1024]{2,1,0:T(8,128)(2,1)S(1)}, u32[]{:S(2)}, u32[]{:S(2)}) collective-permute-start(bf16[2,144,1024]{2,1,0:T(8,128)(2,1)S(1)} %get-tuple-element.71), channel_id=1, source_target_pairs={{0,96},{8,104},{16,112},{24,120},{32,0},{40,8},{48,16},{56,24},{64... | collective-permute-start | bytes 1769480 | tf_op jit(solution)/shard_map/cond/branch_1_fun/ppermute | solution.py:52
  130.3 14.0 %collective-permute-start.6 = (bf16[2,144,1024]{2,1,0:T(8,128)(2,1)S(1)}, bf16[2,144,1024]{2,1,0:T(8,128)(2,1)S(1)}, u32[]{:S(2)}, u32[]{:S(2)}) collective-permute-start(bf16[2,144,1024]{2,1,0:T(8,128)(2,1)S(1)} %get-tuple-element.72), channel_id=1, source_target_pairs={{0,8},{8,16},{16,24},{24,0},{32,40},{40,48},{48,56},{56,32},{64,72... | collective-permute-start | bytes 1769480 | tf_op jit(solution)/shard_map/cond/branch_1_fun/ppermute | solution.py:52
  132.3 12.6 %copy-start.3 = (bf16[4,144,1024]{2,1,0:T(8,128)(2,1)S(1)}, bf16[4,144,1024]{2,1,0:T(8,128)(2,1)}, u32[]{:S(2)}) copy-start(bf16[4,144,1024]{2,1,0:T(8,128)(2,1)} %copy-done.2) | copy-start | bytes 3538948 | tf_op jit(solution)/shard_map/cond
  132.3 12.6 %copy-start.5 = (bf16[4,144,1024]{2,1,0:T(8,128)(2,1)S(1)}, bf16[4,144,1024]{2,1,0:T(8,128)(2,1)}, u32[]{:S(2)}) copy-start(bf16[4,144,1024]{2,1,0:T(8,128)(2,1)} %copy-done.4) | copy-start | bytes 3538948 | tf_op jit(solution)/shard_map/cond
  132.3 12.5 %collective-permute-start.7 = (bf16[2,144,1024]{2,1,0:T(8,128)(2,1)S(1)}, bf16[2,144,1024]{2,1,0:T(8,128)(2,1)S(1)}, u32[]{:S(2)}, u32[]{:S(2)}) collective-permute-start(bf16[2,144,1024]{2,1,0:T(8,128)(2,1)S(1)} %get-tuple-element.73), channel_id=1, source_target_pairs={{0,24},{8,0},{16,8},{24,16},{32,56},{40,32},{48,40},{56,48},{64,88... | collective-permute-start | bytes 1769480 | tf_op jit(solution)/shard_map/cond/branch_1_fun/ppermute | solution.py:52
  147.9 7.2 %collective-permute-start.8 = (bf16[144,1024]{1,0:T(8,128)(2,1)S(1)}, bf16[144,1024]{1,0:T(8,128)(2,1)S(1)}, u32[]{:S(2)}, u32[]{:S(2)}) collective-permute-start(bf16[144,1024]{1,0:T(8,128)(2,1)S(1)} %get-tuple-element.80), channel_id=1, source_target_pairs={{0,8},{8,16},{16,24},{24,0},{32,40},{40,48},{48,56},{56,32},{64,72... | collective-permute-start | bytes 884744 | tf_op jit(solution)/shard_map/cond/branch_1_fun/ppermute | solution.py:52
  148.5 12.4 %collective-permute-start.9 = (bf16[144,1024]{1,0:T(8,128)(2,1)}, bf16[144,1024]{1,0:T(8,128)(2,1)S(1)}, u32[]{:S(2)}, u32[]{:S(2)}) collective-permute-start(bf16[144,1024]{1,0:T(8,128)(2,1)} %get-tuple-element.81), channel_id=1, source_target_pairs={{0,16},{8,24},{16,0},{24,8},{32,48},{40,56},{48,32},{56,40},{64,80... | collective-permute-start | bytes 884744 | tf_op jit(solution)/shard_map/cond/branch_1_fun/ppermute | solution.py:52
  151.0 12.4 %collective-permute-start.10 = (bf16[144,1024]{1,0:T(8,128)(2,1)}, bf16[144,1024]{1,0:T(8,128)(2,1)S(1)}, u32[]{:S(2)}, u32[]{:S(2)}) collective-permute-start(bf16[144,1024]{1,0:T(8,128)(2,1)} %get-tuple-element.82), channel_id=1, source_target_pairs={{0,24},{8,0},{16,8},{24,16},{32,56},{40,32},{48,40},{56,48},{64,88... | collective-permute-start | bytes 884744 | tf_op jit(solution)/shard_map/cond/branch_1_fun/ppermute | solution.py:52
  151.0 12.4 %collective-permute-start.11 = (bf16[144,1024]{1,0:T(8,128)(2,1)}, bf16[144,1024]{1,0:T(8,128)(2,1)S(1)}, u32[]{:S(2)}, u32[]{:S(2)}) collective-permute-start(bf16[144,1024]{1,0:T(8,128)(2,1)} %get-tuple-element.84), channel_id=1, source_target_pairs={{0,32},{8,40},{16,48},{24,56},{32,64},{40,72},{48,80},{56,88},{64,... | collective-permute-start | bytes 884744 | tf_op jit(solution)/shard_map/cond/branch_1_fun/ppermute | solution.py:52
  152.3 12.0 %collective-permute-start.12 = (bf16[144,1024]{1,0:T(8,128)(2,1)}, bf16[144,1024]{1,0:T(8,128)(2,1)S(1)}, u32[]{:S(2)}, u32[]{:S(2)}) collective-permute-start(bf16[144,1024]{1,0:T(8,128)(2,1)} %get-tuple-element.85), channel_id=1, source_target_pairs={{0,64},{8,72},{16,80},{24,88},{32,96},{40,104},{48,112},{56,120},{... | collective-permute-start | bytes 884744 | tf_op jit(solution)/shard_map/cond/branch_1_fun/ppermute | solution.py:52
  155.1 9.2 %collective-permute-start.13 = (bf16[144,1024]{1,0:T(8,128)(2,1)}, bf16[144,1024]{1,0:T(8,128)(2,1)S(1)}, u32[]{:S(2)}, u32[]{:S(2)}) collective-permute-start(bf16[144,1024]{1,0:T(8,128)(2,1)} %get-tuple-element.86), channel_id=1, source_target_pairs={{0,96},{8,104},{16,112},{24,120},{32,0},{40,8},{48,16},{56,24},{64... | collective-permute-start | bytes 884744 | tf_op jit(solution)/shard_map/cond/branch_1_fun/ppermute | solution.py:52
  167.7 8.7 %collective-permute-start.14 = (f32[512,128]{1,0:T(8,128)S(1)}, f32[512,128]{1,0:T(8,128)S(1)}, u32[]{:S(2)}, u32[]{:S(2)}) collective-permute-start(f32[512,128]{1,0:T(8,128)S(1)} %constant_dynamic-slice_fusion.3), channel_id=1, source_target_pairs={{0,1},{1,0},{2,3},{3,2},{4,5},{5,4},{6,7},{7,6},{8,9},{9,8},{10,11... | collective-permute-start | bytes 786440 | tf_op jit(solution)/shard_map/cond/branch_1_fun/ppermute | solution.py:385
  176.5 5.2 %collective-permute-start.17 = (f32[128,128]{1,0:T(8,128)S(1)}, f32[128,128]{1,0:T(8,128)S(1)}, u32[]{:S(2)}, u32[]{:S(2)}) collective-permute-start(f32[128,128]{1,0:T(8,128)S(1)} %get-tuple-element.98), channel_id=1, source_target_pairs={{0,6},{1,7},{2,0},{3,1},{4,2},{5,3},{6,4},{7,5},{8,14},{9,15},{10,... | collective-permute-start | bytes 196616 | tf_op jit(solution)/shard_map/cond/branch_1_fun/ppermute | solution.py:389
  180.3 6.2 %collective-permute-start.15 = (f32[128,128]{1,0:T(8,128)S(1)}, f32[128,128]{1,0:T(8,128)S(1)}, u32[]{:S(2)}, u32[]{:S(2)}) collective-permute-start(f32[128,128]{1,0:T(8,128)S(1)} %get-tuple-element.99), channel_id=1, source_target_pairs={{0,2},{1,3},{2,4},{3,5},{4,6},{5,7},{6,0},{7,1},{8,10},{9,11},{10,... | collective-permute-start | bytes 196616 | tf_op jit(solution)/shard_map/cond/branch_1_fun/ppermute | solution.py:389
  180.3 6.2 %collective-permute-start.16 = (f32[128,128]{1,0:T(8,128)S(1)}, f32[128,128]{1,0:T(8,128)S(1)}, u32[]{:S(2)}, u32[]{:S(2)}) collective-permute-start(f32[128,128]{1,0:T(8,128)S(1)} %get-tuple-element.97), channel_id=1, source_target_pairs={{0,4},{1,5},{2,6},{3,7},{4,0},{5,1},{6,2},{7,3},{8,12},{9,13},{10,... | collective-permute-start | bytes 196616 | tf_op jit(solution)/shard_map/cond/branch_1_fun/ppermute | solution.py:389
  186.6 2.8 %collective-permute-start.20 = (bf16[128,128]{1,0:T(8,128)(2,1)S(1)}, bf16[128,128]{1,0:T(8,128)(2,1)S(1)}, u32[]{:S(2)}, u32[]{:S(2)}) collective-permute-start(bf16[128,128]{1,0:T(8,128)(2,1)S(1)} %add_convert_fusion), channel_id=1, source_target_pairs={{0,6},{1,7},{2,0},{3,1},{4,2},{5,3},{6,4},{7,5},{8,14},{9,15},{10,... | collective-permute-start | bytes 98312 | tf_op jit(solution)/shard_map/cond/branch_1_fun/ppermute | solution.py:397
  187.7 4.4 %collective-permute-start.19 = (bf16[128,128]{1,0:T(8,128)(2,1)S(1)}, bf16[128,128]{1,0:T(8,128)(2,1)S(1)}, u32[]{:S(2)}, u32[]{:S(2)}) collective-permute-start(bf16[128,128]{1,0:T(8,128)(2,1)S(1)} %add_convert_fusion), channel_id=1, source_target_pairs={{0,4},{1,5},{2,6},{3,7},{4,0},{5,1},{6,2},{7,3},{8,12},{9,13},{10,... | collective-permute-start | bytes 98312 | tf_op jit(solution)/shard_map/cond/branch_1_fun/ppermute | solution.py:397
  187.7 4.4 %collective-permute-start.18 = (bf16[128,128]{1,0:T(8,128)(2,1)S(1)}, bf16[128,128]{1,0:T(8,128)(2,1)S(1)}, u32[]{:S(2)}, u32[]{:S(2)}) collective-permute-start(bf16[128,128]{1,0:T(8,128)(2,1)S(1)} %add_convert_fusion), channel_id=1, source_target_pairs={{0,2},{1,3},{2,4},{3,5},{4,6},{5,7},{6,0},{7,1},{8,10},{9,11},{10,... | collective-permute-start | bytes 98312 | tf_op jit(solution)/shard_map/cond/branch_1_fun/ppermute | solution.py:397
  192.2 4.5 %collective-permute-start.21 = (bf16[4,128,128]{2,1,0:T(8,128)(2,1)S(1)}, bf16[4,128,128]{2,1,0:T(8,128)(2,1)S(1)}, u32[]{:S(2)}, u32[]{:S(2)}) collective-permute-start(bf16[4,128,128]{2,1,0:T(8,128)(2,1)S(1)} %pad_maximum_fusion.own), channel_id=1, source_target_pairs={{0,1},{1,0},{2,3},{3,2},{4,5},{5,4},{6,7},{7,6},{8,9},{9,8},{10,11... | collective-permute-start | bytes 393224 | tf_op jit(solution)/shard_map/cond/branch_1_fun/ppermute | solution.py:398
  (10 other events, 9.8 us)
Sparse Core Ops, SparseCore 0:
  122.3 56.2 reduce-scatter.4

commit v12 on v11

--- a/solution.py
+++ b/solution.py
@@ -169,34 +169,39 @@
         copy.wait()
 
 
-def main_kernel(served, mine, down, up, out, *scratch):
-    rows = [(served[p, 0], served[p, 1]) for p in range(out.shape[0])]
-    copy_units([(out, p, pair) for p, pair in enumerate(rows)], down, up, *scratch)
+def extra_rows(lines, outs, served, mine):
+    side = math.isqrt(served.shape[0])
+    hot = mine[FLAGS, HOT]
+    hot_x, hot_y = lax.div(hot, side), lax.rem(hot, side)
+    wanted = []
+    for out, (x_first, units) in zip(outs, lines):
+        for i, (a, b) in enumerate(units):
+            dx, dy = (a, b) if x_first else (b, a)
+            peer = lax.rem(hot_x + dx, side) * side + lax.rem(hot_y + dy, side)
+            first = MAIN if x_first else MAIN + 2
+            wanted.append((out, i, (served[peer, first], served[peer, first + 1])))
+    return wanted
 
 
 def extra_kernel(lines, served, mine, down, up, *refs):
     outs, scratch = refs[: len(lines)], refs[len(lines) :]
-    dp_count = served.shape[0]
-    side = math.isqrt(dp_count)
-    hot = mine[FLAGS, HOT]
 
     @pl.when((mine[FLAGS, AT] == 0) & (mine[FLAGS, AT + 1] == 0))
     def _():
-        hot_x, hot_y = lax.div(hot, side), lax.rem(hot, side)
-        wanted = []
-        for out, (x_first, units) in zip(outs, lines):
-            for i, (a, b) in enumerate(units):
-                dx, dy = (a, b) if x_first else (b, a)
-                peer = lax.rem(hot_x + dx, side) * side + lax.rem(hot_y + dy, side)
-                first = MAIN if x_first else MAIN + 2
-                wanted.append((out, i, (served[peer, first], served[peer, first + 1])))
-        copy_units(wanted, down, up, *scratch)
+        copy_units(extra_rows(lines, outs, served, mine), down, up, *scratch)
+
+
+def gather_kernel(lines, served, mine, down, up, main, *refs):
+    extra_kernel(lines, served, mine, down, up, *refs)
+    rows = [(served[p, 0], served[p, 1]) for p in range(main.shape[0])]
+    wanted = [(main, p, pair) for p, pair in enumerate(rows)]
+    copy_units(wanted, down, up, *refs[len(lines) :])
 
 
 def gather_units(kernel, shapes, served, mine, down, up):
     _, rank, width = down.shape
     lanes = up.shape[2]
-    count = sum(shapes)
+    count = 16
     return pl.pallas_call(
         kernel,
         out_shape=[jax.ShapeDtypeStruct((n, 2 * rank + 16, width), down.dtype) for n in shapes],
@@ -207,7 +212,7 @@
             pltpu.SemaphoreType.DMA((2 * count,)),
             pltpu.SemaphoreType.DMA((2 * count,)),
         ],
-        compiler_params=pltpu.CompilerParams(vmem_limit_bytes=(count // 2 << 20)),
+        compiler_params=pltpu.CompilerParams(vmem_limit_bytes=14 << 20),
         cost_estimate=pl.CostEstimate(
             flops=0, bytes_accessed=count * rank * (width + lanes) * 8, transcendentals=0
         ),
@@ -534,32 +539,35 @@
         turned = ((0, 1), (0, 2), (0, -1), (1, 0), (2, 0), (-1, 0))
         send = lambda values, ways: [shift(v, *way) for v, way in zip(values, ways)]
         barrier = lax.optimization_barrier
-        (main_sent,) = gather_units(
-            main_kernel, [dp_count], served, mine, down_weights, up_weights
-        )
-        main = lax.all_to_all(main_sent, "dp", 0, 0, tiled=True)
+        main_sent, *gathered = gather_units(
+            functools.partial(gather_kernel, soon),
+            [dp_count] + [len(units) for _, units in soon],
+            served,
+            mine,
+            down_weights,
+            up_weights,
+        )
         unit, dtype = main_sent.shape[1:], main_sent.dtype
-        later_served, _ = barrier((served, main_sent))
-        wanted = soon + late
-        gathered = gather_units(
-            functools.partial(extra_kernel, wanted),
-            [len(units) for _, units in wanted],
+        fresh = send(gathered, moves)
+        later_served, _ = barrier((served, gathered))
+        later = gather_units(
+            functools.partial(extra_kernel, late),
+            [len(units) for _, units in late],
             later_served,
             mine,
             down_weights,
             up_weights,
         )
-        near, homes = gathered[4:8], gathered[8:]
-        fresh = send(gathered[:4], moves)
+        near, homes = later[:4], later[4:]
         base_hidden, _ = barrier((hidden, gathered))
         base_terms = base_product(base_hidden, value_weight)
-        main, fresh, base_terms = barrier((main, fresh, base_terms))
-        base = lax.psum_scatter(base_terms, "tp", scatter_dimension=1, tiled=True)
-        partial = low_call(low_main_kernel, cap, rank, mine, hidden, (main,), {})
+        fresh, near, base_terms = barrier((fresh, near, base_terms))
         relayed = vmem_call(
             relay_kernel, ((2,) + unit,) * 4, dtype, (mine,), (*fresh, *near)
         )
-        near_a, partial = barrier((send(relayed, moves), partial))
+        near_a, main_sent, base_terms = barrier((send(relayed, moves), main_sent, base_terms))
+        base = lax.psum_scatter(base_terms, "tp", scatter_dimension=1, tiled=True)
+        main = lax.all_to_all(main_sent, "dp", 0, 0, tiled=True)
         tree_arrays = [
             (homes[h], near_a[2 * h], near_a[2 * h + 1], fresh[2 * h], fresh[2 * h + 1])
             for h in range(2)
@@ -568,6 +576,8 @@
             line_kernel, (unit,) * 8, dtype, (mine,), tree_arrays[0] + tree_arrays[1]
         )
         got = send(lines[1:4] + lines[5:8], turned)
+        partial = low_call(low_main_kernel, cap, rank, mine, hidden, (main,), {})
+        got, partial = barrier((got, partial))
         extras = vmem_call(
             pick_kernel, (unit,) * 2, dtype, (mine,), (lines[0], *got[:3], lines[4], *got[3:])
         )

time: 209 us -> 194 us (0.928)
  waiting for transfers between devices: 100 us -> 68.6 us
  local copies, waits for them, and re-layouts: 17.4 us -> 31.2 us
  starting transfers between devices: 45.1 us -> 49.5 us
    ppermute x14, waiting for transfers between devices: 89.3 us -> 59.8 us  [shift(): return lax.ppermute(value, 'dp', pairs)]
    cond x34 -> x68, local copies, waits for them, and re-layouts: 14.4 us -> 28.2 us
    ppermute x1, starting transfers between devices: 7.56 us -> 12.5 us  [low_rank_down(): lax.ppermute(cut(partial, (1 - core) * half, half), 'tp', swap())]
    all_to_all x1, starting transfers between devices: 7.76 us -> 4.57 us  [narrow(): main = lax.all_to_all(main_sent, 'dp', 0, 0, tiled=True)]
    ppermute x3, waiting for transfers between devices: 4.9 us -> 2.68 us  [low_rank_down(): lax.ppermute(cut(total, (z + d) % chips * piece, piece), 'tp', turn(d))]
  transfers between devices with their start and end apart: 24 -> 24, of which waited for: 15 -> 17; matrix products, arithmetic and copies ran while one was open for 0% -> 0% of each run, Pallas kernels for 11% -> 9%
where the time goes in v12:
time: 194 us
  waiting for transfers between devices  68.6 us (35%)
  starting transfers between devices  49.5 us (26%)
  local copies, waits for them, and re-layouts  31.2 us (16%)
  Pallas kernels  29.7 us (15%)
  between operations  14.1 us (7%)
    ppermute x14, waiting for transfers between devices, shift(): return lax.ppermute(value, 'dp', pairs)  59.8 us
    cond x68, local copies, waits for them, and re-layouts  28.2 us
    ppermute x14, starting transfers between devices, shift(): return lax.ppermute(value, 'dp', pairs)  20.4 us
    ppermute x1, starting transfers between devices, low_rank_down(): lax.ppermute(cut(partial, (1 - core) * half, half), 'tp', swap())  12.5 us
    pallas_call x2, Pallas kernels, gather_units(): pl.pallas_call(kernel, out_shape=[jax.ShapeDtypeStruct((n, 2 * rank + 16,...  7.74 us
    pallas_call x2, Pallas kernels, low_call(): pl.pallas_call(functools.partial(kernel, cap), out_shape=jax.ShapeDtypeSt...  6.81 us
    ppermute x3, starting transfers between devices, low_rank_down(): lax.ppermute(cut(total, (z + d) % chips * piece, piece), 'tp', turn(d))  5.74 us
    pallas_call x1, Pallas kernels, base_product(): pl.pallas_call(base_kernel, grid=(rows // block,), out_shape=jax.ShapeDty...  5.68 us
  transfers between devices with their start and end apart: 24, of which 17 were waited for; matrix products, arithmetic and copies ran while one was open for 0% of the time, Pallas kernels for 9%

profile of v12, /device:TPU:1, one launch (start us, length us, event | category | flops | bytes accessed | tf_op | source)
XLA Modules:
  0.0 193.8 jit_solution(10952930542347828293)
XLA Ops:
  8.2 1.8 shard_map.75
  11.3 174.8 %conditional.1 = (bf16[2048,128]{1,0:T(8,128)(2,1)S(1)}) conditional(s32[]{:T(128)} %bitcast.16, (s32[32]{0:T(128)S(1)}, bf16[2048,1024]{1,0:T(8,128)(2,1)}, bf16[1024,1024]{1,0:T(8,128)(2,1)}, s32[512]{0:T(512)}, s32[2048]{0:T(1024)}, /*index=5*/s32[]{:T(128)}, bf16[128,64,1024]{2,1,0:T(8,128)(2,1)}, bf16[128,64,128]{2,1,0:T(8,128)(2,1)}) %tuple.16, ...), branch_computations={%region_0.5_spmd, %region_5.7_spmd} | conditional | flops 4865720320 | bytes 370117408 | solution.py:590
  11.6 6.4 %branch_1_fun.9 = (bf16[16,144,1024]{2,1,0:T(8,128)(2,1)S(1)}, bf16[4,144,1024]{2,1,0:T(8,128)(2,1)}, bf16[4,144,1024]{2,1,0:T(8,128)(2,1)}, bf16[4,144,1024]{2,1,0:T(8,128)(2,1)}, bf16[4,144,1024]{2,1,0:T(8,128)(2,1)}) custom-call(s32[16,128]{1,0:T(8,128)S(1)} %get-tuple-element.55.served, s32[8,128]{1,0:T(8,128)S(1)} %get-tuple-element.46.mine, ...), custom_call_target="tpu_custom_call" | custom-call | bytes 9437184 | tf_op jit(solution)/shard_map/cond/branch_1_fun/pallas_call | solution.py:205
  18.0 2.4 %copy-done.1 = bf16[16,144,1024]{2,1,0:T(8,128)(2,1)} copy-done((bf16[16,144,1024]{2,1,0:T(8,128)(2,1)}, bf16[16,144,1024]{2,1,0:T(8,128)(2,1)S(1)}, u32[]{:S(2)}) %copy-start.1) | copy-done | bytes 4718616 | tf_op jit(solution)/shard_map/cond
  20.4 2.0 %collective-permute-start = (bf16[4,144,1024]{2,1,0:T(8,128)(2,1)}, bf16[4,144,1024]{2,1,0:T(8,128)(2,1)S(1)}, u32[]{:S(2)}, u32[]{:S(2)}) collective-permute-start(bf16[4,144,1024]{2,1,0:T(8,128)(2,1)} %get-tuple-element.51), channel_id=1, source_target_pairs={{0,32},{8,40},{16,48},{24,56},{32,64},{40,72},{48,80},{56,88},{64,... | collective-permute-start | bytes 3538952 | tf_op jit(solution)/shard_map/cond/branch_1_fun/ppermute | solution.py:52
  23.7 4.5 %collective-permute-start.2 = (bf16[4,144,1024]{2,1,0:T(8,128)(2,1)}, bf16[4,144,1024]{2,1,0:T(8,128)(2,1)S(1)}, u32[]{:S(2)}, u32[]{:S(2)}) collective-permute-start(bf16[4,144,1024]{2,1,0:T(8,128)(2,1)} %get-tuple-element.53), channel_id=1, source_target_pairs={{0,8},{8,16},{16,24},{24,0},{32,40},{40,48},{48,56},{56,32},{64,72... | collective-permute-start | bytes 3538952 | tf_op jit(solution)/shard_map/cond/branch_1_fun/ppermute | solution.py:52
  28.2 1.3 branch_1_fun.10
  34.9 5.7 %branch_1_fun.11 = f32[2048,1024]{1,0:T(8,128)S(1)} custom-call(bf16[2048,1024]{1,0:T(8,128)(2,1)S(1)} %copy-done.29, bf16[1024,1024]{1,0:T(8,128)(2,1)S(1)} %copy-done.37), custom_call_target="tpu_custom_call" | custom-call | flops 4294967296 | bytes 14680064 | tf_op jit(solution)/shard_map/cond/branch_1_fun/pallas_call | solution.py:296
  40.6 3.3 %copy-done = f32[2048,1024]{1,0:T(8,128)} copy-done((f32[2048,1024]{1,0:T(8,128)}, f32[2048,1024]{1,0:T(8,128)S(1)}, u32[]{:S(2)}) %copy-start) | copy-done | bytes 8388632 | tf_op jit(solution)/shard_map/cond
  43.9 5.2 %collective-permute-done.refs_0_.refs_3_ = bf16[4,144,1024]{2,1,0:T(8,128)(2,1)S(1)} collective-permute-done((bf16[4,144,1024]{2,1,0:T(8,128)(2,1)}, bf16[4,144,1024]{2,1,0:T(8,128)(2,1)S(1)}, u32[]{:S(2)}, u32[]{:S(2)}) %collective-permute-start) | collective-permute-done | bytes 1179680 | tf_op jit(solution)/shard_map/cond/branch_1_fun/ppermute | solution.py:52
  49.3 3.3 %collective-permute-done.2.refs_2_.refs_8_ = bf16[4,144,1024]{2,1,0:T(8,128)(2,1)S(1)} collective-permute-done((bf16[4,144,1024]{2,1,0:T(8,128)(2,1)}, bf16[4,144,1024]{2,1,0:T(8,128)(2,1)S(1)}, u32[]{:S(2)}, u32[]{:S(2)}) %collective-permute-start.2) | collective-permute-done | bytes 1179680 | tf_op jit(solution)/shard_map/cond/branch_1_fun/ppermute | solution.py:52
  52.6 1.9 collective-permute-done.3.refs_3_.refs_9_
  58.7 1.6 branch_1_fun.12
  60.4 2.7 %collective-permute-start.5 = (bf16[2,144,1024]{2,1,0:T(8,128)(2,1)S(1)}, bf16[2,144,1024]{2,1,0:T(8,128)(2,1)S(1)}, u32[]{:S(2)}, u32[]{:S(2)}) collective-permute-start(bf16[2,144,1024]{2,1,0:T(8,128)(2,1)S(1)} %get-tuple-element.72), channel_id=1, source_target_pairs={{0,96},{8,104},{16,112},{24,120},{32,0},{40,8},{48,16},{56,24},{64... | collective-permute-start | bytes 1769480 | tf_op jit(solution)/shard_map/cond/branch_1_fun/ppermute | solution.py:52
  63.4 2.4 %collective-permute-start.7 = (bf16[2,144,1024]{2,1,0:T(8,128)(2,1)S(1)}, bf16[2,144,1024]{2,1,0:T(8,128)(2,1)S(1)}, u32[]{:S(2)}, u32[]{:S(2)}) collective-permute-start(bf16[2,144,1024]{2,1,0:T(8,128)(2,1)S(1)} %get-tuple-element.74), channel_id=1, source_target_pairs={{0,24},{8,0},{16,8},{24,16},{32,56},{40,32},{48,40},{56,48},{64,88... | collective-permute-start | bytes 1769480 | tf_op jit(solution)/shard_map/cond/branch_1_fun/ppermute | solution.py:52
  65.8 8.2 %collective-permute-done.4.refs_1_ = bf16[2,144,1024]{2,1,0:T(8,128)(2,1)S(1)} collective-permute-done((bf16[2,144,1024]{2,1,0:T(8,128)(2,1)S(1)}, bf16[2,144,1024]{2,1,0:T(8,128)(2,1)S(1)}, u32[]{:S(2)}, u32[]{:S(2)}) %collective-permute-start.4) | collective-permute-done | bytes 589856 | tf_op jit(solution)/shard_map/cond/branch_1_fun/ppermute | solution.py:52
  77.9 4.6 %all-to-all-start = ((bf16[16,144,1024]{2,1,0:T(8,128)(2,1)}), bf16[16,144,1024]{2,1,0:T(8,128)(2,1)}, u32[]{:S(2)}, u32[]{:S(2)}) async-start(bf16[16,144,1024]{2,1,0:T(8,128)(2,1)} %copy-done.1), calls=%async_computation.1 | async-start | bytes 9437184 | tf_op jit(solution)/shard_map/cond/branch_1_fun/all_to_all | solution.py:570
  89.3 2.9 %branch_1_fun.13 = (bf16[144,1024]{1,0:T(8,128)(2,1)S(1)}, bf16[144,1024]{1,0:T(8,128)(2,1)}, bf16[144,1024]{1,0:T(8,128)(2,1)}, bf16[144,1024]{1,0:T(8,128)(2,1...) custom-call(s32[8,128]{1,0:T(8,128)S(1)} %get-tuple-element.46.mine,, ...), custom_call_target="tpu_custom_call" | custom-call | bytes 4718592 | tf_op jit(solution)/shard_map/cond/branch_1_fun/pallas_call | solution.py:223
  93.6 2.4 %collective-permute-start.10 = (bf16[144,1024]{1,0:T(8,128)(2,1)S(1)}, bf16[144,1024]{1,0:T(8,128)(2,1)S(1)}, u32[]{:S(2)}, u32[]{:S(2)}) collective-permute-start(bf16[144,1024]{1,0:T(8,128)(2,1)S(1)} %get-tuple-element.87), channel_id=1, source_target_pairs={{0,24},{8,0},{16,8},{24,16},{32,56},{40,32},{48,40},{56,48},{64,88... | collective-permute-start | bytes 884744 | tf_op jit(solution)/shard_map/cond/branch_1_fun/ppermute | solution.py:52
  97.2 2.4 %collective-permute-start.12 = (bf16[144,1024]{1,0:T(8,128)(2,1)}, bf16[144,1024]{1,0:T(8,128)(2,1)S(1)}, u32[]{:S(2)}, u32[]{:S(2)}) collective-permute-start(bf16[144,1024]{1,0:T(8,128)(2,1)} %get-tuple-element.89), channel_id=1, source_target_pairs={{0,64},{8,72},{16,80},{24,88},{32,96},{40,104},{48,112},{56,120},{... | collective-permute-start | bytes 884744 | tf_op jit(solution)/shard_map/cond/branch_1_fun/ppermute | solution.py:52
  100.8 38.0 %collective-permute-done.10.refs_3_ = bf16[144,1024]{1,0:T(8,128)(2,1)S(1)} collective-permute-done((bf16[144,1024]{1,0:T(8,128)(2,1)S(1)}, bf16[144,1024]{1,0:T(8,128)(2,1)S(1)}, u32[]{:S(2)}, u32[]{:S(2)}) %collective-permute-start.10) | collective-permute-done | bytes 294944 | tf_op jit(solution)/shard_map/cond/branch_1_fun/ppermute | solution.py:52
  138.8 5.9 %branch_1_fun.14._ = f32[1024,128]{1,0:T(8,128)S(1)} custom-call(s32[8,128]{1,0:T(8,128)S(1)} %get-tuple-element.46.mine, bf16[2048,1024]{1,0:T(8,128)(2,1)} %get-tuple-element.61.hidden, bf16[16,144,1024]{2,1,0:T(8,128)(2,1)} %all-to-all-done.main), custom_call_target="tpu_custom_call" | custom-call | flops 268435456 | bytes 4718592 | tf_op jit(solution)/shard_map/cond/branch_1_fun/pallas_call | solution.py:359
  144.8 1.5 collective-permute-done.12.refs_6_
  149.0 12.5 %collective-permute-start.14 = (f32[512,128]{1,0:T(8,128)S(1)}, f32[512,128]{1,0:T(8,128)S(1)}, u32[]{:S(2)}, u32[]{:S(2)}) collective-permute-start(f32[512,128]{1,0:T(8,128)S(1)} %constant_dynamic-slice_fusion.3), channel_id=1, source_target_pairs={{0,1},{1,0},{2,3},{3,2},{4,5},{5,4},{6,7},{7,6},{8,9},{9,8},{10,11... | collective-permute-start | bytes 786440 | tf_op jit(solution)/shard_map/cond/branch_1_fun/ppermute | solution.py:390
  162.7 1.7 collective-permute-start.15
  164.4 3.3 %collective-permute-start.16 = (f32[128,128]{1,0:T(8,128)S(1)}, f32[128,128]{1,0:T(8,128)S(1)}, u32[]{:S(2)}, u32[]{:S(2)}) collective-permute-start(f32[128,128]{1,0:T(8,128)S(1)} %get-tuple-element.109), channel_id=1, source_target_pairs={{0,4},{1,5},{2,6},{3,7},{4,0},{5,1},{6,2},{7,3},{8,12},{9,13},{10,... | collective-permute-start | bytes 196616 | tf_op jit(solution)/shard_map/cond/branch_1_fun/ppermute | solution.py:394
  168.7 2.0 %collective-permute-done.16 = f32[128,128]{1,0:T(8,128)S(1)} collective-permute-done((f32[128,128]{1,0:T(8,128)S(1)}, f32[128,128]{1,0:T(8,128)S(1)}, u32[]{:S(2)}, u32[]{:S(2)}) %collective-permute-start.16) | collective-permute-done | bytes 65568 | tf_op jit(solution)/shard_map/cond/branch_1_fun/ppermute | solution.py:394
  172.5 1.8 collective-permute-start.20
  174.2 1.3 collective-permute-done.19
  175.5 2.7 %collective-permute-done.18 = bf16[128,128]{1,0:T(8,128)(2,1)S(1)} collective-permute-done((bf16[128,128]{1,0:T(8,128)(2,1)S(1)}, bf16[128,128]{1,0:T(8,128)(2,1)S(1)}, u32[]{:S(2)}, u32[]{:S(2)}) %collective-permute-start.18) | collective-permute-done | bytes 32800 | tf_op jit(solution)/shard_map/cond/branch_1_fun/ppermute | solution.py:402
  178.2 3.2 %collective-permute-start.21 = (bf16[4,128,128]{2,1,0:T(8,128)(2,1)S(1)}, bf16[4,128,128]{2,1,0:T(8,128)(2,1)S(1)}, u32[]{:S(2)}, u32[]{:S(2)}) collective-permute-start(bf16[4,128,128]{2,1,0:T(8,128)(2,1)S(1)} %pad_maximum_fusion.own), channel_id=1, source_target_pairs={{0,1},{1,0},{2,3},{3,2},{4,5},{5,4},{6,7},{7,6},{8,9},{9,8},{10,11... | collective-permute-start | bytes 393224 | tf_op jit(solution)/shard_map/cond/branch_1_fun/ppermute | solution.py:403
  183.6 2.5 %branch_1_fun.17 = bf16[2048,128]{1,0:T(8,128)(2,1)S(1)} custom-call(s32[8,128]{1,0:T(8,128)S(1)} %get-tuple-element.46.mine, s32[32]{0:T(128)S(1)} %copy-done.36, f32[2048,128]{1,0:T(8,128)S(1)} %copy-done.6, bf16[4,128,128]{2,1,0:T(8,128)(2,1)S(1)} %pad_maximum_fusion.own, bf16[4,128,128]{2,1,0:T(8,128)(2,1)S(1)} %collective-permute-done.21.other, ...), custom_call_target="tpu_custom_call" | custom-call | flops 33554432 | bytes 2097152 | tf_op jit(solution)/shard_map/cond/branch_1_fun/pallas_call | solution.py:470
  (107 shorter events, 37.9 us)
Async XLA Ops:
  11.5 170.9 %reduce-scatter.5.cloned.1.call-start = ((), (), s32[]{:S(2)}) async-start(), calls=%async_computation.7 | async-start | bytes 9437184 | tf_op jit(solution)/shard_map/cond/branch_1_fun/reduce_scatter | solution.py:569
  11.5 16.7 %copy-start.28 = (bf16[128,64,1024]{2,1,0:T(8,128)(2,1)S(1)}, bf16[128,64,1024]{2,1,0:T(8,128)(2,1)}, u32[]{:S(2)}) copy-start(bf16[128,64,1024]{2,1,0:T(8,128)(2,1)} %get-tuple-element.49.down) | copy-start | bytes 50331652 | tf_op jit(solution)/shard_map/cond
  11.5 16.7 %copy-start.32 = (bf16[128,64,128]{2,1,0:T(8,128)(2,1)S(1)}, bf16[128,64,128]{2,1,0:T(8,128)(2,1)}, u32[]{:S(2)}) copy-start(bf16[128,64,128]{2,1,0:T(8,128)(2,1)} %get-tuple-element.50.up) | copy-start | bytes 6291460 | tf_op jit(solution)/shard_map/cond
  20.4 28.8 %collective-permute-start = (bf16[4,144,1024]{2,1,0:T(8,128)(2,1)}, bf16[4,144,1024]{2,1,0:T(8,128)(2,1)S(1)}, u32[]{:S(2)}, u32[]{:S(2)}) collective-permute-start(bf16[4,144,1024]{2,1,0:T(8,128)(2,1)} %get-tuple-element.51), channel_id=1, source_target_pairs={{0,32},{8,40},{16,48},{24,56},{32,64},{40,72},{48,80},{56,88},{64,... | collective-permute-start | bytes 3538952 | tf_op jit(solution)/shard_map/cond/branch_1_fun/ppermute | solution.py:52
  22.4 26.8 %collective-permute-start.1 = (bf16[4,144,1024]{2,1,0:T(8,128)(2,1)}, bf16[4,144,1024]{2,1,0:T(8,128)(2,1)S(1)}, u32[]{:S(2)}, u32[]{:S(2)}) collective-permute-start(bf16[4,144,1024]{2,1,0:T(8,128)(2,1)} %get-tuple-element.52), channel_id=1, source_target_pairs={{0,96},{8,104},{16,112},{24,120},{32,0},{40,8},{48,16},{56,24},{64... | collective-permute-start | bytes 3538952 | tf_op jit(solution)/shard_map/cond/branch_1_fun/ppermute | solution.py:52
  23.7 28.9 %collective-permute-start.2 = (bf16[4,144,1024]{2,1,0:T(8,128)(2,1)}, bf16[4,144,1024]{2,1,0:T(8,128)(2,1)S(1)}, u32[]{:S(2)}, u32[]{:S(2)}) collective-permute-start(bf16[4,144,1024]{2,1,0:T(8,128)(2,1)} %get-tuple-element.53), channel_id=1, source_target_pairs={{0,8},{8,16},{16,24},{24,0},{32,40},{40,48},{48,56},{56,32},{64,72... | collective-permute-start | bytes 3538952 | tf_op jit(solution)/shard_map/cond/branch_1_fun/ppermute | solution.py:52
  28.2 6.7 %copy-start.29 = (bf16[2048,1024]{1,0:T(8,128)(2,1)S(1)}, bf16[2048,1024]{1,0:T(8,128)(2,1)}, u32[]{:S(2)}) copy-start(bf16[2048,1024]{1,0:T(8,128)(2,1)} %get-tuple-element.61.hidden) | copy-start | bytes 12582916 | tf_op jit(solution)/shard_map/cond
  28.2 6.7 %copy-start.37 = (bf16[1024,1024]{1,0:T(8,128)(2,1)S(1)}, bf16[1024,1024]{1,0:T(8,128)(2,1)}, u32[]{:S(2)}) copy-start(bf16[1024,1024]{1,0:T(8,128)(2,1)} %get-tuple-element.62.weight) | copy-start | bytes 6291460 | tf_op jit(solution)/shard_map/cond
  28.2 26.3 %collective-permute-start.3 = (bf16[4,144,1024]{2,1,0:T(8,128)(2,1)}, bf16[4,144,1024]{2,1,0:T(8,128)(2,1)}, u32[]{:S(2)}, u32[]{:S(2)}) collective-permute-start(bf16[4,144,1024]{2,1,0:T(8,128)(2,1)} %get-tuple-element.54), channel_id=1, source_target_pairs={{0,24},{8,0},{16,8},{24,16},{32,56},{40,32},{48,40},{56,48},{64,88... | collective-permute-start | bytes 3538952 | tf_op jit(solution)/shard_map/cond/branch_1_fun/ppermute | solution.py:52
  60.3 13.7 %collective-permute-start.4 = (bf16[2,144,1024]{2,1,0:T(8,128)(2,1)S(1)}, bf16[2,144,1024]{2,1,0:T(8,128)(2,1)S(1)}, u32[]{:S(2)}, u32[]{:S(2)}) collective-permute-start(bf16[2,144,1024]{2,1,0:T(8,128)(2,1)S(1)} %get-tuple-element.71), channel_id=1, source_target_pairs={{0,32},{8,40},{16,48},{24,56},{32,64},{40,72},{48,80},{56,88},{64,... | collective-permute-start | bytes 1769480 | tf_op jit(solution)/shard_map/cond/branch_1_fun/ppermute | solution.py:52
  60.4 14.4 %collective-permute-start.5 = (bf16[2,144,1024]{2,1,0:T(8,128)(2,1)S(1)}, bf16[2,144,1024]{2,1,0:T(8,128)(2,1)S(1)}, u32[]{:S(2)}, u32[]{:S(2)}) collective-permute-start(bf16[2,144,1024]{2,1,0:T(8,128)(2,1)S(1)} %get-tuple-element.72), channel_id=1, source_target_pairs={{0,96},{8,104},{16,112},{24,120},{32,0},{40,8},{48,16},{56,24},{64... | collective-permute-start | bytes 1769480 | tf_op jit(solution)/shard_map/cond/branch_1_fun/ppermute | solution.py:52
  63.1 13.0 %collective-permute-start.6 = (bf16[2,144,1024]{2,1,0:T(8,128)(2,1)S(1)}, bf16[2,144,1024]{2,1,0:T(8,128)(2,1)S(1)}, u32[]{:S(2)}, u32[]{:S(2)}) collective-permute-start(bf16[2,144,1024]{2,1,0:T(8,128)(2,1)S(1)} %get-tuple-element.73), channel_id=1, source_target_pairs={{0,8},{8,16},{16,24},{24,0},{32,40},{40,48},{48,56},{56,32},{64,72... | collective-permute-start | bytes 1769480 | tf_op jit(solution)/shard_map/cond/branch_1_fun/ppermute | solution.py:52
  63.4 13.6 %collective-permute-start.7 = (bf16[2,144,1024]{2,1,0:T(8,128)(2,1)S(1)}, bf16[2,144,1024]{2,1,0:T(8,128)(2,1)S(1)}, u32[]{:S(2)}, u32[]{:S(2)}) collective-permute-start(bf16[2,144,1024]{2,1,0:T(8,128)(2,1)S(1)} %get-tuple-element.74), channel_id=1, source_target_pairs={{0,24},{8,0},{16,8},{24,16},{32,56},{40,32},{48,40},{56,48},{64,88... | collective-permute-start | bytes 1769480 | tf_op jit(solution)/shard_map/cond/branch_1_fun/ppermute | solution.py:52
  77.9 61.0 %all-to-all-start = ((bf16[16,144,1024]{2,1,0:T(8,128)(2,1)}), bf16[16,144,1024]{2,1,0:T(8,128)(2,1)}, u32[]{:S(2)}, u32[]{:S(2)}) async-start(bf16[16,144,1024]{2,1,0:T(8,128)(2,1)} %copy-done.1), calls=%async_computation.1 | async-start | bytes 9437184 | tf_op jit(solution)/shard_map/cond/branch_1_fun/all_to_all | solution.py:570
  93.6 45.2 %collective-permute-start.10 = (bf16[144,1024]{1,0:T(8,128)(2,1)S(1)}, bf16[144,1024]{1,0:T(8,128)(2,1)S(1)}, u32[]{:S(2)}, u32[]{:S(2)}) collective-permute-start(bf16[144,1024]{1,0:T(8,128)(2,1)S(1)} %get-tuple-element.87), channel_id=1, source_target_pairs={{0,24},{8,0},{16,8},{24,16},{32,56},{40,32},{48,40},{56,48},{64,88... | collective-permute-start | bytes 884744 | tf_op jit(solution)/shard_map/cond/branch_1_fun/ppermute | solution.py:52
  96.0 48.8 %collective-permute-start.11 = (bf16[144,1024]{1,0:T(8,128)(2,1)}, bf16[144,1024]{1,0:T(8,128)(2,1)S(1)}, u32[]{:S(2)}, u32[]{:S(2)}) collective-permute-start(bf16[144,1024]{1,0:T(8,128)(2,1)} %get-tuple-element.88), channel_id=1, source_target_pairs={{0,32},{8,40},{16,48},{24,56},{32,64},{40,72},{48,80},{56,88},{64,... | collective-permute-start | bytes 884744 | tf_op jit(solution)/shard_map/cond/branch_1_fun/ppermute | solution.py:52
  97.2 49.1 %collective-permute-start.12 = (bf16[144,1024]{1,0:T(8,128)(2,1)}, bf16[144,1024]{1,0:T(8,128)(2,1)S(1)}, u32[]{:S(2)}, u32[]{:S(2)}) collective-permute-start(bf16[144,1024]{1,0:T(8,128)(2,1)} %get-tuple-element.89), channel_id=1, source_target_pairs={{0,64},{8,72},{16,80},{24,88},{32,96},{40,104},{48,112},{56,120},{... | collective-permute-start | bytes 884744 | tf_op jit(solution)/shard_map/cond/branch_1_fun/ppermute | solution.py:52
  99.7 47.3 %collective-permute-start.13 = (bf16[144,1024]{1,0:T(8,128)(2,1)}, bf16[144,1024]{1,0:T(8,128)(2,1)S(1)}, u32[]{:S(2)}, u32[]{:S(2)}) collective-permute-start(bf16[144,1024]{1,0:T(8,128)(2,1)} %get-tuple-element.90), channel_id=1, source_target_pairs={{0,96},{8,104},{16,112},{24,120},{32,0},{40,8},{48,16},{56,24},{64... | collective-permute-start | bytes 884744 | tf_op jit(solution)/shard_map/cond/branch_1_fun/ppermute | solution.py:52
  100.8 46.1 %collective-permute-start.8 = (bf16[144,1024]{1,0:T(8,128)(2,1)}, bf16[144,1024]{1,0:T(8,128)(2,1)S(1)}, u32[]{:S(2)}, u32[]{:S(2)}) collective-permute-start(bf16[144,1024]{1,0:T(8,128)(2,1)} %get-tuple-element.85), channel_id=1, source_target_pairs={{0,8},{8,16},{16,24},{24,0},{32,40},{40,48},{48,56},{56,32},{64,72... | collective-permute-start | bytes 884744 | tf_op jit(solution)/shard_map/cond/branch_1_fun/ppermute | solution.py:52
  138.8 8.5 %collective-permute-start.9 = (bf16[144,1024]{1,0:T(8,128)(2,1)}, bf16[144,1024]{1,0:T(8,128)(2,1)S(1)}, u32[]{:S(2)}, u32[]{:S(2)}) collective-permute-start(bf16[144,1024]{1,0:T(8,128)(2,1)} %get-tuple-element.86), channel_id=1, source_target_pairs={{0,16},{8,24},{16,0},{24,8},{32,48},{40,56},{48,32},{56,40},{64,80... | collective-permute-start | bytes 884744 | tf_op jit(solution)/shard_map/cond/branch_1_fun/ppermute | solution.py:52
  138.8 8.5 %copy-start.24 = (bf16[144,1024]{1,0:T(8,128)(2,1)S(1)}, bf16[144,1024]{1,0:T(8,128)(2,1)}, u32[]{:S(2)}) copy-start(bf16[144,1024]{1,0:T(8,128)(2,1)} %copy-done.23) | copy-start | bytes 884740 | tf_op jit(solution)/shard_map/cond
  138.8 8.5 %copy-start.26 = (bf16[144,1024]{1,0:T(8,128)(2,1)S(1)}, bf16[144,1024]{1,0:T(8,128)(2,1)}, u32[]{:S(2)}) copy-start(bf16[144,1024]{1,0:T(8,128)(2,1)} %copy-done.25) | copy-start | bytes 884740 | tf_op jit(solution)/shard_map/cond
  138.8 9.2 %copy-start.30 = (bf16[2048,1024]{1,0:T(8,128)(2,1)S(1)}, bf16[2048,1024]{1,0:T(8,128)(2,1)}, u32[]{:S(2)}) copy-start(bf16[2048,1024]{1,0:T(8,128)(2,1)} %get-tuple-element.61.hidden) | copy-start | bytes 12582916 | tf_op jit(solution)/shard_map/cond
  148.0 34.4 %copy-start.36 = (s32[32]{0:T(128)S(1)}, s32[32]{0:T(128)}, u32[]{:S(2)}) copy-start(s32[32]{0:T(128)} %copy-done.35) | copy-start | bytes 388 | tf_op jit(solution)/shard_map/cond
  149.0 13.7 %collective-permute-start.14 = (f32[512,128]{1,0:T(8,128)S(1)}, f32[512,128]{1,0:T(8,128)S(1)}, u32[]{:S(2)}, u32[]{:S(2)}) collective-permute-start(f32[512,128]{1,0:T(8,128)S(1)} %constant_dynamic-slice_fusion.3), channel_id=1, source_target_pairs={{0,1},{1,0},{2,3},{3,2},{4,5},{5,4},{6,7},{7,6},{8,9},{9,8},{10,11... | collective-permute-start | bytes 786440 | tf_op jit(solution)/shard_map/cond/branch_1_fun/ppermute | solution.py:390
  162.7 6.0 %collective-permute-start.15 = (f32[128,128]{1,0:T(8,128)S(1)}, f32[128,128]{1,0:T(8,128)S(1)}, u32[]{:S(2)}, u32[]{:S(2)}) collective-permute-start(f32[128,128]{1,0:T(8,128)S(1)} %get-tuple-element.111), channel_id=1, source_target_pairs={{0,2},{1,3},{2,4},{3,5},{4,6},{5,7},{6,0},{7,1},{8,10},{9,11},{10,... | collective-permute-start | bytes 196616 | tf_op jit(solution)/shard_map/cond/branch_1_fun/ppermute | solution.py:394
  164.4 6.3 %collective-permute-start.16 = (f32[128,128]{1,0:T(8,128)S(1)}, f32[128,128]{1,0:T(8,128)S(1)}, u32[]{:S(2)}, u32[]{:S(2)}) collective-permute-start(f32[128,128]{1,0:T(8,128)S(1)} %get-tuple-element.109), channel_id=1, source_target_pairs={{0,4},{1,5},{2,6},{3,7},{4,0},{5,1},{6,2},{7,3},{8,12},{9,13},{10,... | collective-permute-start | bytes 196616 | tf_op jit(solution)/shard_map/cond/branch_1_fun/ppermute | solution.py:394
  167.7 3.4 %collective-permute-start.17 = (f32[128,128]{1,0:T(8,128)S(1)}, f32[128,128]{1,0:T(8,128)S(1)}, u32[]{:S(2)}, u32[]{:S(2)}) collective-permute-start(f32[128,128]{1,0:T(8,128)S(1)} %get-tuple-element.110), channel_id=1, source_target_pairs={{0,6},{1,7},{2,0},{3,1},{4,2},{5,3},{6,4},{7,5},{8,14},{9,15},{10,... | collective-permute-start | bytes 196616 | tf_op jit(solution)/shard_map/cond/branch_1_fun/ppermute | solution.py:394
  171.2 4.3 %collective-permute-start.19 = (bf16[128,128]{1,0:T(8,128)(2,1)S(1)}, bf16[128,128]{1,0:T(8,128)(2,1)S(1)}, u32[]{:S(2)}, u32[]{:S(2)}) collective-permute-start(bf16[128,128]{1,0:T(8,128)(2,1)S(1)} %add_convert_fusion), channel_id=1, source_target_pairs={{0,4},{1,5},{2,6},{3,7},{4,0},{5,1},{6,2},{7,3},{8,12},{9,13},{10,... | collective-permute-start | bytes 98312 | tf_op jit(solution)/shard_map/cond/branch_1_fun/ppermute | solution.py:402
  172.5 3.1 %collective-permute-start.20 = (bf16[128,128]{1,0:T(8,128)(2,1)S(1)}, bf16[128,128]{1,0:T(8,128)(2,1)S(1)}, u32[]{:S(2)}, u32[]{:S(2)}) collective-permute-start(bf16[128,128]{1,0:T(8,128)(2,1)S(1)} %add_convert_fusion), channel_id=1, source_target_pairs={{0,6},{1,7},{2,0},{3,1},{4,2},{5,3},{6,4},{7,5},{8,14},{9,15},{10,... | collective-permute-start | bytes 98312 | tf_op jit(solution)/shard_map/cond/branch_1_fun/ppermute | solution.py:402
  174.2 4.0 %collective-permute-start.18 = (bf16[128,128]{1,0:T(8,128)(2,1)S(1)}, bf16[128,128]{1,0:T(8,128)(2,1)S(1)}, u32[]{:S(2)}, u32[]{:S(2)}) collective-permute-start(bf16[128,128]{1,0:T(8,128)(2,1)S(1)} %add_convert_fusion), channel_id=1, source_target_pairs={{0,2},{1,3},{2,4},{3,5},{4,6},{5,7},{6,0},{7,1},{8,10},{9,11},{10,... | collective-permute-start | bytes 98312 | tf_op jit(solution)/shard_map/cond/branch_1_fun/ppermute | solution.py:402
  178.2 4.2 %collective-permute-start.21 = (bf16[4,128,128]{2,1,0:T(8,128)(2,1)S(1)}, bf16[4,128,128]{2,1,0:T(8,128)(2,1)S(1)}, u32[]{:S(2)}, u32[]{:S(2)}) collective-permute-start(bf16[4,128,128]{2,1,0:T(8,128)(2,1)S(1)} %pad_maximum_fusion.own), channel_id=1, source_target_pairs={{0,1},{1,0},{2,3},{3,2},{4,5},{5,4},{6,7},{7,6},{8,9},{9,8},{10,11... | collective-permute-start | bytes 393224 | tf_op jit(solution)/shard_map/cond/branch_1_fun/ppermute | solution.py:403
  (27 other events, 35.6 us)
Sparse Core Ops, SparseCore 0:
  78.0 54.2 reduce-scatter.4

commit v13 on v12

--- a/solution.py
+++ b/solution.py
@@ -539,32 +539,32 @@
         turned = ((0, 1), (0, 2), (0, -1), (1, 0), (2, 0), (-1, 0))
         send = lambda values, ways: [shift(v, *way) for v, way in zip(values, ways)]
         barrier = lax.optimization_barrier
-        main_sent, *gathered = gather_units(
-            functools.partial(gather_kernel, soon),
-            [dp_count] + [len(units) for _, units in soon],
+        gathered = gather_units(
+            functools.partial(extra_kernel, soon),
+            [len(units) for _, units in soon],
             served,
             mine,
             down_weights,
             up_weights,
         )
-        unit, dtype = main_sent.shape[1:], main_sent.dtype
+        unit, dtype = gathered[0].shape[1:], gathered[0].dtype
         fresh = send(gathered, moves)
         later_served, _ = barrier((served, gathered))
-        later = gather_units(
-            functools.partial(extra_kernel, late),
-            [len(units) for _, units in late],
+        main_sent, *later = gather_units(
+            functools.partial(gather_kernel, late),
+            [dp_count] + [len(units) for _, units in late],
             later_served,
             mine,
             down_weights,
             up_weights,
         )
         near, homes = later[:4], later[4:]
-        base_hidden, _ = barrier((hidden, gathered))
-        base_terms = base_product(base_hidden, value_weight)
-        fresh, near, base_terms = barrier((fresh, near, base_terms))
+        fresh, near, main_sent = barrier((fresh, near, main_sent))
         relayed = vmem_call(
             relay_kernel, ((2,) + unit,) * 4, dtype, (mine,), (*fresh, *near)
         )
+        base_hidden, relayed = barrier((hidden, relayed))
+        base_terms = base_product(base_hidden, value_weight)
         near_a, main_sent, base_terms = barrier((send(relayed, moves), main_sent, base_terms))
         base = lax.psum_scatter(base_terms, "tp", scatter_dimension=1, tiled=True)
         main = lax.all_to_all(main_sent, "dp", 0, 0, tiled=True)

time: 194 us -> 180 us (0.928)
  local copies, waits for them, and re-layouts: 31.2 us -> 16.1 us
  starting transfers between devices: 49.5 us -> 45.9 us
  Pallas kernels: 29.7 us -> 33 us
    cond x68 -> x40, local copies, waits for them, and re-layouts: 28.2 us -> 13.1 us
    pallas_call x2, Pallas kernels: 7.74 us -> 10.1 us  [gather_units(): pl.pallas_call(kernel, out_shape=[jax.ShapeDtypeStruct((n, 2 * rank + 16,...]
    ppermute x1, starting transfers between devices: 12.5 us -> 10.1 us  [low_rank_down(): lax.ppermute(cut(partial, (1 - core) * half, half), 'tp', swap())]
  transfers between devices with their start and end apart: 24 -> 24, of which waited for: 17 -> 15; matrix products, arithmetic and copies ran while one was open for 0% -> 0% of each run, Pallas kernels for 9% -> 14%
where the time goes in v13:
time: 180 us; the launch traced here: 179 us
  waiting for transfers between devices  69.5 us (39%)
  starting transfers between devices  45.9 us (26%)
  Pallas kernels  33 us (18%)
  local copies, waits for them, and re-layouts  16.1 us (9%)
  between operations  14.1 us (8%)
    ppermute x14, waiting for transfers between devices, shift(): return lax.ppermute(value, 'dp', pairs)  60.6 us
    ppermute x14, starting transfers between devices, shift(): return lax.ppermute(value, 'dp', pairs)  19.1 us
    cond x40, local copies, waits for them, and re-layouts  13.1 us
    pallas_call x2, Pallas kernels, gather_units(): pl.pallas_call(kernel, out_shape=[jax.ShapeDtypeStruct((n, 2 * rank + 16,...  10.1 us
    ppermute x1, starting transfers between devices, low_rank_down(): lax.ppermute(cut(partial, (1 - core) * half, half), 'tp', swap())  10.1 us
    pallas_call x2, Pallas kernels, low_call(): pl.pallas_call(functools.partial(kernel, cap), out_shape=jax.ShapeDtypeSt...  6.8 us
    pallas_call x3, Pallas kernels, vmem_call(): pl.pallas_call(kernel, out_shape=[jax.ShapeDtypeStruct(shape, dtype) for...  6.09 us
    ppermute x3, starting transfers between devices, low_rank_down(): lax.ppermute(cut(total, (z + d) % chips * piece, piece), 'tp', turn(d))  5.74 us
  transfers between devices with their start and end apart: 24, of which 15 were waited for; matrix products, arithmetic and copies ran while one was open for 0% of the time, Pallas kernels for 14%

profile of v13, /device:TPU:1, one launch (start us, length us, event | category | flops | bytes accessed | tf_op | source)
XLA Modules:
  0.0 179.1 jit_solution(8728706511987810698)
XLA Ops:
  8.2 1.8 %shard_map.75 = (s32[16,128]{1,0:T(8,128)S(1)}, s32[8,128]{1,0:T(8,128)S(1)}) custom-call(s32[2]{0:T(128)S(1)} %pad_add_fusion.spot_ref, s32[512,1]{1,0:T(8,128)S(1)} %copy.23.ids_ref, s32[16,128]{1,0:T(8,128)} %bitcast.29), custom_call_target="tpu_custom_call" | custom-call | tf_op jit(solution)/shard_map/pallas_call | solution.py:130
  11.3 160.2 %conditional.1 = (bf16[2048,128]{1,0:T(8,128)(2,1)S(1)}) conditional(s32[]{:T(128)} %bitcast.16, (s32[32]{0:T(128)S(1)}, bf16[2048,1024]{1,0:T(8,128)(2,1)}, bf16[1024,1024]{1,0:T(8,128)(2,1)}, s32[512]{0:T(512)}, s32[2048]{0:T(1024)}, /*index=5*/s32[]{:T(128)}, bf16[128,64,1024]{2,1,0:T(8,128)(2,1)}, bf16[128,64,128]{2,1,0:T(8,128)(2,1)}) %tuple.16, ...), branch_computations={%region_0.5_spmd, %region_5.7_spmd} | conditional | flops 4865720320 | bytes 341805408 | solution.py:590
  12.9 2.1 %collective-permute-start = (bf16[4,144,1024]{2,1,0:T(8,128)(2,1)S(1)}, bf16[4,144,1024]{2,1,0:T(8,128)(2,1)S(1)}, u32[]{:S(2)}, u32[]{:S(2)}) collective-permute-start(bf16[4,144,1024]{2,1,0:T(8,128)(2,1)S(1)} %get-tuple-element.52), channel_id=1, source_target_pairs={{0,32},{8,40},{16,48},{24,56},{32,64},{40,72},{48,80},{56,88},{64,... | collective-permute-start | bytes 3538952 | tf_op jit(solution)/shard_map/cond/branch_1_fun/ppermute | solution.py:52
  15.0 1.3 collective-permute-start.1
  16.3 1.4 collective-permute-start.2
  17.8 1.4 collective-permute-start.3
  19.2 8.8 %branch_1_fun.10 = (bf16[16,144,1024]{2,1,0:T(8,128)(2,1)S(1)}, bf16[2,144,1024]{2,1,0:T(8,128)(2,1)S(1)}, bf16[2,144,1024]{2,1,0:T(8,128)(2,1)S(1)}, bf16[2,144...) custom-call(s32[16,128]{1,0:T(8,128)S(1)} %get-tuple-element.56.serv, ...), custom_call_target="tpu_custom_call" | custom-call | bytes 9437184 | tf_op jit(solution)/shard_map/cond/branch_1_fun/pallas_call | solution.py:205
  28.0 2.3 %copy-done.1 = bf16[16,144,1024]{2,1,0:T(8,128)(2,1)} copy-done((bf16[16,144,1024]{2,1,0:T(8,128)(2,1)}, bf16[16,144,1024]{2,1,0:T(8,128)(2,1)S(1)}, u32[]{:S(2)}) %copy-start.1) | copy-done | bytes 4718616 | tf_op jit(solution)/shard_map/cond
  31.3 10.2 %collective-permute-done.refs_0_.refs_3_ = bf16[4,144,1024]{2,1,0:T(8,128)(2,1)S(1)} collective-permute-done((bf16[4,144,1024]{2,1,0:T(8,128)(2,1)S(1)}, bf16[4,144,1024]{2,1,0:T(8,128)(2,1)S(1)}, u32[]{:S(2)}, u32[]{:S(2)}) %collective-permute-start) | collective-permute-done | bytes 1179680 | tf_op jit(solution)/shard_map/cond/branch_1_fun/ppermute | solution.py:52
  41.5 2.6 %collective-permute-done.2.refs_2_.refs_8_ = bf16[4,144,1024]{2,1,0:T(8,128)(2,1)S(1)} collective-permute-done((bf16[4,144,1024]{2,1,0:T(8,128)(2,1)S(1)}, bf16[4,144,1024]{2,1,0:T(8,128)(2,1)S(1)}, u32[]{:S(2)}, u32[]{:S(2)}) %collective-permute-start.2) | collective-permute-done | bytes 1179680 | tf_op jit(solution)/shard_map/cond/branch_1_fun/ppermute | solution.py:52
  44.1 2.6 %collective-permute-done.3.refs_3_.refs_9_ = bf16[4,144,1024]{2,1,0:T(8,128)(2,1)S(1)} collective-permute-done((bf16[4,144,1024]{2,1,0:T(8,128)(2,1)S(1)}, bf16[4,144,1024]{2,1,0:T(8,128)(2,1)S(1)}, u32[]{:S(2)}, u32[]{:S(2)}) %collective-permute-start.3) | collective-permute-done | bytes 1179680 | tf_op jit(solution)/shard_map/cond/branch_1_fun/ppermute | solution.py:52
  46.7 2.3 %branch_1_fun.11 = (bf16[2,144,1024]{2,1,0:T(8,128)(2,1)}, bf16[2,144,1024]{2,1,0:T(8,128)(2,1)}, bf16[2,144,1024]{2,1,0:T(8,128)(2,1)}, bf16[2,144,1024]{2,1,0:T(8,128)(2,1)}) custom-call(s32[8,128]{1,0:T(8,128)S(1)} %get-tuple-element.46.mine, bf16[4,144,1024]{2,1,0:T(8,128)(2,1)S(1)} %collective-permute-done.refs_0_.refs_3_, ...), custom_call_target="tpu_custom_call" | custom-call | bytes 4718592 | tf_op jit(solution)/shard_map/cond/branch_1_fun/pallas_call | solution.py:223
  49.1 2.7 %collective-permute-start.5 = (bf16[2,144,1024]{2,1,0:T(8,128)(2,1)}, bf16[2,144,1024]{2,1,0:T(8,128)(2,1)}, u32[]{:S(2)}, u32[]{:S(2)}) collective-permute-start(bf16[2,144,1024]{2,1,0:T(8,128)(2,1)} %get-tuple-element.75), channel_id=1, source_target_pairs={{0,96},{8,104},{16,112},{24,120},{32,0},{40,8},{48,16},{56,24},{64... | collective-permute-start | bytes 1769480 | tf_op jit(solution)/shard_map/cond/branch_1_fun/ppermute | solution.py:52
  52.9 1.5 collective-permute-start.7
  54.4 5.7 %branch_1_fun.12 = f32[2048,1024]{1,0:T(8,128)S(1)} custom-call(bf16[2048,1024]{1,0:T(8,128)(2,1)S(1)} %copy-done.15, bf16[1024,1024]{1,0:T(8,128)(2,1)S(1)} %copy-done.23), custom_call_target="tpu_custom_call" | custom-call | flops 4294967296 | bytes 14680064 | tf_op jit(solution)/shard_map/cond/branch_1_fun/pallas_call | solution.py:296
  60.1 3.3 %copy-done = f32[2048,1024]{1,0:T(8,128)} copy-done((f32[2048,1024]{1,0:T(8,128)}, f32[2048,1024]{1,0:T(8,128)S(1)}, u32[]{:S(2)}) %copy-start) | copy-done | bytes 8388632 | tf_op jit(solution)/shard_map/cond
  63.5 2.1 %collective-permute-done.6.refs_6_ = bf16[2,144,1024]{2,1,0:T(8,128)(2,1)} collective-permute-done((bf16[2,144,1024]{2,1,0:T(8,128)(2,1)}, bf16[2,144,1024]{2,1,0:T(8,128)(2,1)}, u32[]{:S(2)}, u32[]{:S(2)}) %collective-permute-start.6) | collective-permute-done | bytes 589856 | tf_op jit(solution)/shard_map/cond/branch_1_fun/ppermute | solution.py:52
  65.7 4.6 %all-to-all-start = ((bf16[16,144,1024]{2,1,0:T(8,128)(2,1)}), bf16[16,144,1024]{2,1,0:T(8,128)(2,1)}, u32[]{:S(2)}, u32[]{:S(2)}) async-start(bf16[16,144,1024]{2,1,0:T(8,128)(2,1)} %copy-done.1), calls=%async_computation.1 | async-start | bytes 9437184 | tf_op jit(solution)/shard_map/cond/branch_1_fun/all_to_all | solution.py:570
  74.1 3.0 %branch_1_fun.13 = (bf16[144,1024]{1,0:T(8,128)(2,1)S(1)}, bf16[144,1024]{1,0:T(8,128)(2,1)}, bf16[144,1024]{1,0:T(8,128)(2,1)}, bf16[144,1024]{1,0:T(8,128)(2,1...) custom-call(s32[8,128]{1,0:T(8,128)S(1)} %get-tuple-element.46.mine,, ...), custom_call_target="tpu_custom_call" | custom-call | bytes 4718592 | tf_op jit(solution)/shard_map/cond/branch_1_fun/pallas_call | solution.py:223
  78.6 2.4 %collective-permute-start.10 = (bf16[144,1024]{1,0:T(8,128)(2,1)S(1)}, bf16[144,1024]{1,0:T(8,128)(2,1)S(1)}, u32[]{:S(2)}, u32[]{:S(2)}) collective-permute-start(bf16[144,1024]{1,0:T(8,128)(2,1)S(1)} %get-tuple-element.91), channel_id=1, source_target_pairs={{0,24},{8,0},{16,8},{24,16},{32,56},{40,32},{48,40},{56,48},{64,88... | collective-permute-start | bytes 884744 | tf_op jit(solution)/shard_map/cond/branch_1_fun/ppermute | solution.py:52
  82.2 2.5 %collective-permute-start.12 = (bf16[144,1024]{1,0:T(8,128)(2,1)}, bf16[144,1024]{1,0:T(8,128)(2,1)S(1)}, u32[]{:S(2)}, u32[]{:S(2)}) collective-permute-start(bf16[144,1024]{1,0:T(8,128)(2,1)} %get-tuple-element.93), channel_id=1, source_target_pairs={{0,64},{8,72},{16,80},{24,88},{32,96},{40,104},{48,112},{56,120},{... | collective-permute-start | bytes 884744 | tf_op jit(solution)/shard_map/cond/branch_1_fun/ppermute | solution.py:52
  85.8 40.6 %collective-permute-done.10.refs_3_ = bf16[144,1024]{1,0:T(8,128)(2,1)S(1)} collective-permute-done((bf16[144,1024]{1,0:T(8,128)(2,1)S(1)}, bf16[144,1024]{1,0:T(8,128)(2,1)S(1)}, u32[]{:S(2)}, u32[]{:S(2)}) %collective-permute-start.10) | collective-permute-done | bytes 294944 | tf_op jit(solution)/shard_map/cond/branch_1_fun/ppermute | solution.py:52
  126.7 5.9 %branch_1_fun.14._ = f32[1024,128]{1,0:T(8,128)S(1)} custom-call(s32[8,128]{1,0:T(8,128)S(1)} %get-tuple-element.46.mine, bf16[2048,1024]{1,0:T(8,128)(2,1)} %get-tuple-element.79.hidden, bf16[16,144,1024]{2,1,0:T(8,128)(2,1)} %all-to-all-done.main), custom_call_target="tpu_custom_call" | custom-call | flops 268435456 | bytes 4718592 | tf_op jit(solution)/shard_map/cond/branch_1_fun/pallas_call | solution.py:359
  132.6 2.1 %collective-permute-done.12.refs_6_ = bf16[144,1024]{1,0:T(8,128)(2,1)S(1)} collective-permute-done((bf16[144,1024]{1,0:T(8,128)(2,1)}, bf16[144,1024]{1,0:T(8,128)(2,1)S(1)}, u32[]{:S(2)}, u32[]{:S(2)}) %collective-permute-start.12) | collective-permute-done | bytes 294944 | tf_op jit(solution)/shard_map/cond/branch_1_fun/ppermute | solution.py:52
  136.7 10.1 %collective-permute-start.14 = (f32[512,128]{1,0:T(8,128)S(1)}, f32[512,128]{1,0:T(8,128)S(1)}, u32[]{:S(2)}, u32[]{:S(2)}) collective-permute-start(f32[512,128]{1,0:T(8,128)S(1)} %constant_dynamic-slice_fusion.3), channel_id=1, source_target_pairs={{0,1},{1,0},{2,3},{3,2},{4,5},{5,4},{6,7},{7,6},{8,9},{9,8},{10,11... | collective-permute-start | bytes 786440 | tf_op jit(solution)/shard_map/cond/branch_1_fun/ppermute | solution.py:390
  148.0 1.7 collective-permute-start.15
  149.8 3.3 %collective-permute-start.16 = (f32[128,128]{1,0:T(8,128)S(1)}, f32[128,128]{1,0:T(8,128)S(1)}, u32[]{:S(2)}, u32[]{:S(2)}) collective-permute-start(f32[128,128]{1,0:T(8,128)S(1)} %get-tuple-element.113), channel_id=1, source_target_pairs={{0,4},{1,5},{2,6},{3,7},{4,0},{5,1},{6,2},{7,3},{8,12},{9,13},{10,... | collective-permute-start | bytes 196616 | tf_op jit(solution)/shard_map/cond/branch_1_fun/ppermute | solution.py:394
  154.0 2.0 %collective-permute-done.16 = f32[128,128]{1,0:T(8,128)S(1)} collective-permute-done((f32[128,128]{1,0:T(8,128)S(1)}, f32[128,128]{1,0:T(8,128)S(1)}, u32[]{:S(2)}, u32[]{:S(2)}) %collective-permute-start.16) | collective-permute-done | bytes 65568 | tf_op jit(solution)/shard_map/cond/branch_1_fun/ppermute | solution.py:394
  157.8 1.8 collective-permute-start.20
  160.8 2.7 %collective-permute-done.18 = bf16[128,128]{1,0:T(8,128)(2,1)S(1)} collective-permute-done((bf16[128,128]{1,0:T(8,128)(2,1)S(1)}, bf16[128,128]{1,0:T(8,128)(2,1)S(1)}, u32[]{:S(2)}, u32[]{:S(2)}) %collective-permute-start.18) | collective-permute-done | bytes 32800 | tf_op jit(solution)/shard_map/cond/branch_1_fun/ppermute | solution.py:402
  163.6 3.2 %collective-permute-start.21 = (bf16[4,128,128]{2,1,0:T(8,128)(2,1)S(1)}, bf16[4,128,128]{2,1,0:T(8,128)(2,1)S(1)}, u32[]{:S(2)}, u32[]{:S(2)}) collective-permute-start(bf16[4,128,128]{2,1,0:T(8,128)(2,1)S(1)} %pad_maximum_fusion.own), channel_id=1, source_target_pairs={{0,1},{1,0},{2,3},{3,2},{4,5},{5,4},{6,7},{7,6},{8,9},{9,8},{10,11... | collective-permute-start | bytes 393224 | tf_op jit(solution)/shard_map/cond/branch_1_fun/ppermute | solution.py:403
  169.0 2.5 %branch_1_fun.17 = bf16[2048,128]{1,0:T(8,128)(2,1)S(1)} custom-call(s32[8,128]{1,0:T(8,128)S(1)} %get-tuple-element.46.mine, s32[32]{0:T(128)S(1)} %copy-done.22, f32[2048,128]{1,0:T(8,128)S(1)} %copy-done.8, bf16[4,128,128]{2,1,0:T(8,128)(2,1)S(1)} %pad_maximum_fusion.own, bf16[4,128,128]{2,1,0:T(8,128)(2,1)S(1)} %collective-permute-done.21.other, ...), custom_call_target="tpu_custom_call" | custom-call | flops 33554432 | bytes 2097152 | tf_op jit(solution)/shard_map/cond/branch_1_fun/pallas_call | solution.py:470
  (79 shorter events, 24.0 us)
Async XLA Ops:
  11.5 156.2 %reduce-scatter.5.cloned.1.call-start = ((), (), s32[]{:S(2)}) async-start(), calls=%async_computation.7 | async-start | bytes 9437184 | tf_op jit(solution)/shard_map/cond/branch_1_fun/reduce_scatter | solution.py:569
  12.9 28.6 %collective-permute-start = (bf16[4,144,1024]{2,1,0:T(8,128)(2,1)S(1)}, bf16[4,144,1024]{2,1,0:T(8,128)(2,1)S(1)}, u32[]{:S(2)}, u32[]{:S(2)}) collective-permute-start(bf16[4,144,1024]{2,1,0:T(8,128)(2,1)S(1)} %get-tuple-element.52), channel_id=1, source_target_pairs={{0,32},{8,40},{16,48},{24,56},{32,64},{40,72},{48,80},{56,88},{64,... | collective-permute-start | bytes 3538952 | tf_op jit(solution)/shard_map/cond/branch_1_fun/ppermute | solution.py:52
  15.0 26.5 %collective-permute-start.1 = (bf16[4,144,1024]{2,1,0:T(8,128)(2,1)S(1)}, bf16[4,144,1024]{2,1,0:T(8,128)(2,1)S(1)}, u32[]{:S(2)}, u32[]{:S(2)}) collective-permute-start(bf16[4,144,1024]{2,1,0:T(8,128)(2,1)S(1)} %get-tuple-element.53), channel_id=1, source_target_pairs={{0,96},{8,104},{16,112},{24,120},{32,0},{40,8},{48,16},{56,24},{64... | collective-permute-start | bytes 3538952 | tf_op jit(solution)/shard_map/cond/branch_1_fun/ppermute | solution.py:52
  16.3 27.8 %collective-permute-start.2 = (bf16[4,144,1024]{2,1,0:T(8,128)(2,1)S(1)}, bf16[4,144,1024]{2,1,0:T(8,128)(2,1)S(1)}, u32[]{:S(2)}, u32[]{:S(2)}) collective-permute-start(bf16[4,144,1024]{2,1,0:T(8,128)(2,1)S(1)} %get-tuple-element.54), channel_id=1, source_target_pairs={{0,8},{8,16},{16,24},{24,0},{32,40},{40,48},{48,56},{56,32},{64,72... | collective-permute-start | bytes 3538952 | tf_op jit(solution)/shard_map/cond/branch_1_fun/ppermute | solution.py:52
  17.8 29.0 %collective-permute-start.3 = (bf16[4,144,1024]{2,1,0:T(8,128)(2,1)S(1)}, bf16[4,144,1024]{2,1,0:T(8,128)(2,1)S(1)}, u32[]{:S(2)}, u32[]{:S(2)}) collective-permute-start(bf16[4,144,1024]{2,1,0:T(8,128)(2,1)S(1)} %get-tuple-element.55), channel_id=1, source_target_pairs={{0,24},{8,0},{16,8},{24,16},{32,56},{40,32},{48,40},{56,48},{64,88... | collective-permute-start | bytes 3538952 | tf_op jit(solution)/shard_map/cond/branch_1_fun/ppermute | solution.py:52
  31.3 23.1 %copy-start.6 = (bf16[4,144,1024]{2,1,0:T(8,128)(2,1)}, bf16[4,144,1024]{2,1,0:T(8,128)(2,1)S(1)}, u32[]{:S(2)}) copy-start(bf16[4,144,1024]{2,1,0:T(8,128)(2,1)S(1)} %get-tuple-element.85.refs_5_) | copy-start | bytes 3538948 | tf_op jit(solution)/shard_map/cond
  31.3 23.1 %copy-start.15 = (bf16[2048,1024]{1,0:T(8,128)(2,1)S(1)}, bf16[2048,1024]{1,0:T(8,128)(2,1)}, u32[]{:S(2)}) copy-start(bf16[2048,1024]{1,0:T(8,128)(2,1)} %get-tuple-element.79.hidden) | copy-start | bytes 12582916 | tf_op jit(solution)/shard_map/cond
  31.3 23.1 %copy-start.23 = (bf16[1024,1024]{1,0:T(8,128)(2,1)S(1)}, bf16[1024,1024]{1,0:T(8,128)(2,1)}, u32[]{:S(2)}) copy-start(bf16[1024,1024]{1,0:T(8,128)(2,1)} %get-tuple-element.80.weight) | copy-start | bytes 6291460 | tf_op jit(solution)/shard_map/cond
  46.7 7.7 %copy-start.2 = (bf16[4,144,1024]{2,1,0:T(8,128)(2,1)}, bf16[4,144,1024]{2,1,0:T(8,128)(2,1)S(1)}, u32[]{:S(2)}) copy-start(bf16[4,144,1024]{2,1,0:T(8,128)(2,1)S(1)} %collective-permute-done.3.refs_3_.refs_9_) | copy-start | bytes 3538948 | tf_op jit(solution)/shard_map/cond
  49.0 14.5 %collective-permute-start.4 = (bf16[2,144,1024]{2,1,0:T(8,128)(2,1)}, bf16[2,144,1024]{2,1,0:T(8,128)(2,1)}, u32[]{:S(2)}, u32[]{:S(2)}) collective-permute-start(bf16[2,144,1024]{2,1,0:T(8,128)(2,1)} %get-tuple-element.74), channel_id=1, source_target_pairs={{0,32},{8,40},{16,48},{24,56},{32,64},{40,72},{48,80},{56,88},{64,... | collective-permute-start | bytes 1769480 | tf_op jit(solution)/shard_map/cond/branch_1_fun/ppermute | solution.py:52
  49.1 14.5 %collective-permute-start.5 = (bf16[2,144,1024]{2,1,0:T(8,128)(2,1)}, bf16[2,144,1024]{2,1,0:T(8,128)(2,1)}, u32[]{:S(2)}, u32[]{:S(2)}) collective-permute-start(bf16[2,144,1024]{2,1,0:T(8,128)(2,1)} %get-tuple-element.75), channel_id=1, source_target_pairs={{0,96},{8,104},{16,112},{24,120},{32,0},{40,8},{48,16},{56,24},{64... | collective-permute-start | bytes 1769480 | tf_op jit(solution)/shard_map/cond/branch_1_fun/ppermute | solution.py:52
  51.7 13.9 %collective-permute-start.6 = (bf16[2,144,1024]{2,1,0:T(8,128)(2,1)}, bf16[2,144,1024]{2,1,0:T(8,128)(2,1)}, u32[]{:S(2)}, u32[]{:S(2)}) collective-permute-start(bf16[2,144,1024]{2,1,0:T(8,128)(2,1)} %get-tuple-element.76), channel_id=1, source_target_pairs={{0,8},{8,16},{16,24},{24,0},{32,40},{40,48},{48,56},{56,32},{64,72... | collective-permute-start | bytes 1769480 | tf_op jit(solution)/shard_map/cond/branch_1_fun/ppermute | solution.py:52
  52.9 12.8 %collective-permute-start.7 = (bf16[2,144,1024]{2,1,0:T(8,128)(2,1)}, bf16[2,144,1024]{2,1,0:T(8,128)(2,1)}, u32[]{:S(2)}, u32[]{:S(2)}) collective-permute-start(bf16[2,144,1024]{2,1,0:T(8,128)(2,1)} %get-tuple-element.77), channel_id=1, source_target_pairs={{0,24},{8,0},{16,8},{24,16},{32,56},{40,32},{48,40},{56,48},{64,88... | collective-permute-start | bytes 1769480 | tf_op jit(solution)/shard_map/cond/branch_1_fun/ppermute | solution.py:52
  65.7 61.0 %all-to-all-start = ((bf16[16,144,1024]{2,1,0:T(8,128)(2,1)}), bf16[16,144,1024]{2,1,0:T(8,128)(2,1)}, u32[]{:S(2)}, u32[]{:S(2)}) async-start(bf16[16,144,1024]{2,1,0:T(8,128)(2,1)} %copy-done.1), calls=%async_computation.1 | async-start | bytes 9437184 | tf_op jit(solution)/shard_map/cond/branch_1_fun/all_to_all | solution.py:570
  78.6 47.9 %collective-permute-start.10 = (bf16[144,1024]{1,0:T(8,128)(2,1)S(1)}, bf16[144,1024]{1,0:T(8,128)(2,1)S(1)}, u32[]{:S(2)}, u32[]{:S(2)}) collective-permute-start(bf16[144,1024]{1,0:T(8,128)(2,1)S(1)} %get-tuple-element.91), channel_id=1, source_target_pairs={{0,24},{8,0},{16,8},{24,16},{32,56},{40,32},{48,40},{56,48},{64,88... | collective-permute-start | bytes 884744 | tf_op jit(solution)/shard_map/cond/branch_1_fun/ppermute | solution.py:52
  81.0 51.6 %collective-permute-start.11 = (bf16[144,1024]{1,0:T(8,128)(2,1)}, bf16[144,1024]{1,0:T(8,128)(2,1)S(1)}, u32[]{:S(2)}, u32[]{:S(2)}) collective-permute-start(bf16[144,1024]{1,0:T(8,128)(2,1)} %get-tuple-element.92), channel_id=1, source_target_pairs={{0,32},{8,40},{16,48},{24,56},{32,64},{40,72},{48,80},{56,88},{64,... | collective-permute-start | bytes 884744 | tf_op jit(solution)/shard_map/cond/branch_1_fun/ppermute | solution.py:52
  82.2 52.5 %collective-permute-start.12 = (bf16[144,1024]{1,0:T(8,128)(2,1)}, bf16[144,1024]{1,0:T(8,128)(2,1)S(1)}, u32[]{:S(2)}, u32[]{:S(2)}) collective-permute-start(bf16[144,1024]{1,0:T(8,128)(2,1)} %get-tuple-element.93), channel_id=1, source_target_pairs={{0,64},{8,72},{16,80},{24,88},{32,96},{40,104},{48,112},{56,120},{... | collective-permute-start | bytes 884744 | tf_op jit(solution)/shard_map/cond/branch_1_fun/ppermute | solution.py:52
  84.7 50.0 %collective-permute-start.13 = (bf16[144,1024]{1,0:T(8,128)(2,1)}, bf16[144,1024]{1,0:T(8,128)(2,1)S(1)}, u32[]{:S(2)}, u32[]{:S(2)}) collective-permute-start(bf16[144,1024]{1,0:T(8,128)(2,1)} %get-tuple-element.94), channel_id=1, source_target_pairs={{0,96},{8,104},{16,112},{24,120},{32,0},{40,8},{48,16},{56,24},{64... | collective-permute-start | bytes 884744 | tf_op jit(solution)/shard_map/cond/branch_1_fun/ppermute | solution.py:52
  85.8 48.9 %collective-permute-start.8 = (bf16[144,1024]{1,0:T(8,128)(2,1)}, bf16[144,1024]{1,0:T(8,128)(2,1)S(1)}, u32[]{:S(2)}, u32[]{:S(2)}) collective-permute-start(bf16[144,1024]{1,0:T(8,128)(2,1)} %get-tuple-element.89), channel_id=1, source_target_pairs={{0,8},{8,16},{16,24},{24,0},{32,40},{40,48},{48,56},{56,32},{64,72... | collective-permute-start | bytes 884744 | tf_op jit(solution)/shard_map/cond/branch_1_fun/ppermute | solution.py:52
  126.4 8.6 %collective-permute-start.9 = (bf16[144,1024]{1,0:T(8,128)(2,1)}, bf16[144,1024]{1,0:T(8,128)(2,1)S(1)}, u32[]{:S(2)}, u32[]{:S(2)}) collective-permute-start(bf16[144,1024]{1,0:T(8,128)(2,1)} %get-tuple-element.90), channel_id=1, source_target_pairs={{0,16},{8,24},{16,0},{24,8},{32,48},{40,56},{48,32},{56,40},{64,80... | collective-permute-start | bytes 884744 | tf_op jit(solution)/shard_map/cond/branch_1_fun/ppermute | solution.py:52
  126.6 8.4 %copy-start.10 = (bf16[144,1024]{1,0:T(8,128)(2,1)S(1)}, bf16[144,1024]{1,0:T(8,128)(2,1)}, u32[]{:S(2)}) copy-start(bf16[144,1024]{1,0:T(8,128)(2,1)} %copy-done.9) | copy-start | bytes 884740 | tf_op jit(solution)/shard_map/cond
  126.7 8.4 %copy-start.12 = (bf16[144,1024]{1,0:T(8,128)(2,1)S(1)}, bf16[144,1024]{1,0:T(8,128)(2,1)}, u32[]{:S(2)}) copy-start(bf16[144,1024]{1,0:T(8,128)(2,1)} %copy-done.11) | copy-start | bytes 884740 | tf_op jit(solution)/shard_map/cond
  126.7 9.1 %copy-start.16 = (bf16[2048,1024]{1,0:T(8,128)(2,1)S(1)}, bf16[2048,1024]{1,0:T(8,128)(2,1)}, u32[]{:S(2)}) copy-start(bf16[2048,1024]{1,0:T(8,128)(2,1)} %get-tuple-element.79.hidden) | copy-start | bytes 12582916 | tf_op jit(solution)/shard_map/cond
  135.7 32.0 %copy-start.22 = (s32[32]{0:T(128)S(1)}, s32[32]{0:T(128)}, u32[]{:S(2)}) copy-start(s32[32]{0:T(128)} %copy-done.21) | copy-start | bytes 388 | tf_op jit(solution)/shard_map/cond
  136.7 11.3 %collective-permute-start.14 = (f32[512,128]{1,0:T(8,128)S(1)}, f32[512,128]{1,0:T(8,128)S(1)}, u32[]{:S(2)}, u32[]{:S(2)}) collective-permute-start(f32[512,128]{1,0:T(8,128)S(1)} %constant_dynamic-slice_fusion.3), channel_id=1, source_target_pairs={{0,1},{1,0},{2,3},{3,2},{4,5},{5,4},{6,7},{7,6},{8,9},{9,8},{10,11... | collective-permute-start | bytes 786440 | tf_op jit(solution)/shard_map/cond/branch_1_fun/ppermute | solution.py:390
  148.0 6.0 %collective-permute-start.15 = (f32[128,128]{1,0:T(8,128)S(1)}, f32[128,128]{1,0:T(8,128)S(1)}, u32[]{:S(2)}, u32[]{:S(2)}) collective-permute-start(f32[128,128]{1,0:T(8,128)S(1)} %get-tuple-element.115), channel_id=1, source_target_pairs={{0,2},{1,3},{2,4},{3,5},{4,6},{5,7},{6,0},{7,1},{8,10},{9,11},{10,... | collective-permute-start | bytes 196616 | tf_op jit(solution)/shard_map/cond/branch_1_fun/ppermute | solution.py:394
  149.8 6.3 %collective-permute-start.16 = (f32[128,128]{1,0:T(8,128)S(1)}, f32[128,128]{1,0:T(8,128)S(1)}, u32[]{:S(2)}, u32[]{:S(2)}) collective-permute-start(f32[128,128]{1,0:T(8,128)S(1)} %get-tuple-element.113), channel_id=1, source_target_pairs={{0,4},{1,5},{2,6},{3,7},{4,0},{5,1},{6,2},{7,3},{8,12},{9,13},{10,... | collective-permute-start | bytes 196616 | tf_op jit(solution)/shard_map/cond/branch_1_fun/ppermute | solution.py:394
  153.1 3.4 %collective-permute-start.17 = (f32[128,128]{1,0:T(8,128)S(1)}, f32[128,128]{1,0:T(8,128)S(1)}, u32[]{:S(2)}, u32[]{:S(2)}) collective-permute-start(f32[128,128]{1,0:T(8,128)S(1)} %get-tuple-element.114), channel_id=1, source_target_pairs={{0,6},{1,7},{2,0},{3,1},{4,2},{5,3},{6,4},{7,5},{8,14},{9,15},{10,... | collective-permute-start | bytes 196616 | tf_op jit(solution)/shard_map/cond/branch_1_fun/ppermute | solution.py:394
  156.5 4.3 %collective-permute-start.19 = (bf16[128,128]{1,0:T(8,128)(2,1)S(1)}, bf16[128,128]{1,0:T(8,128)(2,1)S(1)}, u32[]{:S(2)}, u32[]{:S(2)}) collective-permute-start(bf16[128,128]{1,0:T(8,128)(2,1)S(1)} %add_convert_fusion), channel_id=1, source_target_pairs={{0,4},{1,5},{2,6},{3,7},{4,0},{5,1},{6,2},{7,3},{8,12},{9,13},{10,... | collective-permute-start | bytes 98312 | tf_op jit(solution)/shard_map/cond/branch_1_fun/ppermute | solution.py:402
  157.8 3.1 %collective-permute-start.20 = (bf16[128,128]{1,0:T(8,128)(2,1)S(1)}, bf16[128,128]{1,0:T(8,128)(2,1)S(1)}, u32[]{:S(2)}, u32[]{:S(2)}) collective-permute-start(bf16[128,128]{1,0:T(8,128)(2,1)S(1)} %add_convert_fusion), channel_id=1, source_target_pairs={{0,6},{1,7},{2,0},{3,1},{4,2},{5,3},{6,4},{7,5},{8,14},{9,15},{10,... | collective-permute-start | bytes 98312 | tf_op jit(solution)/shard_map/cond/branch_1_fun/ppermute | solution.py:402
  159.6 4.0 %collective-permute-start.18 = (bf16[128,128]{1,0:T(8,128)(2,1)S(1)}, bf16[128,128]{1,0:T(8,128)(2,1)S(1)}, u32[]{:S(2)}, u32[]{:S(2)}) collective-permute-start(bf16[128,128]{1,0:T(8,128)(2,1)S(1)} %add_convert_fusion), channel_id=1, source_target_pairs={{0,2},{1,3},{2,4},{3,5},{4,6},{5,7},{6,0},{7,1},{8,10},{9,11},{10,... | collective-permute-start | bytes 98312 | tf_op jit(solution)/shard_map/cond/branch_1_fun/ppermute | solution.py:402
  163.6 4.2 %collective-permute-start.21 = (bf16[4,128,128]{2,1,0:T(8,128)(2,1)S(1)}, bf16[4,128,128]{2,1,0:T(8,128)(2,1)S(1)}, u32[]{:S(2)}, u32[]{:S(2)}) collective-permute-start(bf16[4,128,128]{2,1,0:T(8,128)(2,1)S(1)} %pad_maximum_fusion.own), channel_id=1, source_target_pairs={{0,1},{1,0},{2,3},{3,2},{4,5},{5,4},{6,7},{7,6},{8,9},{9,8},{10,11... | collective-permute-start | bytes 393224 | tf_op jit(solution)/shard_map/cond/branch_1_fun/ppermute | solution.py:403
  (13 other events, 30.6 us)
Sparse Core Ops, SparseCore 0:
  65.8 54.2 reduce-scatter.4

commit v14 on v13

--- a/solution.py
+++ b/solution.py
@@ -39,7 +39,7 @@
 HBM = pl.BlockSpec(memory_space=pltpu.HBM)
 LANES = 128
 ORDER, PLACE, FLAGS = 0, 1, 2
-HOT, FITS, AT, CHIP, CORE = 0, 1, 2, 4, 5
+HOT, FITS, AT, CHIP, CORE, ME = 0, 1, 2, 4, 5, 6
 
 
 def shift(value, dx, dy):
@@ -118,6 +118,7 @@
         (AT + 1, lax.rem(y - lax.rem(hot, side) + side, side)),
         (CHIP, lax.div(spot_ref[1], 2)),
         (CORE, lax.rem(spot_ref[1], 2)),
+        (ME, me),
     )
     row = jnp.zeros((1, LANES), jnp.int32)
     for at, value in flags:
@@ -333,13 +334,25 @@
         unit = lax.div(place, 2)
         return main[unit, pl.ds(pl.multiple_of((place - 2 * unit) * rank, rank), rank), :]
 
+    def rows(j):
+        return hidden[pl.ds(pl.multiple_of(mine[ORDER, j] * cap, cap), cap), :]
+
     def body(i, carry):
-        at = pl.ds(pl.multiple_of(i * cap, cap), cap)
-        spots = (i, i + pairs)
-        out[at, :] = paired(hidden, mine, spots, cap, weights(i), weights(i + pairs))
+        spots = (2 * i, 2 * i + pairs, 2 * i + 1, 2 * i + 1 + pairs)
+        product = lax.dot_general(
+            jnp.concatenate([rows(j) for j in spots], axis=0),
+            jnp.concatenate([weights(j) for j in spots], axis=0),
+            (((1,), (1,)), ((), ())),
+            preferred_element_type=jnp.float32,
+        )
+        lane = lax.broadcasted_iota(jnp.int32, (cap, 2 * rank), 1)
+        for n in range(2):
+            part = product[2 * n * cap : 2 * (n + 1) * cap, 2 * n * rank : 2 * (n + 1) * rank]
+            at = pl.ds(pl.multiple_of((2 * i + n) * cap, cap), cap)
+            out[at, :] = jnp.where(lane < rank, part[:cap], part[cap:])
         return carry
 
-    lax.fori_loop(0, pairs, body, 0, unroll=2)
+    lax.fori_loop(0, pairs // 2, body, 0)
 
 
 def low_extra_kernel(cap, mine, hidden, first, second, _, out):
@@ -405,6 +418,7 @@
 
 def blend(base, out, counts, mine, j, both, ups, cap):
     rank = both.shape[1] // 2
+    groups = base.shape[0] // cap
     lane = lax.broadcasted_iota(jnp.int32, both.shape, 1)
     none = jnp.zeros_like(both)
     left = jnp.concatenate(
@@ -416,13 +430,12 @@
         g = mine[ORDER, j[n]]
         here = pl.ds(pl.multiple_of(g * cap, cap), cap)
         merged = base[here, :] + ADAPTER_SCALE * delta[n * cap : (n + 1) * cap]
-        out[here, :] = jnp.where(rows < counts[g], merged, 0.0).astype(out.dtype)
-
-
-def out_kernel(mine, counts, base, own, other, main, *refs):
+        out[here, :] = jnp.where(rows < counts[mine[FLAGS, ME] * groups + g], merged, 0.0).astype(out.dtype)
+
+
+def out_kernel(cap, mine, counts, base, own, other, main, *refs):
     extras, out, low = refs[:2], refs[2], refs[3]
-    groups = counts.shape[0]
-    cap = base.shape[0] // groups
+    groups = base.shape[0] // cap
     chips, piece, rank = own.shape[0], own.shape[1], own.shape[2] // 2
     lanes = base.shape[1]
     z, core = mine[FLAGS, CHIP], mine[FLAGS, CORE]
@@ -464,11 +477,11 @@
     return pl.BlockSpec(array.shape, lambda i: (0,) * array.ndim)
 
 
-def combine(mine, counts, base, own, other, main, extras, rank):
+def combine(mine, counts, base, own, other, main, extras, cap, rank):
     packs = pl.BlockSpec((main.shape[0], 16, main.shape[2]), lambda i: (0, rank // 8, 0))
     pack = pl.BlockSpec((16, main.shape[2]), lambda i: (rank // 8, 0))
     return pl.pallas_call(
-        out_kernel,
+        functools.partial(out_kernel, cap),
         grid=(1,),
         out_shape=jax.ShapeDtypeStruct(base.shape, jnp.bfloat16),
         in_specs=[SMEM, SMEM, whole(base), whole(own), whole(other), packs, pack, pack],
@@ -499,7 +512,6 @@
     cap = hidden.shape[0] // groups
     spot = jnp.stack([me, lax.axis_index("tp")]).astype(jnp.int32)
     served, mine = index_tables(spot, group_adapter_id, adapter_storage_row, dp_count)
-    counts = lax.dynamic_slice_in_dim(group_live_count, me * groups, groups)
 
     def wide(hidden, value_weight, down_weights, up_weights):
         stored = adapter_storage_row[group_adapter_id]
@@ -524,6 +536,7 @@
             preferred_element_type=jnp.float32,
         )
         low = low_rank_sum(partial.reshape(groups * cap, rank))
+        counts = lax.dynamic_slice_in_dim(group_live_count, me * groups, groups)
         return finish(base, low, ups[picked], counts)
 
     def narrow(hidden, value_weight, down_weights, up_weights):
@@ -585,7 +598,7 @@
             low_extra_kernel, cap, rank, mine, hidden, (*extras, partial), {4: 0}
         )
         own, other = low_rank_up(low_rank_down(partial))
-        return combine(mine, counts, base, own, other, main, extras, rank)
+        return combine(mine, group_live_count, base, own, other, main, extras, cap, rank)
 
     return lax.cond(
         mine[FLAGS, FITS] == 1, narrow, wide, hidden, value_weight, down_weights, up_weights

time: 180 us -> 180 us (level)
    cond x40 -> x38, local copies, waits for them, and re-layouts: 13.1 us -> 13.1 us
  transfers between devices with their start and end apart: 24 -> 24, of which waited for: 15 -> 16; matrix products, arithmetic and copies ran while one was open for 0% -> 0% of each run, Pallas kernels for 14% -> 14%
where the time goes in v14:
time: 180 us; the launch traced here: 178 us
  waiting for transfers between devices  67.9 us (38%)
  starting transfers between devices  47.2 us (26%)
  Pallas kernels  33.4 us (19%)
  local copies, waits for them, and re-layouts  15.3 us (8%)
  between operations  14.1 us (8%)
    ppermute x14, waiting for transfers between devices, shift(): return lax.ppermute(value, 'dp', pairs)  59.1 us
    ppermute x14, starting transfers between devices, shift(): return lax.ppermute(value, 'dp', pairs)  18.9 us
    cond x38, local copies, waits for them, and re-layouts  13.1 us
    ppermute x1, starting transfers between devices, low_rank_down(): lax.ppermute(cut(partial, (1 - core) * half, half), 'tp', swap())  11.7 us
    pallas_call x2, Pallas kernels, gather_units(): pl.pallas_call(kernel, out_shape=[jax.ShapeDtypeStruct((n, 2 * rank + 16,...  10.1 us
    pallas_call x2, Pallas kernels, low_call(): pl.pallas_call(functools.partial(kernel, cap), out_shape=jax.ShapeDtypeSt...  7.13 us
    pallas_call x3, Pallas kernels, vmem_call(): pl.pallas_call(kernel, out_shape=[jax.ShapeDtypeStruct(shape, dtype) for...  6.07 us
    ppermute x3, starting transfers between devices, low_rank_down(): lax.ppermute(cut(total, (z + d) % chips * piece, piece), 'tp', turn(d))  5.74 us
  transfers between devices with their start and end apart: 24, of which 16 were waited for; matrix products, arithmetic and copies ran while one was open for 0% of the time, Pallas kernels for 14%

profile of v14, /device:TPU:1, one launch (start us, length us, event | category | flops | bytes accessed | tf_op | source)
XLA Modules:
  0.0 178.4 jit_solution(9544541828626392693)
XLA Ops:
  7.4 1.8 %shard_map.75 = (s32[16,128]{1,0:T(8,128)S(1)}, s32[8,128]{1,0:T(8,128)S(1)}) custom-call(s32[2]{0:T(128)S(1)} %pad_add_fusion.spot_ref, s32[512,1]{1,0:T(8,128)S(1)} %copy.23.ids_ref, s32[16,128]{1,0:T(8,128)} %bitcast.29), custom_call_target="tpu_custom_call" | custom-call | tf_op jit(solution)/shard_map/pallas_call | solution.py:131
  10.5 160.3 %conditional.1 = (bf16[2048,128]{1,0:T(8,128)(2,1)S(1)}) conditional(s32[]{:T(128)} %bitcast.16, (s32[]{:T(128)}, s32[512]{0:T(512)}, bf16[2048,1024]{1,0:T(8,128)(2,1)}, bf16[1024,1024]{1,0:T(8,128)(2,1)}, s32[512]{0:T(512)}, /*index=5*/s32[2048]{0:T(1024)}, bf16[128,64,1024]{2,1,0:T(8,128)(2,1)}, bf16[128,64,128]{2,1,0:T(8,128)(2,1)}) %tuple.16, ...), branch_computations={%region_0.5_spmd, %region_5.7_spmd} | conditional | flops 4865720320 | bytes 341812576 | solution.py:603
  10.8 1.3 branch_1_fun.9
  12.1 2.1 %collective-permute-start = (bf16[4,144,1024]{2,1,0:T(8,128)(2,1)S(1)}, bf16[4,144,1024]{2,1,0:T(8,128)(2,1)S(1)}, u32[]{:S(2)}, u32[]{:S(2)}) collective-permute-start(bf16[4,144,1024]{2,1,0:T(8,128)(2,1)S(1)} %get-tuple-element.52), channel_id=1, source_target_pairs={{0,32},{8,40},{16,48},{24,56},{32,64},{40,72},{48,80},{56,88},{64,... | collective-permute-start | bytes 3538952 | tf_op jit(solution)/shard_map/cond/branch_1_fun/ppermute | solution.py:52
  14.2 1.3 collective-permute-start.1
  15.6 1.4 collective-permute-start.2
  17.0 1.4 collective-permute-start.3
  18.4 8.8 %branch_1_fun.10 = (bf16[16,144,1024]{2,1,0:T(8,128)(2,1)S(1)}, bf16[2,144,1024]{2,1,0:T(8,128)(2,1)S(1)}, bf16[2,144,1024]{2,1,0:T(8,128)(2,1)S(1)}, bf16[2,144...) custom-call(s32[16,128]{1,0:T(8,128)S(1)} %get-tuple-element.56.serv, ...), custom_call_target="tpu_custom_call" | custom-call | bytes 9437184 | tf_op jit(solution)/shard_map/cond/branch_1_fun/pallas_call | solution.py:206
  27.3 2.2 %copy-done.1 = bf16[16,144,1024]{2,1,0:T(8,128)(2,1)} copy-done((bf16[16,144,1024]{2,1,0:T(8,128)(2,1)}, bf16[16,144,1024]{2,1,0:T(8,128)(2,1)S(1)}, u32[]{:S(2)}) %copy-start.1) | copy-done | bytes 4718616 | tf_op jit(solution)/shard_map/cond
  30.5 10.2 %collective-permute-done.refs_0_.refs_3_ = bf16[4,144,1024]{2,1,0:T(8,128)(2,1)S(1)} collective-permute-done((bf16[4,144,1024]{2,1,0:T(8,128)(2,1)S(1)}, bf16[4,144,1024]{2,1,0:T(8,128)(2,1)S(1)}, u32[]{:S(2)}, u32[]{:S(2)}) %collective-permute-start) | collective-permute-done | bytes 1179680 | tf_op jit(solution)/shard_map/cond/branch_1_fun/ppermute | solution.py:52
  40.7 2.6 %collective-permute-done.2.refs_2_.refs_8_ = bf16[4,144,1024]{2,1,0:T(8,128)(2,1)S(1)} collective-permute-done((bf16[4,144,1024]{2,1,0:T(8,128)(2,1)S(1)}, bf16[4,144,1024]{2,1,0:T(8,128)(2,1)S(1)}, u32[]{:S(2)}, u32[]{:S(2)}) %collective-permute-start.2) | collective-permute-done | bytes 1179680 | tf_op jit(solution)/shard_map/cond/branch_1_fun/ppermute | solution.py:52
  44.6 2.3 %branch_1_fun.11 = (bf16[2,144,1024]{2,1,0:T(8,128)(2,1)}, bf16[2,144,1024]{2,1,0:T(8,128)(2,1)}, bf16[2,144,1024]{2,1,0:T(8,128)(2,1)}, bf16[2,144,1024]{2,1,0:T(8,128)(2,1)}) custom-call(s32[8,128]{1,0:T(8,128)S(1)} %get-tuple-element.46.mine, bf16[4,144,1024]{2,1,0:T(8,128)(2,1)S(1)} %collective-permute-done.refs_0_.refs_3_, ...), custom_call_target="tpu_custom_call" | custom-call | bytes 4718592 | tf_op jit(solution)/shard_map/cond/branch_1_fun/pallas_call | solution.py:224
  48.1 1.5 collective-permute-start.5
  50.8 1.5 collective-permute-start.7
  52.3 5.7 %branch_1_fun.12 = f32[2048,1024]{1,0:T(8,128)S(1)} custom-call(bf16[2048,1024]{1,0:T(8,128)(2,1)S(1)} %copy-done.15, bf16[1024,1024]{1,0:T(8,128)(2,1)S(1)} %copy-done.22), custom_call_target="tpu_custom_call" | custom-call | flops 4294967296 | bytes 14680064 | tf_op jit(solution)/shard_map/cond/branch_1_fun/pallas_call | solution.py:297
  58.0 3.3 %copy-done = f32[2048,1024]{1,0:T(8,128)} copy-done((f32[2048,1024]{1,0:T(8,128)}, f32[2048,1024]{1,0:T(8,128)S(1)}, u32[]{:S(2)}) %copy-start) | copy-done | bytes 8388632 | tf_op jit(solution)/shard_map/cond
  61.4 2.1 %collective-permute-done.6.refs_6_ = bf16[2,144,1024]{2,1,0:T(8,128)(2,1)} collective-permute-done((bf16[2,144,1024]{2,1,0:T(8,128)(2,1)}, bf16[2,144,1024]{2,1,0:T(8,128)(2,1)}, u32[]{:S(2)}, u32[]{:S(2)}) %collective-permute-start.6) | collective-permute-done | bytes 589856 | tf_op jit(solution)/shard_map/cond/branch_1_fun/ppermute | solution.py:52
  63.6 4.6 %all-to-all-start = ((bf16[16,144,1024]{2,1,0:T(8,128)(2,1)}), bf16[16,144,1024]{2,1,0:T(8,128)(2,1)}, u32[]{:S(2)}, u32[]{:S(2)}) async-start(bf16[16,144,1024]{2,1,0:T(8,128)(2,1)} %copy-done.1), calls=%async_computation.1 | async-start | bytes 9437184 | tf_op jit(solution)/shard_map/cond/branch_1_fun/all_to_all | solution.py:583
  72.0 3.0 %branch_1_fun.13 = (bf16[144,1024]{1,0:T(8,128)(2,1)S(1)}, bf16[144,1024]{1,0:T(8,128)(2,1)}, bf16[144,1024]{1,0:T(8,128)(2,1)}, bf16[144,1024]{1,0:T(8,128)(2,1...) custom-call(s32[8,128]{1,0:T(8,128)S(1)} %get-tuple-element.46.mine,, ...), custom_call_target="tpu_custom_call" | custom-call | bytes 4718592 | tf_op jit(solution)/shard_map/cond/branch_1_fun/pallas_call | solution.py:224
  76.4 2.4 %collective-permute-start.10 = (bf16[144,1024]{1,0:T(8,128)(2,1)S(1)}, bf16[144,1024]{1,0:T(8,128)(2,1)S(1)}, u32[]{:S(2)}, u32[]{:S(2)}) collective-permute-start(bf16[144,1024]{1,0:T(8,128)(2,1)S(1)} %get-tuple-element.91), channel_id=1, source_target_pairs={{0,24},{8,0},{16,8},{24,16},{32,56},{40,32},{48,40},{56,48},{64,88... | collective-permute-start | bytes 884744 | tf_op jit(solution)/shard_map/cond/branch_1_fun/ppermute | solution.py:52
  80.1 2.4 %collective-permute-start.12 = (bf16[144,1024]{1,0:T(8,128)(2,1)}, bf16[144,1024]{1,0:T(8,128)(2,1)S(1)}, u32[]{:S(2)}, u32[]{:S(2)}) collective-permute-start(bf16[144,1024]{1,0:T(8,128)(2,1)} %get-tuple-element.93), channel_id=1, source_target_pairs={{0,64},{8,72},{16,80},{24,88},{32,96},{40,104},{48,112},{56,120},{... | collective-permute-start | bytes 884744 | tf_op jit(solution)/shard_map/cond/branch_1_fun/ppermute | solution.py:52
  83.7 40.7 %collective-permute-done.10.refs_3_ = bf16[144,1024]{1,0:T(8,128)(2,1)S(1)} collective-permute-done((bf16[144,1024]{1,0:T(8,128)(2,1)S(1)}, bf16[144,1024]{1,0:T(8,128)(2,1)S(1)}, u32[]{:S(2)}, u32[]{:S(2)}) %collective-permute-start.10) | collective-permute-done | bytes 294944 | tf_op jit(solution)/shard_map/cond/branch_1_fun/ppermute | solution.py:52
  124.4 6.2 %branch_1_fun.14._ = f32[1024,128]{1,0:T(8,128)S(1)} custom-call(s32[8,128]{1,0:T(8,128)S(1)} %get-tuple-element.46.mine, bf16[2048,1024]{1,0:T(8,128)(2,1)} %get-tuple-element.79.hidden, bf16[16,144,1024]{2,1,0:T(8,128)(2,1)} %all-to-all-done.main), custom_call_target="tpu_custom_call" | custom-call | flops 268435456 | bytes 4718592 | tf_op jit(solution)/shard_map/cond/branch_1_fun/pallas_call | solution.py:372
  130.7 1.5 collective-permute-done.12.refs_6_
  134.4 11.7 %collective-permute-start.14 = (f32[512,128]{1,0:T(8,128)S(1)}, f32[512,128]{1,0:T(8,128)S(1)}, u32[]{:S(2)}, u32[]{:S(2)}) collective-permute-start(f32[512,128]{1,0:T(8,128)S(1)} %constant_dynamic-slice_fusion.3), channel_id=1, source_target_pairs={{0,1},{1,0},{2,3},{3,2},{4,5},{5,4},{6,7},{7,6},{8,9},{9,8},{10,11... | collective-permute-start | bytes 786440 | tf_op jit(solution)/shard_map/cond/branch_1_fun/ppermute | solution.py:403
  147.4 1.7 collective-permute-start.15
  149.1 3.3 %collective-permute-start.16 = (f32[128,128]{1,0:T(8,128)S(1)}, f32[128,128]{1,0:T(8,128)S(1)}, u32[]{:S(2)}, u32[]{:S(2)}) collective-permute-start(f32[128,128]{1,0:T(8,128)S(1)} %get-tuple-element.113), channel_id=1, source_target_pairs={{0,4},{1,5},{2,6},{3,7},{4,0},{5,1},{6,2},{7,3},{8,12},{9,13},{10,... | collective-permute-start | bytes 196616 | tf_op jit(solution)/shard_map/cond/branch_1_fun/ppermute | solution.py:407
  153.4 2.0 %collective-permute-done.16 = f32[128,128]{1,0:T(8,128)S(1)} collective-permute-done((f32[128,128]{1,0:T(8,128)S(1)}, f32[128,128]{1,0:T(8,128)S(1)}, u32[]{:S(2)}, u32[]{:S(2)}) %collective-permute-start.16) | collective-permute-done | bytes 65568 | tf_op jit(solution)/shard_map/cond/branch_1_fun/ppermute | solution.py:407
  157.1 1.7 collective-permute-start.20
  160.2 2.7 %collective-permute-done.18 = bf16[128,128]{1,0:T(8,128)(2,1)S(1)} collective-permute-done((bf16[128,128]{1,0:T(8,128)(2,1)S(1)}, bf16[128,128]{1,0:T(8,128)(2,1)S(1)}, u32[]{:S(2)}, u32[]{:S(2)}) %collective-permute-start.18) | collective-permute-done | bytes 32800 | tf_op jit(solution)/shard_map/cond/branch_1_fun/ppermute | solution.py:415
  162.9 3.2 %collective-permute-start.21 = (bf16[4,128,128]{2,1,0:T(8,128)(2,1)S(1)}, bf16[4,128,128]{2,1,0:T(8,128)(2,1)S(1)}, u32[]{:S(2)}, u32[]{:S(2)}) collective-permute-start(bf16[4,128,128]{2,1,0:T(8,128)(2,1)S(1)} %pad_maximum_fusion.own), channel_id=1, source_target_pairs={{0,1},{1,0},{2,3},{3,2},{4,5},{5,4},{6,7},{7,6},{8,9},{9,8},{10,11... | collective-permute-start | bytes 393224 | tf_op jit(solution)/shard_map/cond/branch_1_fun/ppermute | solution.py:416
  168.3 2.5 %branch_1_fun.17 = bf16[2048,128]{1,0:T(8,128)(2,1)S(1)} custom-call(s32[8,128]{1,0:T(8,128)S(1)} %get-tuple-element.46.mine, s32[512]{0:T(512)S(1)} %copy-done.21, f32[2048,128]{1,0:T(8,128)S(1)} %copy-done.8, bf16[4,128,128]{2,1,0:T(8,128)(2,1)S(1)} %pad_maximum_fusion.own, bf16[4,128,128]{2,1,0:T(8,128)(2,1)S(1)} %collective-permute-done.21.other, ...), custom_call_target="tpu_custom_call" | custom-call | flops 33554432 | bytes 2097152 | tf_op jit(solution)/shard_map/cond/branch_1_fun/pallas_call | solution.py:483
  (76 shorter events, 24.4 us)
Async XLA Ops:
  10.7 156.3 %reduce-scatter.5.cloned.1.call-start = ((), (), s32[]{:S(2)}) async-start(), calls=%async_computation.7 | async-start | bytes 9437184 | tf_op jit(solution)/shard_map/cond/branch_1_fun/reduce_scatter | solution.py:582
  12.1 28.6 %collective-permute-start = (bf16[4,144,1024]{2,1,0:T(8,128)(2,1)S(1)}, bf16[4,144,1024]{2,1,0:T(8,128)(2,1)S(1)}, u32[]{:S(2)}, u32[]{:S(2)}) collective-permute-start(bf16[4,144,1024]{2,1,0:T(8,128)(2,1)S(1)} %get-tuple-element.52), channel_id=1, source_target_pairs={{0,32},{8,40},{16,48},{24,56},{32,64},{40,72},{48,80},{56,88},{64,... | collective-permute-start | bytes 3538952 | tf_op jit(solution)/shard_map/cond/branch_1_fun/ppermute | solution.py:52
  14.2 26.5 %collective-permute-start.1 = (bf16[4,144,1024]{2,1,0:T(8,128)(2,1)S(1)}, bf16[4,144,1024]{2,1,0:T(8,128)(2,1)S(1)}, u32[]{:S(2)}, u32[]{:S(2)}) collective-permute-start(bf16[4,144,1024]{2,1,0:T(8,128)(2,1)S(1)} %get-tuple-element.53), channel_id=1, source_target_pairs={{0,96},{8,104},{16,112},{24,120},{32,0},{40,8},{48,16},{56,24},{64... | collective-permute-start | bytes 3538952 | tf_op jit(solution)/shard_map/cond/branch_1_fun/ppermute | solution.py:52
  15.6 27.8 %collective-permute-start.2 = (bf16[4,144,1024]{2,1,0:T(8,128)(2,1)S(1)}, bf16[4,144,1024]{2,1,0:T(8,128)(2,1)S(1)}, u32[]{:S(2)}, u32[]{:S(2)}) collective-permute-start(bf16[4,144,1024]{2,1,0:T(8,128)(2,1)S(1)} %get-tuple-element.54), channel_id=1, source_target_pairs={{0,8},{8,16},{16,24},{24,0},{32,40},{40,48},{48,56},{56,32},{64,72... | collective-permute-start | bytes 3538952 | tf_op jit(solution)/shard_map/cond/branch_1_fun/ppermute | solution.py:52
  17.0 27.6 %collective-permute-start.3 = (bf16[4,144,1024]{2,1,0:T(8,128)(2,1)S(1)}, bf16[4,144,1024]{2,1,0:T(8,128)(2,1)S(1)}, u32[]{:S(2)}, u32[]{:S(2)}) collective-permute-start(bf16[4,144,1024]{2,1,0:T(8,128)(2,1)S(1)} %get-tuple-element.55), channel_id=1, source_target_pairs={{0,24},{8,0},{16,8},{24,16},{32,56},{40,32},{48,40},{56,48},{64,88... | collective-permute-start | bytes 3538952 | tf_op jit(solution)/shard_map/cond/branch_1_fun/ppermute | solution.py:52
  30.5 21.7 %copy-start.6 = (bf16[4,144,1024]{2,1,0:T(8,128)(2,1)}, bf16[4,144,1024]{2,1,0:T(8,128)(2,1)S(1)}, u32[]{:S(2)}) copy-start(bf16[4,144,1024]{2,1,0:T(8,128)(2,1)S(1)} %get-tuple-element.85.refs_5_) | copy-start | bytes 3538948 | tf_op jit(solution)/shard_map/cond
  30.5 21.7 %copy-start.15 = (bf16[2048,1024]{1,0:T(8,128)(2,1)S(1)}, bf16[2048,1024]{1,0:T(8,128)(2,1)}, u32[]{:S(2)}) copy-start(bf16[2048,1024]{1,0:T(8,128)(2,1)} %get-tuple-element.79.hidden) | copy-start | bytes 12582916 | tf_op jit(solution)/shard_map/cond
  30.5 21.7 %copy-start.22 = (bf16[1024,1024]{1,0:T(8,128)(2,1)S(1)}, bf16[1024,1024]{1,0:T(8,128)(2,1)}, u32[]{:S(2)}) copy-start(bf16[1024,1024]{1,0:T(8,128)(2,1)} %get-tuple-element.80.weight) | copy-start | bytes 6291460 | tf_op jit(solution)/shard_map/cond
  44.6 7.7 %copy-start.2 = (bf16[4,144,1024]{2,1,0:T(8,128)(2,1)}, bf16[4,144,1024]{2,1,0:T(8,128)(2,1)S(1)}, u32[]{:S(2)}) copy-start(bf16[4,144,1024]{2,1,0:T(8,128)(2,1)S(1)} %collective-permute-done.3.refs_3_.refs_9_) | copy-start | bytes 3538948 | tf_op jit(solution)/shard_map/cond
  46.9 14.5 %collective-permute-start.4 = (bf16[2,144,1024]{2,1,0:T(8,128)(2,1)}, bf16[2,144,1024]{2,1,0:T(8,128)(2,1)}, u32[]{:S(2)}, u32[]{:S(2)}) collective-permute-start(bf16[2,144,1024]{2,1,0:T(8,128)(2,1)} %get-tuple-element.74), channel_id=1, source_target_pairs={{0,32},{8,40},{16,48},{24,56},{32,64},{40,72},{48,80},{56,88},{64,... | collective-permute-start | bytes 1769480 | tf_op jit(solution)/shard_map/cond/branch_1_fun/ppermute | solution.py:52
  48.1 13.3 %collective-permute-start.5 = (bf16[2,144,1024]{2,1,0:T(8,128)(2,1)}, bf16[2,144,1024]{2,1,0:T(8,128)(2,1)}, u32[]{:S(2)}, u32[]{:S(2)}) collective-permute-start(bf16[2,144,1024]{2,1,0:T(8,128)(2,1)} %get-tuple-element.75), channel_id=1, source_target_pairs={{0,96},{8,104},{16,112},{24,120},{32,0},{40,8},{48,16},{56,24},{64... | collective-permute-start | bytes 1769480 | tf_op jit(solution)/shard_map/cond/branch_1_fun/ppermute | solution.py:52
  49.6 13.9 %collective-permute-start.6 = (bf16[2,144,1024]{2,1,0:T(8,128)(2,1)}, bf16[2,144,1024]{2,1,0:T(8,128)(2,1)}, u32[]{:S(2)}, u32[]{:S(2)}) collective-permute-start(bf16[2,144,1024]{2,1,0:T(8,128)(2,1)} %get-tuple-element.76), channel_id=1, source_target_pairs={{0,8},{8,16},{16,24},{24,0},{32,40},{40,48},{48,56},{56,32},{64,72... | collective-permute-start | bytes 1769480 | tf_op jit(solution)/shard_map/cond/branch_1_fun/ppermute | solution.py:52
  50.8 12.8 %collective-permute-start.7 = (bf16[2,144,1024]{2,1,0:T(8,128)(2,1)}, bf16[2,144,1024]{2,1,0:T(8,128)(2,1)}, u32[]{:S(2)}, u32[]{:S(2)}) collective-permute-start(bf16[2,144,1024]{2,1,0:T(8,128)(2,1)} %get-tuple-element.77), channel_id=1, source_target_pairs={{0,24},{8,0},{16,8},{24,16},{32,56},{40,32},{48,40},{56,48},{64,88... | collective-permute-start | bytes 1769480 | tf_op jit(solution)/shard_map/cond/branch_1_fun/ppermute | solution.py:52
  63.6 60.8 %all-to-all-start = ((bf16[16,144,1024]{2,1,0:T(8,128)(2,1)}), bf16[16,144,1024]{2,1,0:T(8,128)(2,1)}, u32[]{:S(2)}, u32[]{:S(2)}) async-start(bf16[16,144,1024]{2,1,0:T(8,128)(2,1)} %copy-done.1), calls=%async_computation.1 | async-start | bytes 9437184 | tf_op jit(solution)/shard_map/cond/branch_1_fun/all_to_all | solution.py:583
  76.4 47.9 %collective-permute-start.10 = (bf16[144,1024]{1,0:T(8,128)(2,1)S(1)}, bf16[144,1024]{1,0:T(8,128)(2,1)S(1)}, u32[]{:S(2)}, u32[]{:S(2)}) collective-permute-start(bf16[144,1024]{1,0:T(8,128)(2,1)S(1)} %get-tuple-element.91), channel_id=1, source_target_pairs={{0,24},{8,0},{16,8},{24,16},{32,56},{40,32},{48,40},{56,48},{64,88... | collective-permute-start | bytes 884744 | tf_op jit(solution)/shard_map/cond/branch_1_fun/ppermute | solution.py:52
  78.8 51.8 %collective-permute-start.11 = (bf16[144,1024]{1,0:T(8,128)(2,1)}, bf16[144,1024]{1,0:T(8,128)(2,1)S(1)}, u32[]{:S(2)}, u32[]{:S(2)}) collective-permute-start(bf16[144,1024]{1,0:T(8,128)(2,1)} %get-tuple-element.92), channel_id=1, source_target_pairs={{0,32},{8,40},{16,48},{24,56},{32,64},{40,72},{48,80},{56,88},{64,... | collective-permute-start | bytes 884744 | tf_op jit(solution)/shard_map/cond/branch_1_fun/ppermute | solution.py:52
  80.1 52.1 %collective-permute-start.12 = (bf16[144,1024]{1,0:T(8,128)(2,1)}, bf16[144,1024]{1,0:T(8,128)(2,1)S(1)}, u32[]{:S(2)}, u32[]{:S(2)}) collective-permute-start(bf16[144,1024]{1,0:T(8,128)(2,1)} %get-tuple-element.93), channel_id=1, source_target_pairs={{0,64},{8,72},{16,80},{24,88},{32,96},{40,104},{48,112},{56,120},{... | collective-permute-start | bytes 884744 | tf_op jit(solution)/shard_map/cond/branch_1_fun/ppermute | solution.py:52
  82.5 50.1 %collective-permute-start.13 = (bf16[144,1024]{1,0:T(8,128)(2,1)}, bf16[144,1024]{1,0:T(8,128)(2,1)S(1)}, u32[]{:S(2)}, u32[]{:S(2)}) collective-permute-start(bf16[144,1024]{1,0:T(8,128)(2,1)} %get-tuple-element.94), channel_id=1, source_target_pairs={{0,96},{8,104},{16,112},{24,120},{32,0},{40,8},{48,16},{56,24},{64... | collective-permute-start | bytes 884744 | tf_op jit(solution)/shard_map/cond/branch_1_fun/ppermute | solution.py:52
  83.7 49.0 %collective-permute-start.8 = (bf16[144,1024]{1,0:T(8,128)(2,1)}, bf16[144,1024]{1,0:T(8,128)(2,1)S(1)}, u32[]{:S(2)}, u32[]{:S(2)}) collective-permute-start(bf16[144,1024]{1,0:T(8,128)(2,1)} %get-tuple-element.89), channel_id=1, source_target_pairs={{0,8},{8,16},{16,24},{24,0},{32,40},{40,48},{48,56},{56,32},{64,72... | collective-permute-start | bytes 884744 | tf_op jit(solution)/shard_map/cond/branch_1_fun/ppermute | solution.py:52
  124.4 8.4 %collective-permute-start.9 = (bf16[144,1024]{1,0:T(8,128)(2,1)}, bf16[144,1024]{1,0:T(8,128)(2,1)S(1)}, u32[]{:S(2)}, u32[]{:S(2)}) collective-permute-start(bf16[144,1024]{1,0:T(8,128)(2,1)} %get-tuple-element.90), channel_id=1, source_target_pairs={{0,16},{8,24},{16,0},{24,8},{32,48},{40,56},{48,32},{56,40},{64,80... | collective-permute-start | bytes 884744 | tf_op jit(solution)/shard_map/cond/branch_1_fun/ppermute | solution.py:52
  124.4 8.4 %copy-start.10 = (bf16[144,1024]{1,0:T(8,128)(2,1)S(1)}, bf16[144,1024]{1,0:T(8,128)(2,1)}, u32[]{:S(2)}) copy-start(bf16[144,1024]{1,0:T(8,128)(2,1)} %copy-done.9) | copy-start | bytes 884740 | tf_op jit(solution)/shard_map/cond
  124.4 8.4 %copy-start.12 = (bf16[144,1024]{1,0:T(8,128)(2,1)S(1)}, bf16[144,1024]{1,0:T(8,128)(2,1)}, u32[]{:S(2)}) copy-start(bf16[144,1024]{1,0:T(8,128)(2,1)} %copy-done.11) | copy-start | bytes 884740 | tf_op jit(solution)/shard_map/cond
  124.4 9.1 %copy-start.16 = (bf16[2048,1024]{1,0:T(8,128)(2,1)S(1)}, bf16[2048,1024]{1,0:T(8,128)(2,1)}, u32[]{:S(2)}) copy-start(bf16[2048,1024]{1,0:T(8,128)(2,1)} %get-tuple-element.79.hidden) | copy-start | bytes 12582916 | tf_op jit(solution)/shard_map/cond
  133.5 33.6 %copy-start.21 = (s32[512]{0:T(512)S(1)}, s32[512]{0:T(512)}, u32[]{:S(2)}) copy-start(s32[512]{0:T(512)} %get-tuple-element.47.counts) | copy-start | bytes 6148 | tf_op jit(solution)/shard_map/cond
  134.4 12.9 %collective-permute-start.14 = (f32[512,128]{1,0:T(8,128)S(1)}, f32[512,128]{1,0:T(8,128)S(1)}, u32[]{:S(2)}, u32[]{:S(2)}) collective-permute-start(f32[512,128]{1,0:T(8,128)S(1)} %constant_dynamic-slice_fusion.3), channel_id=1, source_target_pairs={{0,1},{1,0},{2,3},{3,2},{4,5},{5,4},{6,7},{7,6},{8,9},{9,8},{10,11... | collective-permute-start | bytes 786440 | tf_op jit(solution)/shard_map/cond/branch_1_fun/ppermute | solution.py:403
  147.4 6.0 %collective-permute-start.15 = (f32[128,128]{1,0:T(8,128)S(1)}, f32[128,128]{1,0:T(8,128)S(1)}, u32[]{:S(2)}, u32[]{:S(2)}) collective-permute-start(f32[128,128]{1,0:T(8,128)S(1)} %get-tuple-element.115), channel_id=1, source_target_pairs={{0,2},{1,3},{2,4},{3,5},{4,6},{5,7},{6,0},{7,1},{8,10},{9,11},{10,... | collective-permute-start | bytes 196616 | tf_op jit(solution)/shard_map/cond/branch_1_fun/ppermute | solution.py:407
  149.1 6.3 %collective-permute-start.16 = (f32[128,128]{1,0:T(8,128)S(1)}, f32[128,128]{1,0:T(8,128)S(1)}, u32[]{:S(2)}, u32[]{:S(2)}) collective-permute-start(f32[128,128]{1,0:T(8,128)S(1)} %get-tuple-element.113), channel_id=1, source_target_pairs={{0,4},{1,5},{2,6},{3,7},{4,0},{5,1},{6,2},{7,3},{8,12},{9,13},{10,... | collective-permute-start | bytes 196616 | tf_op jit(solution)/shard_map/cond/branch_1_fun/ppermute | solution.py:407
  152.4 3.4 %collective-permute-start.17 = (f32[128,128]{1,0:T(8,128)S(1)}, f32[128,128]{1,0:T(8,128)S(1)}, u32[]{:S(2)}, u32[]{:S(2)}) collective-permute-start(f32[128,128]{1,0:T(8,128)S(1)} %get-tuple-element.114), channel_id=1, source_target_pairs={{0,6},{1,7},{2,0},{3,1},{4,2},{5,3},{6,4},{7,5},{8,14},{9,15},{10,... | collective-permute-start | bytes 196616 | tf_op jit(solution)/shard_map/cond/branch_1_fun/ppermute | solution.py:407
  155.8 4.3 %collective-permute-start.19 = (bf16[128,128]{1,0:T(8,128)(2,1)S(1)}, bf16[128,128]{1,0:T(8,128)(2,1)S(1)}, u32[]{:S(2)}, u32[]{:S(2)}) collective-permute-start(bf16[128,128]{1,0:T(8,128)(2,1)S(1)} %add_convert_fusion), channel_id=1, source_target_pairs={{0,4},{1,5},{2,6},{3,7},{4,0},{5,1},{6,2},{7,3},{8,12},{9,13},{10,... | collective-permute-start | bytes 98312 | tf_op jit(solution)/shard_map/cond/branch_1_fun/ppermute | solution.py:415
  157.1 3.1 %collective-permute-start.20 = (bf16[128,128]{1,0:T(8,128)(2,1)S(1)}, bf16[128,128]{1,0:T(8,128)(2,1)S(1)}, u32[]{:S(2)}, u32[]{:S(2)}) collective-permute-start(bf16[128,128]{1,0:T(8,128)(2,1)S(1)} %add_convert_fusion), channel_id=1, source_target_pairs={{0,6},{1,7},{2,0},{3,1},{4,2},{5,3},{6,4},{7,5},{8,14},{9,15},{10,... | collective-permute-start | bytes 98312 | tf_op jit(solution)/shard_map/cond/branch_1_fun/ppermute | solution.py:415
  158.9 4.0 %collective-permute-start.18 = (bf16[128,128]{1,0:T(8,128)(2,1)S(1)}, bf16[128,128]{1,0:T(8,128)(2,1)S(1)}, u32[]{:S(2)}, u32[]{:S(2)}) collective-permute-start(bf16[128,128]{1,0:T(8,128)(2,1)S(1)} %add_convert_fusion), channel_id=1, source_target_pairs={{0,2},{1,3},{2,4},{3,5},{4,6},{5,7},{6,0},{7,1},{8,10},{9,11},{10,... | collective-permute-start | bytes 98312 | tf_op jit(solution)/shard_map/cond/branch_1_fun/ppermute | solution.py:415
  162.9 4.2 %collective-permute-start.21 = (bf16[4,128,128]{2,1,0:T(8,128)(2,1)S(1)}, bf16[4,128,128]{2,1,0:T(8,128)(2,1)S(1)}, u32[]{:S(2)}, u32[]{:S(2)}) collective-permute-start(bf16[4,128,128]{2,1,0:T(8,128)(2,1)S(1)} %pad_maximum_fusion.own), channel_id=1, source_target_pairs={{0,1},{1,0},{2,3},{3,2},{4,5},{5,4},{6,7},{7,6},{8,9},{9,8},{10,11... | collective-permute-start | bytes 393224 | tf_op jit(solution)/shard_map/cond/branch_1_fun/ppermute | solution.py:416
  (12 other events, 29.2 us)
Sparse Core Ops, SparseCore 0:
  63.7 54.6 reduce-scatter.4

commit v15 on v14

--- a/solution.py
+++ b/solution.py
@@ -352,7 +352,7 @@
             out[at, :] = jnp.where(lane < rank, part[:cap], part[cap:])
         return carry
 
-    lax.fori_loop(0, pairs // 2, body, 0)
+    lax.fori_loop(0, pairs // 2, body, 0, unroll=True)
 
 
 def low_extra_kernel(cap, mine, hidden, first, second, _, out):
@@ -461,7 +461,7 @@
         blend(base, out, counts, mine, (i, i + pairs), both, up(i) + up(i + pairs), cap)
         return carry
 
-    lax.fori_loop(0, pairs, body, 0, unroll=2)
+    lax.fori_loop(0, pairs, body, 0, unroll=True)
     for e in range(EXTRA // 2):
         ups = [
             pack[:, (e * steps + part) * lanes : (e * steps + part + 1) * lanes]

time: 180 us -> 179 us (level)
  Pallas kernels: 33.4 us -> 31.1 us
  starting transfers between devices: 47.2 us -> 49.3 us
  transfers between devices with their start and end apart: 24 -> 24, of which waited for: 16 -> 15; matrix products, arithmetic and copies ran while one was open for 0% -> 0% of each run, Pallas kernels for 14% -> 13%
where the time goes in v15:
time: 179 us
  waiting for transfers between devices  68.6 us (38%)
  starting transfers between devices  49.3 us (28%)
  Pallas kernels  31.1 us (17%)
  local copies, waits for them, and re-layouts  15.3 us (9%)
  between operations  14.1 us (8%)
    ppermute x14, waiting for transfers between devices, shift(): return lax.ppermute(value, 'dp', pairs)  59.8 us
    ppermute x14, starting transfers between devices, shift(): return lax.ppermute(value, 'dp', pairs)  19.3 us
    cond x38, local copies, waits for them, and re-layouts  13.1 us
    ppermute x1, starting transfers between devices, low_rank_down(): lax.ppermute(cut(partial, (1 - core) * half, half), 'tp', swap())  12.7 us
    pallas_call x2, Pallas kernels, gather_units(): pl.pallas_call(kernel, out_shape=[jax.ShapeDtypeStruct((n, 2 * rank + 16,...  10.1 us
    pallas_call x3, Pallas kernels, vmem_call(): pl.pallas_call(kernel, out_shape=[jax.ShapeDtypeStruct(shape, dtype) for...  6.07 us
    pallas_call x2, Pallas kernels, low_call(): pl.pallas_call(functools.partial(kernel, cap), out_shape=jax.ShapeDtypeSt...  5.81 us
    ppermute x3, starting transfers between devices, low_rank_down(): lax.ppermute(cut(total, (z + d) % chips * piece, piece), 'tp', turn(d))  5.74 us
  transfers between devices with their start and end apart: 24, of which 15 were waited for; matrix products, arithmetic and copies ran while one was open for 0% of the time, Pallas kernels for 13%

profile of v15, /device:TPU:1, one launch (start us, length us, event | category | flops | bytes accessed | tf_op | source)
XLA Modules:
  0.0 179.1 jit_solution(6566772296141070373)
XLA Ops:
  7.4 1.8 %shard_map.75 = (s32[16,128]{1,0:T(8,128)S(1)}, s32[8,128]{1,0:T(8,128)S(1)}) custom-call(s32[2]{0:T(128)S(1)} %pad_add_fusion.spot_ref, s32[512,1]{1,0:T(8,128)S(1)} %copy.23.ids_ref, s32[16,128]{1,0:T(8,128)} %bitcast.29), custom_call_target="tpu_custom_call" | custom-call | tf_op jit(solution)/shard_map/pallas_call | solution.py:131
  10.5 160.9 %conditional.1 = (bf16[2048,128]{1,0:T(8,128)(2,1)S(1)}) conditional(s32[]{:T(128)} %bitcast.16, (s32[]{:T(128)}, s32[512]{0:T(512)}, bf16[2048,1024]{1,0:T(8,128)(2,1)}, bf16[1024,1024]{1,0:T(8,128)(2,1)}, s32[512]{0:T(512)}, /*index=5*/s32[2048]{0:T(1024)}, bf16[128,64,1024]{2,1,0:T(8,128)(2,1)}, bf16[128,64,128]{2,1,0:T(8,128)(2,1)}) %tuple.16, ...), branch_computations={%region_0.5_spmd, %region_5.7_spmd} | conditional | flops 4865720320 | bytes 341812576 | solution.py:603
  10.8 1.3 branch_1_fun.9
  12.1 2.1 %collective-permute-start = (bf16[4,144,1024]{2,1,0:T(8,128)(2,1)S(1)}, bf16[4,144,1024]{2,1,0:T(8,128)(2,1)S(1)}, u32[]{:S(2)}, u32[]{:S(2)}) collective-permute-start(bf16[4,144,1024]{2,1,0:T(8,128)(2,1)S(1)} %get-tuple-element.52), channel_id=1, source_target_pairs={{0,32},{8,40},{16,48},{24,56},{32,64},{40,72},{48,80},{56,88},{64,... | collective-permute-start | bytes 3538952 | tf_op jit(solution)/shard_map/cond/branch_1_fun/ppermute | solution.py:52
  14.2 1.3 collective-permute-start.1
  15.6 1.4 collective-permute-start.2
  17.0 1.4 collective-permute-start.3
  18.4 8.8 %branch_1_fun.10 = (bf16[16,144,1024]{2,1,0:T(8,128)(2,1)S(1)}, bf16[2,144,1024]{2,1,0:T(8,128)(2,1)S(1)}, bf16[2,144,1024]{2,1,0:T(8,128)(2,1)S(1)}, bf16[2,144...) custom-call(s32[16,128]{1,0:T(8,128)S(1)} %get-tuple-element.56.serv, ...), custom_call_target="tpu_custom_call" | custom-call | bytes 9437184 | tf_op jit(solution)/shard_map/cond/branch_1_fun/pallas_call | solution.py:206
  27.3 2.2 %copy-done.1 = bf16[16,144,1024]{2,1,0:T(8,128)(2,1)} copy-done((bf16[16,144,1024]{2,1,0:T(8,128)(2,1)}, bf16[16,144,1024]{2,1,0:T(8,128)(2,1)S(1)}, u32[]{:S(2)}) %copy-start.1) | copy-done | bytes 4718616 | tf_op jit(solution)/shard_map/cond
  30.5 10.2 %collective-permute-done.refs_0_.refs_3_ = bf16[4,144,1024]{2,1,0:T(8,128)(2,1)S(1)} collective-permute-done((bf16[4,144,1024]{2,1,0:T(8,128)(2,1)S(1)}, bf16[4,144,1024]{2,1,0:T(8,128)(2,1)S(1)}, u32[]{:S(2)}, u32[]{:S(2)}) %collective-permute-start) | collective-permute-done | bytes 1179680 | tf_op jit(solution)/shard_map/cond/branch_1_fun/ppermute | solution.py:52
  40.7 2.8 %collective-permute-done.1.refs_1_.refs_4_ = bf16[4,144,1024]{2,1,0:T(8,128)(2,1)S(1)} collective-permute-done((bf16[4,144,1024]{2,1,0:T(8,128)(2,1)S(1)}, bf16[4,144,1024]{2,1,0:T(8,128)(2,1)S(1)}, u32[]{:S(2)}, u32[]{:S(2)}) %collective-permute-start.1) | collective-permute-done | bytes 1179680 | tf_op jit(solution)/shard_map/cond/branch_1_fun/ppermute | solution.py:52
  43.5 2.3 %branch_1_fun.11 = (bf16[2,144,1024]{2,1,0:T(8,128)(2,1)}, bf16[2,144,1024]{2,1,0:T(8,128)(2,1)}, bf16[2,144,1024]{2,1,0:T(8,128)(2,1)}, bf16[2,144,1024]{2,1,0:T(8,128)(2,1)}) custom-call(s32[8,128]{1,0:T(8,128)S(1)} %get-tuple-element.46.mine, bf16[4,144,1024]{2,1,0:T(8,128)(2,1)S(1)} %collective-permute-done.refs_0_.refs_3_, ...), custom_call_target="tpu_custom_call" | custom-call | bytes 4718592 | tf_op jit(solution)/shard_map/cond/branch_1_fun/pallas_call | solution.py:224
  45.9 2.4 %collective-permute-start.4 = (bf16[2,144,1024]{2,1,0:T(8,128)(2,1)}, bf16[2,144,1024]{2,1,0:T(8,128)(2,1)}, u32[]{:S(2)}, u32[]{:S(2)}) collective-permute-start(bf16[2,144,1024]{2,1,0:T(8,128)(2,1)} %get-tuple-element.74), channel_id=1, source_target_pairs={{0,32},{8,40},{16,48},{24,56},{32,64},{40,72},{48,80},{56,88},{64,... | collective-permute-start | bytes 1769480 | tf_op jit(solution)/shard_map/cond/branch_1_fun/ppermute | solution.py:52
  49.2 2.3 %collective-permute-start.7 = (bf16[2,144,1024]{2,1,0:T(8,128)(2,1)}, bf16[2,144,1024]{2,1,0:T(8,128)(2,1)}, u32[]{:S(2)}, u32[]{:S(2)}) collective-permute-start(bf16[2,144,1024]{2,1,0:T(8,128)(2,1)} %get-tuple-element.77), channel_id=1, source_target_pairs={{0,24},{8,0},{16,8},{24,16},{32,56},{40,32},{48,40},{56,48},{64,88... | collective-permute-start | bytes 1769480 | tf_op jit(solution)/shard_map/cond/branch_1_fun/ppermute | solution.py:52
  51.6 5.7 %branch_1_fun.12 = f32[2048,1024]{1,0:T(8,128)S(1)} custom-call(bf16[2048,1024]{1,0:T(8,128)(2,1)S(1)} %copy-done.15, bf16[1024,1024]{1,0:T(8,128)(2,1)S(1)} %copy-done.22), custom_call_target="tpu_custom_call" | custom-call | flops 4294967296 | bytes 14680064 | tf_op jit(solution)/shard_map/cond/branch_1_fun/pallas_call | solution.py:297
  57.3 3.3 %copy-done = f32[2048,1024]{1,0:T(8,128)} copy-done((f32[2048,1024]{1,0:T(8,128)}, f32[2048,1024]{1,0:T(8,128)S(1)}, u32[]{:S(2)}) %copy-start) | copy-done | bytes 8388632 | tf_op jit(solution)/shard_map/cond
  61.2 1.9 %collective-permute-done.6.refs_6_ = bf16[2,144,1024]{2,1,0:T(8,128)(2,1)} collective-permute-done((bf16[2,144,1024]{2,1,0:T(8,128)(2,1)}, bf16[2,144,1024]{2,1,0:T(8,128)(2,1)}, u32[]{:S(2)}, u32[]{:S(2)}) %collective-permute-start.6) | collective-permute-done | bytes 589856 | tf_op jit(solution)/shard_map/cond/branch_1_fun/ppermute | solution.py:52
  63.1 5.2 %all-to-all-start = ((bf16[16,144,1024]{2,1,0:T(8,128)(2,1)}), bf16[16,144,1024]{2,1,0:T(8,128)(2,1)}, u32[]{:S(2)}, u32[]{:S(2)}) async-start(bf16[16,144,1024]{2,1,0:T(8,128)(2,1)} %copy-done.1), calls=%async_computation.1 | async-start | bytes 9437184 | tf_op jit(solution)/shard_map/cond/branch_1_fun/all_to_all | solution.py:583
  72.2 3.0 %branch_1_fun.13 = (bf16[144,1024]{1,0:T(8,128)(2,1)S(1)}, bf16[144,1024]{1,0:T(8,128)(2,1)}, bf16[144,1024]{1,0:T(8,128)(2,1)}, bf16[144,1024]{1,0:T(8,128)(2,1...) custom-call(s32[8,128]{1,0:T(8,128)S(1)} %get-tuple-element.46.mine,, ...), custom_call_target="tpu_custom_call" | custom-call | bytes 4718592 | tf_op jit(solution)/shard_map/cond/branch_1_fun/pallas_call | solution.py:224
  76.7 2.5 %collective-permute-start.10 = (bf16[144,1024]{1,0:T(8,128)(2,1)S(1)}, bf16[144,1024]{1,0:T(8,128)(2,1)S(1)}, u32[]{:S(2)}, u32[]{:S(2)}) collective-permute-start(bf16[144,1024]{1,0:T(8,128)(2,1)S(1)} %get-tuple-element.91), channel_id=1, source_target_pairs={{0,24},{8,0},{16,8},{24,16},{32,56},{40,32},{48,40},{56,48},{64,88... | collective-permute-start | bytes 884744 | tf_op jit(solution)/shard_map/cond/branch_1_fun/ppermute | solution.py:52
  80.4 2.4 %collective-permute-start.12 = (bf16[144,1024]{1,0:T(8,128)(2,1)}, bf16[144,1024]{1,0:T(8,128)(2,1)S(1)}, u32[]{:S(2)}, u32[]{:S(2)}) collective-permute-start(bf16[144,1024]{1,0:T(8,128)(2,1)} %get-tuple-element.93), channel_id=1, source_target_pairs={{0,64},{8,72},{16,80},{24,88},{32,96},{40,104},{48,112},{56,120},{... | collective-permute-start | bytes 884744 | tf_op jit(solution)/shard_map/cond/branch_1_fun/ppermute | solution.py:52
  84.0 40.7 %collective-permute-done.10.refs_3_ = bf16[144,1024]{1,0:T(8,128)(2,1)S(1)} collective-permute-done((bf16[144,1024]{1,0:T(8,128)(2,1)S(1)}, bf16[144,1024]{1,0:T(8,128)(2,1)S(1)}, u32[]{:S(2)}, u32[]{:S(2)}) %collective-permute-start.10) | collective-permute-done | bytes 294944 | tf_op jit(solution)/shard_map/cond/branch_1_fun/ppermute | solution.py:52
  124.7 4.9 %branch_1_fun.14._ = f32[1024,128]{1,0:T(8,128)S(1)} custom-call(s32[8,128]{1,0:T(8,128)S(1)} %get-tuple-element.46.mine, bf16[2048,1024]{1,0:T(8,128)(2,1)} %get-tuple-element.79.hidden, bf16[16,144,1024]{2,1,0:T(8,128)(2,1)} %all-to-all-done.main), custom_call_target="tpu_custom_call" | custom-call | flops 268435456 | bytes 4718592 | tf_op jit(solution)/shard_map/cond/branch_1_fun/pallas_call | solution.py:372
  129.6 3.1 %collective-permute-done.12.refs_6_ = bf16[144,1024]{1,0:T(8,128)(2,1)S(1)} collective-permute-done((bf16[144,1024]{1,0:T(8,128)(2,1)}, bf16[144,1024]{1,0:T(8,128)(2,1)S(1)}, u32[]{:S(2)}, u32[]{:S(2)}) %collective-permute-start.12) | collective-permute-done | bytes 294944 | tf_op jit(solution)/shard_map/cond/branch_1_fun/ppermute | solution.py:52
  135.0 12.7 %collective-permute-start.14 = (f32[512,128]{1,0:T(8,128)S(1)}, f32[512,128]{1,0:T(8,128)S(1)}, u32[]{:S(2)}, u32[]{:S(2)}) collective-permute-start(f32[512,128]{1,0:T(8,128)S(1)} %constant_dynamic-slice_fusion.3), channel_id=1, source_target_pairs={{0,1},{1,0},{2,3},{3,2},{4,5},{5,4},{6,7},{7,6},{8,9},{9,8},{10,11... | collective-permute-start | bytes 786440 | tf_op jit(solution)/shard_map/cond/branch_1_fun/ppermute | solution.py:403
  148.9 1.7 collective-permute-start.15
  150.7 3.3 %collective-permute-start.16 = (f32[128,128]{1,0:T(8,128)S(1)}, f32[128,128]{1,0:T(8,128)S(1)}, u32[]{:S(2)}, u32[]{:S(2)}) collective-permute-start(f32[128,128]{1,0:T(8,128)S(1)} %get-tuple-element.113), channel_id=1, source_target_pairs={{0,4},{1,5},{2,6},{3,7},{4,0},{5,1},{6,2},{7,3},{8,12},{9,13},{10,... | collective-permute-start | bytes 196616 | tf_op jit(solution)/shard_map/cond/branch_1_fun/ppermute | solution.py:407
  154.9 2.0 %collective-permute-done.16 = f32[128,128]{1,0:T(8,128)S(1)} collective-permute-done((f32[128,128]{1,0:T(8,128)S(1)}, f32[128,128]{1,0:T(8,128)S(1)}, u32[]{:S(2)}, u32[]{:S(2)}) %collective-permute-start.16) | collective-permute-done | bytes 65568 | tf_op jit(solution)/shard_map/cond/branch_1_fun/ppermute | solution.py:407
  158.7 1.8 collective-permute-start.20
  161.7 2.7 %collective-permute-done.18 = bf16[128,128]{1,0:T(8,128)(2,1)S(1)} collective-permute-done((bf16[128,128]{1,0:T(8,128)(2,1)S(1)}, bf16[128,128]{1,0:T(8,128)(2,1)S(1)}, u32[]{:S(2)}, u32[]{:S(2)}) %collective-permute-start.18) | collective-permute-done | bytes 32800 | tf_op jit(solution)/shard_map/cond/branch_1_fun/ppermute | solution.py:415
  164.4 3.2 %collective-permute-start.21 = (bf16[4,128,128]{2,1,0:T(8,128)(2,1)S(1)}, bf16[4,128,128]{2,1,0:T(8,128)(2,1)S(1)}, u32[]{:S(2)}, u32[]{:S(2)}) collective-permute-start(bf16[4,128,128]{2,1,0:T(8,128)(2,1)S(1)} %pad_maximum_fusion.own), channel_id=1, source_target_pairs={{0,1},{1,0},{2,3},{3,2},{4,5},{5,4},{6,7},{7,6},{8,9},{9,8},{10,11... | collective-permute-start | bytes 393224 | tf_op jit(solution)/shard_map/cond/branch_1_fun/ppermute | solution.py:416
  169.9 1.6 branch_1_fun.17
  (76 shorter events, 22.4 us)
Async XLA Ops:
  10.7 157.9 %reduce-scatter.5.cloned.1.call-start = ((), (), s32[]{:S(2)}) async-start(), calls=%async_computation.7 | async-start | bytes 9437184 | tf_op jit(solution)/shard_map/cond/branch_1_fun/reduce_scatter | solution.py:582
  12.1 28.6 %collective-permute-start = (bf16[4,144,1024]{2,1,0:T(8,128)(2,1)S(1)}, bf16[4,144,1024]{2,1,0:T(8,128)(2,1)S(1)}, u32[]{:S(2)}, u32[]{:S(2)}) collective-permute-start(bf16[4,144,1024]{2,1,0:T(8,128)(2,1)S(1)} %get-tuple-element.52), channel_id=1, source_target_pairs={{0,32},{8,40},{16,48},{24,56},{32,64},{40,72},{48,80},{56,88},{64,... | collective-permute-start | bytes 3538952 | tf_op jit(solution)/shard_map/cond/branch_1_fun/ppermute | solution.py:52
  14.2 29.3 %collective-permute-start.1 = (bf16[4,144,1024]{2,1,0:T(8,128)(2,1)S(1)}, bf16[4,144,1024]{2,1,0:T(8,128)(2,1)S(1)}, u32[]{:S(2)}, u32[]{:S(2)}) collective-permute-start(bf16[4,144,1024]{2,1,0:T(8,128)(2,1)S(1)} %get-tuple-element.53), channel_id=1, source_target_pairs={{0,96},{8,104},{16,112},{24,120},{32,0},{40,8},{48,16},{56,24},{64... | collective-permute-start | bytes 3538952 | tf_op jit(solution)/shard_map/cond/branch_1_fun/ppermute | solution.py:52
  15.6 28.0 %collective-permute-start.2 = (bf16[4,144,1024]{2,1,0:T(8,128)(2,1)S(1)}, bf16[4,144,1024]{2,1,0:T(8,128)(2,1)S(1)}, u32[]{:S(2)}, u32[]{:S(2)}) collective-permute-start(bf16[4,144,1024]{2,1,0:T(8,128)(2,1)S(1)} %get-tuple-element.54), channel_id=1, source_target_pairs={{0,8},{8,16},{16,24},{24,0},{32,40},{40,48},{48,56},{56,32},{64,72... | collective-permute-start | bytes 3538952 | tf_op jit(solution)/shard_map/cond/branch_1_fun/ppermute | solution.py:52
  17.0 26.5 %collective-permute-start.3 = (bf16[4,144,1024]{2,1,0:T(8,128)(2,1)S(1)}, bf16[4,144,1024]{2,1,0:T(8,128)(2,1)S(1)}, u32[]{:S(2)}, u32[]{:S(2)}) collective-permute-start(bf16[4,144,1024]{2,1,0:T(8,128)(2,1)S(1)} %get-tuple-element.55), channel_id=1, source_target_pairs={{0,24},{8,0},{16,8},{24,16},{32,56},{40,32},{48,40},{56,48},{64,88... | collective-permute-start | bytes 3538952 | tf_op jit(solution)/shard_map/cond/branch_1_fun/ppermute | solution.py:52
  30.5 21.0 %copy-start.6 = (bf16[4,144,1024]{2,1,0:T(8,128)(2,1)}, bf16[4,144,1024]{2,1,0:T(8,128)(2,1)S(1)}, u32[]{:S(2)}) copy-start(bf16[4,144,1024]{2,1,0:T(8,128)(2,1)S(1)} %get-tuple-element.85.refs_5_) | copy-start | bytes 3538948 | tf_op jit(solution)/shard_map/cond
  30.5 21.0 %copy-start.15 = (bf16[2048,1024]{1,0:T(8,128)(2,1)S(1)}, bf16[2048,1024]{1,0:T(8,128)(2,1)}, u32[]{:S(2)}) copy-start(bf16[2048,1024]{1,0:T(8,128)(2,1)} %get-tuple-element.79.hidden) | copy-start | bytes 12582916 | tf_op jit(solution)/shard_map/cond
  30.5 21.1 %copy-start.22 = (bf16[1024,1024]{1,0:T(8,128)(2,1)S(1)}, bf16[1024,1024]{1,0:T(8,128)(2,1)}, u32[]{:S(2)}) copy-start(bf16[1024,1024]{1,0:T(8,128)(2,1)} %get-tuple-element.80.weight) | copy-start | bytes 6291460 | tf_op jit(solution)/shard_map/cond
  43.5 8.1 %copy-start.2 = (bf16[4,144,1024]{2,1,0:T(8,128)(2,1)}, bf16[4,144,1024]{2,1,0:T(8,128)(2,1)S(1)}, u32[]{:S(2)}) copy-start(bf16[4,144,1024]{2,1,0:T(8,128)(2,1)S(1)} %collective-permute-done.3.refs_3_.refs_9_) | copy-start | bytes 3538948 | tf_op jit(solution)/shard_map/cond
  45.9 15.1 %collective-permute-start.4 = (bf16[2,144,1024]{2,1,0:T(8,128)(2,1)}, bf16[2,144,1024]{2,1,0:T(8,128)(2,1)}, u32[]{:S(2)}, u32[]{:S(2)}) collective-permute-start(bf16[2,144,1024]{2,1,0:T(8,128)(2,1)} %get-tuple-element.74), channel_id=1, source_target_pairs={{0,32},{8,40},{16,48},{24,56},{32,64},{40,72},{48,80},{56,88},{64,... | collective-permute-start | bytes 1769480 | tf_op jit(solution)/shard_map/cond/branch_1_fun/ppermute | solution.py:52
  48.2 13.0 %collective-permute-start.5 = (bf16[2,144,1024]{2,1,0:T(8,128)(2,1)}, bf16[2,144,1024]{2,1,0:T(8,128)(2,1)}, u32[]{:S(2)}, u32[]{:S(2)}) collective-permute-start(bf16[2,144,1024]{2,1,0:T(8,128)(2,1)} %get-tuple-element.75), channel_id=1, source_target_pairs={{0,96},{8,104},{16,112},{24,120},{32,0},{40,8},{48,16},{56,24},{64... | collective-permute-start | bytes 1769480 | tf_op jit(solution)/shard_map/cond/branch_1_fun/ppermute | solution.py:52
  48.9 14.2 %collective-permute-start.6 = (bf16[2,144,1024]{2,1,0:T(8,128)(2,1)}, bf16[2,144,1024]{2,1,0:T(8,128)(2,1)}, u32[]{:S(2)}, u32[]{:S(2)}) collective-permute-start(bf16[2,144,1024]{2,1,0:T(8,128)(2,1)} %get-tuple-element.76), channel_id=1, source_target_pairs={{0,8},{8,16},{16,24},{24,0},{32,40},{40,48},{48,56},{56,32},{64,72... | collective-permute-start | bytes 1769480 | tf_op jit(solution)/shard_map/cond/branch_1_fun/ppermute | solution.py:52
  49.2 13.9 %collective-permute-start.7 = (bf16[2,144,1024]{2,1,0:T(8,128)(2,1)}, bf16[2,144,1024]{2,1,0:T(8,128)(2,1)}, u32[]{:S(2)}, u32[]{:S(2)}) collective-permute-start(bf16[2,144,1024]{2,1,0:T(8,128)(2,1)} %get-tuple-element.77), channel_id=1, source_target_pairs={{0,24},{8,0},{16,8},{24,16},{32,56},{40,32},{48,40},{56,48},{64,88... | collective-permute-start | bytes 1769480 | tf_op jit(solution)/shard_map/cond/branch_1_fun/ppermute | solution.py:52
  63.1 61.6 %all-to-all-start = ((bf16[16,144,1024]{2,1,0:T(8,128)(2,1)}), bf16[16,144,1024]{2,1,0:T(8,128)(2,1)}, u32[]{:S(2)}, u32[]{:S(2)}) async-start(bf16[16,144,1024]{2,1,0:T(8,128)(2,1)} %copy-done.1), calls=%async_computation.1 | async-start | bytes 9437184 | tf_op jit(solution)/shard_map/cond/branch_1_fun/all_to_all | solution.py:583
  76.7 48.0 %collective-permute-start.10 = (bf16[144,1024]{1,0:T(8,128)(2,1)S(1)}, bf16[144,1024]{1,0:T(8,128)(2,1)S(1)}, u32[]{:S(2)}, u32[]{:S(2)}) collective-permute-start(bf16[144,1024]{1,0:T(8,128)(2,1)S(1)} %get-tuple-element.91), channel_id=1, source_target_pairs={{0,24},{8,0},{16,8},{24,16},{32,56},{40,32},{48,40},{56,48},{64,88... | collective-permute-start | bytes 884744 | tf_op jit(solution)/shard_map/cond/branch_1_fun/ppermute | solution.py:52
  79.2 50.4 %collective-permute-start.11 = (bf16[144,1024]{1,0:T(8,128)(2,1)}, bf16[144,1024]{1,0:T(8,128)(2,1)S(1)}, u32[]{:S(2)}, u32[]{:S(2)}) collective-permute-start(bf16[144,1024]{1,0:T(8,128)(2,1)} %get-tuple-element.92), channel_id=1, source_target_pairs={{0,32},{8,40},{16,48},{24,56},{32,64},{40,72},{48,80},{56,88},{64,... | collective-permute-start | bytes 884744 | tf_op jit(solution)/shard_map/cond/branch_1_fun/ppermute | solution.py:52
  80.4 52.3 %collective-permute-start.12 = (bf16[144,1024]{1,0:T(8,128)(2,1)}, bf16[144,1024]{1,0:T(8,128)(2,1)S(1)}, u32[]{:S(2)}, u32[]{:S(2)}) collective-permute-start(bf16[144,1024]{1,0:T(8,128)(2,1)} %get-tuple-element.93), channel_id=1, source_target_pairs={{0,64},{8,72},{16,80},{24,88},{32,96},{40,104},{48,112},{56,120},{... | collective-permute-start | bytes 884744 | tf_op jit(solution)/shard_map/cond/branch_1_fun/ppermute | solution.py:52
  82.8 49.9 %collective-permute-start.13 = (bf16[144,1024]{1,0:T(8,128)(2,1)}, bf16[144,1024]{1,0:T(8,128)(2,1)S(1)}, u32[]{:S(2)}, u32[]{:S(2)}) collective-permute-start(bf16[144,1024]{1,0:T(8,128)(2,1)} %get-tuple-element.94), channel_id=1, source_target_pairs={{0,96},{8,104},{16,112},{24,120},{32,0},{40,8},{48,16},{56,24},{64... | collective-permute-start | bytes 884744 | tf_op jit(solution)/shard_map/cond/branch_1_fun/ppermute | solution.py:52
  84.0 48.7 %collective-permute-start.8 = (bf16[144,1024]{1,0:T(8,128)(2,1)}, bf16[144,1024]{1,0:T(8,128)(2,1)S(1)}, u32[]{:S(2)}, u32[]{:S(2)}) collective-permute-start(bf16[144,1024]{1,0:T(8,128)(2,1)} %get-tuple-element.89), channel_id=1, source_target_pairs={{0,8},{8,16},{16,24},{24,0},{32,40},{40,48},{48,56},{56,32},{64,72... | collective-permute-start | bytes 884744 | tf_op jit(solution)/shard_map/cond/branch_1_fun/ppermute | solution.py:52
  124.7 8.6 %collective-permute-start.9 = (bf16[144,1024]{1,0:T(8,128)(2,1)}, bf16[144,1024]{1,0:T(8,128)(2,1)S(1)}, u32[]{:S(2)}, u32[]{:S(2)}) collective-permute-start(bf16[144,1024]{1,0:T(8,128)(2,1)} %get-tuple-element.90), channel_id=1, source_target_pairs={{0,16},{8,24},{16,0},{24,8},{32,48},{40,56},{48,32},{56,40},{64,80... | collective-permute-start | bytes 884744 | tf_op jit(solution)/shard_map/cond/branch_1_fun/ppermute | solution.py:52
  124.7 8.6 %copy-start.10 = (bf16[144,1024]{1,0:T(8,128)(2,1)S(1)}, bf16[144,1024]{1,0:T(8,128)(2,1)}, u32[]{:S(2)}) copy-start(bf16[144,1024]{1,0:T(8,128)(2,1)} %copy-done.9) | copy-start | bytes 884740 | tf_op jit(solution)/shard_map/cond
  124.7 8.6 %copy-start.12 = (bf16[144,1024]{1,0:T(8,128)(2,1)S(1)}, bf16[144,1024]{1,0:T(8,128)(2,1)}, u32[]{:S(2)}) copy-start(bf16[144,1024]{1,0:T(8,128)(2,1)} %copy-done.11) | copy-start | bytes 884740 | tf_op jit(solution)/shard_map/cond
  124.7 9.3 %copy-start.16 = (bf16[2048,1024]{1,0:T(8,128)(2,1)S(1)}, bf16[2048,1024]{1,0:T(8,128)(2,1)}, u32[]{:S(2)}) copy-start(bf16[2048,1024]{1,0:T(8,128)(2,1)} %get-tuple-element.79.hidden) | copy-start | bytes 12582916 | tf_op jit(solution)/shard_map/cond
  134.0 34.6 %copy-start.21 = (s32[512]{0:T(512)S(1)}, s32[512]{0:T(512)}, u32[]{:S(2)}) copy-start(s32[512]{0:T(512)} %get-tuple-element.47.counts) | copy-start | bytes 6148 | tf_op jit(solution)/shard_map/cond
  135.0 13.9 %collective-permute-start.14 = (f32[512,128]{1,0:T(8,128)S(1)}, f32[512,128]{1,0:T(8,128)S(1)}, u32[]{:S(2)}, u32[]{:S(2)}) collective-permute-start(f32[512,128]{1,0:T(8,128)S(1)} %constant_dynamic-slice_fusion.3), channel_id=1, source_target_pairs={{0,1},{1,0},{2,3},{3,2},{4,5},{5,4},{6,7},{7,6},{8,9},{9,8},{10,11... | collective-permute-start | bytes 786440 | tf_op jit(solution)/shard_map/cond/branch_1_fun/ppermute | solution.py:403
  148.9 6.0 %collective-permute-start.15 = (f32[128,128]{1,0:T(8,128)S(1)}, f32[128,128]{1,0:T(8,128)S(1)}, u32[]{:S(2)}, u32[]{:S(2)}) collective-permute-start(f32[128,128]{1,0:T(8,128)S(1)} %get-tuple-element.115), channel_id=1, source_target_pairs={{0,2},{1,3},{2,4},{3,5},{4,6},{5,7},{6,0},{7,1},{8,10},{9,11},{10,... | collective-permute-start | bytes 196616 | tf_op jit(solution)/shard_map/cond/branch_1_fun/ppermute | solution.py:407
  150.7 6.3 %collective-permute-start.16 = (f32[128,128]{1,0:T(8,128)S(1)}, f32[128,128]{1,0:T(8,128)S(1)}, u32[]{:S(2)}, u32[]{:S(2)}) collective-permute-start(f32[128,128]{1,0:T(8,128)S(1)} %get-tuple-element.113), channel_id=1, source_target_pairs={{0,4},{1,5},{2,6},{3,7},{4,0},{5,1},{6,2},{7,3},{8,12},{9,13},{10,... | collective-permute-start | bytes 196616 | tf_op jit(solution)/shard_map/cond/branch_1_fun/ppermute | solution.py:407
  154.0 3.4 %collective-permute-start.17 = (f32[128,128]{1,0:T(8,128)S(1)}, f32[128,128]{1,0:T(8,128)S(1)}, u32[]{:S(2)}, u32[]{:S(2)}) collective-permute-start(f32[128,128]{1,0:T(8,128)S(1)} %get-tuple-element.114), channel_id=1, source_target_pairs={{0,6},{1,7},{2,0},{3,1},{4,2},{5,3},{6,4},{7,5},{8,14},{9,15},{10,... | collective-permute-start | bytes 196616 | tf_op jit(solution)/shard_map/cond/branch_1_fun/ppermute | solution.py:407
  157.4 4.3 %collective-permute-start.19 = (bf16[128,128]{1,0:T(8,128)(2,1)S(1)}, bf16[128,128]{1,0:T(8,128)(2,1)S(1)}, u32[]{:S(2)}, u32[]{:S(2)}) collective-permute-start(bf16[128,128]{1,0:T(8,128)(2,1)S(1)} %add_convert_fusion), channel_id=1, source_target_pairs={{0,4},{1,5},{2,6},{3,7},{4,0},{5,1},{6,2},{7,3},{8,12},{9,13},{10,... | collective-permute-start | bytes 98312 | tf_op jit(solution)/shard_map/cond/branch_1_fun/ppermute | solution.py:415
  158.7 3.1 %collective-permute-start.20 = (bf16[128,128]{1,0:T(8,128)(2,1)S(1)}, bf16[128,128]{1,0:T(8,128)(2,1)S(1)}, u32[]{:S(2)}, u32[]{:S(2)}) collective-permute-start(bf16[128,128]{1,0:T(8,128)(2,1)S(1)} %add_convert_fusion), channel_id=1, source_target_pairs={{0,6},{1,7},{2,0},{3,1},{4,2},{5,3},{6,4},{7,5},{8,14},{9,15},{10,... | collective-permute-start | bytes 98312 | tf_op jit(solution)/shard_map/cond/branch_1_fun/ppermute | solution.py:415
  160.4 4.0 %collective-permute-start.18 = (bf16[128,128]{1,0:T(8,128)(2,1)S(1)}, bf16[128,128]{1,0:T(8,128)(2,1)S(1)}, u32[]{:S(2)}, u32[]{:S(2)}) collective-permute-start(bf16[128,128]{1,0:T(8,128)(2,1)S(1)} %add_convert_fusion), channel_id=1, source_target_pairs={{0,2},{1,3},{2,4},{3,5},{4,6},{5,7},{6,0},{7,1},{8,10},{9,11},{10,... | collective-permute-start | bytes 98312 | tf_op jit(solution)/shard_map/cond/branch_1_fun/ppermute | solution.py:415
  164.4 4.2 %collective-permute-start.21 = (bf16[4,128,128]{2,1,0:T(8,128)(2,1)S(1)}, bf16[4,128,128]{2,1,0:T(8,128)(2,1)S(1)}, u32[]{:S(2)}, u32[]{:S(2)}) collective-permute-start(bf16[4,128,128]{2,1,0:T(8,128)(2,1)S(1)} %pad_maximum_fusion.own), channel_id=1, source_target_pairs={{0,1},{1,0},{2,3},{3,2},{4,5},{5,4},{6,7},{7,6},{8,9},{9,8},{10,11... | collective-permute-start | bytes 393224 | tf_op jit(solution)/shard_map/cond/branch_1_fun/ppermute | solution.py:416
  (12 other events, 29.2 us)
Sparse Core Ops, SparseCore 0:
  63.3 55.9 reduce-scatter.4
